TPU v7x, 32 devices: a whole 2x2x4 slice. The times are simulated.
32 devices in a mesh: mol: 2 (over y), pair: 4 (over z), aux: 4 (over x, core).
Axes of the slice: x: 2, y: 2, z: 4, core: 2. Of those that a mesh axis runs over, the one named last changes fastest.
Arguments:
- ints: bfloat16 [16, 6144, 128], P(('mol', 'pair'), 'aux'), parts along dimension 0, may hold values from -1.75 to 1.75
- proj_first: bfloat16 [128, 128, 128], P(('mol', 'pair')), parts along dimension 0, may hold values from -0.5 to 0.5
- proj_second: bfloat16 [128, 128, 128], P(('mol', 'pair')), parts along dimension 0, may hold values from -0.5 to 0.5
- intersections: bfloat16 [128, 4, 128, 128], P(('mol', 'pair')), parts along dimension 0, may hold values from -0.5 to 0.5
- couple: float32 [128, 4], P(('mol', 'pair')), parts along dimension 0, may hold values from -1.2 to 1.2
- virt_energy: float32 [128, 128], P(('mol', 'pair')), parts along dimension 0, may hold values from 0.2 to 3
- occ_energy: float32 [128, 2], P(('mol', 'pair')), parts along dimension 0, may hold values from -1.2 to -0.2
- pno_count: int32 [128], P(('mol', 'pair')), parts along dimension 0, may hold values from 64 to 128, as said below
- pair_orbitals: int32 [128, 2], P(('mol', 'pair')), parts along dimension 0, may hold values from 0 to 7, as said below
- neighbours: int32 [128, 4], P('mol'), parts along dimension 0, may hold values from 0 to 63, as said below
Outputs:
- amps: float32 [128, 128, 128], P(('mol', 'pair')), parts along dimension 0
- density: float32 [16, 128, 128], P(('mol', 'pair')), parts along dimension 0
There are 2 independent parts, one for each index of `mol`. A program takes and returns all parts, laid end to end along the dimension named above; each array names one. Nothing has to cross between parts.
Inputs may be any that keep to these rules, and one draw needn't show every extreme that they name: `pno_count`: used slots are at least half of 128; some pair uses all 128. `pair_orbitals`: orbitals come in blocks of 2, pairs in aligned blocks of 16. The first orbital of a pair in pair block b lies in orbital block b; the second lies in block b - 1, b or b + 1 and differs from the first. In every pair block some second orbital lies in the block below and some in the block above, where those exist. `neighbours`: all coupled pairs listed for the 16 pairs of one aligned block b lie in 3 consecutive aligned blocks of pairs that contain b, centered on b where the ends of the pair list allow. At most 32 of them lie in any one aligned block, and for every block some aligned block supplies exactly 32.
All inputs are finite; a program needn't handle non-finite values.
Results may differ from a plain program's by a relative error of at most 0.0043.
Values may be sent and summed in bfloat16 or wider, within the bound.
No kernel may reach another device: no remote copies, remote signals or barrier semaphores. Data moves between devices by JAX's collectives and lax.ppermute only.
A program may use at most 64 MiB of HBM per device.

v0:
```python
import jax
import jax.numpy as jnp
from jax import lax
from jax.sharding import PartitionSpec as P

ITERS = 2


HIGH = lax.Precision.HIGHEST


def padded(cells, sides, width):
    for axis, dim in sides:
        count = lax.axis_size(axis)
        ends = count - 1
        head = lax.slice_in_dim(cells, 0, width, axis=dim)
        tail = lax.slice_in_dim(cells, cells.shape[dim] - width, cells.shape[dim], axis=dim)
        cells = jnp.concatenate(
            [
                lax.ppermute(tail, axis, [(i, (i + 1) % count) for i in range(ends)]),
                cells,
                lax.ppermute(head, axis, [((i + 1) % count, i) for i in range(ends)]),
            ],
            axis=dim,
        )
    return cells


def from_behind(value, axis, steps):
    count = lax.axis_size(axis)
    first, last = (max(0, -steps), min(count, count - steps))
    return lax.ppermute(value, axis, [(source, source + steps) for source in range(first, last)])


def same_owner_rank(owners):
    count = owners.shape[-1]
    places = jnp.arange(count)
    earlier = places[:, None] > places[None, :]
    same = owners[..., :, None] == owners[..., None, :]
    return jnp.sum(same & earlier, axis=-1)


def shards(
    ints,
    proj_first,
    proj_second,
    intersections,
    couple,
    virt_energy,
    occ_energy,
    pno_count,
    pair_orbitals,
    neighbours,
):
    groups = lax.axis_size("pair")
    here = lax.axis_index("pair")
    occ_dev = ints.shape[0]
    pair_dev = proj_first.shape[0]
    width = proj_first.shape[1]
    nbr_count = couple.shape[1]
    wanted = pair_dev * nbr_count
    cap = 2 * wanted // groups
    window = padded(ints, (("pair", 0),), occ_dev)
    base = (here - 1) * occ_dev
    first_slot = pair_orbitals[:, 0] - base
    second_slot = pair_orbitals[:, 1] - base

    def pair_block(item):
        first, second, left_map, right_map = item
        left = jnp.dot(window[first], left_map, preferred_element_type=jnp.float32).astype(
            jnp.bfloat16
        )
        right = jnp.dot(window[second], right_map, preferred_element_type=jnp.float32).astype(
            jnp.bfloat16
        )
        return lax.dot_general(
            left, right, (((0,), (0,)), ((), ())), preferred_element_type=jnp.float32
        )

    exch = lax.psum(lax.map(pair_block, (first_slot, second_slot, proj_first, proj_second)), "aux")
    valid = jnp.arange(width)[None, :] < pno_count[:, None]
    mask = (valid[:, :, None] & valid[:, None, :]).astype(jnp.float32)
    denom = (
        virt_energy[:, :, None]
        + virt_energy[:, None, :]
        - occ_energy[:, 0, None, None]
        - occ_energy[:, 1, None, None]
    )
    amps = -mask * exch / denom
    requests = neighbours.reshape(groups, wanted)
    owners = requests // pair_dev
    ranks = same_owner_rank(owners)
    at_home = owners == here
    slot_ids = jnp.arange(cap)
    pick = at_home[:, None, :] & (ranks[:, None, :] == slot_ids[None, :, None])
    local = requests % pair_dev
    select = jnp.any(
        pick[..., None] & (local[:, None, :, None] == jnp.arange(pair_dev)[None, None, None, :]),
        axis=2,
    )
    select = select.astype(jnp.bfloat16).reshape(groups * cap, pair_dev)
    own_requests = lax.dynamic_slice_in_dim(requests, here, 1, 0)[0]
    own_ranks = lax.dynamic_slice_in_dim(ranks, here, 1, 0)[0]
    row_index = own_requests // pair_dev * cap + own_ranks
    over_flat = intersections.reshape(pair_dev * nbr_count, width, width)
    for sweep in range(ITERS):
        low = amps.astype(jnp.bfloat16)
        flat = low.reshape(pair_dev, width * width)
        outgoing = jnp.dot(select, flat, preferred_element_type=jnp.float32).astype(jnp.bfloat16)
        outgoing = outgoing.reshape(groups, cap, width, width)
        received = lax.all_to_all(outgoing, "pair", split_axis=0, concat_axis=0, tiled=True)
        taken = received.reshape(groups * cap, width, width)[row_index]
        half = jnp.einsum(
            "kab,kbc->kac", over_flat, taken, preferred_element_type=jnp.float32
        ).astype(jnp.bfloat16)
        full = jnp.einsum("kac,kdc->kad", half, over_flat, preferred_element_type=jnp.float32)
        full = full.reshape(pair_dev, nbr_count, width, width)
        coupled = jnp.sum(couple[:, :, None, None] * full, axis=1)
        amps = -mask * (exch - coupled) / denom
    left_full = proj_first.astype(jnp.float32)
    right_full = proj_second.astype(jnp.float32)
    outer = jnp.einsum("pab,pcb->pac", amps, amps, precision=HIGH)
    inner = jnp.einsum("pba,pbc->pac", amps, amps, precision=HIGH)
    first_terms = jnp.einsum(
        "pac,pdc->pad",
        jnp.einsum("pab,pbc->pac", left_full, outer, precision=HIGH),
        left_full,
        precision=HIGH,
    )
    second_terms = jnp.einsum(
        "pac,pdc->pad",
        jnp.einsum("pab,pbc->pac", right_full, inner, precision=HIGH),
        right_full,
        precision=HIGH,
    )
    spots = jnp.arange(3 * occ_dev)
    hit_first = (spots[:, None] == first_slot[None, :]).astype(jnp.float32)
    hit_second = (spots[:, None] == second_slot[None, :]).astype(jnp.float32)
    collected = jnp.einsum("wp,pab->wab", hit_first, first_terms, precision=HIGH) + jnp.einsum(
        "wp,pab->wab", hit_second, second_terms, precision=HIGH
    )
    middle = collected[occ_dev : 2 * occ_dev]
    from_below = from_behind(collected[2 * occ_dev :], "pair", 1)
    from_above = from_behind(collected[:occ_dev], "pair", -1)
    density = (middle + from_below + from_above) / width
    return (amps, density)


def solution(mesh):
    return jax.shard_map(
        shards,
        mesh=mesh,
        in_specs=(
            P(("mol", "pair"), "aux", None),
            P(("mol", "pair"), None, None),
            P(("mol", "pair"), None, None),
            P(("mol", "pair"), None, None, None),
            P(("mol", "pair"), None),
            P(("mol", "pair"), None),
            P(("mol", "pair"), None),
            P(("mol", "pair")),
            P(("mol", "pair"), None),
            P("mol", None),
        ),
        out_specs=(P(("mol", "pair"), None, None), P(("mol", "pair"), None, None)),
        check_vma=False,
    )
```

profile of v0, /device:TPU:15, one launch (start us, length us, event | category | flops | bytes accessed | tf_op | source)
XLA Modules:
  0.0 464.9 jit_solution(2451277184772283894)
XLA Ops:
  7.2 3.3 collective-permute-start
  10.6 2.1 collective-permute-start.1
  14.7 13.3 %collective-permute-done = bf16[2,1536,128]{2,1,0:T(8,128)(2,1)S(1)} collective-permute-done((bf16[2,1536,128]{2,1,0:T(8,128)(2,1)}, bf16[2,1536,128]{2,1,0:T(8,128)(2,1)S(1)}, u32[]{:S(2)}, u32[]{:S(2)}) %collective-permute-start) | collective-permute-done | bytes 786464 | tf_op jit(solution)/shard_map/ppermute | solution.py:20
  28.0 2.9 collective-permute-done.1
  30.9 3.0 pad_maximum_fusion
  33.9 142.3 %while.10 = (s32[]{:T(128)}, f32[16,128,128]{2,1,0:T(8,128)}, s32[16]{0:T(128)S(1)}, bf16[6,1536,128]{2,1,0:T(8,128)(2,1)}, bf16[16,128,128]{2,1,0:T(8,128)(2,1)...) while((s32[]{:T(128)}, f32[16,128,128]{2,1,0:T(8,128)}, ...), condition=%wide.region_1.2_spmd, body=%wide.region_0.1_spmd.sunk | while | flops 151388160 | bytes 1705673 | solution.py:80
  36.7 1.2 convolution_convert_fusion.5
  40.6 2.2 fusion.85
  45.5 1.3 convolution_convert_fusion.5
  49.5 2.2 fusion.85
  54.4 1.3 convolution_convert_fusion.5
  58.5 2.2 fusion.85
  63.4 1.2 convolution_convert_fusion.5
  67.3 2.2 fusion.85
  72.2 1.2 convolution_convert_fusion.5
  76.2 2.2 fusion.85
  81.1 1.2 convolution_convert_fusion.5
  85.1 2.2 fusion.85
  90.0 1.3 convolution_convert_fusion.5
  94.0 2.2 fusion.85
  98.9 1.3 convolution_convert_fusion.5
  102.9 2.2 fusion.85
  107.8 1.3 convolution_convert_fusion.5
  111.8 2.2 fusion.85
  116.7 1.2 convolution_convert_fusion.5
  120.7 2.2 fusion.85
  125.6 1.2 convolution_convert_fusion.5
  129.6 2.2 fusion.85
  134.5 1.2 convolution_convert_fusion.5
  138.5 2.2 fusion.85
  143.4 1.3 convolution_convert_fusion.5
  147.4 2.2 fusion.85
  152.3 1.3 convolution_convert_fusion.5
  156.3 2.2 fusion.85
  161.2 1.3 convolution_convert_fusion.5
  165.2 2.2 fusion.85
  170.1 1.2 convolution_convert_fusion.5
  174.1 2.2 fusion.85
  176.3 2.3 and_reduce_fusion
  178.7 34.4 %all-reduce.2.cloned.1.call-done = f32[16,128,128]{2,1,0:T(8,128)} async-done(((f32[16,128,128]{2,1,0:T(8,128)}), f32[16,128,128]{2,1,0:T(8,128)}) %all-reduce.2.cloned.1.call-update) | async-done | bytes 1048592 | tf_op jit(solution)/shard_map/psum | solution.py:80
  213.1 1.8 divide_convert_fusion.1
  214.9 1.2 fusion.18
  216.1 3.2 copy.53
  219.4 5.2 %all-to-all-start = ((bf16[4,32,128,128]{3,2,1,0:T(8,128)(2,1)}), bf16[4,32,128,128]{3,2,1,0:T(8,128)(2,1)}, u32[]{:S(2)}, u32[]{:S(2)}) async-start(bf16[4,32,128,128]{3,2,1,0:T(8,128)(2,1)} %bitcast.113), calls=%async_computation | async-start | bytes 8388608 | tf_op jit(solution)/shard_map/all_to_all | solution.py:111
  224.7 89.3 %all-to-all-done = bf16[4,32,128,128]{3,2,1,0:T(8,128)(2,1)} async-done(((bf16[4,32,128,128]{3,2,1,0:T(8,128)(2,1)}), bf16[4,32,128,128]{3,2,1,0:T(8,128)(2,1)}, u32[]{:S(2)}, u32[]{:S(2)}) %all-to-all-start) | async-done | bytes 4194336 | tf_op jit(solution)/shard_map/all_to_all | solution.py:111
  314.0 4.3 gather_fusion
  318.3 5.7 %multiply_reduce_fusion.1 = f32[16,128,128]{2,1,0:T(8,128)} fusion(f32[16,4]{1,0:T(8,128)S(1)} %copy.29, bf16[64,128,128]{2,1,0:T(8,128)(2,1)S(1)} %bitcast.112, bf16[64,128,128]{2,1,0:T(8,128)(2,1)} %gather_fusion), kind=kOutput, calls=%fused_computation.20 | convolution fusion | flops 539754496 | bytes 5243136 | tf_op jit(solution)/shard_map/kac,kdc->kad/dot_general | solution.py:116
  323.9 1.8 divide_convert_fusion
  325.7 1.2 fusion.19
  327.0 1.2 copy.55
  328.2 97.1 %all_to_all.10 = bf16[4,32,128,128]{3,2,1,0:T(8,128)(2,1)} all-to-all(bf16[4,32,128,128]{3,2,1,0:T(8,128)(2,1)S(1)} %bitcast.114), channel_id=1, replica_groups=mesh['mol'=2,'pair'=4,'aux'=4] {'pair'}, dimensions={0} | all-to-all | bytes 8388608 | tf_op jit(solution)/shard_map/all_to_all | solution.py:111
  425.3 4.3 gather_fusion.1
  429.6 5.6 %multiply_reduce_fusion = f32[16,128,128]{2,1,0:T(8,128)} fusion(f32[16,4]{1,0:T(8,128)S(1)} %copy.29, bf16[64,128,128]{2,1,0:T(8,128)(2,1)S(1)} %bitcast.111, bf16[64,128,128]{2,1,0:T(8,128)(2,1)} %gather_fusion.1), kind=kOutput, calls=%fused_computation.19 | convolution fusion | flops 539754496 | bytes 5243136 | tf_op jit(solution)/shard_map/kac,kdc->kad/dot_general | solution.py:116
  435.2 1.8 multiply_divide_fusion
  437.0 2.3 fusion.47
  439.3 1.8 fusion.50
  441.2 1.2 fusion.48
  442.4 1.2 fusion.49
  444.7 1.2 fusion.51
  445.9 1.2 fusion.52
  447.1 1.1 convolution_add_fusion
  448.3 2.8 collective-permute-start.2
  451.1 2.4 collective-permute-start.3
  454.0 3.3 collective-permute-done.3
  (72 shorter events, 25.9 us)
Async XLA Ops:
  7.2 311.1 %copy-start = (bf16[16,4,128,128]{3,2,1,0:T(8,128)(2,1)S(1)}, bf16[16,4,128,128]{3,2,1,0:T(8,128)(2,1)}, u32[]{:S(2)}) copy-start(bf16[16,4,128,128]{3,2,1,0:T(8,128)(2,1)} %param.15) | copy-start | bytes 6291460
  7.2 205.9 %all-reduce.2.cloned.1.call-start = ((), (), s32[]{:S(2)}) async-start(), calls=%async_computation.2 | async-start | bytes 2097152 | tf_op jit(solution)/shard_map/psum | solution.py:80
  7.2 20.8 %collective-permute-start = (bf16[2,1536,128]{2,1,0:T(8,128)(2,1)}, bf16[2,1536,128]{2,1,0:T(8,128)(2,1)S(1)}, u32[]{:S(2)}, u32[]{:S(2)}) collective-permute-start(bf16[2,1536,128]{2,1,0:T(8,128)(2,1)} %param.12), channel_id=1, source_target_pairs={{0,4},{4,8},{8,12},{1,5},{5,9},{9,13},{2,6},{6,10},{10,14},{3,7},{... | collective-permute-start | bytes 2359304 | tf_op jit(solution)/shard_map/ppermute | solution.py:20
  10.6 20.3 %collective-permute-start.1 = (bf16[2,1536,128]{2,1,0:T(8,128)(2,1)}, bf16[2,1536,128]{2,1,0:T(8,128)(2,1)}, u32[]{:S(2)}, u32[]{:S(2)}) collective-permute-start(bf16[2,1536,128]{2,1,0:T(8,128)(2,1)} %param.12), channel_id=1, source_target_pairs={{4,0},{8,4},{12,8},{5,1},{9,5},{13,9},{6,2},{10,6},{14,10},{7,3},{... | collective-permute-start | bytes 2359304 | tf_op jit(solution)/shard_map/ppermute | solution.py:22
  33.9 144.7 %copy-start.7 = (f32[16,2]{0,1:T(2,128)S(1)}, f32[16,2]{0,1:T(2,128)}, u32[]{:S(2)}) copy-start(f32[16,2]{0,1:T(2,128)} %param.18) | copy-start | bytes 388
  33.9 144.7 %copy-start.8 = (s32[16]{0:T(128)S(1)}, s32[16]{0:T(128)}, u32[]{:S(2)}) copy-start(s32[16]{0:T(128)} %param.19) | copy-start | bytes 196
  33.9 179.2 %copy-start.5 = (f32[16,128]{1,0:T(8,128)S(1)}, f32[16,128]{1,0:T(8,128)}, u32[]{:S(2)}) copy-start(f32[16,128]{1,0:T(8,128)} %param.17) | copy-start | bytes 24580
  219.4 5.2 %copy-start.6 = (f32[16,4]{0,1:T(4,128)S(1)}, f32[16,4]{0,1:T(4,128)}, u32[]{:S(2)}) copy-start(f32[16,4]{0,1:T(4,128)} %param.16) | copy-start | bytes 772
  219.4 94.6 %all-to-all-start = ((bf16[4,32,128,128]{3,2,1,0:T(8,128)(2,1)}), bf16[4,32,128,128]{3,2,1,0:T(8,128)(2,1)}, u32[]{:S(2)}, u32[]{:S(2)}) async-start(bf16[4,32,128,128]{3,2,1,0:T(8,128)(2,1)} %bitcast.113), calls=%async_computation | async-start | bytes 8388608 | tf_op jit(solution)/shard_map/all_to_all | solution.py:111
  318.3 5.7 %copy-start.2 = (f32[16,128,128]{2,1,0:T(8,128)S(1)}, f32[16,128,128]{2,1,0:T(8,128)}, u32[]{:S(2)}) copy-start(f32[16,128,128]{2,1,0:T(8,128)} %all-reduce.2.cloned.1.call-done) | copy-start | bytes 3145732
  437.0 4.1 copy-start.1
  439.3 1.8 copy-start.4
  442.4 2.3 copy-start.3
  448.3 5.7 %collective-permute-start.2 = (f32[2,128,128]{2,0,1:T(2,128)S(1)}, f32[2,128,128]{2,0,1:T(2,128)S(1)}, u32[]{:S(2)}, u32[]{:S(2)}) collective-permute-start(f32[2,128,128]{2,0,1:T(2,128)S(1)} %get-tuple-element.64), channel_id=1, source_target_pairs={{0,4},{4,8},{8,12},{1,5},{5,9},{9,13},{2,6},{6,10},{10,14},{3,7},{... | collective-permute-start | bytes 393224 | tf_op jit(solution)/shard_map/ppermute | solution.py:32
  451.1 6.1 %collective-permute-start.3 = (f32[2,128,128]{2,0,1:T(2,128)S(1)}, f32[2,128,128]{2,0,1:T(2,128)S(1)}, u32[]{:S(2)}, u32[]{:S(2)}) collective-permute-start(f32[2,128,128]{2,0,1:T(2,128)S(1)} %get-tuple-element.65), channel_id=1, source_target_pairs={{4,0},{8,4},{12,8},{5,1},{9,5},{13,9},{6,2},{10,6},{14,10},{7,3},{... | collective-permute-start | bytes 393224 | tf_op jit(solution)/shard_map/ppermute | solution.py:32
Sparse Core Ops, SparseCore 0:
  176.4 36.6 all-reduce.1
where the time goes:
time: 472 us; the launch traced here: 465 us
  waiting for transfers between devices  144 us (31%)
  blocking collectives  97.1 us (21%)
  matrix products  79.3 us (17%)
  loops' own time  66.4 us (14%)
  local copies, waits for them, and re-layouts  36.2 us (8%)
  starting transfers between devices  16 us (3%)
  between operations  14.3 us (3%)
  other arithmetic  12 us (3%)
    all_to_all x1, blocking collectives, shards(): lax.all_to_all(outgoing, 'pair', split_axis=0, concat_axis=0, tiled=True)  97.1 us
    all_to_all x1, waiting for transfers between devices, shards(): lax.all_to_all(outgoing, 'pair', split_axis=0, concat_axis=0, tiled=True)  89.3 us
    another operation x1, loops' own time, shards(): lax.map(pair_block, (first_slot, second_slot, proj_first, proj_second))  66.4 us
    dot_general x16, matrix products, pair_block(): lax.dot_general(left, right, (((0,), (0,)), ((), ())), preferred_element_...  34.6 us
    psum x1, waiting for transfers between devices, shards(): lax.psum(lax.map(pair_block, (first_slot, second_slot, proj_first, proj_s...  34.4 us
    dynamic_slice x32, local copies, waits for them, and re-layouts, shards(): lax.map(pair_block, (first_slot, second_slot, proj_first, proj_second))  21.3 us
    dot_general x16, matrix products, pair_block(): jnp.dot(window[second], right_map, preferred_element_type=jnp.float32)  20 us
    ppermute x1, waiting for transfers between devices, padded(): lax.ppermute(tail, axis, [(i, (i + 1) % count) for i in range(ends)])  13.3 us
  transfers between devices with their start and end apart: 6, of which 6 were waited for; matrix products, arithmetic and copies ran while one was open for 1% of the time, Pallas kernels for 0%

commit v1 on v0

v1 whole, which is shorter than its diff:
```python
import functools

import jax
import jax.numpy as jnp
import numpy as np
from jax import lax
from jax.experimental import pallas as pl
from jax.experimental.pallas import tpu as pltpu
from jax.sharding import PartitionSpec as P

ITERS = 2
BF16 = jnp.bfloat16
F32 = jnp.float32
VMEM = pl.BlockSpec(memory_space=pltpu.VMEM)
SMEM = pl.BlockSpec(memory_space=pltpu.SMEM)
ANY = pl.BlockSpec(memory_space=pl.ANY)
PARAMS = pltpu.CompilerParams(vmem_limit_bytes=24 * 2**20)


def dot(left, right, dims):
    return lax.dot_general(left, right, (dims, ((), ())), preferred_element_type=F32)


def split(value):
    high = value.astype(BF16)
    return high, (value - high.astype(F32)).astype(BF16)


def cost(flops, size):
    return pl.CostEstimate(flops=flops, bytes_accessed=size, transcendentals=0)


def product_kernel(with_own, own_ref, up_ref, down_ref, out_ref):
    count, _, width = own_ref.shape
    own = jnp.concatenate([own_ref[i] for i in range(count)], axis=1)
    near = jnp.concatenate([up_ref[0], down_ref[0]], axis=1)
    full = dot(own, near, ((0,), (0,)))
    for i in range(count):
        rows = full[i * width : (i + 1) * width]
        out_ref[i, :width] = rows[:, :width]
        out_ref[i, width : 2 * width] = rows[:, width:]
    if with_own:
        half = width // 2
        inner = dot(own_ref[0], own_ref[1], ((0,), (0,)))
        out_ref[0, 2 * width :] = inner[:half]
        out_ref[1, 2 * width :] = inner[half:]


def products(ints, up, down, with_own):
    count, depth, width = ints.shape
    rows = 2 * width + (width // 2 if with_own else 0)
    return pl.pallas_call(
        functools.partial(product_kernel, with_own),
        out_shape=jax.ShapeDtypeStruct((count, rows, width), F32),
        in_specs=[VMEM] * 3,
        out_specs=VMEM,
        compiler_params=PARAMS,
        cost_estimate=cost(8 * depth * width * width, 8 * depth * width),
        name="products",
    )(ints, up, down)


def exchange_kernel(
    slots_ref, half_ref, *refs
):
    count = slots_ref.shape[0]
    sums = refs[:8]
    first_ref, second_ref, factor_ref, exch_ref, low_ref, table = refs[8:]
    width = first_ref.shape[-1]
    mine = half_ref[0]
    for side in range(2):
        one = sums[4 * side][...] + sums[4 * side + 1][...]
        two = sums[4 * side + 2][...] + sums[4 * side + 3][...]
        i = mine if side == 0 else 1 - mine
        table[i * 6 + 4] = one[:width]
        table[i * 6 + 0] = one[width : 2 * width]
        table[i * 6 + 5] = two[:width]
        table[i * 6 + 1] = two[width : 2 * width]
        table[3, pl.ds(pl.multiple_of(i * (width // 2), width // 2), width // 2)] = one[2 * width :]
    table[6 + 2] = table[3].T
    for p in range(count):
        product = table[slots_ref[p]]
        right = second_ref[p]
        left = first_ref[p]
        high, rest = split(product)
        inner = dot(
            jnp.concatenate([high, rest], axis=1),
            jnp.concatenate([right, right], axis=0),
            ((1,), (0,)),
        )
        high, rest = split(inner)
        exch = dot(
            jnp.concatenate([left, left], axis=0),
            jnp.concatenate([high, rest], axis=0),
            ((0,), (0,)),
        )
        exch_ref[p] = exch
        low_ref[p] = (factor_ref[p] * exch).astype(BF16)


def exchange(slots, half, sums, first, second, factor):
    count, width, _ = first.shape
    return pl.pallas_call(
        exchange_kernel,
        out_shape=(
            jax.ShapeDtypeStruct(first.shape, F32),
            jax.ShapeDtypeStruct(first.shape, BF16),
        ),
        in_specs=[SMEM, SMEM] + [VMEM] * (len(sums) + 3),
        out_specs=(VMEM, VMEM),
        scratch_shapes=[pltpu.VMEM((12, width, width), F32)],
        compiler_params=PARAMS,
        cost_estimate=cost(8 * count * width**3, 20 * count * width * width),
        name="exchange",
    )(slots, half, *sums, first, second, factor)


def sweep_kernel(last, pieces, index_ref, couple_ref, spots_ref, *refs):
    parts = refs[:pieces]
    over_ref, exch_ref, factor_ref, second_ref = refs[pieces : pieces + 4]
    if last:
        amps_ref, terms_ref, table, sems = refs[pieces + 4 :]
    else:
        low_ref, table, sems = refs[pieces + 4 :]
    count = exch_ref.shape[0]
    nbr_count = over_ref.shape[1]
    copies = []
    at = 0
    for i, part in enumerate(parts):
        size = part.shape[0]
        copies.append(pltpu.make_async_copy(part, table.at[pl.ds(at, size)], sems.at[i]))
        at += size
    for copy in copies:
        copy.start()
    for copy in copies:
        copy.wait()
    if last:
        terms_ref[...] = jnp.zeros_like(terms_ref)
    for p in range(count):
        coupled = None
        for n in range(nbr_count):
            over = over_ref[p, n]
            half = dot(over, table[index_ref[p, n]], ((1,), (0,))).astype(BF16)
            full = couple_ref[p, n] * dot(half, over, ((1,), (1,)))
            coupled = full if coupled is None else coupled + full
        amps = factor_ref[p] * (exch_ref[p] - coupled)
        if not last:
            low_ref[p] = amps.astype(BF16)
            continue
        amps_ref[p] = amps
        high, rest = split(amps)
        right = second_ref[p]
        moved = dot(
            jnp.concatenate([right, right], axis=1),
            jnp.concatenate([high, rest], axis=1),
            ((1,), (1,)),
        )
        spot = spots_ref[p]
        terms_ref[spot] = terms_ref[spot] + square(moved)


def square(value):
    high, rest = split(value)
    return dot(
        jnp.concatenate([high, high, rest, rest], axis=1),
        jnp.concatenate([high, rest, high, rest], axis=1),
        ((1,), (1,)),
    )


def sweep(last, index, couple, spots, parts, over, exch, factor, second, occ_dev):
    count, width, _ = exch.shape
    rows = sum(part.shape[0] for part in parts)
    if last:
        out_shape = (
            jax.ShapeDtypeStruct(exch.shape, F32),
            jax.ShapeDtypeStruct((3 * occ_dev, width, width), F32),
        )
        out_specs = (VMEM, VMEM)
    else:
        out_shape = jax.ShapeDtypeStruct(exch.shape, BF16)
        out_specs = VMEM
    return pl.pallas_call(
        functools.partial(sweep_kernel, last, len(parts)),
        out_shape=out_shape,
        in_specs=[SMEM] * 3 + [ANY] * len(parts) + [VMEM] * 4,
        out_specs=out_specs,
        scratch_shapes=[
            pltpu.VMEM((rows, width, width), BF16),
            pltpu.SemaphoreType.DMA((len(parts),)),
        ],
        compiler_params=PARAMS,
        cost_estimate=cost(16 * count * width**3, (rows + 16 * count) * width * width),
        name="last_sweep" if last else "sweep",
    )(index, couple, spots, *parts, over, exch, factor, second)


def first_kernel(spots_ref, amps_ref, first_ref, terms_ref):
    terms_ref[...] = jnp.zeros_like(terms_ref)
    for p in range(amps_ref.shape[0]):
        high, rest = split(amps_ref[p])
        left = first_ref[p]
        moved = dot(
            jnp.concatenate([left, left], axis=1),
            jnp.concatenate([high, rest], axis=0),
            ((1,), (0,)),
        )
        spot = spots_ref[p]
        terms_ref[spot] = terms_ref[spot] + square(moved)


def first_terms(spots, amps, first, occ_dev):
    count, width, _ = amps.shape
    return pl.pallas_call(
        first_kernel,
        out_shape=jax.ShapeDtypeStruct((occ_dev, width, width), F32),
        in_specs=[SMEM, VMEM, VMEM],
        out_specs=VMEM,
        compiler_params=PARAMS,
        cost_estimate=cost(12 * count * width**3, 6 * count * width * width),
        name="first_terms",
    )(spots, amps, first)


def window_rounds(groups):
    reach = groups // 4
    span = 2 * reach + 1
    edges = []
    for block in range(groups):
        start = min(max(block - reach, 0), groups - span)
        edges += [(source, block) for source in range(start, start + span) if source != block]
    edges.sort(key=lambda edge: (abs(edge[0] - edge[1]), edge))
    rounds = []
    for source, block in edges:
        for pairs in rounds:
            if all(source != s and block != d for s, d in pairs):
                pairs.append((source, block))
                break
        else:
            rounds.append([(source, block)])
    return rounds


def same_owner_rank(owners):
    count = owners.shape[-1]
    places = jnp.arange(count)
    earlier = places[:, None] > places[None, :]
    same = owners[..., :, None] == owners[..., None, :]
    return jnp.sum(same & earlier, axis=-1)


def shards(
    ints,
    proj_first,
    proj_second,
    intersections,
    couple,
    virt_energy,
    occ_energy,
    pno_count,
    pair_orbitals,
    neighbours,
):
    groups = lax.axis_size("pair")
    here = lax.axis_index("pair")
    aux_count = lax.axis_size("aux")
    half = lax.axis_index("aux") % 2
    occ_dev, _, width = ints.shape
    pair_dev = proj_first.shape[0]
    nbr_count = couple.shape[1]
    wanted = pair_dev * nbr_count
    cap = 2 * wanted // groups
    count = pair_dev // 2
    up = [(i + 1, i) for i in range(groups - 1)]
    down = [(i, i + 1) for i in range(groups - 1)]

    def swap(value, step=1):
        return lax.ppermute(value, "aux", [(i, i ^ step) for i in range(aux_count)])

    def own(value):
        return lax.dynamic_slice_in_dim(value, half * count, count, 0)

    near = []
    for j in range(occ_dev):
        piece = lax.slice_in_dim(ints, j, j + 1, axis=0)
        near.append((lax.ppermute(piece, "pair", up), lax.ppermute(piece, "pair", down)))

    first = own(proj_first)
    second = own(proj_second)
    over = own(intersections)
    weights = own(couple)
    orbitals = own(pair_orbitals)
    base = (here - 1) * occ_dev
    first_slot = orbitals[:, 0] - base - occ_dev
    second_slot = orbitals[:, 1] - base
    energy = own(virt_energy)
    occupied = own(occ_energy)
    valid = jnp.arange(width)[None, :] < own(pno_count)[:, None]
    mask = (valid[:, :, None] & valid[:, None, :]).astype(F32)
    denom = (
        energy[:, :, None]
        + energy[:, None, :]
        - occupied[:, 0, None, None]
        - occupied[:, 1, None, None]
    )
    factor = -mask / denom

    def reduced(partial):
        kept = lax.dynamic_index_in_dim(partial, half, 0, keepdims=False)
        sent = lax.dynamic_index_in_dim(partial, 1 - half, 0, keepdims=False)
        total = kept + swap(sent)
        step = 2
        while 2 * step < aux_count:
            total = total + swap(total, step)
            step *= 2
        return total, swap(total, step)

    sums = []
    for j in range(occ_dev):
        sums.append(reduced(products(ints, *near[j], j == 0)))
    sums = [value for pair in sums for value in pair]
    sums = sums + [swap(value) for value in sums]
    exch, low = exchange(
        first_slot * 3 * occ_dev + second_slot,
        half.reshape(1),
        sums,
        first,
        second,
        factor,
    )

    if cap < pair_dev:
        requests = neighbours.reshape(groups, wanted)
        owners = requests // pair_dev
        ranks = same_owner_rank(owners)
        at_home = owners == here
        pick = at_home[:, None, :] & (ranks[:, None, :] == jnp.arange(cap)[None, :, None])
        local = requests % pair_dev
        select = jnp.any(
            pick[..., None]
            & (local[:, None, :, None] == jnp.arange(pair_dev)[None, None, None, :]),
            axis=2,
        )
        select = select.astype(BF16).reshape(groups * cap, pair_dev)
        own_requests = lax.dynamic_slice_in_dim(requests, here, 1, 0)[0]
        own_ranks = lax.dynamic_slice_in_dim(ranks, here, 1, 0)[0]
        row_index = own(
            (own_requests // pair_dev * cap + own_ranks).reshape(pair_dev, nbr_count)
        ).reshape(-1)
        index = jnp.arange(count * nbr_count).reshape(count, nbr_count)
    else:
        rounds = window_rounds(groups)
        table = lax.dynamic_slice_in_dim(neighbours, here * pair_dev + half * count, count, 0)
        owners = table // pair_dev
        local = table % pair_dev
        slot = jnp.zeros_like(owners)
        for place, pairs in enumerate(rounds):
            sources = np.full(groups, -1, np.int32)
            for source, block in pairs:
                sources[block] = source
            slot = jnp.where(owners == jnp.asarray(sources)[here], place + 1, slot)
        other = (local // count != half).astype(jnp.int32)
        index = (2 * slot + other) * count + local % count

    def gathered(low):
        if cap < pair_dev:
            others = swap(low)
            flat = jnp.where(
                half == 0, jnp.concatenate([low, others]), jnp.concatenate([others, low])
            ).reshape(pair_dev, width * width)
            outgoing = jnp.dot(select, flat, preferred_element_type=F32).astype(BF16)
            outgoing = outgoing.reshape(groups, cap, width, width)
            received = lax.all_to_all(outgoing, "pair", split_axis=0, concat_axis=0, tiled=True)
            return [received.reshape(groups * cap, width, width)[row_index]]
        pieces = [low] + [lax.ppermute(low, "pair", pairs) for pairs in rounds]
        return [value for piece in pieces for value in (piece, swap(piece))]

    for it in range(ITERS):
        out = sweep(
            it == ITERS - 1,
            index,
            weights,
            second_slot,
            gathered(low),
            over,
            exch,
            factor,
            second,
            occ_dev,
        )
        if it < ITERS - 1:
            low = out
    amps, terms = out

    from_below = lax.ppermute(terms[2 * occ_dev :], "pair", down)
    from_above = lax.ppermute(terms[:occ_dev], "pair", up)
    inner = first_terms(first_slot, amps, first, occ_dev)
    others = swap(amps)
    whole = jnp.where(half == 0, jnp.concatenate([amps, others]), jnp.concatenate([others, amps]))
    density = inner + terms[occ_dev : 2 * occ_dev] + from_below + from_above
    density = (density + swap(density)) / width
    return (whole, density)


def solution(mesh):
    return jax.shard_map(
        shards,
        mesh=mesh,
        in_specs=(
            P(("mol", "pair"), "aux", None),
            P(("mol", "pair"), None, None),
            P(("mol", "pair"), None, None),
            P(("mol", "pair"), None, None, None),
            P(("mol", "pair"), None),
            P(("mol", "pair"), None),
            P(("mol", "pair"), None),
            P(("mol", "pair")),
            P(("mol", "pair"), None),
            P("mol", None),
        ),
        out_specs=(P(("mol", "pair"), None, None), P(("mol", "pair"), None, None)),
        check_vma=False,
    )
```

time: 472 us -> 114 us (0.24)
  the two profiles are of different devices: /device:TPU:15 before, /device:TPU:0 now
where the time goes in v1:
time: 114 us; the launch traced here: 113 us
  waiting for transfers between devices  38.9 us (34%)
  starting transfers between devices  37.4 us (33%)
  Pallas kernels  19.8 us (17%)
  local copies, waits for them, and re-layouts  10.8 us (9%)
  other arithmetic  5.4 us (5%)
    ppermute x6, waiting for transfers between devices, gathered(): pieces = [low] + [lax.ppermute(low, 'pair', pairs) for pairs in rounds]  17.5 us
    ppermute x6, starting transfers between devices, gathered(): pieces = [low] + [lax.ppermute(low, 'pair', pairs) for pairs in rounds]  15.6 us
    pallas_call x2, Pallas kernels, sweep(): pl.pallas_call(functools.partial(sweep_kernel, last, len(parts)), out_sha...  11.5 us
    ppermute x2, starting transfers between devices, shards(): lax.ppermute(piece, 'pair', down)  10.3 us
    ppermute x18, waiting for transfers between devices, swap(): return lax.ppermute(value, 'aux', [(i, i ^ step) for i in range(aux_count)])  8.99 us
    ppermute x2, waiting for transfers between devices, shards(): lax.ppermute(piece, 'pair', up)  8.21 us
    ppermute x18, starting transfers between devices, swap(): return lax.ppermute(value, 'aux', [(i, i ^ step) for i in range(aux_count)])  4.84 us
    dynamic_slice x7, local copies, waits for them, and re-layouts, own(): return lax.dynamic_slice_in_dim(value, half * count, count, 0)  3.46 us
  transfers between devices with their start and end apart: 30, of which 13 were waited for; matrix products, arithmetic and copies ran while one was open for 8% of the time, Pallas kernels for 5%

profile of v1, /device:TPU:0, one launch (start us, length us, event | category | flops | bytes accessed | tf_op | source)
XLA Modules:
  0.0 113.3 jit_solution(9649852444158012607)
XLA Ops:
  0.7 2.2 %fusion.5 = (bf16[1,1536,128]{2,1,0:T(8,128)(2,1)}, bf16[1,1536,128]{2,1,0:T(8,128)(2,1)}) fusion(bf16[2,1536,128]{2,1,0:T(8,128)(2,1)} %own_ref.3), kind=kLoop, calls=%fused_computation.39 | loop fusion | bytes 1572864 | tf_op jit(solution)/shard_map/slice | solution.py:285
  2.8 4.9 %collective-permute-start.5 = (bf16[1,1536,128]{2,1,0:T(8,128)(2,1)}, bf16[1,1536,128]{2,1,0:T(8,128)(2,1)S(1)}, u32[]{:S(2)}, u32[]{:S(2)}) collective-permute-start(bf16[1,1536,128]{2,1,0:T(8,128)(2,1)} %get-tuple-element.13), channel_id=1, source_target_pairs={{0,4},{4,8},{8,12},{1,5},{5,9},{9,13},{2,6},{6,10},{10,14},{3,7},{... | collective-permute-start | bytes 1179656 | tf_op jit(solution)/shard_map/ppermute | solution.py:286
  7.8 1.3 %collective-permute-start.4 = (bf16[1,1536,128]{2,1,0:T(8,128)(2,1)}, bf16[1,1536,128]{2,1,0:T(8,128)(2,1)}, u32[]{:S(2)}, u32[]{:S(2)}) collective-permute-start(bf16[1,1536,128]{2,1,0:T(8,128)(2,1)} %get-tuple-element.13), channel_id=1, source_target_pairs={{4,0},{8,4},{12,8},{5,1},{9,5},{13,9},{6,2},{10,6},{14,10},{7,3},{... | collective-permute-start | bytes 1179656 | tf_op jit(solution)/shard_map/ppermute | solution.py:286
  9.1 5.3 %collective-permute-start.1 = (bf16[1,1536,128]{2,1,0:T(8,128)(2,1)}, bf16[1,1536,128]{2,1,0:T(8,128)(2,1)}, u32[]{:S(2)}, u32[]{:S(2)}) collective-permute-start(bf16[1,1536,128]{2,1,0:T(8,128)(2,1)} %get-tuple-element.14), channel_id=1, source_target_pairs={{0,4},{4,8},{8,12},{1,5},{5,9},{9,13},{2,6},{6,10},{10,14},{3,7},{... | collective-permute-start | bytes 1179656 | tf_op jit(solution)/shard_map/ppermute | solution.py:286
  14.4 1.3 %collective-permute-start = (bf16[1,1536,128]{2,1,0:T(8,128)(2,1)}, bf16[1,1536,128]{2,1,0:T(8,128)(2,1)}, u32[]{:S(2)}, u32[]{:S(2)}) collective-permute-start(bf16[1,1536,128]{2,1,0:T(8,128)(2,1)} %get-tuple-element.14), channel_id=1, source_target_pairs={{4,0},{8,4},{12,8},{5,1},{9,5},{13,9},{6,2},{10,6},{14,10},{7,3},{... | collective-permute-start | bytes 1179656 | tf_op jit(solution)/shard_map/ppermute | solution.py:286
  15.7 0.7 dynamic_slice.62
  16.5 0.1 iota_compare_fusion
  16.5 0.7 constant_dynamic-slice_fusion.2
  17.2 0.7 constant_dynamic-slice_fusion.1
  18.0 4.1 %collective-permute-done.4.up_ref = bf16[1,1536,128]{2,1,0:T(8,128)(2,1)} collective-permute-done((bf16[1,1536,128]{2,1,0:T(8,128)(2,1)}, bf16[1,1536,128]{2,1,0:T(8,128)(2,1)}, u32[]{:S(2)}, u32[]{:S(2)}) %collective-permute-start.4) | collective-permute-done | bytes 393248 | tf_op jit(solution)/shard_map/ppermute | solution.py:286
  22.0 1.4 %products.3 = f32[2,256,128]{2,1,0:T(8,128)S(1)} custom-call(bf16[2,1536,128]{2,1,0:T(8,128)(2,1)S(1)} %copy-done.3, bf16[1,1536,128]{2,1,0:T(8,128)(2,1)} %collective-permute-done.4.up_ref, bf16[1,1536,128]{2,1,0:T(8,128)(2,1)S(1)} %collective-permute-done.5.down_ref), custom_call_target="tpu_custom_call" | custom-call | flops 201326592 | bytes 1572864 | tf_op jit(solution)/shard_map/products/pallas_call | solution.py:52
  23.5 0.1 collective-permute-start.6
  23.6 1.3 %collective-permute-done.1.down_ref = bf16[1,1536,128]{2,1,0:T(8,128)(2,1)} collective-permute-done((bf16[1,1536,128]{2,1,0:T(8,128)(2,1)}, bf16[1,1536,128]{2,1,0:T(8,128)(2,1)}, u32[]{:S(2)}, u32[]{:S(2)}) %collective-permute-start.1) | collective-permute-done | bytes 393248 | tf_op jit(solution)/shard_map/ppermute | solution.py:286
  24.9 4.1 %collective-permute-done.up_ref = bf16[1,1536,128]{2,1,0:T(8,128)(2,1)} collective-permute-done((bf16[1,1536,128]{2,1,0:T(8,128)(2,1)}, bf16[1,1536,128]{2,1,0:T(8,128)(2,1)}, u32[]{:S(2)}, u32[]{:S(2)}) %collective-permute-start) | collective-permute-done | bytes 393248 | tf_op jit(solution)/shard_map/ppermute | solution.py:286
  29.0 1.6 %products.2 = f32[2,320,128]{2,1,0:T(8,128)S(1)} custom-call(bf16[2,1536,128]{2,1,0:T(8,128)(2,1)S(1)} %copy-done.3, bf16[1,1536,128]{2,1,0:T(8,128)(2,1)} %collective-permute-done.up_ref, bf16[1,1536,128]{2,1,0:T(8,128)(2,1)} %collective-permute-done.1.down_ref), custom_call_target="tpu_custom_call" | custom-call | flops 201326592 | bytes 1572864 | tf_op jit(solution)/shard_map/products/pallas_call | solution.py:52
  30.7 0.1 collective-permute-start.2
  30.8 1.6 %collective-permute-start.7 = (f32[256,128]{1,0:T(8,128)S(1)}, f32[256,128]{1,0:T(8,128)}, u32[]{:S(2)}, u32[]{:S(2)}) collective-permute-start(f32[256,128]{1,0:T(8,128)S(1)} %bitcast_add_fusion.1.refs_2_), channel_id=1, source_target_pairs={{0,2},{1,3},{2,0},{3,1},{4,6},{5,7},{6,4},{7,5},{8,10},{9,11},{10,... | collective-permute-start | bytes 393224 | tf_op jit(solution)/shard_map/ppermute | solution.py:278
  32.4 1.3 %collective-permute-start.3 = (f32[320,128]{1,0:T(8,128)S(1)}, f32[320,128]{1,0:T(8,128)}, u32[]{:S(2)}, u32[]{:S(2)}) collective-permute-start(f32[320,128]{1,0:T(8,128)S(1)} %bitcast_add_fusion.refs_0_), channel_id=1, source_target_pairs={{0,2},{1,3},{2,0},{3,1},{4,6},{5,7},{6,4},{7,5},{8,10},{9,11},{10,... | collective-permute-start | bytes 491528 | tf_op jit(solution)/shard_map/ppermute | solution.py:278
  33.7 0.4 subtract_divide_fusion.refs_10_
  34.1 0.1 constant_dynamic-slice_fusion.5
  34.2 0.5 collective-permute-start.8
  34.7 2.6 %collective-permute-done.7.refs_3_ = f32[256,128]{1,0:T(8,128)} collective-permute-done((f32[256,128]{1,0:T(8,128)S(1)}, f32[256,128]{1,0:T(8,128)}, u32[]{:S(2)}, u32[]{:S(2)}) %collective-permute-start.7) | collective-permute-done | bytes 131104 | tf_op jit(solution)/shard_map/ppermute | solution.py:278
  37.3 3.1 %collective-permute-done.3.refs_1_ = f32[320,128]{1,0:T(8,128)} collective-permute-done((f32[320,128]{1,0:T(8,128)S(1)}, f32[320,128]{1,0:T(8,128)}, u32[]{:S(2)}, u32[]{:S(2)}) %collective-permute-start.3) | collective-permute-done | bytes 163872 | tf_op jit(solution)/shard_map/ppermute | solution.py:278
  40.4 1.1 constant_dynamic-slice_fusion.3
  41.5 0.5 collective-permute-done.9.refs_5_
  42.0 2.5 %exchange.1 = (f32[8,128,128]{2,1,0:T(8,128)S(1)}, bf16[8,128,128]{2,1,0:T(8,128)(2,1)}) custom-call(s32[8]{0:T(128)S(1)} %get-tuple-element.10.slots_ref, s32[1]{0:T(128)} %bitcast.5.half_ref, f32[320,128]{1,0:T(8,128)S(1)} %bitcast_add_fusion.refs_0_, f32[320,128]{1,0:T(8,128)} %collective-permute-done.3.refs_1_, ...), custom_call_target="tpu_custom_call" | custom-call | flops 134217728 | bytes 2621440 | tf_op jit(solution)/shard_map/exchange/pallas_call | solution.py:103
  44.4 0.8 copy-done.6
  45.2 1.3 %collective-permute-start.17 = (bf16[8,128,128]{2,1,0:T(8,128)(2,1)}, bf16[8,128,128]{2,1,0:T(8,128)(2,1)}, u32[]{:S(2)}, u32[]{:S(2)}) collective-permute-start(bf16[8,128,128]{2,1,0:T(8,128)(2,1)} %get-tuple-element.6.refs_0_), channel_id=1, source_target_pairs={{4,12},{8,0},{5,13},{9,1},{6,14},{10,2},{7,15},{11,3},{20,28},{24,... | collective-permute-start | bytes 786440 | tf_op jit(solution)/shard_map/ppermute | solution.py:375
  46.5 1.4 %collective-permute-start.15 = (bf16[8,128,128]{2,1,0:T(8,128)(2,1)}, bf16[8,128,128]{2,1,0:T(8,128)(2,1)}, u32[]{:S(2)}, u32[]{:S(2)}) collective-permute-start(bf16[8,128,128]{2,1,0:T(8,128)(2,1)} %get-tuple-element.6.refs_0_), channel_id=1, source_target_pairs={{4,8},{8,4},{5,9},{9,5},{6,10},{10,6},{7,11},{11,7},{20,24},{24,20... | collective-permute-start | bytes 786440 | tf_op jit(solution)/shard_map/ppermute | solution.py:375
  47.9 5.4 %collective-permute-start.13 = (bf16[8,128,128]{2,1,0:T(8,128)(2,1)}, bf16[8,128,128]{2,1,0:T(8,128)(2,1)}, u32[]{:S(2)}, u32[]{:S(2)}) collective-permute-start(bf16[8,128,128]{2,1,0:T(8,128)(2,1)} %get-tuple-element.6.refs_0_), channel_id=1, source_target_pairs={{0,4},{4,0},{8,12},{12,8},{1,5},{5,1},{9,13},{13,9},{2,6},{6,2},{1... | collective-permute-start | bytes 786440 | tf_op jit(solution)/shard_map/ppermute | solution.py:375
  53.3 0.1 constant_dynamic-slice_fusion.6
  53.4 0.1 constant_dynamic-slice_fusion.refs_8_
  53.5 0.1 collective-permute-start.12
  53.5 4.0 %collective-permute-done.17.refs_6_ = bf16[8,128,128]{2,1,0:T(8,128)(2,1)} collective-permute-done((bf16[8,128,128]{2,1,0:T(8,128)(2,1)}, bf16[8,128,128]{2,1,0:T(8,128)(2,1)}, u32[]{:S(2)}, u32[]{:S(2)}) %collective-permute-start.17) | collective-permute-done | bytes 262176 | tf_op jit(solution)/shard_map/ppermute | solution.py:375
  57.5 0.5 collective-permute-start.16
  58.0 4.3 %collective-permute-done.13.refs_2_ = bf16[8,128,128]{2,1,0:T(8,128)(2,1)} collective-permute-done((bf16[8,128,128]{2,1,0:T(8,128)(2,1)}, bf16[8,128,128]{2,1,0:T(8,128)(2,1)}, u32[]{:S(2)}, u32[]{:S(2)}) %collective-permute-start.13) | collective-permute-done | bytes 262176 | tf_op jit(solution)/shard_map/ppermute | solution.py:375
  62.3 0.1 constant_dynamic-slice_fusion.7
  62.4 0.7 dynamic_slice.51
  63.1 0.6 dynamic_slice.52
  63.7 0.6 dynamic_slice.53
  64.3 0.1 copy.17
  64.4 0.1 copy.18.couple_ref
  64.5 1.9 %fusion.1.index_ref = s32[8,4]{1,0:T(8,128)S(1)} fusion(s32[8,4]{1,0:T(8,128)S(1)} %copy.17, s32[]{:T(128)} %select_n.71, s32[]{:T(128)} %bitcast.2, s32[]{:T(128)} %bitcast.1, s32[]{:T(128)} %bitcast), kind=kLoop, calls=%fused_computation.19 | loop fusion | flops 1600 | bytes 272 | tf_op jit(solution)/shard_map/add | solution.py:363
  66.5 1.0 copy-done.2
  67.5 1.0 copy-done.7
  68.5 4.7 %sweep.1.refs_0_ = bf16[8,128,128]{2,1,0:T(8,128)(2,1)S(1)} custom-call(s32[8,4]{1,0:T(8,128)S(1)} %fusion.1.index_ref, f32[8,4]{1,0:T(8,128)S(1)} %copy.18.couple_ref, s32[8]{0:T(128)S(1)} %get-tuple-element.12.spots_ref, bf16[8,128,128]{2,1,0:T(8,128)(2,1)} %get-tuple-element.6.refs_0_, bf16[8,128,128]{2,1,0:T(8,128)(2,1)} %collective-permute-done.12.refs_1_, ...), custom_call_target="tpu_custom_call" | custom-call | flops 268435456 | bytes 3145728 | tf_op jit(solution)/shard_map/sweep/pallas_call | solution.py:183
  73.3 1.4 %collective-permute-start.24 = (bf16[8,128,128]{2,1,0:T(8,128)(2,1)S(1)}, bf16[8,128,128]{2,1,0:T(8,128)(2,1)S(1)}, u32[]{:S(2)}, u32[]{:S(2)}) collective-permute-start(bf16[8,128,128]{2,1,0:T(8,128)(2,1)S(1)} %sweep.1.refs_0_), channel_id=1, source_target_pairs={{4,12},{8,0},{5,13},{9,1},{6,14},{10,2},{7,15},{11,3},{20,28},{24,... | collective-permute-start | bytes 786440 | tf_op jit(solution)/shard_map/ppermute | solution.py:375
  74.7 0.7 collective-permute-start.22
  75.4 5.4 %collective-permute-start.20 = (bf16[8,128,128]{2,1,0:T(8,128)(2,1)S(1)}, bf16[8,128,128]{2,1,0:T(8,128)(2,1)S(1)}, u32[]{:S(2)}, u32[]{:S(2)}) collective-permute-start(bf16[8,128,128]{2,1,0:T(8,128)(2,1)S(1)} %sweep.1.refs_0_), channel_id=1, source_target_pairs={{0,4},{4,0},{8,12},{12,8},{1,5},{5,1},{9,13},{13,9},{2,6},{6,2},{1... | collective-permute-start | bytes 786440 | tf_op jit(solution)/shard_map/ppermute | solution.py:375
  80.8 4.5 %collective-permute-done.24.refs_6_ = bf16[8,128,128]{2,1,0:T(8,128)(2,1)S(1)} collective-permute-done((bf16[8,128,128]{2,1,0:T(8,128)(2,1)S(1)}, bf16[8,128,128]{2,1,0:T(8,128)(2,1)S(1)}, u32[]{:S(2)}, u32[]{:S(2)}) %collective-permute-start.24) | collective-permute-done | bytes 262176 | tf_op jit(solution)/shard_map/ppermute | solution.py:375
  85.4 0.5 collective-permute-start.23
  85.9 4.7 %collective-permute-done.20.refs_2_ = bf16[8,128,128]{2,1,0:T(8,128)(2,1)S(1)} collective-permute-done((bf16[8,128,128]{2,1,0:T(8,128)(2,1)S(1)}, bf16[8,128,128]{2,1,0:T(8,128)(2,1)S(1)}, u32[]{:S(2)}, u32[]{:S(2)}) %collective-permute-start.20) | collective-permute-done | bytes 262176 | tf_op jit(solution)/shard_map/ppermute | solution.py:375
  90.5 0.0 collective-permute-start.21
  90.6 1.5 %collective-permute-done.21.refs_3_ = bf16[8,128,128]{2,1,0:T(8,128)(2,1)S(1)} collective-permute-done((bf16[8,128,128]{2,1,0:T(8,128)(2,1)S(1)}, bf16[8,128,128]{2,1,0:T(8,128)(2,1)S(1)}, u32[]{:S(2)}, u32[]{:S(2)}) %collective-permute-start.21) | collective-permute-done | bytes 262176 | tf_op jit(solution)/shard_map/ppermute | solution.py:278
  92.1 6.8 %last_sweep.1 = (f32[8,128,128]{2,1,0:T(8,128)}, f32[6,128,128]{2,1,0:T(8,128)S(1)}) custom-call(s32[8,4]{1,0:T(8,128)S(1)} %fusion.1.index_ref, f32[8,4]{1,0:T(8,128)S(1)} %copy.18.couple_ref, s32[8]{0:T(128)S(1)} %get-tuple-element.12.spots_ref, bf16[8,128,128]{2,1,0:T(8,128)(2,1)S(1)} %sweep.1.refs_0_, ...), custom_call_target="tpu_custom_call" | custom-call | flops 268435456 | bytes 3145728 | tf_op jit(solution)/shard_map/last_sweep/pallas_call | solution.py:183
  98.9 2.9 %collective-permute-start.27 = (f32[2,128,128]{2,1,0:T(8,128)S(1)}, f32[2,128,128]{2,1,0:T(8,128)S(1)}, u32[]{:S(2)}, u32[]{:S(2)}) collective-permute-start(f32[2,128,128]{2,1,0:T(8,128)S(1)} %get-tuple-element.15), channel_id=1, source_target_pairs={{0,4},{4,8},{8,12},{1,5},{5,9},{9,13},{2,6},{6,10},{10,14},{3,7},{... | collective-permute-start | bytes 393224 | tf_op jit(solution)/shard_map/ppermute | solution.py:395
  101.8 1.3 %collective-permute-start.28 = (f32[2,128,128]{2,1,0:T(8,128)S(1)}, f32[2,128,128]{2,1,0:T(8,128)S(1)}, u32[]{:S(2)}, u32[]{:S(2)}) collective-permute-start(f32[2,128,128]{2,1,0:T(8,128)S(1)} %get-tuple-element.16), channel_id=1, source_target_pairs={{4,0},{8,4},{12,8},{5,1},{9,5},{13,9},{6,2},{10,6},{14,10},{7,3},{... | collective-permute-start | bytes 393224 | tf_op jit(solution)/shard_map/ppermute | solution.py:396
  103.1 0.1 collective-permute-start.26
  103.2 2.8 %first_terms.1 = f32[2,128,128]{2,1,0:T(8,128)S(1)} custom-call(s32[8]{0:T(128)S(1)} %get-tuple-element.11.spots_ref, f32[8,128,128]{2,1,0:T(8,128)} %get-tuple-element.8.amps_ref, bf16[8,128,128]{2,1,0:T(8,128)(2,1)S(1)} %copy-done.5), custom_call_target="tpu_custom_call" | custom-call | flops 201326592 | bytes 786432 | tf_op jit(solution)/shard_map/first_terms/pallas_call | solution.py:214
  106.0 2.9 %collective-permute-done.28 = f32[2,128,128]{2,1,0:T(8,128)S(1)} collective-permute-done((f32[2,128,128]{2,1,0:T(8,128)S(1)}, f32[2,128,128]{2,1,0:T(8,128)S(1)}, u32[]{:S(2)}, u32[]{:S(2)}) %collective-permute-start.28) | collective-permute-done | bytes 131104 | tf_op jit(solution)/shard_map/ppermute | solution.py:396
  109.0 0.1 collective-permute-start.29
  109.0 1.3 %collective-permute-done.29 = f32[2,128,128]{2,1,0:T(8,128)S(1)} collective-permute-done((f32[2,128,128]{2,1,0:T(8,128)S(1)}, f32[2,128,128]{2,1,0:T(8,128)S(1)}, u32[]{:S(2)}, u32[]{:S(2)}) %collective-permute-start.29) | collective-permute-done | bytes 131104 | tf_op jit(solution)/shard_map/ppermute | solution.py:278
  110.4 0.7 add_multiply_fusion
  111.0 2.3 %maximum_select_fusion = f32[16,128,128]{2,1,0:T(8,128)} fusion(f32[8,128,128]{2,1,0:T(8,128)S(1)} %collective-permute-done.26, f32[8,128,128]{2,1,0:T(8,128)} %get-tuple-element.8.amps_ref, pred[]{:T(512)S(6)} %eq.26), kind=kLoop, calls=%fused_computation | loop fusion | flops 786432 | bytes 2097153 | tf_op jit(solution)/shard_map/jit(_where)/select_n | solution.py:399
  (57 shorter events, 0.3 us)
Async XLA Ops:
  0.6 52.7 %copy-start = (bf16[16,4,128,128]{3,2,1,0:T(8,128)(2,1)S(1)}, bf16[16,4,128,128]{3,2,1,0:T(8,128)(2,1)}, u32[]{:S(2)}) copy-start(bf16[16,4,128,128]{3,2,1,0:T(8,128)(2,1)} %param.16) | copy-start | bytes 6291460
  0.6 21.4 %copy-start.3 = (bf16[2,1536,128]{2,1,0:T(8,128)(2,1)S(1)}, bf16[2,1536,128]{2,1,0:T(8,128)(2,1)}, u32[]{:S(2)}) copy-start(bf16[2,1536,128]{2,1,0:T(8,128)(2,1)} %own_ref.3) | copy-start | bytes 2359300
  2.8 15.1 %collective-permute-start.5 = (bf16[1,1536,128]{2,1,0:T(8,128)(2,1)}, bf16[1,1536,128]{2,1,0:T(8,128)(2,1)S(1)}, u32[]{:S(2)}, u32[]{:S(2)}) collective-permute-start(bf16[1,1536,128]{2,1,0:T(8,128)(2,1)} %get-tuple-element.13), channel_id=1, source_target_pairs={{0,4},{4,8},{8,12},{1,5},{5,9},{9,13},{2,6},{6,10},{10,14},{3,7},{... | collective-permute-start | bytes 1179656 | tf_op jit(solution)/shard_map/ppermute | solution.py:286
  7.8 14.3 %collective-permute-start.4 = (bf16[1,1536,128]{2,1,0:T(8,128)(2,1)}, bf16[1,1536,128]{2,1,0:T(8,128)(2,1)}, u32[]{:S(2)}, u32[]{:S(2)}) collective-permute-start(bf16[1,1536,128]{2,1,0:T(8,128)(2,1)} %get-tuple-element.13), channel_id=1, source_target_pairs={{4,0},{8,4},{12,8},{5,1},{9,5},{13,9},{6,2},{10,6},{14,10},{7,3},{... | collective-permute-start | bytes 1179656 | tf_op jit(solution)/shard_map/ppermute | solution.py:286
  9.1 15.8 %collective-permute-start.1 = (bf16[1,1536,128]{2,1,0:T(8,128)(2,1)}, bf16[1,1536,128]{2,1,0:T(8,128)(2,1)}, u32[]{:S(2)}, u32[]{:S(2)}) collective-permute-start(bf16[1,1536,128]{2,1,0:T(8,128)(2,1)} %get-tuple-element.14), channel_id=1, source_target_pairs={{0,4},{4,8},{8,12},{1,5},{5,9},{9,13},{2,6},{6,10},{10,14},{3,7},{... | collective-permute-start | bytes 1179656 | tf_op jit(solution)/shard_map/ppermute | solution.py:286
  14.4 14.6 %collective-permute-start = (bf16[1,1536,128]{2,1,0:T(8,128)(2,1)}, bf16[1,1536,128]{2,1,0:T(8,128)(2,1)}, u32[]{:S(2)}, u32[]{:S(2)}) collective-permute-start(bf16[1,1536,128]{2,1,0:T(8,128)(2,1)} %get-tuple-element.14), channel_id=1, source_target_pairs={{4,0},{8,4},{12,8},{5,1},{9,5},{13,9},{6,2},{10,6},{14,10},{7,3},{... | collective-permute-start | bytes 1179656 | tf_op jit(solution)/shard_map/ppermute | solution.py:286
  23.5 10.6 %copy-start.10 = (s32[16,2]{0,1:T(2,128)S(1)}, s32[16,2]{0,1:T(2,128)}, u32[]{:S(2)}) copy-start(s32[16,2]{0,1:T(2,128)} %param.21) | copy-start | bytes 388
  23.5 7.2 %collective-permute-start.6 = (f32[256,128]{1,0:T(8,128)S(1)}, f32[256,128]{1,0:T(8,128)S(1)}, u32[]{:S(2)}, u32[]{:S(2)}) collective-permute-start(f32[256,128]{1,0:T(8,128)S(1)} %dynamic-slice_bitcast_fusion.1), channel_id=1, source_target_pairs={{0,1},{1,0},{2,3},{3,2},{4,5},{5,4},{6,7},{7,6},{8,9},{9,8},{10,11... | collective-permute-start | bytes 393224 | tf_op jit(solution)/shard_map/ppermute | solution.py:278
  30.7 1.7 %collective-permute-start.2 = (f32[320,128]{1,0:T(8,128)S(1)}, f32[320,128]{1,0:T(8,128)S(1)}, u32[]{:S(2)}, u32[]{:S(2)}) collective-permute-start(f32[320,128]{1,0:T(8,128)S(1)} %dynamic-slice_bitcast_fusion), channel_id=1, source_target_pairs={{0,1},{1,0},{2,3},{3,2},{4,5},{5,4},{6,7},{7,6},{8,9},{9,8},{10,11... | collective-permute-start | bytes 491528 | tf_op jit(solution)/shard_map/ppermute | solution.py:278
  30.8 22.5 %copy-start.8 = (f32[16,4]{0,1:T(4,128)S(1)}, f32[16,4]{0,1:T(4,128)}, u32[]{:S(2)}) copy-start(f32[16,4]{0,1:T(4,128)} %param.17) | copy-start | bytes 772
  30.8 6.5 %collective-permute-start.7 = (f32[256,128]{1,0:T(8,128)S(1)}, f32[256,128]{1,0:T(8,128)}, u32[]{:S(2)}, u32[]{:S(2)}) collective-permute-start(f32[256,128]{1,0:T(8,128)S(1)} %bitcast_add_fusion.1.refs_2_), channel_id=1, source_target_pairs={{0,2},{1,3},{2,0},{3,1},{4,6},{5,7},{6,4},{7,5},{8,10},{9,11},{10,... | collective-permute-start | bytes 393224 | tf_op jit(solution)/shard_map/ppermute | solution.py:278
  32.4 8.0 %collective-permute-start.3 = (f32[320,128]{1,0:T(8,128)S(1)}, f32[320,128]{1,0:T(8,128)}, u32[]{:S(2)}, u32[]{:S(2)}) collective-permute-start(f32[320,128]{1,0:T(8,128)S(1)} %bitcast_add_fusion.refs_0_), channel_id=1, source_target_pairs={{0,2},{1,3},{2,0},{3,1},{4,6},{5,7},{6,4},{7,5},{8,10},{9,11},{10,... | collective-permute-start | bytes 491528 | tf_op jit(solution)/shard_map/ppermute | solution.py:278
  34.1 19.2 %copy-start.1 = (f32[8,128,128]{2,1,0:T(8,128)}, f32[8,128,128]{2,1,0:T(8,128)S(1)}, u32[]{:S(2)}) copy-start(f32[8,128,128]{2,1,0:T(8,128)S(1)} %subtract_divide_fusion.refs_10_) | copy-start | bytes 1572868
  34.2 7.3 %collective-permute-start.10 = (f32[256,128]{1,0:T(8,128)S(1)}, f32[256,128]{1,0:T(8,128)S(1)}, u32[]{:S(2)}, u32[]{:S(2)}) collective-permute-start(f32[256,128]{1,0:T(8,128)S(1)} %bitcast_add_fusion.1.refs_2_), channel_id=1, source_target_pairs={{0,1},{1,0},{2,3},{3,2},{4,5},{5,4},{6,7},{7,6},{8,9},{9,8},{10,11... | collective-permute-start | bytes 393224 | tf_op jit(solution)/shard_map/ppermute | solution.py:278
  34.2 7.3 %collective-permute-start.8 = (f32[320,128]{1,0:T(8,128)S(1)}, f32[320,128]{1,0:T(8,128)S(1)}, u32[]{:S(2)}, u32[]{:S(2)}) collective-permute-start(f32[320,128]{1,0:T(8,128)S(1)} %bitcast_add_fusion.refs_0_), channel_id=1, source_target_pairs={{0,1},{1,0},{2,3},{3,2},{4,5},{5,4},{6,7},{7,6},{8,9},{9,8},{10,11... | collective-permute-start | bytes 491528 | tf_op jit(solution)/shard_map/ppermute | solution.py:278
  37.3 4.2 %collective-permute-start.11 = (f32[256,128]{1,0:T(8,128)}, f32[256,128]{1,0:T(8,128)S(1)}, u32[]{:S(2)}, u32[]{:S(2)}) collective-permute-start(f32[256,128]{1,0:T(8,128)} %collective-permute-done.7.refs_3_), channel_id=1, source_target_pairs={{0,1},{1,0},{2,3},{3,2},{4,5},{5,4},{6,7},{7,6},{8,9},{9,8},{10,11... | collective-permute-start | bytes 393224 | tf_op jit(solution)/shard_map/ppermute | solution.py:278
  40.4 1.6 %collective-permute-start.9 = (f32[320,128]{1,0:T(8,128)}, f32[320,128]{1,0:T(8,128)S(1)}, u32[]{:S(2)}, u32[]{:S(2)}) collective-permute-start(f32[320,128]{1,0:T(8,128)} %collective-permute-done.3.refs_1_), channel_id=1, source_target_pairs={{0,1},{1,0},{2,3},{3,2},{4,5},{5,4},{6,7},{7,6},{8,9},{9,8},{10,11... | collective-permute-start | bytes 491528 | tf_op jit(solution)/shard_map/ppermute | solution.py:278
  41.4 11.9 %copy-start.4 = (bf16[8,128,128]{2,1,0:T(8,128)(2,1)}, bf16[8,128,128]{2,1,0:T(8,128)(2,1)S(1)}, u32[]{:S(2)}) copy-start(bf16[8,128,128]{2,1,0:T(8,128)(2,1)S(1)} %get-tuple-element.20.refs_8_.first_ref) | copy-start | bytes 786436
  42.0 20.4 %copy-start.9 = (s32[64,4]{0,1:T(4,128)S(1)}, s32[64,4]{0,1:T(4,128)}, u32[]{:S(2)}) copy-start(s32[64,4]{0,1:T(4,128)} %param.22) | copy-start | bytes 3076
  42.0 20.4 %copy-start.13 = (s32[4]{0:T(128)S(1)}, s32[4]{0:T(128)}, u32[]{:S(2)}) copy-start(s32[4]{0:T(128)} %constant.106.clone) | copy-start | bytes 52
  42.0 21.1 %copy-start.12 = (s32[4]{0:T(128)S(1)}, s32[4]{0:T(128)}, u32[]{:S(2)}) copy-start(s32[4]{0:T(128)} %constant.105.clone) | copy-start | bytes 52
  42.0 21.7 %copy-start.11 = (s32[4]{0:T(128)S(1)}, s32[4]{0:T(128)}, u32[]{:S(2)}) copy-start(s32[4]{0:T(128)} %constant.104.clone) | copy-start | bytes 52
  44.4 0.8 copy-start.6
  45.2 12.3 %collective-permute-start.17 = (bf16[8,128,128]{2,1,0:T(8,128)(2,1)}, bf16[8,128,128]{2,1,0:T(8,128)(2,1)}, u32[]{:S(2)}, u32[]{:S(2)}) collective-permute-start(bf16[8,128,128]{2,1,0:T(8,128)(2,1)} %get-tuple-element.6.refs_0_), channel_id=1, source_target_pairs={{4,12},{8,0},{5,13},{9,1},{6,14},{10,2},{7,15},{11,3},{20,28},{24,... | collective-permute-start | bytes 786440 | tf_op jit(solution)/shard_map/ppermute | solution.py:375
  46.5 11.0 %collective-permute-start.15 = (bf16[8,128,128]{2,1,0:T(8,128)(2,1)}, bf16[8,128,128]{2,1,0:T(8,128)(2,1)}, u32[]{:S(2)}, u32[]{:S(2)}) collective-permute-start(bf16[8,128,128]{2,1,0:T(8,128)(2,1)} %get-tuple-element.6.refs_0_), channel_id=1, source_target_pairs={{4,8},{8,4},{5,9},{9,5},{6,10},{10,6},{7,11},{11,7},{20,24},{24,20... | collective-permute-start | bytes 786440 | tf_op jit(solution)/shard_map/ppermute | solution.py:375
  47.9 14.4 %collective-permute-start.13 = (bf16[8,128,128]{2,1,0:T(8,128)(2,1)}, bf16[8,128,128]{2,1,0:T(8,128)(2,1)}, u32[]{:S(2)}, u32[]{:S(2)}) collective-permute-start(bf16[8,128,128]{2,1,0:T(8,128)(2,1)} %get-tuple-element.6.refs_0_), channel_id=1, source_target_pairs={{0,4},{4,0},{8,12},{12,8},{1,5},{5,1},{9,13},{13,9},{2,6},{6,2},{1... | collective-permute-start | bytes 786440 | tf_op jit(solution)/shard_map/ppermute | solution.py:375
  53.5 13.0 %collective-permute-start.12 = (bf16[8,128,128]{2,1,0:T(8,128)(2,1)}, bf16[8,128,128]{2,1,0:T(8,128)(2,1)}, u32[]{:S(2)}, u32[]{:S(2)}) collective-permute-start(bf16[8,128,128]{2,1,0:T(8,128)(2,1)} %get-tuple-element.6.refs_0_), channel_id=1, source_target_pairs={{0,1},{1,0},{2,3},{3,2},{4,5},{5,4},{6,7},{7,6},{8,9},{9,8},{10,11... | collective-permute-start | bytes 786440 | tf_op jit(solution)/shard_map/ppermute | solution.py:278
  57.5 8.9 %collective-permute-start.18 = (bf16[8,128,128]{2,1,0:T(8,128)(2,1)}, bf16[8,128,128]{2,1,0:T(8,128)(2,1)}, u32[]{:S(2)}, u32[]{:S(2)}) collective-permute-start(bf16[8,128,128]{2,1,0:T(8,128)(2,1)} %collective-permute-done.17.refs_6_), channel_id=1, source_target_pairs={{0,1},{1,0},{2,3},{3,2},{4,5},{5,4},{6,7},{7,6},{8,9},{9,8},{10,11... | collective-permute-start | bytes 786440 | tf_op jit(solution)/shard_map/ppermute | solution.py:278
  57.5 8.9 %collective-permute-start.16 = (bf16[8,128,128]{2,1,0:T(8,128)(2,1)}, bf16[8,128,128]{2,1,0:T(8,128)(2,1)}, u32[]{:S(2)}, u32[]{:S(2)}) collective-permute-start(bf16[8,128,128]{2,1,0:T(8,128)(2,1)} %collective-permute-done.15.refs_4_), channel_id=1, source_target_pairs={{0,1},{1,0},{2,3},{3,2},{4,5},{5,4},{6,7},{7,6},{8,9},{9,8},{10,11... | collective-permute-start | bytes 786440 | tf_op jit(solution)/shard_map/ppermute | solution.py:278
  62.3 4.1 %collective-permute-start.14 = (bf16[8,128,128]{2,1,0:T(8,128)(2,1)}, bf16[8,128,128]{2,1,0:T(8,128)(2,1)}, u32[]{:S(2)}, u32[]{:S(2)}) collective-permute-start(bf16[8,128,128]{2,1,0:T(8,128)(2,1)} %collective-permute-done.13.refs_2_), channel_id=1, source_target_pairs={{0,1},{1,0},{2,3},{3,2},{4,5},{5,4},{6,7},{7,6},{8,9},{9,8},{10,11... | collective-permute-start | bytes 786440 | tf_op jit(solution)/shard_map/ppermute | solution.py:278
  66.5 1.0 copy-start.2
  67.5 1.0 copy-start.7
  73.3 29.9 %copy-start.5 = (bf16[8,128,128]{2,1,0:T(8,128)(2,1)S(1)}, bf16[8,128,128]{2,1,0:T(8,128)(2,1)}, u32[]{:S(2)}) copy-start(bf16[8,128,128]{2,1,0:T(8,128)(2,1)} %copy-done.4) | copy-start | bytes 786436
  73.3 12.1 %collective-permute-start.24 = (bf16[8,128,128]{2,1,0:T(8,128)(2,1)S(1)}, bf16[8,128,128]{2,1,0:T(8,128)(2,1)S(1)}, u32[]{:S(2)}, u32[]{:S(2)}) collective-permute-start(bf16[8,128,128]{2,1,0:T(8,128)(2,1)S(1)} %sweep.1.refs_0_), channel_id=1, source_target_pairs={{4,12},{8,0},{5,13},{9,1},{6,14},{10,2},{7,15},{11,3},{20,28},{24,... | collective-permute-start | bytes 786440 | tf_op jit(solution)/shard_map/ppermute | solution.py:375
  74.7 10.6 %collective-permute-start.22 = (bf16[8,128,128]{2,1,0:T(8,128)(2,1)S(1)}, bf16[8,128,128]{2,1,0:T(8,128)(2,1)S(1)}, u32[]{:S(2)}, u32[]{:S(2)}) collective-permute-start(bf16[8,128,128]{2,1,0:T(8,128)(2,1)S(1)} %sweep.1.refs_0_), channel_id=1, source_target_pairs={{4,8},{8,4},{5,9},{9,5},{6,10},{10,6},{7,11},{11,7},{20,24},{24,20... | collective-permute-start | bytes 786440 | tf_op jit(solution)/shard_map/ppermute | solution.py:375
  75.4 15.1 %collective-permute-start.20 = (bf16[8,128,128]{2,1,0:T(8,128)(2,1)S(1)}, bf16[8,128,128]{2,1,0:T(8,128)(2,1)S(1)}, u32[]{:S(2)}, u32[]{:S(2)}) collective-permute-start(bf16[8,128,128]{2,1,0:T(8,128)(2,1)S(1)} %sweep.1.refs_0_), channel_id=1, source_target_pairs={{0,4},{4,0},{8,12},{12,8},{1,5},{5,1},{9,13},{13,9},{2,6},{6,2},{1... | collective-permute-start | bytes 786440 | tf_op jit(solution)/shard_map/ppermute | solution.py:375
  80.8 9.8 %collective-permute-start.19 = (bf16[8,128,128]{2,1,0:T(8,128)(2,1)S(1)}, bf16[8,128,128]{2,1,0:T(8,128)(2,1)S(1)}, u32[]{:S(2)}, u32[]{:S(2)}) collective-permute-start(bf16[8,128,128]{2,1,0:T(8,128)(2,1)S(1)} %sweep.1.refs_0_), channel_id=1, source_target_pairs={{0,1},{1,0},{2,3},{3,2},{4,5},{5,4},{6,7},{7,6},{8,9},{9,8},{10,11... | collective-permute-start | bytes 786440 | tf_op jit(solution)/shard_map/ppermute | solution.py:278
  85.3 5.2 %collective-permute-start.25 = (bf16[8,128,128]{2,1,0:T(8,128)(2,1)S(1)}, bf16[8,128,128]{2,1,0:T(8,128)(2,1)S(1)}, u32[]{:S(2)}, u32[]{:S(2)}) collective-permute-start(bf16[8,128,128]{2,1,0:T(8,128)(2,1)S(1)} %collective-permute-done.24.refs_6_), channel_id=1, source_target_pairs={{0,1},{1,0},{2,3},{3,2},{4,5},{5,4},{6,7},{7,6},{8,9},{9,8},{10,11... | collective-permute-start | bytes 786440 | tf_op jit(solution)/shard_map/ppermute | solution.py:278
  85.4 5.2 %collective-permute-start.23 = (bf16[8,128,128]{2,1,0:T(8,128)(2,1)S(1)}, bf16[8,128,128]{2,1,0:T(8,128)(2,1)S(1)}, u32[]{:S(2)}, u32[]{:S(2)}) collective-permute-start(bf16[8,128,128]{2,1,0:T(8,128)(2,1)S(1)} %collective-permute-done.22.refs_4_), channel_id=1, source_target_pairs={{0,1},{1,0},{2,3},{3,2},{4,5},{5,4},{6,7},{7,6},{8,9},{9,8},{10,11... | collective-permute-start | bytes 786440 | tf_op jit(solution)/shard_map/ppermute | solution.py:278
  90.5 1.5 %collective-permute-start.21 = (bf16[8,128,128]{2,1,0:T(8,128)(2,1)S(1)}, bf16[8,128,128]{2,1,0:T(8,128)(2,1)S(1)}, u32[]{:S(2)}, u32[]{:S(2)}) collective-permute-start(bf16[8,128,128]{2,1,0:T(8,128)(2,1)S(1)} %collective-permute-done.20.refs_2_), channel_id=1, source_target_pairs={{0,1},{1,0},{2,3},{3,2},{4,5},{5,4},{6,7},{7,6},{8,9},{9,8},{10,11... | collective-permute-start | bytes 786440 | tf_op jit(solution)/shard_map/ppermute | solution.py:278
  98.9 7.1 %collective-permute-start.27 = (f32[2,128,128]{2,1,0:T(8,128)S(1)}, f32[2,128,128]{2,1,0:T(8,128)S(1)}, u32[]{:S(2)}, u32[]{:S(2)}) collective-permute-start(f32[2,128,128]{2,1,0:T(8,128)S(1)} %get-tuple-element.15), channel_id=1, source_target_pairs={{0,4},{4,8},{8,12},{1,5},{5,9},{9,13},{2,6},{6,10},{10,14},{3,7},{... | collective-permute-start | bytes 393224 | tf_op jit(solution)/shard_map/ppermute | solution.py:395
  101.8 7.2 %collective-permute-start.28 = (f32[2,128,128]{2,1,0:T(8,128)S(1)}, f32[2,128,128]{2,1,0:T(8,128)S(1)}, u32[]{:S(2)}, u32[]{:S(2)}) collective-permute-start(f32[2,128,128]{2,1,0:T(8,128)S(1)} %get-tuple-element.16), channel_id=1, source_target_pairs={{4,0},{8,4},{12,8},{5,1},{9,5},{13,9},{6,2},{10,6},{14,10},{7,3},{... | collective-permute-start | bytes 393224 | tf_op jit(solution)/shard_map/ppermute | solution.py:396
  103.1 8.0 %collective-permute-start.26 = (f32[8,128,128]{2,1,0:T(8,128)}, f32[8,128,128]{2,1,0:T(8,128)S(1)}, u32[]{:S(2)}, u32[]{:S(2)}) collective-permute-start(f32[8,128,128]{2,1,0:T(8,128)} %get-tuple-element.8.amps_ref), channel_id=1, source_target_pairs={{0,1},{1,0},{2,3},{3,2},{4,5},{5,4},{6,7},{7,6},{8,9},{9,8},{10,11... | collective-permute-start | bytes 1572872 | tf_op jit(solution)/shard_map/ppermute | solution.py:278
  109.0 1.4 %collective-permute-start.29 = (f32[2,128,128]{2,1,0:T(8,128)S(1)}, f32[2,128,128]{2,1,0:T(8,128)S(1)}, u32[]{:S(2)}, u32[]{:S(2)}) collective-permute-start(f32[2,128,128]{2,1,0:T(8,128)S(1)} %add_add_fusion), channel_id=1, source_target_pairs={{0,1},{1,0},{2,3},{3,2},{4,5},{5,4},{6,7},{7,6},{8,9},{9,8},{10,11... | collective-permute-start | bytes 393224 | tf_op jit(solution)/shard_map/ppermute | solution.py:278

commit v2 on v1

v2 whole, which is shorter than its diff:
```python
import functools

import jax
import jax.numpy as jnp
from jax import lax
from jax.experimental import pallas as pl
from jax.experimental.pallas import tpu as pltpu
from jax.sharding import PartitionSpec as P

ITERS = 2
BF16 = jnp.bfloat16
F32 = jnp.float32
VMEM = pl.BlockSpec(memory_space=pltpu.VMEM)
SMEM = pl.BlockSpec(memory_space=pltpu.SMEM)
ANY = pl.BlockSpec(memory_space=pl.ANY)


def params(mib):
    return pltpu.CompilerParams(vmem_limit_bytes=mib * 2**20)


def dot(left, right, dims):
    return lax.dot_general(left, right, (dims, ((), ())), preferred_element_type=F32)


def split(value):
    high = value.astype(BF16)
    return high, (value - high.astype(F32)).astype(BF16)


def square(value):
    high, rest = split(value)
    return dot(
        jnp.concatenate([high, high, rest, rest], axis=1),
        jnp.concatenate([high, rest, high, rest], axis=1),
        ((1,), (1,)),
    )


def cost(flops, size):
    return pl.CostEstimate(flops=flops, bytes_accessed=size, transcendentals=0)


def product_kernel(own_ref, up_ref, down_ref, out_ref):
    count, _, width = own_ref.shape
    own = jnp.concatenate([own_ref[i] for i in range(count)], axis=1)
    at = 0
    for near_ref in (up_ref, down_ref):
        near = jnp.concatenate([near_ref[i] for i in range(count)], axis=1)
        full = dot(own, near, ((0,), (0,)))
        for j in range(count):
            for i in range(count):
                out_ref[i, at : at + width] = full[
                    i * width : (i + 1) * width, j * width : (j + 1) * width
                ]
            at += width
    half = width // 2
    inner = dot(own_ref[0], own_ref[1], ((0,), (0,)))
    out_ref[0, at:] = inner[:half]
    out_ref[1, at:] = inner[half:]


def products(ints, up, down):
    count, depth, width = ints.shape
    rows = 2 * count * width + width // 2
    return pl.pallas_call(
        product_kernel,
        out_shape=jax.ShapeDtypeStruct((count, rows, width), F32),
        in_specs=[VMEM] * 3,
        out_specs=VMEM,
        compiler_params=params(12),
        cost_estimate=cost(18 * depth * width * width, 12 * depth * width),
        name="products",
    )(ints, up, down)


def exchange_kernel(
    here_ref, half_ref, orbitals_ref, total_ref, far_ref, total_other, far_other,
    first_ref, second_ref, factor_ref, exch_ref, low_ref, table,
):
    count, width, _ = exch_ref.shape
    half = half_ref[0]
    base = here_ref[0] * 2 - 2
    for i, total in (
        (half, total_ref[...] + far_ref[...]),
        (1 - half, total_other[...] + far_other[...]),
    ):
        for at, slot in enumerate((4, 5, 0, 1)):
            table[i * 6 + slot] = total[at * width : (at + 1) * width]
        table[3, pl.ds(pl.multiple_of(i * (width // 2), width // 2), width // 2)] = total[4 * width :]
    table[6 + 2] = table[3].T
    for p in range(count):
        row = half * count + p
        slot = (orbitals_ref[0, row] - base - 2) * 6 + orbitals_ref[1, row] - base
        right = second_ref[p]
        left = first_ref[p]
        high, rest = split(table[slot])
        inner = dot(
            jnp.concatenate([high, rest], axis=1),
            jnp.concatenate([right, right], axis=0),
            ((1,), (0,)),
        )
        high, rest = split(inner)
        exch = dot(
            jnp.concatenate([left, left], axis=0),
            jnp.concatenate([high, rest], axis=0),
            ((0,), (0,)),
        )
        exch_ref[p] = exch
        low_ref[p] = (factor_ref[p] * exch).astype(BF16)


def exchange(here, half, orbitals, sums, first, second, factor):
    shape = first.shape
    count, width, _ = shape
    return pl.pallas_call(
        exchange_kernel,
        out_shape=(jax.ShapeDtypeStruct(shape, F32), jax.ShapeDtypeStruct(shape, BF16)),
        in_specs=[SMEM] * 3 + [VMEM] * (len(sums) + 3),
        out_specs=(VMEM, VMEM),
        scratch_shapes=[pltpu.VMEM((12, width, width), F32)],
        compiler_params=params(12),
        cost_estimate=cost(8 * count * width**3, 20 * count * width * width),
        name="exchange",
    )(here, half, orbitals, *sums, first, second, factor)


def sweep_kernel(last, pieces, rounds, here_ref, half_ref, orbitals_ref, near_ref, couple_ref, *refs):
    parts = refs[:pieces]
    over_ref, exch_ref, factor_ref, second_ref = refs[pieces : pieces + 4]
    if last:
        amps_ref, terms_ref, table = refs[pieces + 4 :]
    else:
        low_ref, table = refs[pieces + 4 :]
    count, width, _ = exch_ref.shape
    pair_dev, nbr_count = over_ref.shape[:2]
    here = here_ref[0]
    half = half_ref[0]
    at = 0
    for part in parts:
        table[at : at + part.shape[0]] = part[...]
        at += part.shape[0]
    sources = []
    for pairs in rounds or ():
        source = -1
        for start, end in pairs:
            source = jnp.where(here == end, start, source)
        sources.append(source)

    def place(p, n):
        if rounds is None:
            return p * nbr_count + n
        wanted = near_ref[n, here * pair_dev + half * count + p]
        owner = wanted // pair_dev
        local = wanted - owner * pair_dev
        slot = 0
        for at, source in enumerate(sources):
            slot = jnp.where(owner == source, 2 * at + 2, slot)
        side = local // count
        return (slot + jnp.where(side == half, 0, 1)) * count + local - side * count

    done = []
    for p in range(count):
        row = half * count + p
        halves = []
        for n in range(nbr_count):
            moved = dot(over_ref[row, n], table[place(p, n)], ((1,), (0,)))
            halves.append((couple_ref[n, row] * moved).astype(BF16))
        coupled = dot(
            jnp.concatenate(halves, axis=1),
            jnp.concatenate([over_ref[row, n] for n in range(nbr_count)], axis=1),
            ((1,), (1,)),
        )
        amps = factor_ref[p] * (exch_ref[p] - coupled)
        if last:
            amps_ref[p] = amps
            done.append(amps)
        else:
            low_ref[p] = amps.astype(BF16)
    if last:
        terms = []
        for p in range(count):
            right = second_ref[p]
            high, rest = split(done[p])
            moved = dot(
                jnp.concatenate([right, right], axis=1),
                jnp.concatenate([high, rest], axis=1),
                ((1,), (1,)),
            )
            terms.append(square(moved))
        terms_ref[...] = jnp.zeros_like(terms_ref)
        for p in range(count):
            spot = orbitals_ref[1, half * count + p] - here * 2 + 2
            terms_ref[spot] += terms[p]


def sweep(last, rounds, here, half, orbitals, near, couple, parts, over, exch, factor, second):
    count, width, _ = exch.shape
    rows = sum(part.shape[0] for part in parts)
    if last:
        out_shape = (
            jax.ShapeDtypeStruct(exch.shape, F32),
            jax.ShapeDtypeStruct((6, width, width), F32),
        )
        out_specs = (VMEM, VMEM)
    else:
        out_shape = jax.ShapeDtypeStruct(exch.shape, BF16)
        out_specs = VMEM
    return pl.pallas_call(
        functools.partial(sweep_kernel, last, len(parts), rounds),
        out_shape=out_shape,
        in_specs=[SMEM] * 5 + [VMEM] * (len(parts) + 4),
        out_specs=out_specs,
        scratch_shapes=[pltpu.VMEM((rows, width, width), BF16)],
        compiler_params=params(16),
        cost_estimate=cost(16 * count * width**3, (rows + 16 * count) * width * width),
        name="last_sweep" if last else "sweep",
    )(here, half, orbitals, near, couple, *parts, over, exch, factor, second)


def first_kernel(
    here_ref, half_ref, orbitals_ref, amps_ref, others_ref, first_ref, whole_ref, terms_ref, sems
):
    count = amps_ref.shape[0]
    half = half_ref[0]
    copies = [
        pltpu.make_async_copy(amps_ref, whole_ref.at[pl.ds(half * count, count)], sems.at[0]),
        pltpu.make_async_copy(others_ref, whole_ref.at[pl.ds((1 - half) * count, count)], sems.at[1]),
    ]
    for copy in copies:
        copy.start()
    terms = []
    for p in range(count):
        high, rest = split(amps_ref[p])
        left = first_ref[p]
        moved = dot(
            jnp.concatenate([left, left], axis=1),
            jnp.concatenate([high, rest], axis=0),
            ((1,), (0,)),
        )
        terms.append(square(moved))
    terms_ref[...] = jnp.zeros_like(terms_ref)
    for p in range(count):
        spot = orbitals_ref[0, half * count + p] - here_ref[0] * 2
        terms_ref[spot] += terms[p]
    for copy in copies:
        copy.wait()


def first_terms(here, half, orbitals, amps, others, first):
    count, width, _ = amps.shape
    return pl.pallas_call(
        first_kernel,
        out_shape=(
            jax.ShapeDtypeStruct((2 * count, width, width), F32),
            jax.ShapeDtypeStruct((2, width, width), F32),
        ),
        in_specs=[SMEM] * 3 + [VMEM] * 3,
        out_specs=(ANY, VMEM),
        scratch_shapes=[pltpu.SemaphoreType.DMA((2,))],
        compiler_params=params(12),
        cost_estimate=cost(12 * count * width**3, 16 * count * width * width),
        name="first_terms",
    )(here, half, orbitals, amps, others, first)


def window_rounds(groups):
    reach = groups // 4
    span = 2 * reach + 1
    edges = []
    for block in range(groups):
        start = min(max(block - reach, 0), groups - span)
        edges += [(source, block) for source in range(start, start + span) if source != block]
    edges.sort(key=lambda edge: (abs(edge[0] - edge[1]), edge))
    rounds = []
    for source, block in edges:
        for pairs in rounds:
            if all(source != s and block != d for s, d in pairs):
                pairs.append((source, block))
                break
        else:
            rounds.append([(source, block)])
    return rounds[::-1]


def same_owner_rank(owners):
    count = owners.shape[-1]
    places = jnp.arange(count)
    earlier = places[:, None] > places[None, :]
    same = owners[..., :, None] == owners[..., None, :]
    return jnp.sum(same & earlier, axis=-1)


def shards(
    ints,
    proj_first,
    proj_second,
    intersections,
    couple,
    virt_energy,
    occ_energy,
    pno_count,
    pair_orbitals,
    neighbours,
):
    groups = lax.axis_size("pair")
    here = lax.axis_index("pair")
    aux_count = lax.axis_size("aux")
    half = lax.axis_index("aux") % 2
    occ_dev, _, width = ints.shape
    pair_dev = proj_first.shape[0]
    nbr_count = couple.shape[1]
    wanted = pair_dev * nbr_count
    cap = 2 * wanted // groups
    count = pair_dev // 2
    up = [(i + 1, i) for i in range(groups - 1)]
    down = [(i, i + 1) for i in range(groups - 1)]
    here_s = here.reshape(1)
    half_s = half.reshape(1)
    orbitals = pair_orbitals.T

    def swap(value, step=1):
        return lax.ppermute(value, "aux", [(i, i ^ step) for i in range(aux_count)])

    above = lax.ppermute(ints, "pair", up)
    below = lax.ppermute(ints, "pair", down)

    def own(value):
        return lax.dynamic_slice_in_dim(value, half * count, count, 0)

    first = own(proj_first)
    second = own(proj_second)
    valid = jnp.arange(width)[None, :] < pno_count[:, None]
    mask = (valid[:, :, None] & valid[:, None, :]).astype(F32)
    denom = (
        virt_energy[:, :, None]
        + virt_energy[:, None, :]
        - occ_energy[:, 0, None, None]
        - occ_energy[:, 1, None, None]
    )
    factor = own(-mask / denom)
    above, first, second, factor = lax.optimization_barrier((above, first, second, factor))

    partial = products(ints, above, below)
    kept = lax.dynamic_index_in_dim(partial, half, 0, keepdims=False)
    sent = lax.dynamic_index_in_dim(partial, 1 - half, 0, keepdims=False)
    total = kept + swap(sent)
    step = 2
    while 2 * step < aux_count:
        total = total + swap(total, step)
        step *= 2
    far = swap(total, step)
    exch, low = exchange(
        here_s, half_s, orbitals, (total, far, swap(total), swap(far)), first, second, factor
    )

    if cap < pair_dev:
        rounds = None
        requests = neighbours.reshape(groups, wanted)
        owners = requests // pair_dev
        ranks = same_owner_rank(owners)
        at_home = owners == here
        pick = at_home[:, None, :] & (ranks[:, None, :] == jnp.arange(cap)[None, :, None])
        local = requests % pair_dev
        select = jnp.any(
            pick[..., None]
            & (local[:, None, :, None] == jnp.arange(pair_dev)[None, None, None, :]),
            axis=2,
        )
        select = select.astype(BF16).reshape(groups * cap, pair_dev)
        own_requests = lax.dynamic_slice_in_dim(requests, here, 1, 0)[0]
        own_ranks = lax.dynamic_slice_in_dim(ranks, here, 1, 0)[0]
        row_index = lax.dynamic_slice_in_dim(
            own_requests // pair_dev * cap + own_ranks,
            half * count * nbr_count,
            count * nbr_count,
            0,
        )
    else:
        rounds = window_rounds(groups)

    def gathered(low):
        if rounds is None:
            others = swap(low)
            flat = jnp.where(
                half == 0, jnp.concatenate([low, others]), jnp.concatenate([others, low])
            ).reshape(pair_dev, width * width)
            outgoing = jnp.dot(select, flat, preferred_element_type=F32).astype(BF16)
            outgoing = outgoing.reshape(groups, cap, width, width)
            received = lax.all_to_all(outgoing, "pair", split_axis=0, concat_axis=0, tiled=True)
            return [received.reshape(groups * cap, width, width)[row_index]]
        pieces = [low] + [lax.ppermute(low, "pair", pairs) for pairs in rounds]
        return [value for piece in pieces for value in (piece, swap(piece))]

    for it in range(ITERS):
        out = sweep(
            it == ITERS - 1,
            rounds,
            here_s,
            half_s,
            orbitals,
            neighbours.T,
            couple.T,
            gathered(low),
            intersections,
            exch,
            factor,
            second,
        )
        if it < ITERS - 1:
            low = out
    amps, terms = out

    from_below = lax.ppermute(terms[2 * occ_dev :], "pair", down)
    from_above = lax.ppermute(terms[:occ_dev], "pair", up)
    whole, inner = first_terms(here_s, half_s, orbitals, amps, swap(amps), first)
    density = inner + terms[occ_dev : 2 * occ_dev] + from_below + from_above
    density = (density + swap(density)) / width
    return (whole, density)


def solution(mesh):
    return jax.shard_map(
        shards,
        mesh=mesh,
        in_specs=(
            P(("mol", "pair"), "aux", None),
            P(("mol", "pair"), None, None),
            P(("mol", "pair"), None, None),
            P(("mol", "pair"), None, None, None),
            P(("mol", "pair"), None),
            P(("mol", "pair"), None),
            P(("mol", "pair"), None),
            P(("mol", "pair")),
            P(("mol", "pair"), None),
            P("mol", None),
        ),
        out_specs=(P(("mol", "pair"), None, None), P(("mol", "pair"), None, None)),
        check_vma=False,
    )
```

time: 114 us -> 98 us (0.86)
  the two profiles are of different devices: /device:TPU:0 before, /device:TPU:15 now
where the time goes in v2:
time: 98 us; the launch traced here: 97.2 us
  starting transfers between devices  40.7 us (42%)
  waiting for transfers between devices  39.8 us (41%)
  Pallas kernels  10.1 us (10%)
  local copies, waits for them, and re-layouts  2.87 us (3%)
  other arithmetic  2.86 us (3%)
    ppermute x14, starting transfers between devices, swap(): return lax.ppermute(value, 'aux', [(i, i ^ step) for i in range(aux_count)])  17.4 us
    ppermute x14, waiting for transfers between devices, swap(): return lax.ppermute(value, 'aux', [(i, i ^ step) for i in range(aux_count)])  13.6 us
    ppermute x6, starting transfers between devices, gathered(): pieces = [low] + [lax.ppermute(low, 'pair', pairs) for pairs in rounds]  12.6 us
    ppermute x1, waiting for transfers between devices, shards(): above = lax.ppermute(ints, 'pair', up)  12.1 us
    ppermute x6, waiting for transfers between devices, gathered(): pieces = [low] + [lax.ppermute(low, 'pair', pairs) for pairs in rounds]  9.75 us
    pallas_call x2, Pallas kernels, sweep(): pl.pallas_call(functools.partial(sweep_kernel, last, len(parts), rounds),...  4.77 us
    ppermute x1, starting transfers between devices, shards(): from_above = lax.ppermute(terms[:occ_dev], 'pair', up)  3.37 us
    ppermute x1, starting transfers between devices, shards(): below = lax.ppermute(ints, 'pair', down)  3.2 us
  transfers between devices with their start and end apart: 24, of which 15 were waited for; matrix products, arithmetic and copies ran while one was open for 3% of the time, Pallas kernels for 3%

profile of v2, /device:TPU:15, one launch (start us, length us, event | category | flops | bytes accessed | tf_op | source)
XLA Modules:
  0.0 97.2 jit_solution(5616934975585382811)
XLA Ops:
  0.6 0.0 copy-start
  0.7 2.2 %collective-permute-start = (bf16[2,1536,128]{2,1,0:T(8,128)(2,1)}, bf16[2,1536,128]{2,1,0:T(8,128)(2,1)S(1)}, u32[]{:S(2)}, u32[]{:S(2)}) collective-permute-start(bf16[2,1536,128]{2,1,0:T(8,128)(2,1)} %own_ref.1), channel_id=1, source_target_pairs={{4,0},{8,4},{12,8},{5,1},{9,5},{13,9},{6,2},{10,6},{14,10},{7,3},{... | collective-permute-start | bytes 2359304 | tf_op jit(solution)/shard_map/ppermute | solution.py:325
  2.9 3.2 %collective-permute-start.1 = (bf16[2,1536,128]{2,1,0:T(8,128)(2,1)}, bf16[2,1536,128]{2,1,0:T(8,128)(2,1)S(1)}, u32[]{:S(2)}, u32[]{:S(2)}) collective-permute-start(bf16[2,1536,128]{2,1,0:T(8,128)(2,1)} %own_ref.1), channel_id=1, source_target_pairs={{0,4},{4,8},{8,12},{1,5},{5,9},{9,13},{2,6},{6,10},{10,14},{3,7},{... | collective-permute-start | bytes 2359304 | tf_op jit(solution)/shard_map/ppermute | solution.py:326
  6.1 0.8 slice_bitcast_fusion.1
  6.9 0.1 dynamic-slice.4
  6.9 0.1 dynamic-slice.5
  7.0 0.7 iota_compare_fusion
  7.8 1.1 %constant_dynamic-slice_fusion.2 = (bf16[8,128,128]{2,1,0:T(8,128)(2,1)S(1)}, bf16[8,128,128]{2,1,0:T(8,128)(2,1)S(1)}) fusion(bf16[16,128,128]{2,1,0:T(8,128)(2,1)} %param.12, s32[]{:T(128)S(6)} %select_n.20, bf16[16,128,128]{2,1,0:T(8,128)(2,1)} %param.11), kind=kLoop, calls=%fused_computation.8 | loop fusion | bytes 1048580 | tf_op jit(solution)/shard_map/dynamic_slice | solution.py:329
  8.8 0.4 subtract_divide_fusion.factor_ref.refs_10_
  9.2 12.1 %collective-permute-done.up_ref = bf16[2,1536,128]{2,1,0:T(8,128)(2,1)S(1)} collective-permute-done((bf16[2,1536,128]{2,1,0:T(8,128)(2,1)}, bf16[2,1536,128]{2,1,0:T(8,128)(2,1)S(1)}, u32[]{:S(2)}, u32[]{:S(2)}) %collective-permute-start) | collective-permute-done | bytes 786464 | tf_op jit(solution)/shard_map/ppermute | solution.py:325
  21.3 1.8 %collective-permute-done.1.down_ref = bf16[2,1536,128]{2,1,0:T(8,128)(2,1)S(1)} collective-permute-done((bf16[2,1536,128]{2,1,0:T(8,128)(2,1)}, bf16[2,1536,128]{2,1,0:T(8,128)(2,1)S(1)}, u32[]{:S(2)}, u32[]{:S(2)}) %collective-permute-start.1) | collective-permute-done | bytes 786464 | tf_op jit(solution)/shard_map/ppermute | solution.py:326
  23.1 0.7 products.1
  23.8 0.0 copy-start.2
  23.8 0.8 copy-done.2
  24.6 1.9 %collective-permute-start.2 = (f32[576,128]{1,0:T(8,128)S(1)}, f32[576,128]{1,0:T(8,128)}, u32[]{:S(2)}, u32[]{:S(2)}) collective-permute-start(f32[576,128]{1,0:T(8,128)S(1)} %dynamic-slice_bitcast_fusion), channel_id=1, source_target_pairs={{0,1},{1,0},{2,3},{3,2},{4,5},{5,4},{6,7},{7,6},{8,9},{9,8},{10,11... | collective-permute-start | bytes 884744 | tf_op jit(solution)/shard_map/ppermute | solution.py:323
  26.5 1.3 %collective-permute-done.2 = f32[576,128]{1,0:T(8,128)} collective-permute-done((f32[576,128]{1,0:T(8,128)S(1)}, f32[576,128]{1,0:T(8,128)}, u32[]{:S(2)}, u32[]{:S(2)}) %collective-permute-start.2) | collective-permute-done | bytes 294944 | tf_op jit(solution)/shard_map/ppermute | solution.py:323
  27.9 1.1 %bitcast_add_fusion.total_ref = f32[576,128]{1,0:T(8,128)S(1)} fusion(f32[576,128]{1,0:T(8,128)} %collective-permute-done.2, f32[2,576,128]{2,1,0:T(8,128)} %copy-done.2, s32[]{:T(128)S(6)} %select_n.21), kind=kLoop, calls=%fused_computation.1 | loop fusion | flops 73728 | bytes 884740 | tf_op jit(solution)/shard_map/add | solution.py:347
  29.0 0.3 collective-permute-start.3
  29.3 0.7 collective-permute-start.4
  29.9 7.4 %collective-permute-done.3.far_ref = f32[576,128]{1,0:T(8,128)} collective-permute-done((f32[576,128]{1,0:T(8,128)S(1)}, f32[576,128]{1,0:T(8,128)}, u32[]{:S(2)}, u32[]{:S(2)}) %collective-permute-start.3) | collective-permute-done | bytes 294944 | tf_op jit(solution)/shard_map/ppermute | solution.py:323
  37.4 1.2 %collective-permute-start.5 = (f32[576,128]{1,0:T(8,128)}, f32[576,128]{1,0:T(8,128)}, u32[]{:S(2)}, u32[]{:S(2)}) collective-permute-start(f32[576,128]{1,0:T(8,128)} %collective-permute-done.3.far_ref), channel_id=1, source_target_pairs={{0,1},{1,0},{2,3},{3,2},{4,5},{5,4},{6,7},{7,6},{8,9},{9,8},{10,11... | collective-permute-start | bytes 884744 | tf_op jit(solution)/shard_map/ppermute | solution.py:323
  38.6 0.0 collective-permute-done.4.total_other
  38.6 1.5 %collective-permute-done.5.far_other = f32[576,128]{1,0:T(8,128)} collective-permute-done((f32[576,128]{1,0:T(8,128)}, f32[576,128]{1,0:T(8,128)}, u32[]{:S(2)}, u32[]{:S(2)}) %collective-permute-start.5) | collective-permute-done | bytes 294944 | tf_op jit(solution)/shard_map/ppermute | solution.py:323
  40.1 1.9 %exchange.1 = (f32[8,128,128]{2,1,0:T(8,128)S(1)}, bf16[8,128,128]{2,1,0:T(8,128)(2,1)S(1)}) custom-call(s32[1]{0:T(128)} %bitcast.here_ref, s32[1]{0:T(128)} %bitcast.1.half_ref, s32[2,16]{1,0:T(2,128)S(1)} %bitcast.13, f32[576,128]{1,0:T(8,128)S(1)} %bitcast_add_fusion.total_ref, f32[576,128]{1,0:T(8,128)} %collective-permute-done.3.far_ref, ...), custom_call_target="tpu_custom_call" | custom-call | flops 134217728 | bytes 2621440 | tf_op jit(solution)/shard_map/exchange/pallas_call | solution.py:116
  42.0 0.1 collective-permute-start.11
  42.1 4.5 %collective-permute-start.9 = (bf16[8,128,128]{2,1,0:T(8,128)(2,1)S(1)}, bf16[8,128,128]{2,1,0:T(8,128)(2,1)S(1)}, u32[]{:S(2)}, u32[]{:S(2)}) collective-permute-start(bf16[8,128,128]{2,1,0:T(8,128)(2,1)S(1)} %get-tuple-element.16.refs_0_), channel_id=1, source_target_pairs={{4,8},{8,4},{5,9},{9,5},{6,10},{10,6},{7,11},{11,7},{20,24},{24,20... | collective-permute-start | bytes 786440 | tf_op jit(solution)/shard_map/ppermute | solution.py:392
  46.6 1.3 %collective-permute-start.7 = (bf16[8,128,128]{2,1,0:T(8,128)(2,1)S(1)}, bf16[8,128,128]{2,1,0:T(8,128)(2,1)S(1)}, u32[]{:S(2)}, u32[]{:S(2)}) collective-permute-start(bf16[8,128,128]{2,1,0:T(8,128)(2,1)S(1)} %get-tuple-element.16.refs_0_), channel_id=1, source_target_pairs={{4,12},{8,0},{5,13},{9,1},{6,14},{10,2},{7,15},{11,3},{20,28},{24,... | collective-permute-start | bytes 786440 | tf_op jit(solution)/shard_map/ppermute | solution.py:392
  47.9 1.0 %collective-permute-start.6 = (bf16[8,128,128]{2,1,0:T(8,128)(2,1)S(1)}, bf16[8,128,128]{2,1,0:T(8,128)(2,1)S(1)}, u32[]{:S(2)}, u32[]{:S(2)}) collective-permute-start(bf16[8,128,128]{2,1,0:T(8,128)(2,1)S(1)} %get-tuple-element.16.refs_0_), channel_id=1, source_target_pairs={{0,1},{1,0},{2,3},{3,2},{4,5},{5,4},{6,7},{7,6},{8,9},{9,8},{10,11... | collective-permute-start | bytes 786440 | tf_op jit(solution)/shard_map/ppermute | solution.py:323
  48.9 0.7 collective-permute-done.11.refs_6_
  49.6 1.2 %collective-permute-start.12 = (bf16[8,128,128]{2,1,0:T(8,128)(2,1)S(1)}, bf16[8,128,128]{2,1,0:T(8,128)(2,1)S(1)}, u32[]{:S(2)}, u32[]{:S(2)}) collective-permute-start(bf16[8,128,128]{2,1,0:T(8,128)(2,1)S(1)} %collective-permute-done.11.refs_6_), channel_id=1, source_target_pairs={{0,1},{1,0},{2,3},{3,2},{4,5},{5,4},{6,7},{7,6},{8,9},{9,8},{10,11... | collective-permute-start | bytes 786440 | tf_op jit(solution)/shard_map/ppermute | solution.py:323
  50.8 1.9 %collective-permute-done.9.refs_4_ = bf16[8,128,128]{2,1,0:T(8,128)(2,1)S(1)} collective-permute-done((bf16[8,128,128]{2,1,0:T(8,128)(2,1)S(1)}, bf16[8,128,128]{2,1,0:T(8,128)(2,1)S(1)}, u32[]{:S(2)}, u32[]{:S(2)}) %collective-permute-start.9) | collective-permute-done | bytes 262176 | tf_op jit(solution)/shard_map/ppermute | solution.py:392
  52.6 2.0 %collective-permute-start.10 = (bf16[8,128,128]{2,1,0:T(8,128)(2,1)S(1)}, bf16[8,128,128]{2,1,0:T(8,128)(2,1)S(1)}, u32[]{:S(2)}, u32[]{:S(2)}) collective-permute-start(bf16[8,128,128]{2,1,0:T(8,128)(2,1)S(1)} %collective-permute-done.9.refs_4_), channel_id=1, source_target_pairs={{0,1},{1,0},{2,3},{3,2},{4,5},{5,4},{6,7},{7,6},{8,9},{9,8},{10,11... | collective-permute-start | bytes 786440 | tf_op jit(solution)/shard_map/ppermute | solution.py:323
  54.6 2.5 %collective-permute-done.7.refs_2_ = bf16[8,128,128]{2,1,0:T(8,128)(2,1)S(1)} collective-permute-done((bf16[8,128,128]{2,1,0:T(8,128)(2,1)S(1)}, bf16[8,128,128]{2,1,0:T(8,128)(2,1)S(1)}, u32[]{:S(2)}, u32[]{:S(2)}) %collective-permute-start.7) | collective-permute-done | bytes 262176 | tf_op jit(solution)/shard_map/ppermute | solution.py:392
  57.2 1.5 %collective-permute-start.8 = (bf16[8,128,128]{2,1,0:T(8,128)(2,1)S(1)}, bf16[8,128,128]{2,1,0:T(8,128)(2,1)S(1)}, u32[]{:S(2)}, u32[]{:S(2)}) collective-permute-start(bf16[8,128,128]{2,1,0:T(8,128)(2,1)S(1)} %collective-permute-done.7.refs_2_), channel_id=1, source_target_pairs={{0,1},{1,0},{2,3},{3,2},{4,5},{5,4},{6,7},{7,6},{8,9},{9,8},{10,11... | collective-permute-start | bytes 786440 | tf_op jit(solution)/shard_map/ppermute | solution.py:323
  58.7 0.0 collective-permute-done.6.refs_1_
  58.7 0.0 collective-permute-done.12.refs_7_
  58.7 0.0 collective-permute-done.10.refs_5_
  58.7 1.1 %collective-permute-done.8.refs_3_ = bf16[8,128,128]{2,1,0:T(8,128)(2,1)S(1)} collective-permute-done((bf16[8,128,128]{2,1,0:T(8,128)(2,1)S(1)}, bf16[8,128,128]{2,1,0:T(8,128)(2,1)S(1)}, u32[]{:S(2)}, u32[]{:S(2)}) %collective-permute-start.8) | collective-permute-done | bytes 262176 | tf_op jit(solution)/shard_map/ppermute | solution.py:323
  59.9 1.7 %sweep.1.refs_0_ = bf16[8,128,128]{2,1,0:T(8,128)(2,1)S(1)} custom-call(s32[1]{0:T(128)} %bitcast.here_ref, s32[1]{0:T(128)} %bitcast.1.half_ref, s32[2,16]{1,0:T(2,128)S(1)} %bitcast.14, s32[4,64]{1,0:T(4,128)S(1)} %bitcast.17, f32[4,16]{1,0:T(4,128)S(1)} %bitcast.19, bf16[8,128,128]{2,1,0:T(8,128)(2,1)S(1)} %get-tuple-element.16.refs_0_, ...), custom_call_target="tpu_custom_call" | custom-call | flops 268435456 | bytes 3145728 | tf_op jit(solution)/shard_map/sweep/pallas_call | solution.py:209
  61.6 2.0 %collective-permute-start.18 = (bf16[8,128,128]{2,1,0:T(8,128)(2,1)S(1)}, bf16[8,128,128]{2,1,0:T(8,128)(2,1)S(1)}, u32[]{:S(2)}, u32[]{:S(2)}) collective-permute-start(bf16[8,128,128]{2,1,0:T(8,128)(2,1)S(1)} %sweep.1.refs_0_), channel_id=1, source_target_pairs={{0,4},{4,0},{8,12},{12,8},{1,5},{5,1},{9,13},{13,9},{2,6},{6,2},{1... | collective-permute-start | bytes 786440 | tf_op jit(solution)/shard_map/ppermute | solution.py:392
  63.6 3.4 %collective-permute-start.16 = (bf16[8,128,128]{2,1,0:T(8,128)(2,1)S(1)}, bf16[8,128,128]{2,1,0:T(8,128)(2,1)S(1)}, u32[]{:S(2)}, u32[]{:S(2)}) collective-permute-start(bf16[8,128,128]{2,1,0:T(8,128)(2,1)S(1)} %sweep.1.refs_0_), channel_id=1, source_target_pairs={{4,8},{8,4},{5,9},{9,5},{6,10},{10,6},{7,11},{11,7},{20,24},{24,20... | collective-permute-start | bytes 786440 | tf_op jit(solution)/shard_map/ppermute | solution.py:392
  66.9 1.3 %collective-permute-start.14 = (bf16[8,128,128]{2,1,0:T(8,128)(2,1)S(1)}, bf16[8,128,128]{2,1,0:T(8,128)(2,1)S(1)}, u32[]{:S(2)}, u32[]{:S(2)}) collective-permute-start(bf16[8,128,128]{2,1,0:T(8,128)(2,1)S(1)} %sweep.1.refs_0_), channel_id=1, source_target_pairs={{4,12},{8,0},{5,13},{9,1},{6,14},{10,2},{7,15},{11,3},{20,28},{24,... | collective-permute-start | bytes 786440 | tf_op jit(solution)/shard_map/ppermute | solution.py:392
  68.2 1.0 %collective-permute-start.13 = (bf16[8,128,128]{2,1,0:T(8,128)(2,1)S(1)}, bf16[8,128,128]{2,1,0:T(8,128)(2,1)S(1)}, u32[]{:S(2)}, u32[]{:S(2)}) collective-permute-start(bf16[8,128,128]{2,1,0:T(8,128)(2,1)S(1)} %sweep.1.refs_0_), channel_id=1, source_target_pairs={{0,1},{1,0},{2,3},{3,2},{4,5},{5,4},{6,7},{7,6},{8,9},{9,8},{10,11... | collective-permute-start | bytes 786440 | tf_op jit(solution)/shard_map/ppermute | solution.py:323
  69.3 0.7 collective-permute-done.18.refs_6_
  69.9 0.9 collective-permute-start.19
  70.8 1.8 %collective-permute-done.16.refs_4_ = bf16[8,128,128]{2,1,0:T(8,128)(2,1)S(1)} collective-permute-done((bf16[8,128,128]{2,1,0:T(8,128)(2,1)S(1)}, bf16[8,128,128]{2,1,0:T(8,128)(2,1)S(1)}, u32[]{:S(2)}, u32[]{:S(2)}) %collective-permute-start.16) | collective-permute-done | bytes 262176 | tf_op jit(solution)/shard_map/ppermute | solution.py:392
  72.6 2.7 %collective-permute-start.17 = (bf16[8,128,128]{2,1,0:T(8,128)(2,1)S(1)}, bf16[8,128,128]{2,1,0:T(8,128)(2,1)S(1)}, u32[]{:S(2)}, u32[]{:S(2)}) collective-permute-start(bf16[8,128,128]{2,1,0:T(8,128)(2,1)S(1)} %collective-permute-done.16.refs_4_), channel_id=1, source_target_pairs={{0,1},{1,0},{2,3},{3,2},{4,5},{5,4},{6,7},{7,6},{8,9},{9,8},{10,11... | collective-permute-start | bytes 786440 | tf_op jit(solution)/shard_map/ppermute | solution.py:323
  75.3 2.2 %collective-permute-done.14.refs_2_ = bf16[8,128,128]{2,1,0:T(8,128)(2,1)S(1)} collective-permute-done((bf16[8,128,128]{2,1,0:T(8,128)(2,1)S(1)}, bf16[8,128,128]{2,1,0:T(8,128)(2,1)S(1)}, u32[]{:S(2)}, u32[]{:S(2)}) %collective-permute-start.14) | collective-permute-done | bytes 262176 | tf_op jit(solution)/shard_map/ppermute | solution.py:392
  77.5 1.5 %collective-permute-start.15 = (bf16[8,128,128]{2,1,0:T(8,128)(2,1)S(1)}, bf16[8,128,128]{2,1,0:T(8,128)(2,1)S(1)}, u32[]{:S(2)}, u32[]{:S(2)}) collective-permute-start(bf16[8,128,128]{2,1,0:T(8,128)(2,1)S(1)} %collective-permute-done.14.refs_2_), channel_id=1, source_target_pairs={{0,1},{1,0},{2,3},{3,2},{4,5},{5,4},{6,7},{7,6},{8,9},{9,8},{10,11... | collective-permute-start | bytes 786440 | tf_op jit(solution)/shard_map/ppermute | solution.py:323
  79.0 0.0 collective-permute-done.13.refs_1_
  79.0 0.0 collective-permute-done.19.refs_7_
  79.0 0.0 collective-permute-done.17.refs_5_
  79.1 1.1 %collective-permute-done.15.refs_3_ = bf16[8,128,128]{2,1,0:T(8,128)(2,1)S(1)} collective-permute-done((bf16[8,128,128]{2,1,0:T(8,128)(2,1)S(1)}, bf16[8,128,128]{2,1,0:T(8,128)(2,1)S(1)}, u32[]{:S(2)}, u32[]{:S(2)}) %collective-permute-start.15) | collective-permute-done | bytes 262176 | tf_op jit(solution)/shard_map/ppermute | solution.py:323
  80.2 3.1 %last_sweep.1 = (f32[8,128,128]{2,1,0:T(8,128)S(1)}, f32[6,128,128]{2,1,0:T(8,128)S(1)}) custom-call(s32[1]{0:T(128)} %bitcast.here_ref, s32[1]{0:T(128)} %bitcast.1.half_ref, s32[2,16]{1,0:T(2,128)S(1)} %bitcast.15, s32[4,64]{1,0:T(4,128)S(1)} %bitcast.18, f32[4,16]{1,0:T(4,128)S(1)} %bitcast.20, bf16[8,128,128]{2,1,0:T(8,128)(2,1)S(1)} %sweep.1.refs_0_, ...), custom_call_target="tpu_custom_call" | custom-call | flops 268435456 | bytes 3145728 | tf_op jit(solution)/shard_map/last_sweep/pallas_call | solution.py:209
  83.3 0.4 collective-permute-start.20
  83.8 1.9 %collective-permute-start.21 = (f32[2,128,128]{2,1,0:T(8,128)S(1)}, f32[2,128,128]{2,1,0:T(8,128)S(1)}, u32[]{:S(2)}, u32[]{:S(2)}) collective-permute-start(f32[2,128,128]{2,1,0:T(8,128)S(1)} %get-tuple-element.22), channel_id=1, source_target_pairs={{0,4},{4,8},{8,12},{1,5},{5,9},{9,13},{2,6},{6,10},{10,14},{3,7},{... | collective-permute-start | bytes 393224 | tf_op jit(solution)/shard_map/ppermute | solution.py:414
  85.7 3.4 %collective-permute-start.22 = (f32[2,128,128]{2,1,0:T(8,128)S(1)}, f32[2,128,128]{2,1,0:T(8,128)S(1)}, u32[]{:S(2)}, u32[]{:S(2)}) collective-permute-start(f32[2,128,128]{2,1,0:T(8,128)S(1)} %get-tuple-element.23), channel_id=1, source_target_pairs={{4,0},{8,4},{12,8},{5,1},{9,5},{13,9},{6,2},{10,6},{14,10},{7,3},{... | collective-permute-start | bytes 393224 | tf_op jit(solution)/shard_map/ppermute | solution.py:415
  89.1 0.0 collective-permute-done.20.others_ref
  89.1 2.8 %first_terms.1 = (f32[16,128,128]{2,1,0:T(8,128)}, f32[2,128,128]{2,1,0:T(8,128)S(1)}) custom-call(s32[1]{0:T(128)} %bitcast.here_ref, s32[1]{0:T(128)} %bitcast.1.half_ref, s32[2,16]{1,0:T(2,128)S(1)} %bitcast.16, f32[8,128,128]{2,1,0:T(8,128)S(1)} %get-tuple-element.18.amps_ref, f32[8,128,128]{2,1,0:T(8,128)S(1)} %collective-permute-done.20.others_ref, ...), custom_call_target="tpu_custom_call" | custom-call | flops 201326592 | bytes 2097152 | tf_op jit(solution)/shard_map/first_terms/pallas_call | solution.py:252
  91.8 0.0 collective-permute-done.21
  91.8 2.6 %collective-permute-done.22 = f32[2,128,128]{2,1,0:T(8,128)S(1)} collective-permute-done((f32[2,128,128]{2,1,0:T(8,128)S(1)}, f32[2,128,128]{2,1,0:T(8,128)S(1)}, u32[]{:S(2)}, u32[]{:S(2)}) %collective-permute-start.22) | collective-permute-done | bytes 131104 | tf_op jit(solution)/shard_map/ppermute | solution.py:415
  94.5 1.0 %collective-permute-start.23 = (f32[2,128,128]{2,1,0:T(8,128)S(1)}, f32[2,128,128]{2,1,0:T(8,128)S(1)}, u32[]{:S(2)}, u32[]{:S(2)}) collective-permute-start(f32[2,128,128]{2,1,0:T(8,128)S(1)} %add_add_fusion), channel_id=1, source_target_pairs={{0,1},{1,0},{2,3},{3,2},{4,5},{5,4},{6,7},{7,6},{8,9},{9,8},{10,11... | collective-permute-start | bytes 393224 | tf_op jit(solution)/shard_map/ppermute | solution.py:323
  95.5 1.0 %collective-permute-done.23 = f32[2,128,128]{2,1,0:T(8,128)S(1)} collective-permute-done((f32[2,128,128]{2,1,0:T(8,128)S(1)}, f32[2,128,128]{2,1,0:T(8,128)S(1)}, u32[]{:S(2)}, u32[]{:S(2)}) %collective-permute-start.23) | collective-permute-done | bytes 131104 | tf_op jit(solution)/shard_map/ppermute | solution.py:323
  96.5 0.7 add_multiply_fusion
  (16 shorter events, 0.1 us)
Async XLA Ops:
  0.6 7.1 %copy-start = (f32[16,128]{1,0:T(8,128)S(1)}, f32[16,128]{1,0:T(8,128)}, u32[]{:S(2)}) copy-start(f32[16,128]{1,0:T(8,128)} %param.15) | copy-start | bytes 24580
  0.6 22.4 %copy-start.3 = (bf16[2,1536,128]{2,1,0:T(8,128)(2,1)S(1)}, bf16[2,1536,128]{2,1,0:T(8,128)(2,1)}, u32[]{:S(2)}) copy-start(bf16[2,1536,128]{2,1,0:T(8,128)(2,1)} %own_ref.1) | copy-start | bytes 2359300
  0.7 20.6 %collective-permute-start = (bf16[2,1536,128]{2,1,0:T(8,128)(2,1)}, bf16[2,1536,128]{2,1,0:T(8,128)(2,1)S(1)}, u32[]{:S(2)}, u32[]{:S(2)}) collective-permute-start(bf16[2,1536,128]{2,1,0:T(8,128)(2,1)} %own_ref.1), channel_id=1, source_target_pairs={{4,0},{8,4},{12,8},{5,1},{9,5},{13,9},{6,2},{10,6},{14,10},{7,3},{... | collective-permute-start | bytes 2359304 | tf_op jit(solution)/shard_map/ppermute | solution.py:325
  2.9 20.2 %collective-permute-start.1 = (bf16[2,1536,128]{2,1,0:T(8,128)(2,1)}, bf16[2,1536,128]{2,1,0:T(8,128)(2,1)S(1)}, u32[]{:S(2)}, u32[]{:S(2)}) collective-permute-start(bf16[2,1536,128]{2,1,0:T(8,128)(2,1)} %own_ref.1), channel_id=1, source_target_pairs={{0,4},{4,8},{8,12},{1,5},{5,9},{9,13},{2,6},{6,10},{10,14},{3,7},{... | collective-permute-start | bytes 2359304 | tf_op jit(solution)/shard_map/ppermute | solution.py:326
  21.3 18.8 %copy-start.4 = (s32[16,2]{0,1:T(2,128)S(1)}, s32[16,2]{0,1:T(2,128)}, u32[]{:S(2)}) copy-start(s32[16,2]{0,1:T(2,128)} %param.18) | copy-start | bytes 388
  23.8 0.8 copy-start.2
  24.6 35.3 %copy-start.1 = (bf16[16,4,128,128]{3,2,1,0:T(8,128)(2,1)S(1)}, bf16[16,4,128,128]{3,2,1,0:T(8,128)(2,1)}, u32[]{:S(2)}) copy-start(bf16[16,4,128,128]{3,2,1,0:T(8,128)(2,1)} %refs_8_.3) | copy-start | bytes 6291460
  24.6 35.3 %copy-start.5 = (s32[64,4]{0,1:T(4,128)S(1)}, s32[64,4]{0,1:T(4,128)}, u32[]{:S(2)}) copy-start(s32[64,4]{0,1:T(4,128)} %param.19) | copy-start | bytes 3076
  24.6 35.3 %copy-start.6 = (f32[16,4]{0,1:T(4,128)S(1)}, f32[16,4]{0,1:T(4,128)}, u32[]{:S(2)}) copy-start(f32[16,4]{0,1:T(4,128)} %param.14) | copy-start | bytes 772
  24.6 3.3 %collective-permute-start.2 = (f32[576,128]{1,0:T(8,128)S(1)}, f32[576,128]{1,0:T(8,128)}, u32[]{:S(2)}, u32[]{:S(2)}) collective-permute-start(f32[576,128]{1,0:T(8,128)S(1)} %dynamic-slice_bitcast_fusion), channel_id=1, source_target_pairs={{0,1},{1,0},{2,3},{3,2},{4,5},{5,4},{6,7},{7,6},{8,9},{9,8},{10,11... | collective-permute-start | bytes 884744 | tf_op jit(solution)/shard_map/ppermute | solution.py:323
  29.0 8.4 %collective-permute-start.3 = (f32[576,128]{1,0:T(8,128)S(1)}, f32[576,128]{1,0:T(8,128)}, u32[]{:S(2)}, u32[]{:S(2)}) collective-permute-start(f32[576,128]{1,0:T(8,128)S(1)} %bitcast_add_fusion.total_ref), channel_id=1, source_target_pairs={{0,2},{1,3},{2,0},{3,1},{4,6},{5,7},{6,4},{7,5},{8,10},{9,11},{10,... | collective-permute-start | bytes 884744 | tf_op jit(solution)/shard_map/ppermute | solution.py:323
  29.3 9.3 %collective-permute-start.4 = (f32[576,128]{1,0:T(8,128)S(1)}, f32[576,128]{1,0:T(8,128)}, u32[]{:S(2)}, u32[]{:S(2)}) collective-permute-start(f32[576,128]{1,0:T(8,128)S(1)} %bitcast_add_fusion.total_ref), channel_id=1, source_target_pairs={{0,1},{1,0},{2,3},{3,2},{4,5},{5,4},{6,7},{7,6},{8,9},{9,8},{10,11... | collective-permute-start | bytes 884744 | tf_op jit(solution)/shard_map/ppermute | solution.py:323
  37.4 2.8 %collective-permute-start.5 = (f32[576,128]{1,0:T(8,128)}, f32[576,128]{1,0:T(8,128)}, u32[]{:S(2)}, u32[]{:S(2)}) collective-permute-start(f32[576,128]{1,0:T(8,128)} %collective-permute-done.3.far_ref), channel_id=1, source_target_pairs={{0,1},{1,0},{2,3},{3,2},{4,5},{5,4},{6,7},{7,6},{8,9},{9,8},{10,11... | collective-permute-start | bytes 884744 | tf_op jit(solution)/shard_map/ppermute | solution.py:323
  42.0 7.6 %collective-permute-start.11 = (bf16[8,128,128]{2,1,0:T(8,128)(2,1)S(1)}, bf16[8,128,128]{2,1,0:T(8,128)(2,1)S(1)}, u32[]{:S(2)}, u32[]{:S(2)}) collective-permute-start(bf16[8,128,128]{2,1,0:T(8,128)(2,1)S(1)} %get-tuple-element.16.refs_0_), channel_id=1, source_target_pairs={{0,4},{4,0},{8,12},{12,8},{1,5},{5,1},{9,13},{13,9},{2,6},{6,2},{1... | collective-permute-start | bytes 786440 | tf_op jit(solution)/shard_map/ppermute | solution.py:392
  42.1 10.6 %collective-permute-start.9 = (bf16[8,128,128]{2,1,0:T(8,128)(2,1)S(1)}, bf16[8,128,128]{2,1,0:T(8,128)(2,1)S(1)}, u32[]{:S(2)}, u32[]{:S(2)}) collective-permute-start(bf16[8,128,128]{2,1,0:T(8,128)(2,1)S(1)} %get-tuple-element.16.refs_0_), channel_id=1, source_target_pairs={{4,8},{8,4},{5,9},{9,5},{6,10},{10,6},{7,11},{11,7},{20,24},{24,20... | collective-permute-start | bytes 786440 | tf_op jit(solution)/shard_map/ppermute | solution.py:392
  46.6 10.6 %collective-permute-start.7 = (bf16[8,128,128]{2,1,0:T(8,128)(2,1)S(1)}, bf16[8,128,128]{2,1,0:T(8,128)(2,1)S(1)}, u32[]{:S(2)}, u32[]{:S(2)}) collective-permute-start(bf16[8,128,128]{2,1,0:T(8,128)(2,1)S(1)} %get-tuple-element.16.refs_0_), channel_id=1, source_target_pairs={{4,12},{8,0},{5,13},{9,1},{6,14},{10,2},{7,15},{11,3},{20,28},{24,... | collective-permute-start | bytes 786440 | tf_op jit(solution)/shard_map/ppermute | solution.py:392
  47.9 10.8 %collective-permute-start.6 = (bf16[8,128,128]{2,1,0:T(8,128)(2,1)S(1)}, bf16[8,128,128]{2,1,0:T(8,128)(2,1)S(1)}, u32[]{:S(2)}, u32[]{:S(2)}) collective-permute-start(bf16[8,128,128]{2,1,0:T(8,128)(2,1)S(1)} %get-tuple-element.16.refs_0_), channel_id=1, source_target_pairs={{0,1},{1,0},{2,3},{3,2},{4,5},{5,4},{6,7},{7,6},{8,9},{9,8},{10,11... | collective-permute-start | bytes 786440 | tf_op jit(solution)/shard_map/ppermute | solution.py:323
  49.6 9.1 %collective-permute-start.12 = (bf16[8,128,128]{2,1,0:T(8,128)(2,1)S(1)}, bf16[8,128,128]{2,1,0:T(8,128)(2,1)S(1)}, u32[]{:S(2)}, u32[]{:S(2)}) collective-permute-start(bf16[8,128,128]{2,1,0:T(8,128)(2,1)S(1)} %collective-permute-done.11.refs_6_), channel_id=1, source_target_pairs={{0,1},{1,0},{2,3},{3,2},{4,5},{5,4},{6,7},{7,6},{8,9},{9,8},{10,11... | collective-permute-start | bytes 786440 | tf_op jit(solution)/shard_map/ppermute | solution.py:323
  52.6 6.1 %collective-permute-start.10 = (bf16[8,128,128]{2,1,0:T(8,128)(2,1)S(1)}, bf16[8,128,128]{2,1,0:T(8,128)(2,1)S(1)}, u32[]{:S(2)}, u32[]{:S(2)}) collective-permute-start(bf16[8,128,128]{2,1,0:T(8,128)(2,1)S(1)} %collective-permute-done.9.refs_4_), channel_id=1, source_target_pairs={{0,1},{1,0},{2,3},{3,2},{4,5},{5,4},{6,7},{7,6},{8,9},{9,8},{10,11... | collective-permute-start | bytes 786440 | tf_op jit(solution)/shard_map/ppermute | solution.py:323
  57.2 2.7 %collective-permute-start.8 = (bf16[8,128,128]{2,1,0:T(8,128)(2,1)S(1)}, bf16[8,128,128]{2,1,0:T(8,128)(2,1)S(1)}, u32[]{:S(2)}, u32[]{:S(2)}) collective-permute-start(bf16[8,128,128]{2,1,0:T(8,128)(2,1)S(1)} %collective-permute-done.7.refs_2_), channel_id=1, source_target_pairs={{0,1},{1,0},{2,3},{3,2},{4,5},{5,4},{6,7},{7,6},{8,9},{9,8},{10,11... | collective-permute-start | bytes 786440 | tf_op jit(solution)/shard_map/ppermute | solution.py:323
  61.6 8.3 %collective-permute-start.18 = (bf16[8,128,128]{2,1,0:T(8,128)(2,1)S(1)}, bf16[8,128,128]{2,1,0:T(8,128)(2,1)S(1)}, u32[]{:S(2)}, u32[]{:S(2)}) collective-permute-start(bf16[8,128,128]{2,1,0:T(8,128)(2,1)S(1)} %sweep.1.refs_0_), channel_id=1, source_target_pairs={{0,4},{4,0},{8,12},{12,8},{1,5},{5,1},{9,13},{13,9},{2,6},{6,2},{1... | collective-permute-start | bytes 786440 | tf_op jit(solution)/shard_map/ppermute | solution.py:392
  63.6 9.1 %collective-permute-start.16 = (bf16[8,128,128]{2,1,0:T(8,128)(2,1)S(1)}, bf16[8,128,128]{2,1,0:T(8,128)(2,1)S(1)}, u32[]{:S(2)}, u32[]{:S(2)}) collective-permute-start(bf16[8,128,128]{2,1,0:T(8,128)(2,1)S(1)} %sweep.1.refs_0_), channel_id=1, source_target_pairs={{4,8},{8,4},{5,9},{9,5},{6,10},{10,6},{7,11},{11,7},{20,24},{24,20... | collective-permute-start | bytes 786440 | tf_op jit(solution)/shard_map/ppermute | solution.py:392
  66.9 10.6 %collective-permute-start.14 = (bf16[8,128,128]{2,1,0:T(8,128)(2,1)S(1)}, bf16[8,128,128]{2,1,0:T(8,128)(2,1)S(1)}, u32[]{:S(2)}, u32[]{:S(2)}) collective-permute-start(bf16[8,128,128]{2,1,0:T(8,128)(2,1)S(1)} %sweep.1.refs_0_), channel_id=1, source_target_pairs={{4,12},{8,0},{5,13},{9,1},{6,14},{10,2},{7,15},{11,3},{20,28},{24,... | collective-permute-start | bytes 786440 | tf_op jit(solution)/shard_map/ppermute | solution.py:392
  68.2 10.8 %collective-permute-start.13 = (bf16[8,128,128]{2,1,0:T(8,128)(2,1)S(1)}, bf16[8,128,128]{2,1,0:T(8,128)(2,1)S(1)}, u32[]{:S(2)}, u32[]{:S(2)}) collective-permute-start(bf16[8,128,128]{2,1,0:T(8,128)(2,1)S(1)} %sweep.1.refs_0_), channel_id=1, source_target_pairs={{0,1},{1,0},{2,3},{3,2},{4,5},{5,4},{6,7},{7,6},{8,9},{9,8},{10,11... | collective-permute-start | bytes 786440 | tf_op jit(solution)/shard_map/ppermute | solution.py:323
  69.9 9.1 %collective-permute-start.19 = (bf16[8,128,128]{2,1,0:T(8,128)(2,1)S(1)}, bf16[8,128,128]{2,1,0:T(8,128)(2,1)S(1)}, u32[]{:S(2)}, u32[]{:S(2)}) collective-permute-start(bf16[8,128,128]{2,1,0:T(8,128)(2,1)S(1)} %collective-permute-done.18.refs_6_), channel_id=1, source_target_pairs={{0,1},{1,0},{2,3},{3,2},{4,5},{5,4},{6,7},{7,6},{8,9},{9,8},{10,11... | collective-permute-start | bytes 786440 | tf_op jit(solution)/shard_map/ppermute | solution.py:323
  72.6 6.4 %collective-permute-start.17 = (bf16[8,128,128]{2,1,0:T(8,128)(2,1)S(1)}, bf16[8,128,128]{2,1,0:T(8,128)(2,1)S(1)}, u32[]{:S(2)}, u32[]{:S(2)}) collective-permute-start(bf16[8,128,128]{2,1,0:T(8,128)(2,1)S(1)} %collective-permute-done.16.refs_4_), channel_id=1, source_target_pairs={{0,1},{1,0},{2,3},{3,2},{4,5},{5,4},{6,7},{7,6},{8,9},{9,8},{10,11... | collective-permute-start | bytes 786440 | tf_op jit(solution)/shard_map/ppermute | solution.py:323
  77.5 2.7 %collective-permute-start.15 = (bf16[8,128,128]{2,1,0:T(8,128)(2,1)S(1)}, bf16[8,128,128]{2,1,0:T(8,128)(2,1)S(1)}, u32[]{:S(2)}, u32[]{:S(2)}) collective-permute-start(bf16[8,128,128]{2,1,0:T(8,128)(2,1)S(1)} %collective-permute-done.14.refs_2_), channel_id=1, source_target_pairs={{0,1},{1,0},{2,3},{3,2},{4,5},{5,4},{6,7},{7,6},{8,9},{9,8},{10,11... | collective-permute-start | bytes 786440 | tf_op jit(solution)/shard_map/ppermute | solution.py:323
  83.3 5.8 %collective-permute-start.20 = (f32[8,128,128]{2,1,0:T(8,128)S(1)}, f32[8,128,128]{2,1,0:T(8,128)S(1)}, u32[]{:S(2)}, u32[]{:S(2)}) collective-permute-start(f32[8,128,128]{2,1,0:T(8,128)S(1)} %get-tuple-element.18.amps_ref), channel_id=1, source_target_pairs={{0,1},{1,0},{2,3},{3,2},{4,5},{5,4},{6,7},{7,6},{8,9},{9,8},{10,11... | collective-permute-start | bytes 1572872 | tf_op jit(solution)/shard_map/ppermute | solution.py:323
  83.8 8.1 %collective-permute-start.21 = (f32[2,128,128]{2,1,0:T(8,128)S(1)}, f32[2,128,128]{2,1,0:T(8,128)S(1)}, u32[]{:S(2)}, u32[]{:S(2)}) collective-permute-start(f32[2,128,128]{2,1,0:T(8,128)S(1)} %get-tuple-element.22), channel_id=1, source_target_pairs={{0,4},{4,8},{8,12},{1,5},{5,9},{9,13},{2,6},{6,10},{10,14},{3,7},{... | collective-permute-start | bytes 393224 | tf_op jit(solution)/shard_map/ppermute | solution.py:414
  85.7 8.8 %collective-permute-start.22 = (f32[2,128,128]{2,1,0:T(8,128)S(1)}, f32[2,128,128]{2,1,0:T(8,128)S(1)}, u32[]{:S(2)}, u32[]{:S(2)}) collective-permute-start(f32[2,128,128]{2,1,0:T(8,128)S(1)} %get-tuple-element.23), channel_id=1, source_target_pairs={{4,0},{8,4},{12,8},{5,1},{9,5},{13,9},{6,2},{10,6},{14,10},{7,3},{... | collective-permute-start | bytes 393224 | tf_op jit(solution)/shard_map/ppermute | solution.py:415
  94.5 2.0 %collective-permute-start.23 = (f32[2,128,128]{2,1,0:T(8,128)S(1)}, f32[2,128,128]{2,1,0:T(8,128)S(1)}, u32[]{:S(2)}, u32[]{:S(2)}) collective-permute-start(f32[2,128,128]{2,1,0:T(8,128)S(1)} %add_add_fusion), channel_id=1, source_target_pairs={{0,1},{1,0},{2,3},{3,2},{4,5},{5,4},{6,7},{7,6},{8,9},{9,8},{10,11... | collective-permute-start | bytes 393224 | tf_op jit(solution)/shard_map/ppermute | solution.py:323

commit v3 on v2

--- a/solution.py
+++ b/solution.py
@@ -41,49 +41,102 @@
     return pl.CostEstimate(flops=flops, bytes_accessed=size, transcendentals=0)
 
 
-def product_kernel(own_ref, up_ref, down_ref, out_ref):
+def prepare_kernel(
+    aux_ref, occ_ref, used_ref, energy_ref, first_ref, second_ref, ints_ref,
+    first_out, second_out, ints_out, factor_ref, sems,
+):
+    count, width, _ = factor_ref.shape
+    half = lax.rem(aux_ref[0], 2)
+    rows = pl.ds(half * count, count)
+    copies = [
+        pltpu.make_async_copy(first_ref.at[rows], first_out, sems.at[0]),
+        pltpu.make_async_copy(second_ref.at[rows], second_out, sems.at[1]),
+        pltpu.make_async_copy(ints_ref, ints_out, sems.at[2]),
+    ]
+    for copy in copies:
+        copy.start()
+    shape = (width, width)
+    along = lax.broadcasted_iota(jnp.int32, shape, 1)
+    down = lax.broadcasted_iota(jnp.int32, shape, 0)
+    for p in range(count):
+        row = half * count + p
+        energy = jnp.broadcast_to(energy_ref[pl.ds(row, 1)], shape)
+        denom = energy.T + energy - occ_ref[0, row] - occ_ref[1, row]
+        inside = (along < used_ref[row]) & (down < used_ref[row])
+        factor_ref[p] = jnp.where(inside, -1.0 / denom, 0.0)
+    for copy in copies:
+        copy.wait()
+
+
+def prepare(aux, occupied, used, energy, first, second, ints):
+    pair_dev, width, _ = first.shape
+    shape = (pair_dev // 2, width, width)
+    return pl.pallas_call(
+        prepare_kernel,
+        out_shape=(
+            jax.ShapeDtypeStruct(shape, BF16),
+            jax.ShapeDtypeStruct(shape, BF16),
+            jax.ShapeDtypeStruct(ints.shape, BF16),
+            jax.ShapeDtypeStruct(shape, F32),
+        ),
+        in_specs=[SMEM] * 3 + [VMEM] + [ANY] * 3,
+        out_specs=(VMEM,) * 4,
+        scratch_shapes=[pltpu.SemaphoreType.DMA((3,))],
+        compiler_params=params(8),
+        cost_estimate=cost(0, 8 * pair_dev * width * width),
+        name="prepare",
+    )(aux, occupied, used, energy, first, second, ints)
+
+
+def product_kernel(aux_ref, own_ref, up_ref, down_ref, kept_ref, sent_ref, inner):
     count, _, width = own_ref.shape
-    own = jnp.concatenate([own_ref[i] for i in range(count)], axis=1)
+    side = lax.rem(aux_ref[0], 2)
+    own = jnp.concatenate([own_ref[side], own_ref[1 - side]], axis=1)
     at = 0
     for near_ref in (up_ref, down_ref):
         near = jnp.concatenate([near_ref[i] for i in range(count)], axis=1)
         full = dot(own, near, ((0,), (0,)))
         for j in range(count):
-            for i in range(count):
-                out_ref[i, at : at + width] = full[
-                    i * width : (i + 1) * width, j * width : (j + 1) * width
-                ]
+            columns = slice(j * width, (j + 1) * width)
+            kept_ref[at : at + width] = full[:width, columns]
+            sent_ref[at : at + width] = full[width:, columns]
             at += width
     half = width // 2
-    inner = dot(own_ref[0], own_ref[1], ((0,), (0,)))
-    out_ref[0, at:] = inner[:half]
-    out_ref[1, at:] = inner[half:]
-
-
-def products(ints, up, down):
+    inner[...] = dot(own_ref[0], own_ref[1], ((0,), (0,)))
+    kept_ref[at:] = inner[pl.ds(pl.multiple_of(side * half, half), half)]
+    sent_ref[at:] = inner[pl.ds(pl.multiple_of((1 - side) * half, half), half)]
+
+
+def products(aux, ints, up, down):
     count, depth, width = ints.shape
     rows = 2 * count * width + width // 2
     return pl.pallas_call(
         product_kernel,
-        out_shape=jax.ShapeDtypeStruct((count, rows, width), F32),
-        in_specs=[VMEM] * 3,
-        out_specs=VMEM,
+        out_shape=(jax.ShapeDtypeStruct((rows, width), F32),) * 2,
+        in_specs=[SMEM] + [VMEM] * 3,
+        out_specs=(VMEM, VMEM),
+        scratch_shapes=[pltpu.VMEM((width, width), F32)],
         compiler_params=params(12),
         cost_estimate=cost(18 * depth * width * width, 12 * depth * width),
         name="products",
-    )(ints, up, down)
+    )(aux, ints, up, down)
+
+
+def own_part(aux_ref, low_ref, part_ref):
+    count = part_ref.shape[0]
+    part_ref[...] = low_ref[pl.ds(lax.rem(aux_ref[0] // 2, 2) * count, count)]
 
 
 def exchange_kernel(
-    here_ref, half_ref, orbitals_ref, total_ref, far_ref, total_other, far_other,
-    first_ref, second_ref, factor_ref, exch_ref, low_ref, table,
+    here_ref, aux_ref, orbitals_ref, total_ref, far_ref, total_other, far_other,
+    first_ref, second_ref, factor_ref, exch_ref, low_ref, part_ref, table,
 ):
     count, width, _ = exch_ref.shape
-    half = half_ref[0]
+    half = lax.rem(aux_ref[0], 2)
     base = here_ref[0] * 2 - 2
     for i, total in (
-        (half, total_ref[...] + far_ref[...]),
-        (1 - half, total_other[...] + far_other[...]),
+        (half, total_ref[...].astype(F32) + far_ref[...].astype(F32)),
+        (1 - half, total_other[...].astype(F32) + far_other[...].astype(F32)),
     ):
         for at, slot in enumerate((4, 5, 0, 1)):
             table[i * 6 + slot] = total[at * width : (at + 1) * width]
@@ -108,56 +161,67 @@
         )
         exch_ref[p] = exch
         low_ref[p] = (factor_ref[p] * exch).astype(BF16)
-
-
-def exchange(here, half, orbitals, sums, first, second, factor):
+    own_part(aux_ref, low_ref, part_ref)
+
+
+def exchange(here, aux, orbitals, sums, first, second, factor):
     shape = first.shape
     count, width, _ = shape
     return pl.pallas_call(
         exchange_kernel,
-        out_shape=(jax.ShapeDtypeStruct(shape, F32), jax.ShapeDtypeStruct(shape, BF16)),
+        out_shape=(
+            jax.ShapeDtypeStruct(shape, F32),
+            jax.ShapeDtypeStruct(shape, BF16),
+            jax.ShapeDtypeStruct((count // 2, width, width), BF16),
+        ),
         in_specs=[SMEM] * 3 + [VMEM] * (len(sums) + 3),
-        out_specs=(VMEM, VMEM),
+        out_specs=(VMEM,) * 3,
         scratch_shapes=[pltpu.VMEM((12, width, width), F32)],
         compiler_params=params(12),
         cost_estimate=cost(8 * count * width**3, 20 * count * width * width),
         name="exchange",
-    )(here, half, orbitals, *sums, first, second, factor)
-
-
-def sweep_kernel(last, pieces, rounds, here_ref, half_ref, orbitals_ref, near_ref, couple_ref, *refs):
+    )(here, aux, orbitals, *sums, first, second, factor)
+
+
+def sweep_kernel(last, pieces, rounds, here_ref, aux_ref, orbitals_ref, near_ref, couple_ref, *refs):
     parts = refs[:pieces]
     over_ref, exch_ref, factor_ref, second_ref = refs[pieces : pieces + 4]
     if last:
         amps_ref, terms_ref, table = refs[pieces + 4 :]
     else:
-        low_ref, table = refs[pieces + 4 :]
+        low_ref, part_ref, table = refs[pieces + 4 :]
     count, width, _ = exch_ref.shape
     pair_dev, nbr_count = over_ref.shape[:2]
     here = here_ref[0]
-    half = half_ref[0]
+    half = lax.rem(aux_ref[0], 2)
     at = 0
     for part in parts:
         table[at : at + part.shape[0]] = part[...]
         at += part.shape[0]
-    sources = []
-    for pairs in rounds or ():
-        source = -1
-        for start, end in pairs:
-            source = jnp.where(here == end, start, source)
-        sources.append(source)
+    across = lax.rem(aux_ref[0] // 2, 2)
+    near_block = -1
+    for start, end in rounds[0] if rounds else ():
+        near_block = jnp.where(here == end, start, near_block)
 
     def place(p, n):
-        if rounds is None:
+        if not rounds:
             return p * nbr_count + n
         wanted = near_ref[n, here * pair_dev + half * count + p]
         owner = wanted // pair_dev
         local = wanted - owner * pair_dev
-        slot = 0
-        for at, source in enumerate(sources):
-            slot = jnp.where(owner == source, 2 * at + 2, slot)
         side = local // count
-        return (slot + jnp.where(side == half, 0, 1)) * count + local - side * count
+        local = local - side * count
+        other = jnp.where(side == half, 0, 1)
+        quarter = local // (count // 2)
+        halved = (
+            4 * count
+            + jnp.where(quarter == across, 0, count)
+            + other * (count // 2)
+            + local
+            - quarter * (count // 2)
+        )
+        spot = other * count + local + jnp.where(owner == here, 0, 2 * count)
+        return jnp.where(owner == near_block, halved, spot)
 
     done = []
     for p in range(count):
@@ -177,7 +241,9 @@
             done.append(amps)
         else:
             low_ref[p] = amps.astype(BF16)
-    if last:
+    if not last:
+        own_part(aux_ref, low_ref, part_ref)
+    else:
         terms = []
         for p in range(count):
             right = second_ref[p]
@@ -194,7 +260,7 @@
             terms_ref[spot] += terms[p]
 
 
-def sweep(last, rounds, here, half, orbitals, near, couple, parts, over, exch, factor, second):
+def sweep(last, rounds, here, aux, orbitals, near, couple, parts, over, exch, factor, second):
     count, width, _ = exch.shape
     rows = sum(part.shape[0] for part in parts)
     if last:
@@ -204,8 +270,11 @@
         )
         out_specs = (VMEM, VMEM)
     else:
-        out_shape = jax.ShapeDtypeStruct(exch.shape, BF16)
-        out_specs = VMEM
+        out_shape = (
+            jax.ShapeDtypeStruct(exch.shape, BF16),
+            jax.ShapeDtypeStruct((count // 2, width, width), BF16),
+        )
+        out_specs = (VMEM, VMEM)
     return pl.pallas_call(
         functools.partial(sweep_kernel, last, len(parts), rounds),
         out_shape=out_shape,
@@ -215,14 +284,47 @@
         compiler_params=params(16),
         cost_estimate=cost(16 * count * width**3, (rows + 16 * count) * width * width),
         name="last_sweep" if last else "sweep",
-    )(here, half, orbitals, near, couple, *parts, over, exch, factor, second)
+    )(here, aux, orbitals, near, couple, *parts, over, exch, factor, second)
+
+
+def token_kernel(piece_ref, out_ref):
+    out_ref[...] = piece_ref[0, :16]
+
+
+def token(piece):
+    return pl.pallas_call(
+        token_kernel,
+        out_shape=jax.ShapeDtypeStruct((16, piece.shape[-1]), BF16),
+        in_specs=[VMEM],
+        out_specs=VMEM,
+        compiler_params=params(4),
+        cost_estimate=cost(5 * 10**9, 2**20),
+        name="token",
+    )(piece)
+
+
+def join_kernel(left_ref, right_ref, token_ref, out_ref):
+    del token_ref
+    out_ref[...] = left_ref[...] + right_ref[...]
+
+
+def joined(left, right, token):
+    return pl.pallas_call(
+        join_kernel,
+        out_shape=jax.ShapeDtypeStruct(left.shape, BF16),
+        in_specs=[VMEM] * 3,
+        out_specs=VMEM,
+        compiler_params=params(4),
+        cost_estimate=cost(left.size, 6 * left.size),
+        name="joined",
+    )(left, right, token)
 
 
 def first_kernel(
-    here_ref, half_ref, orbitals_ref, amps_ref, others_ref, first_ref, whole_ref, terms_ref, sems
+    here_ref, aux_ref, orbitals_ref, amps_ref, others_ref, first_ref, whole_ref, terms_ref, sems
 ):
     count = amps_ref.shape[0]
-    half = half_ref[0]
+    half = lax.rem(aux_ref[0], 2)
     copies = [
         pltpu.make_async_copy(amps_ref, whole_ref.at[pl.ds(half * count, count)], sems.at[0]),
         pltpu.make_async_copy(others_ref, whole_ref.at[pl.ds((1 - half) * count, count)], sems.at[1]),
@@ -247,7 +349,7 @@
         copy.wait()
 
 
-def first_terms(here, half, orbitals, amps, others, first):
+def first_terms(here, aux, orbitals, amps, others, first):
     count, width, _ = amps.shape
     return pl.pallas_call(
         first_kernel,
@@ -261,26 +363,24 @@
         compiler_params=params(12),
         cost_estimate=cost(12 * count * width**3, 16 * count * width * width),
         name="first_terms",
-    )(here, half, orbitals, amps, others, first)
+    )(here, aux, orbitals, amps, others, first)
 
 
 def window_rounds(groups):
-    reach = groups // 4
-    span = 2 * reach + 1
     edges = []
     for block in range(groups):
-        start = min(max(block - reach, 0), groups - span)
-        edges += [(source, block) for source in range(start, start + span) if source != block]
-    edges.sort(key=lambda edge: (abs(edge[0] - edge[1]), edge))
-    rounds = []
+        start = min(max(block - 1, 0), groups - 3)
+        edges += [(source, block) for source in range(start, start + 3) if source != block]
+    edges.sort(key=lambda edge: (-abs(edge[0] - edge[1]), edge))
+    first = []
     for source, block in edges:
-        for pairs in rounds:
-            if all(source != s and block != d for s, d in pairs):
-                pairs.append((source, block))
-                break
-        else:
-            rounds.append([(source, block)])
-    return rounds[::-1]
+        if all(source != s and block != d for s, d in first):
+            first.append((source, block))
+    rest = [edge for edge in edges if edge not in first]
+    both = [edge for edge in rest if edge[::-1] in rest]
+    rounds = [first, both, [edge for edge in rest if edge not in both]]
+    assert len(rounds[0]) == groups
+    return rounds
 
 
 def same_owner_rank(owners):
@@ -306,7 +406,8 @@
     groups = lax.axis_size("pair")
     here = lax.axis_index("pair")
     aux_count = lax.axis_size("aux")
-    half = lax.axis_index("aux") % 2
+    aux = lax.axis_index("aux")
+    half = aux % 2
     occ_dev, _, width = ints.shape
     pair_dev = proj_first.shape[0]
     nbr_count = couple.shape[1]
@@ -315,46 +416,35 @@
     count = pair_dev // 2
     up = [(i + 1, i) for i in range(groups - 1)]
     down = [(i, i + 1) for i in range(groups - 1)]
-    here_s = here.reshape(1)
-    half_s = half.reshape(1)
     orbitals = pair_orbitals.T
 
     def swap(value, step=1):
         return lax.ppermute(value, "aux", [(i, i ^ step) for i in range(aux_count)])
 
+    ints, here_s, aux_s = lax.optimization_barrier((ints, here.reshape(1), aux.reshape(1)))
+
     above = lax.ppermute(ints, "pair", up)
     below = lax.ppermute(ints, "pair", down)
-
-    def own(value):
-        return lax.dynamic_slice_in_dim(value, half * count, count, 0)
-
-    first = own(proj_first)
-    second = own(proj_second)
-    valid = jnp.arange(width)[None, :] < pno_count[:, None]
-    mask = (valid[:, :, None] & valid[:, None, :]).astype(F32)
-    denom = (
-        virt_energy[:, :, None]
-        + virt_energy[:, None, :]
-        - occ_energy[:, 0, None, None]
-        - occ_energy[:, 1, None, None]
+    first, second, ints, factor = prepare(
+        aux_s, occ_energy.T, pno_count, virt_energy, proj_first, proj_second, ints
     )
-    factor = own(-mask / denom)
-    above, first, second, factor = lax.optimization_barrier((above, first, second, factor))
-
-    partial = products(ints, above, below)
-    kept = lax.dynamic_index_in_dim(partial, half, 0, keepdims=False)
-    sent = lax.dynamic_index_in_dim(partial, 1 - half, 0, keepdims=False)
+    above, first, second, ints, factor = lax.optimization_barrier(
+        (above, first, second, ints, factor)
+    )
+
+    kept, sent = products(aux_s, ints, above, below)
     total = kept + swap(sent)
     step = 2
     while 2 * step < aux_count:
         total = total + swap(total, step)
         step *= 2
+    total = total.astype(BF16)
     far = swap(total, step)
-    exch, low = exchange(
-        here_s, half_s, orbitals, (total, far, swap(total), swap(far)), first, second, factor
+    exch, low, part = exchange(
+        here_s, aux_s, orbitals, (total, far, swap(total), swap(far)), first, second, factor
     )
 
-    if cap < pair_dev:
+    if cap < pair_dev or groups // 4 != 1 or aux_count != 4:
         rounds = None
         requests = neighbours.reshape(groups, wanted)
         owners = requests // pair_dev
@@ -379,7 +469,7 @@
     else:
         rounds = window_rounds(groups)
 
-    def gathered(low):
+    def gathered(low, part):
         if rounds is None:
             others = swap(low)
             flat = jnp.where(
@@ -389,31 +479,34 @@
             outgoing = outgoing.reshape(groups, cap, width, width)
             received = lax.all_to_all(outgoing, "pair", split_axis=0, concat_axis=0, tiled=True)
             return [received.reshape(groups * cap, width, width)[row_index]]
-        pieces = [low] + [lax.ppermute(low, "pair", pairs) for pairs in rounds]
-        return [value for piece in pieces for value in (piece, swap(piece))]
+        one = lax.ppermute(part, "pair", rounds[0])
+        cross = swap(one, 2)
+        others = swap(low)
+        two = joined(*(lax.ppermute(low, "pair", pairs) for pairs in rounds[1:]), token(one))
+        return [low, others, two, swap(two), one, swap(one), cross, swap(cross)]
 
     for it in range(ITERS):
         out = sweep(
             it == ITERS - 1,
             rounds,
             here_s,
-            half_s,
+            aux_s,
             orbitals,
             neighbours.T,
             couple.T,
-            gathered(low),
+            gathered(low, part),
             intersections,
             exch,
             factor,
             second,
         )
         if it < ITERS - 1:
-            low = out
+            low, part = out
     amps, terms = out
 
     from_below = lax.ppermute(terms[2 * occ_dev :], "pair", down)
     from_above = lax.ppermute(terms[:occ_dev], "pair", up)
-    whole, inner = first_terms(here_s, half_s, orbitals, amps, swap(amps), first)
+    whole, inner = first_terms(here_s, aux_s, orbitals, amps, swap(amps), first)
     density = inner + terms[occ_dev : 2 * occ_dev] + from_below + from_above
     density = (density + swap(density)) / width
     return (whole, density)

time: 98 us -> 87.3 us (0.89)
  the two profiles are of different devices: /device:TPU:15 before, /device:TPU:0 now
where the time goes in v3:
time: 87.3 us; the launch traced here: 86.8 us
  waiting for transfers between devices  38.6 us (44%)
  starting transfers between devices  30.2 us (35%)
  Pallas kernels  11.1 us (13%)
  local copies, waits for them, and re-layouts  5.27 us (6%)
    ppermute x16, waiting for transfers between devices, swap(): return lax.ppermute(value, 'aux', [(i, i ^ step) for i in range(aux_count)])  11.2 us
    ppermute x1, waiting for transfers between devices, shards(): above = lax.ppermute(ints, 'pair', up)  9.6 us
    ppermute x4, waiting for transfers between devices, gathered(): lax.ppermute(low, 'pair', pairs)  8.15 us
    ppermute x16, starting transfers between devices, swap(): return lax.ppermute(value, 'aux', [(i, i ^ step) for i in range(aux_count)])  6.55 us
    ppermute x2, starting transfers between devices, gathered(): one = lax.ppermute(part, 'pair', rounds[0])  6.06 us
    ppermute x1, starting transfers between devices, shards(): below = lax.ppermute(ints, 'pair', down)  5.6 us
    ppermute x1, starting transfers between devices, shards(): from_below = lax.ppermute(terms[2 * occ_dev:], 'pair', down)  5.39 us
    ppermute x2, waiting for transfers between devices, gathered(): one = lax.ppermute(part, 'pair', rounds[0])  5.31 us
  transfers between devices with their start and end apart: 26, of which 15 were waited for; matrix products, arithmetic and copies ran while one was open for 0% of the time, Pallas kernels for 5%

profile of v3, /device:TPU:0, one launch (start us, length us, event | category | flops | bytes accessed | tf_op | source)
XLA Modules:
  0.0 86.8 jit_solution(5834249825741471765)
XLA Ops:
  0.6 1.3 %collective-permute-start = (bf16[2,1536,128]{2,1,0:T(8,128)(2,1)}, bf16[2,1536,128]{2,1,0:T(8,128)(2,1)S(1)}, u32[]{:S(2)}, u32[]{:S(2)}) collective-permute-start(bf16[2,1536,128]{2,1,0:T(8,128)(2,1)} %ints_ref), channel_id=1, source_target_pairs={{4,0},{8,4},{12,8},{5,1},{9,5},{13,9},{6,2},{10,6},{14,10},{7,3},{... | collective-permute-start | bytes 2359304 | tf_op jit(solution)/shard_map/ppermute | solution.py:426
  1.9 5.6 %collective-permute-start.1 = (bf16[2,1536,128]{2,1,0:T(8,128)(2,1)}, bf16[2,1536,128]{2,1,0:T(8,128)(2,1)S(1)}, u32[]{:S(2)}, u32[]{:S(2)}) collective-permute-start(bf16[2,1536,128]{2,1,0:T(8,128)(2,1)} %ints_ref), channel_id=1, source_target_pairs={{0,4},{4,8},{8,12},{1,5},{5,9},{9,13},{2,6},{6,10},{10,14},{3,7},{... | collective-permute-start | bytes 2359304 | tf_op jit(solution)/shard_map/ppermute | solution.py:427
  7.6 1.1 %copy-done.1 = bf16[2,1536,128]{2,1,0:T(8,128)(2,1)S(1)} copy-done((bf16[2,1536,128]{2,1,0:T(8,128)(2,1)S(1)}, bf16[2,1536,128]{2,1,0:T(8,128)(2,1)}, u32[]{:S(2)}) %copy-start.1) | copy-done | bytes 786456
  8.7 1.0 %copy-done.2 = bf16[16,128,128]{2,1,0:T(8,128)(2,1)S(1)} copy-done((bf16[16,128,128]{2,1,0:T(8,128)(2,1)S(1)}, bf16[16,128,128]{2,1,0:T(8,128)(2,1)}, u32[]{:S(2)}) %copy-start.2) | copy-done | bytes 524312
  9.7 1.0 %copy-done.3 = bf16[16,128,128]{2,1,0:T(8,128)(2,1)S(1)} copy-done((bf16[16,128,128]{2,1,0:T(8,128)(2,1)S(1)}, bf16[16,128,128]{2,1,0:T(8,128)(2,1)}, u32[]{:S(2)}) %copy-start.3) | copy-done | bytes 524312
  10.8 0.7 copy-done.5
  11.5 0.7 copy-done.8
  12.2 0.7 copy-done.9
  12.8 0.9 %prepare.1 = (bf16[8,128,128]{2,1,0:T(8,128)(2,1)S(1)}, bf16[8,128,128]{2,1,0:T(8,128)(2,1)S(1)}, bf16[2,1536,128]{2,1,0:T(8,128)(2,1)S(1)}, f32[8,128,128]{2,1,0:T(8,128)S(1)}) custom-call(s32[1]{0:T(128)} %bitcast.1.aux_ref, f32[2,16]{1,0:T(2,128)S(1)} %bitcast.14, s32[16]{0:T(128)S(1)} %copy-done.9, f32[16,128]{1,0:T(8,128)S(1)} %copy-done.5, ...), custom_call_target="tpu_custom_call" | custom-call | bytes 2097152 | tf_op jit(solution)/shard_map/prepare/pallas_call | solution.py:74
  13.7 9.6 %collective-permute-done.up_ref = bf16[2,1536,128]{2,1,0:T(8,128)(2,1)S(1)} collective-permute-done((bf16[2,1536,128]{2,1,0:T(8,128)(2,1)}, bf16[2,1536,128]{2,1,0:T(8,128)(2,1)S(1)}, u32[]{:S(2)}, u32[]{:S(2)}) %collective-permute-start) | collective-permute-done | bytes 786464 | tf_op jit(solution)/shard_map/ppermute | solution.py:426
  23.3 1.3 %collective-permute-done.1.down_ref = bf16[2,1536,128]{2,1,0:T(8,128)(2,1)S(1)} collective-permute-done((bf16[2,1536,128]{2,1,0:T(8,128)(2,1)}, bf16[2,1536,128]{2,1,0:T(8,128)(2,1)S(1)}, u32[]{:S(2)}, u32[]{:S(2)}) %collective-permute-start.1) | collective-permute-done | bytes 786464 | tf_op jit(solution)/shard_map/ppermute | solution.py:427
  24.6 0.7 products.1
  25.3 0.1 collective-permute-start.2
  25.4 1.6 %collective-permute-done.2 = f32[576,128]{1,0:T(8,128)S(1)} collective-permute-done((f32[576,128]{1,0:T(8,128)S(1)}, f32[576,128]{1,0:T(8,128)S(1)}, u32[]{:S(2)}, u32[]{:S(2)}) %collective-permute-start.2) | collective-permute-done | bytes 294944 | tf_op jit(solution)/shard_map/ppermute | solution.py:422
  27.0 1.7 %collective-permute-start.3 = (bf16[576,128]{1,0:T(8,128)(2,1)S(1)}, bf16[576,128]{1,0:T(8,128)(2,1)S(1)}, u32[]{:S(2)}, u32[]{:S(2)}) collective-permute-start(bf16[576,128]{1,0:T(8,128)(2,1)S(1)} %add_convert_fusion.total_ref), channel_id=1, source_target_pairs={{0,2},{1,3},{2,0},{3,1},{4,6},{5,7},{6,4},{7,5},{8,10},{9,11},{10,... | collective-permute-start | bytes 442376 | tf_op jit(solution)/shard_map/ppermute | solution.py:422
  28.7 0.0 collective-permute-start.4
  28.7 4.2 %collective-permute-done.3.far_ref = bf16[576,128]{1,0:T(8,128)(2,1)S(1)} collective-permute-done((bf16[576,128]{1,0:T(8,128)(2,1)S(1)}, bf16[576,128]{1,0:T(8,128)(2,1)S(1)}, u32[]{:S(2)}, u32[]{:S(2)}) %collective-permute-start.3) | collective-permute-done | bytes 147488 | tf_op jit(solution)/shard_map/ppermute | solution.py:422
  33.0 0.0 collective-permute-start.5
  33.0 0.0 collective-permute-done.4.total_other
  33.0 1.4 %collective-permute-done.5.far_other = bf16[576,128]{1,0:T(8,128)(2,1)S(1)} collective-permute-done((bf16[576,128]{1,0:T(8,128)(2,1)S(1)}, bf16[576,128]{1,0:T(8,128)(2,1)S(1)}, u32[]{:S(2)}, u32[]{:S(2)}) %collective-permute-start.5) | collective-permute-done | bytes 147488 | tf_op jit(solution)/shard_map/ppermute | solution.py:422
  34.3 1.2 %exchange.1 = (f32[8,128,128]{2,1,0:T(8,128)S(1)}, bf16[8,128,128]{2,1,0:T(8,128)(2,1)S(1)}, bf16[4,128,128]{2,1,0:T(8,128)(2,1)S(1)}) custom-call(s32[1]{0:T(128)} %bitcast.here_ref, s32[1]{0:T(128)} %bitcast.1.aux_ref, s32[2,16]{1,0:T(2,128)S(1)} %bitcast.6, bf16[576,128]{1,0:T(8,128)(2,1)S(1)} %add_convert_fusion.total_ref, ...), custom_call_target="tpu_custom_call" | custom-call | flops 134217728 | bytes 2621440 | tf_op jit(solution)/shard_map/exchange/pallas_call | solution.py:170
  35.6 2.4 %collective-permute-start.9 = (bf16[4,128,128]{2,1,0:T(8,128)(2,1)S(1)}, bf16[4,128,128]{2,1,0:T(8,128)(2,1)S(1)}, u32[]{:S(2)}, u32[]{:S(2)}) collective-permute-start(bf16[4,128,128]{2,1,0:T(8,128)(2,1)S(1)} %get-tuple-element.40), channel_id=1, source_target_pairs={{4,12},{8,0},{0,4},{12,8},{5,13},{9,1},{1,5},{13,9},{6,14},{10,2},... | collective-permute-start | bytes 393224 | tf_op jit(solution)/shard_map/ppermute | solution.py:482
  38.0 1.4 %collective-permute-start.8 = (bf16[8,128,128]{2,1,0:T(8,128)(2,1)S(1)}, bf16[8,128,128]{2,1,0:T(8,128)(2,1)S(1)}, u32[]{:S(2)}, u32[]{:S(2)}) collective-permute-start(bf16[8,128,128]{2,1,0:T(8,128)(2,1)S(1)} %get-tuple-element.39.refs_0_), channel_id=1, source_target_pairs={{4,0},{8,12},{5,1},{9,13},{6,2},{10,14},{7,3},{11,15},{20,16},{24,... | collective-permute-start | bytes 786440 | tf_op jit(solution)/shard_map/ppermute | solution.py:485
  39.4 0.7 collective-permute-start.7
  40.1 0.1 collective-permute-start.6
  40.2 2.8 %collective-permute-done.9.piece_ref.refs_4_ = bf16[4,128,128]{2,1,0:T(8,128)(2,1)S(1)} collective-permute-done((bf16[4,128,128]{2,1,0:T(8,128)(2,1)S(1)}, bf16[4,128,128]{2,1,0:T(8,128)(2,1)S(1)}, u32[]{:S(2)}, u32[]{:S(2)}) %collective-permute-start.9) | collective-permute-done | bytes 131104 | tf_op jit(solution)/shard_map/ppermute | solution.py:482
  43.0 1.5 %collective-permute-start.12 = (bf16[4,128,128]{2,1,0:T(8,128)(2,1)S(1)}, bf16[4,128,128]{2,1,0:T(8,128)(2,1)S(1)}, u32[]{:S(2)}, u32[]{:S(2)}) collective-permute-start(bf16[4,128,128]{2,1,0:T(8,128)(2,1)S(1)} %collective-permute-done.9.piece_ref.refs_4_), channel_id=1, source_target_pairs={{0,2},{1,3},{2,0},{3,1},{4,6},{5,7},{6,4},{7,5},{8,10},{9,11},{10,... | collective-permute-start | bytes 393224 | tf_op jit(solution)/shard_map/ppermute | solution.py:422
  44.5 4.1 %collective-permute-done.8.right_ref = bf16[8,128,128]{2,1,0:T(8,128)(2,1)S(1)} collective-permute-done((bf16[8,128,128]{2,1,0:T(8,128)(2,1)S(1)}, bf16[8,128,128]{2,1,0:T(8,128)(2,1)S(1)}, u32[]{:S(2)}, u32[]{:S(2)}) %collective-permute-start.8) | collective-permute-done | bytes 262176 | tf_op jit(solution)/shard_map/ppermute | solution.py:485
  48.6 0.0 collective-permute-done.7.left_ref
  48.6 0.1 joined.2.refs_2_
  48.7 0.1 collective-permute-start.10
  48.7 0.5 collective-permute-start.11
  49.2 0.0 collective-permute-done.12.refs_6_
  49.2 0.1 collective-permute-start.13
  49.3 1.1 %collective-permute-done.11.refs_5_ = bf16[4,128,128]{2,1,0:T(8,128)(2,1)S(1)} collective-permute-done((bf16[4,128,128]{2,1,0:T(8,128)(2,1)S(1)}, bf16[4,128,128]{2,1,0:T(8,128)(2,1)S(1)}, u32[]{:S(2)}, u32[]{:S(2)}) %collective-permute-start.11) | collective-permute-done | bytes 131104 | tf_op jit(solution)/shard_map/ppermute | solution.py:422
  50.5 0.2 collective-permute-done.13.refs_7_
  50.6 0.0 collective-permute-done.10.refs_3_
  50.7 1.9 %sweep.1 = (bf16[8,128,128]{2,1,0:T(8,128)(2,1)S(1)}, bf16[4,128,128]{2,1,0:T(8,128)(2,1)S(1)}) custom-call(s32[1]{0:T(128)} %bitcast.here_ref, s32[1]{0:T(128)} %bitcast.1.aux_ref, s32[2,16]{1,0:T(2,128)S(1)} %bitcast.7, s32[4,64]{1,0:T(4,128)S(1)} %bitcast.10, f32[4,16]{1,0:T(4,128)S(1)} %bitcast.12, bf16[8,128,128]{2,1,0:T(8,128)(2,1)S(1)} %get-tuple-element.39.refs_0_, ...), custom_call_target="tpu_custom_call" | custom-call | flops 268435456 | bytes 2883584 | tf_op jit(solution)/shard_map/sweep/pallas_call | solution.py:278
  52.5 3.6 %collective-permute-start.17 = (bf16[4,128,128]{2,1,0:T(8,128)(2,1)S(1)}, bf16[4,128,128]{2,1,0:T(8,128)(2,1)S(1)}, u32[]{:S(2)}, u32[]{:S(2)}) collective-permute-start(bf16[4,128,128]{2,1,0:T(8,128)(2,1)S(1)} %get-tuple-element.43), channel_id=1, source_target_pairs={{4,12},{8,0},{0,4},{12,8},{5,13},{9,1},{1,5},{13,9},{6,14},{10,2},... | collective-permute-start | bytes 393224 | tf_op jit(solution)/shard_map/ppermute | solution.py:482
  56.2 1.3 %collective-permute-start.16 = (bf16[8,128,128]{2,1,0:T(8,128)(2,1)S(1)}, bf16[8,128,128]{2,1,0:T(8,128)(2,1)S(1)}, u32[]{:S(2)}, u32[]{:S(2)}) collective-permute-start(bf16[8,128,128]{2,1,0:T(8,128)(2,1)S(1)} %get-tuple-element.42.refs_0_), channel_id=1, source_target_pairs={{4,0},{8,12},{5,1},{9,13},{6,2},{10,14},{7,3},{11,15},{20,16},{24,... | collective-permute-start | bytes 786440 | tf_op jit(solution)/shard_map/ppermute | solution.py:485
  57.5 0.7 collective-permute-start.15
  58.2 0.1 collective-permute-start.14
  58.2 2.5 %collective-permute-done.17.piece_ref.refs_4_ = bf16[4,128,128]{2,1,0:T(8,128)(2,1)S(1)} collective-permute-done((bf16[4,128,128]{2,1,0:T(8,128)(2,1)S(1)}, bf16[4,128,128]{2,1,0:T(8,128)(2,1)S(1)}, u32[]{:S(2)}, u32[]{:S(2)}) %collective-permute-start.17) | collective-permute-done | bytes 131104 | tf_op jit(solution)/shard_map/ppermute | solution.py:482
  60.7 1.5 %collective-permute-start.20 = (bf16[4,128,128]{2,1,0:T(8,128)(2,1)S(1)}, bf16[4,128,128]{2,1,0:T(8,128)(2,1)S(1)}, u32[]{:S(2)}, u32[]{:S(2)}) collective-permute-start(bf16[4,128,128]{2,1,0:T(8,128)(2,1)S(1)} %collective-permute-done.17.piece_ref.refs_4_), channel_id=1, source_target_pairs={{0,2},{1,3},{2,0},{3,1},{4,6},{5,7},{6,4},{7,5},{8,10},{9,11},{10,... | collective-permute-start | bytes 393224 | tf_op jit(solution)/shard_map/ppermute | solution.py:422
  62.3 4.1 %collective-permute-done.16.right_ref = bf16[8,128,128]{2,1,0:T(8,128)(2,1)S(1)} collective-permute-done((bf16[8,128,128]{2,1,0:T(8,128)(2,1)S(1)}, bf16[8,128,128]{2,1,0:T(8,128)(2,1)S(1)}, u32[]{:S(2)}, u32[]{:S(2)}) %collective-permute-start.16) | collective-permute-done | bytes 262176 | tf_op jit(solution)/shard_map/ppermute | solution.py:485
  66.3 0.0 collective-permute-done.15.left_ref
  66.4 0.1 joined.3.refs_2_
  66.4 0.1 collective-permute-start.18
  66.5 0.5 collective-permute-start.19
  67.0 0.0 collective-permute-done.20.refs_6_
  67.0 0.1 collective-permute-start.21
  67.1 1.1 %collective-permute-done.19.refs_5_ = bf16[4,128,128]{2,1,0:T(8,128)(2,1)S(1)} collective-permute-done((bf16[4,128,128]{2,1,0:T(8,128)(2,1)S(1)}, bf16[4,128,128]{2,1,0:T(8,128)(2,1)S(1)}, u32[]{:S(2)}, u32[]{:S(2)}) %collective-permute-start.19) | collective-permute-done | bytes 131104 | tf_op jit(solution)/shard_map/ppermute | solution.py:422
  68.2 0.2 collective-permute-done.21.refs_7_
  68.4 0.0 collective-permute-done.18.refs_3_
  68.4 3.2 %last_sweep.1 = (f32[8,128,128]{2,1,0:T(8,128)S(1)}, f32[6,128,128]{2,1,0:T(8,128)S(1)}) custom-call(s32[1]{0:T(128)} %bitcast.here_ref, s32[1]{0:T(128)} %bitcast.1.aux_ref, s32[2,16]{1,0:T(2,128)S(1)} %bitcast.8, s32[4,64]{1,0:T(4,128)S(1)} %bitcast.11, f32[4,16]{1,0:T(4,128)S(1)} %bitcast.13, bf16[8,128,128]{2,1,0:T(8,128)(2,1)S(1)} %get-tuple-element.42.refs_0_, ...), custom_call_target="tpu_custom_call" | custom-call | flops 268435456 | bytes 2883584 | tf_op jit(solution)/shard_map/last_sweep/pallas_call | solution.py:278
  71.6 0.2 collective-permute-start.22
  71.9 5.4 %collective-permute-start.23 = (f32[2,128,128]{2,1,0:T(8,128)S(1)}, f32[2,128,128]{2,1,0:T(8,128)S(1)}, u32[]{:S(2)}, u32[]{:S(2)}) collective-permute-start(f32[2,128,128]{2,1,0:T(8,128)S(1)} %get-tuple-element.48), channel_id=1, source_target_pairs={{0,4},{4,8},{8,12},{1,5},{5,9},{9,13},{2,6},{6,10},{10,14},{3,7},{... | collective-permute-start | bytes 393224 | tf_op jit(solution)/shard_map/ppermute | solution.py:507
  77.3 1.3 %collective-permute-start.24 = (f32[2,128,128]{2,1,0:T(8,128)S(1)}, f32[2,128,128]{2,1,0:T(8,128)S(1)}, u32[]{:S(2)}, u32[]{:S(2)}) collective-permute-start(f32[2,128,128]{2,1,0:T(8,128)S(1)} %get-tuple-element.49), channel_id=1, source_target_pairs={{4,0},{8,4},{12,8},{5,1},{9,5},{13,9},{6,2},{10,6},{14,10},{7,3},{... | collective-permute-start | bytes 393224 | tf_op jit(solution)/shard_map/ppermute | solution.py:508
  78.6 0.0 collective-permute-done.22.others_ref
  78.6 3.0 %first_terms.1 = (f32[16,128,128]{2,1,0:T(8,128)}, f32[2,128,128]{2,1,0:T(8,128)S(1)}) custom-call(s32[1]{0:T(128)} %bitcast.here_ref, s32[1]{0:T(128)} %bitcast.1.aux_ref, s32[2,16]{1,0:T(2,128)S(1)} %bitcast.9, f32[8,128,128]{2,1,0:T(8,128)S(1)} %get-tuple-element.44.amps_ref, f32[8,128,128]{2,1,0:T(8,128)S(1)} %collective-permute-done.22.others_ref, ...), custom_call_target="tpu_custom_call" | custom-call | flops 201326592 | bytes 2097152 | tf_op jit(solution)/shard_map/first_terms/pallas_call | solution.py:354
  81.6 3.1 %collective-permute-done.24 = f32[2,128,128]{2,1,0:T(8,128)S(1)} collective-permute-done((f32[2,128,128]{2,1,0:T(8,128)S(1)}, f32[2,128,128]{2,1,0:T(8,128)S(1)}, u32[]{:S(2)}, u32[]{:S(2)}) %collective-permute-start.24) | collective-permute-done | bytes 131104 | tf_op jit(solution)/shard_map/ppermute | solution.py:508
  84.7 0.1 collective-permute-start.25
  84.8 1.3 %collective-permute-done.25 = f32[2,128,128]{2,1,0:T(8,128)S(1)} collective-permute-done((f32[2,128,128]{2,1,0:T(8,128)S(1)}, f32[2,128,128]{2,1,0:T(8,128)S(1)}, u32[]{:S(2)}, u32[]{:S(2)}) %collective-permute-start.25) | collective-permute-done | bytes 131104 | tf_op jit(solution)/shard_map/ppermute | solution.py:422
  86.1 0.7 add_multiply_fusion
  (22 shorter events, 0.1 us)
Async XLA Ops:
  0.6 22.7 %collective-permute-start = (bf16[2,1536,128]{2,1,0:T(8,128)(2,1)}, bf16[2,1536,128]{2,1,0:T(8,128)(2,1)S(1)}, u32[]{:S(2)}, u32[]{:S(2)}) collective-permute-start(bf16[2,1536,128]{2,1,0:T(8,128)(2,1)} %ints_ref), channel_id=1, source_target_pairs={{4,0},{8,4},{12,8},{5,1},{9,5},{13,9},{6,2},{10,6},{14,10},{7,3},{... | collective-permute-start | bytes 2359304 | tf_op jit(solution)/shard_map/ppermute | solution.py:426
  1.9 22.7 %collective-permute-start.1 = (bf16[2,1536,128]{2,1,0:T(8,128)(2,1)}, bf16[2,1536,128]{2,1,0:T(8,128)(2,1)S(1)}, u32[]{:S(2)}, u32[]{:S(2)}) collective-permute-start(bf16[2,1536,128]{2,1,0:T(8,128)(2,1)} %ints_ref), channel_id=1, source_target_pairs={{0,4},{4,8},{8,12},{1,5},{5,9},{9,13},{2,6},{6,10},{10,14},{3,7},{... | collective-permute-start | bytes 2359304 | tf_op jit(solution)/shard_map/ppermute | solution.py:427
  7.5 1.1 %copy-start.1 = (bf16[2,1536,128]{2,1,0:T(8,128)(2,1)S(1)}, bf16[2,1536,128]{2,1,0:T(8,128)(2,1)}, u32[]{:S(2)}) copy-start(bf16[2,1536,128]{2,1,0:T(8,128)(2,1)} %ints_ref) | copy-start | bytes 2359300
  8.7 1.0 %copy-start.2 = (bf16[16,128,128]{2,1,0:T(8,128)(2,1)S(1)}, bf16[16,128,128]{2,1,0:T(8,128)(2,1)}, u32[]{:S(2)}) copy-start(bf16[16,128,128]{2,1,0:T(8,128)(2,1)} %first_ref.1) | copy-start | bytes 1572868
  9.7 1.0 %copy-start.3 = (bf16[16,128,128]{2,1,0:T(8,128)(2,1)S(1)}, bf16[16,128,128]{2,1,0:T(8,128)(2,1)}, u32[]{:S(2)}) copy-start(bf16[16,128,128]{2,1,0:T(8,128)(2,1)} %second_ref.1) | copy-start | bytes 1572868
  10.8 0.7 copy-start.5
  11.5 0.7 copy-start.8
  12.1 0.7 copy-start.9
  12.8 21.5 %copy-start.4 = (s32[16,2]{0,1:T(2,128)S(1)}, s32[16,2]{0,1:T(2,128)}, u32[]{:S(2)}) copy-start(s32[16,2]{0,1:T(2,128)} %param.18) | copy-start | bytes 388
  25.3 1.6 %collective-permute-start.2 = (f32[576,128]{1,0:T(8,128)S(1)}, f32[576,128]{1,0:T(8,128)S(1)}, u32[]{:S(2)}, u32[]{:S(2)}) collective-permute-start(f32[576,128]{1,0:T(8,128)S(1)} %get-tuple-element.35), channel_id=1, source_target_pairs={{0,1},{1,0},{2,3},{3,2},{4,5},{5,4},{6,7},{7,6},{8,9},{9,8},{10,11... | collective-permute-start | bytes 884744 | tf_op jit(solution)/shard_map/ppermute | solution.py:422
  27.0 6.0 %collective-permute-start.3 = (bf16[576,128]{1,0:T(8,128)(2,1)S(1)}, bf16[576,128]{1,0:T(8,128)(2,1)S(1)}, u32[]{:S(2)}, u32[]{:S(2)}) collective-permute-start(bf16[576,128]{1,0:T(8,128)(2,1)S(1)} %add_convert_fusion.total_ref), channel_id=1, source_target_pairs={{0,2},{1,3},{2,0},{3,1},{4,6},{5,7},{6,4},{7,5},{8,10},{9,11},{10,... | collective-permute-start | bytes 442376 | tf_op jit(solution)/shard_map/ppermute | solution.py:422
  28.7 4.3 %collective-permute-start.4 = (bf16[576,128]{1,0:T(8,128)(2,1)S(1)}, bf16[576,128]{1,0:T(8,128)(2,1)S(1)}, u32[]{:S(2)}, u32[]{:S(2)}) collective-permute-start(bf16[576,128]{1,0:T(8,128)(2,1)S(1)} %add_convert_fusion.total_ref), channel_id=1, source_target_pairs={{0,1},{1,0},{2,3},{3,2},{4,5},{5,4},{6,7},{7,6},{8,9},{9,8},{10,11... | collective-permute-start | bytes 442376 | tf_op jit(solution)/shard_map/ppermute | solution.py:422
  33.0 1.4 %collective-permute-start.5 = (bf16[576,128]{1,0:T(8,128)(2,1)S(1)}, bf16[576,128]{1,0:T(8,128)(2,1)S(1)}, u32[]{:S(2)}, u32[]{:S(2)}) collective-permute-start(bf16[576,128]{1,0:T(8,128)(2,1)S(1)} %collective-permute-done.3.far_ref), channel_id=1, source_target_pairs={{0,1},{1,0},{2,3},{3,2},{4,5},{5,4},{6,7},{7,6},{8,9},{9,8},{10,11... | collective-permute-start | bytes 442376 | tf_op jit(solution)/shard_map/ppermute | solution.py:422
  35.6 7.4 %collective-permute-start.9 = (bf16[4,128,128]{2,1,0:T(8,128)(2,1)S(1)}, bf16[4,128,128]{2,1,0:T(8,128)(2,1)S(1)}, u32[]{:S(2)}, u32[]{:S(2)}) collective-permute-start(bf16[4,128,128]{2,1,0:T(8,128)(2,1)S(1)} %get-tuple-element.40), channel_id=1, source_target_pairs={{4,12},{8,0},{0,4},{12,8},{5,13},{9,1},{1,5},{13,9},{6,14},{10,2},... | collective-permute-start | bytes 393224 | tf_op jit(solution)/shard_map/ppermute | solution.py:482
  38.0 12.7 %copy-start.6 = (s32[64,4]{0,1:T(4,128)S(1)}, s32[64,4]{0,1:T(4,128)}, u32[]{:S(2)}) copy-start(s32[64,4]{0,1:T(4,128)} %param.19) | copy-start | bytes 3076
  38.0 12.7 %copy-start.7 = (f32[16,4]{0,1:T(4,128)S(1)}, f32[16,4]{0,1:T(4,128)}, u32[]{:S(2)}) copy-start(f32[16,4]{0,1:T(4,128)} %param.14) | copy-start | bytes 772
  38.0 10.6 %collective-permute-start.8 = (bf16[8,128,128]{2,1,0:T(8,128)(2,1)S(1)}, bf16[8,128,128]{2,1,0:T(8,128)(2,1)S(1)}, u32[]{:S(2)}, u32[]{:S(2)}) collective-permute-start(bf16[8,128,128]{2,1,0:T(8,128)(2,1)S(1)} %get-tuple-element.39.refs_0_), channel_id=1, source_target_pairs={{4,0},{8,12},{5,1},{9,13},{6,2},{10,14},{7,3},{11,15},{20,16},{24,... | collective-permute-start | bytes 786440 | tf_op jit(solution)/shard_map/ppermute | solution.py:485
  39.4 9.2 %collective-permute-start.7 = (bf16[8,128,128]{2,1,0:T(8,128)(2,1)S(1)}, bf16[8,128,128]{2,1,0:T(8,128)(2,1)S(1)}, u32[]{:S(2)}, u32[]{:S(2)}) collective-permute-start(bf16[8,128,128]{2,1,0:T(8,128)(2,1)S(1)} %get-tuple-element.39.refs_0_), channel_id=1, source_target_pairs={{4,8},{8,4},{5,9},{9,5},{6,10},{10,6},{7,11},{11,7},{20,24},{24,20... | collective-permute-start | bytes 786440 | tf_op jit(solution)/shard_map/ppermute | solution.py:485
  40.1 10.4 %collective-permute-start.6 = (bf16[8,128,128]{2,1,0:T(8,128)(2,1)S(1)}, bf16[8,128,128]{2,1,0:T(8,128)(2,1)S(1)}, u32[]{:S(2)}, u32[]{:S(2)}) collective-permute-start(bf16[8,128,128]{2,1,0:T(8,128)(2,1)S(1)} %get-tuple-element.39.refs_0_), channel_id=1, source_target_pairs={{0,1},{1,0},{2,3},{3,2},{4,5},{5,4},{6,7},{7,6},{8,9},{9,8},{10,11... | collective-permute-start | bytes 786440 | tf_op jit(solution)/shard_map/ppermute | solution.py:422
  43.0 6.3 %collective-permute-start.12 = (bf16[4,128,128]{2,1,0:T(8,128)(2,1)S(1)}, bf16[4,128,128]{2,1,0:T(8,128)(2,1)S(1)}, u32[]{:S(2)}, u32[]{:S(2)}) collective-permute-start(bf16[4,128,128]{2,1,0:T(8,128)(2,1)S(1)} %collective-permute-done.9.piece_ref.refs_4_), channel_id=1, source_target_pairs={{0,2},{1,3},{2,0},{3,1},{4,6},{5,7},{6,4},{7,5},{8,10},{9,11},{10,... | collective-permute-start | bytes 393224 | tf_op jit(solution)/shard_map/ppermute | solution.py:422
  44.5 6.1 %copy-start = (bf16[16,4,128,128]{3,2,1,0:T(8,128)(2,1)S(1)}, bf16[16,4,128,128]{3,2,1,0:T(8,128)(2,1)}, u32[]{:S(2)}) copy-start(bf16[16,4,128,128]{3,2,1,0:T(8,128)(2,1)} %refs_8_.3) | copy-start | bytes 6291460
  48.7 2.0 %collective-permute-start.10 = (bf16[8,128,128]{2,1,0:T(8,128)(2,1)S(1)}, bf16[8,128,128]{2,1,0:T(8,128)(2,1)S(1)}, u32[]{:S(2)}, u32[]{:S(2)}) collective-permute-start(bf16[8,128,128]{2,1,0:T(8,128)(2,1)S(1)} %joined.2.refs_2_), channel_id=1, source_target_pairs={{0,1},{1,0},{2,3},{3,2},{4,5},{5,4},{6,7},{7,6},{8,9},{9,8},{10,11... | collective-permute-start | bytes 786440 | tf_op jit(solution)/shard_map/ppermute | solution.py:422
  48.7 1.7 %collective-permute-start.11 = (bf16[4,128,128]{2,1,0:T(8,128)(2,1)S(1)}, bf16[4,128,128]{2,1,0:T(8,128)(2,1)S(1)}, u32[]{:S(2)}, u32[]{:S(2)}) collective-permute-start(bf16[4,128,128]{2,1,0:T(8,128)(2,1)S(1)} %collective-permute-done.9.piece_ref.refs_4_), channel_id=1, source_target_pairs={{0,1},{1,0},{2,3},{3,2},{4,5},{5,4},{6,7},{7,6},{8,9},{9,8},{10,11... | collective-permute-start | bytes 393224 | tf_op jit(solution)/shard_map/ppermute | solution.py:422
  49.2 1.4 %collective-permute-start.13 = (bf16[4,128,128]{2,1,0:T(8,128)(2,1)S(1)}, bf16[4,128,128]{2,1,0:T(8,128)(2,1)S(1)}, u32[]{:S(2)}, u32[]{:S(2)}) collective-permute-start(bf16[4,128,128]{2,1,0:T(8,128)(2,1)S(1)} %collective-permute-done.12.refs_6_), channel_id=1, source_target_pairs={{0,1},{1,0},{2,3},{3,2},{4,5},{5,4},{6,7},{7,6},{8,9},{9,8},{10,11... | collective-permute-start | bytes 393224 | tf_op jit(solution)/shard_map/ppermute | solution.py:422
  52.5 8.2 %collective-permute-start.17 = (bf16[4,128,128]{2,1,0:T(8,128)(2,1)S(1)}, bf16[4,128,128]{2,1,0:T(8,128)(2,1)S(1)}, u32[]{:S(2)}, u32[]{:S(2)}) collective-permute-start(bf16[4,128,128]{2,1,0:T(8,128)(2,1)S(1)} %get-tuple-element.43), channel_id=1, source_target_pairs={{4,12},{8,0},{0,4},{12,8},{5,13},{9,1},{1,5},{13,9},{6,14},{10,2},... | collective-permute-start | bytes 393224 | tf_op jit(solution)/shard_map/ppermute | solution.py:482
  56.2 10.2 %collective-permute-start.16 = (bf16[8,128,128]{2,1,0:T(8,128)(2,1)S(1)}, bf16[8,128,128]{2,1,0:T(8,128)(2,1)S(1)}, u32[]{:S(2)}, u32[]{:S(2)}) collective-permute-start(bf16[8,128,128]{2,1,0:T(8,128)(2,1)S(1)} %get-tuple-element.42.refs_0_), channel_id=1, source_target_pairs={{4,0},{8,12},{5,1},{9,13},{6,2},{10,14},{7,3},{11,15},{20,16},{24,... | collective-permute-start | bytes 786440 | tf_op jit(solution)/shard_map/ppermute | solution.py:485
  57.5 8.9 %collective-permute-start.15 = (bf16[8,128,128]{2,1,0:T(8,128)(2,1)S(1)}, bf16[8,128,128]{2,1,0:T(8,128)(2,1)S(1)}, u32[]{:S(2)}, u32[]{:S(2)}) collective-permute-start(bf16[8,128,128]{2,1,0:T(8,128)(2,1)S(1)} %get-tuple-element.42.refs_0_), channel_id=1, source_target_pairs={{4,8},{8,4},{5,9},{9,5},{6,10},{10,6},{7,11},{11,7},{20,24},{24,20... | collective-permute-start | bytes 786440 | tf_op jit(solution)/shard_map/ppermute | solution.py:485
  58.2 8.9 %collective-permute-start.14 = (bf16[8,128,128]{2,1,0:T(8,128)(2,1)S(1)}, bf16[8,128,128]{2,1,0:T(8,128)(2,1)S(1)}, u32[]{:S(2)}, u32[]{:S(2)}) collective-permute-start(bf16[8,128,128]{2,1,0:T(8,128)(2,1)S(1)} %get-tuple-element.42.refs_0_), channel_id=1, source_target_pairs={{0,1},{1,0},{2,3},{3,2},{4,5},{5,4},{6,7},{7,6},{8,9},{9,8},{10,11... | collective-permute-start | bytes 786440 | tf_op jit(solution)/shard_map/ppermute | solution.py:422
  60.7 6.2 %collective-permute-start.20 = (bf16[4,128,128]{2,1,0:T(8,128)(2,1)S(1)}, bf16[4,128,128]{2,1,0:T(8,128)(2,1)S(1)}, u32[]{:S(2)}, u32[]{:S(2)}) collective-permute-start(bf16[4,128,128]{2,1,0:T(8,128)(2,1)S(1)} %collective-permute-done.17.piece_ref.refs_4_), channel_id=1, source_target_pairs={{0,2},{1,3},{2,0},{3,1},{4,6},{5,7},{6,4},{7,5},{8,10},{9,11},{10,... | collective-permute-start | bytes 393224 | tf_op jit(solution)/shard_map/ppermute | solution.py:422
  66.4 2.0 %collective-permute-start.18 = (bf16[8,128,128]{2,1,0:T(8,128)(2,1)S(1)}, bf16[8,128,128]{2,1,0:T(8,128)(2,1)S(1)}, u32[]{:S(2)}, u32[]{:S(2)}) collective-permute-start(bf16[8,128,128]{2,1,0:T(8,128)(2,1)S(1)} %joined.3.refs_2_), channel_id=1, source_target_pairs={{0,1},{1,0},{2,3},{3,2},{4,5},{5,4},{6,7},{7,6},{8,9},{9,8},{10,11... | collective-permute-start | bytes 786440 | tf_op jit(solution)/shard_map/ppermute | solution.py:422
  66.5 1.7 %collective-permute-start.19 = (bf16[4,128,128]{2,1,0:T(8,128)(2,1)S(1)}, bf16[4,128,128]{2,1,0:T(8,128)(2,1)S(1)}, u32[]{:S(2)}, u32[]{:S(2)}) collective-permute-start(bf16[4,128,128]{2,1,0:T(8,128)(2,1)S(1)} %collective-permute-done.17.piece_ref.refs_4_), channel_id=1, source_target_pairs={{0,1},{1,0},{2,3},{3,2},{4,5},{5,4},{6,7},{7,6},{8,9},{9,8},{10,11... | collective-permute-start | bytes 393224 | tf_op jit(solution)/shard_map/ppermute | solution.py:422
  67.0 1.4 %collective-permute-start.21 = (bf16[4,128,128]{2,1,0:T(8,128)(2,1)S(1)}, bf16[4,128,128]{2,1,0:T(8,128)(2,1)S(1)}, u32[]{:S(2)}, u32[]{:S(2)}) collective-permute-start(bf16[4,128,128]{2,1,0:T(8,128)(2,1)S(1)} %collective-permute-done.20.refs_6_), channel_id=1, source_target_pairs={{0,1},{1,0},{2,3},{3,2},{4,5},{5,4},{6,7},{7,6},{8,9},{9,8},{10,11... | collective-permute-start | bytes 393224 | tf_op jit(solution)/shard_map/ppermute | solution.py:422
  71.6 6.9 %collective-permute-start.22 = (f32[8,128,128]{2,1,0:T(8,128)S(1)}, f32[8,128,128]{2,1,0:T(8,128)S(1)}, u32[]{:S(2)}, u32[]{:S(2)}) collective-permute-start(f32[8,128,128]{2,1,0:T(8,128)S(1)} %get-tuple-element.44.amps_ref), channel_id=1, source_target_pairs={{0,1},{1,0},{2,3},{3,2},{4,5},{5,4},{6,7},{7,6},{8,9},{9,8},{10,11... | collective-permute-start | bytes 1572872 | tf_op jit(solution)/shard_map/ppermute | solution.py:422
  71.9 9.7 %collective-permute-start.23 = (f32[2,128,128]{2,1,0:T(8,128)S(1)}, f32[2,128,128]{2,1,0:T(8,128)S(1)}, u32[]{:S(2)}, u32[]{:S(2)}) collective-permute-start(f32[2,128,128]{2,1,0:T(8,128)S(1)} %get-tuple-element.48), channel_id=1, source_target_pairs={{0,4},{4,8},{8,12},{1,5},{5,9},{9,13},{2,6},{6,10},{10,14},{3,7},{... | collective-permute-start | bytes 393224 | tf_op jit(solution)/shard_map/ppermute | solution.py:507
  77.3 7.4 %collective-permute-start.24 = (f32[2,128,128]{2,1,0:T(8,128)S(1)}, f32[2,128,128]{2,1,0:T(8,128)S(1)}, u32[]{:S(2)}, u32[]{:S(2)}) collective-permute-start(f32[2,128,128]{2,1,0:T(8,128)S(1)} %get-tuple-element.49), channel_id=1, source_target_pairs={{4,0},{8,4},{12,8},{5,1},{9,5},{13,9},{6,2},{10,6},{14,10},{7,3},{... | collective-permute-start | bytes 393224 | tf_op jit(solution)/shard_map/ppermute | solution.py:508
  84.7 1.4 %collective-permute-start.25 = (f32[2,128,128]{2,1,0:T(8,128)S(1)}, f32[2,128,128]{2,1,0:T(8,128)S(1)}, u32[]{:S(2)}, u32[]{:S(2)}) collective-permute-start(f32[2,128,128]{2,1,0:T(8,128)S(1)} %add_add_fusion), channel_id=1, source_target_pairs={{0,1},{1,0},{2,3},{3,2},{4,5},{5,4},{6,7},{7,6},{8,9},{9,8},{10,11... | collective-permute-start | bytes 393224 | tf_op jit(solution)/shard_map/ppermute | solution.py:422

commit v4 on v3

--- a/solution.py
+++ b/solution.py
@@ -88,12 +88,12 @@
     )(aux, occupied, used, energy, first, second, ints)
 
 
-def product_kernel(aux_ref, own_ref, up_ref, down_ref, kept_ref, sent_ref, inner):
+def product_kernel(aux_ref, own_ref, one_ref, two_ref, kept_ref, sent_ref, inner):
     count, _, width = own_ref.shape
     side = lax.rem(aux_ref[0], 2)
     own = jnp.concatenate([own_ref[side], own_ref[1 - side]], axis=1)
     at = 0
-    for near_ref in (up_ref, down_ref):
+    for near_ref in (one_ref, two_ref):
         near = jnp.concatenate([near_ref[i] for i in range(count)], axis=1)
         full = dot(own, near, ((0,), (0,)))
         for j in range(count):
@@ -107,7 +107,7 @@
     sent_ref[at:] = inner[pl.ds(pl.multiple_of((1 - side) * half, half), half)]
 
 
-def products(aux, ints, up, down):
+def products(aux, ints, one, two):
     count, depth, width = ints.shape
     rows = 2 * count * width + width // 2
     return pl.pallas_call(
@@ -119,7 +119,7 @@
         compiler_params=params(12),
         cost_estimate=cost(18 * depth * width * width, 12 * depth * width),
         name="products",
-    )(aux, ints, up, down)
+    )(aux, ints, one, two)
 
 
 def own_part(aux_ref, low_ref, part_ref):
@@ -138,7 +138,9 @@
         (half, total_ref[...].astype(F32) + far_ref[...].astype(F32)),
         (1 - half, total_other[...].astype(F32) + far_other[...].astype(F32)),
     ):
-        for at, slot in enumerate((4, 5, 0, 1)):
+        for at in range(4):
+            above = at // 2 == lax.rem(here_ref[0], 2)
+            slot = at % 2 + jnp.where(above, 4, 0)
             table[i * 6 + slot] = total[at * width : (at + 1) * width]
         table[3, pl.ds(pl.multiple_of(i * (width // 2), width // 2), width // 2)] = total[4 * width :]
     table[6 + 2] = table[3].T
@@ -187,7 +189,7 @@
     parts = refs[:pieces]
     over_ref, exch_ref, factor_ref, second_ref = refs[pieces : pieces + 4]
     if last:
-        amps_ref, terms_ref, table = refs[pieces + 4 :]
+        amps_ref, terms_ref, one_ref, two_ref, all_terms, table = refs[pieces + 4 :]
     else:
         low_ref, part_ref, table = refs[pieces + 4 :]
     count, width, _ = exch_ref.shape
@@ -254,10 +256,14 @@
                 ((1,), (1,)),
             )
             terms.append(square(moved))
-        terms_ref[...] = jnp.zeros_like(terms_ref)
+        all_terms[...] = jnp.zeros_like(all_terms)
         for p in range(count):
             spot = orbitals_ref[1, half * count + p] - here * 2 + 2
-            terms_ref[spot] += terms[p]
+            all_terms[spot] += terms[p]
+        terms_ref[...] = all_terms[2:4]
+        below = lax.rem(here, 2) * 4
+        one_ref[...] = all_terms[pl.ds(4 - below, 2)].astype(BF16)
+        two_ref[...] = all_terms[pl.ds(below, 2)].astype(BF16)
 
 
 def sweep(last, rounds, here, aux, orbitals, near, couple, parts, over, exch, factor, second):
@@ -266,21 +272,25 @@
     if last:
         out_shape = (
             jax.ShapeDtypeStruct(exch.shape, F32),
-            jax.ShapeDtypeStruct((6, width, width), F32),
-        )
-        out_specs = (VMEM, VMEM)
+            jax.ShapeDtypeStruct((2, width, width), F32),
+            jax.ShapeDtypeStruct((2, width, width), BF16),
+            jax.ShapeDtypeStruct((2, width, width), BF16),
+        )
+        out_specs = (VMEM,) * 4
+        scratch = [pltpu.VMEM((6, width, width), F32)]
     else:
         out_shape = (
             jax.ShapeDtypeStruct(exch.shape, BF16),
             jax.ShapeDtypeStruct((count // 2, width, width), BF16),
         )
         out_specs = (VMEM, VMEM)
+        scratch = []
     return pl.pallas_call(
         functools.partial(sweep_kernel, last, len(parts), rounds),
         out_shape=out_shape,
         in_specs=[SMEM] * 5 + [VMEM] * (len(parts) + 4),
         out_specs=out_specs,
-        scratch_shapes=[pltpu.VMEM((rows, width, width), BF16)],
+        scratch_shapes=scratch + [pltpu.VMEM((rows, width, width), BF16)],
         compiler_params=params(16),
         cost_estimate=cost(16 * count * width**3, (rows + 16 * count) * width * width),
         name="last_sweep" if last else "sweep",
@@ -303,21 +313,21 @@
     )(piece)
 
 
-def join_kernel(left_ref, right_ref, token_ref, out_ref):
-    del token_ref
+def join_kernel(left_ref, right_ref, token_ref, piece_ref, out_ref):
+    del token_ref, piece_ref
     out_ref[...] = left_ref[...] + right_ref[...]
 
 
-def joined(left, right, token):
+def joined(left, right, token, piece):
     return pl.pallas_call(
         join_kernel,
         out_shape=jax.ShapeDtypeStruct(left.shape, BF16),
-        in_specs=[VMEM] * 3,
+        in_specs=[VMEM] * 3 + [ANY],
         out_specs=VMEM,
         compiler_params=params(4),
         cost_estimate=cost(left.size, 6 * left.size),
         name="joined",
-    )(left, right, token)
+    )(left, right, token, piece)
 
 
 def first_kernel(
@@ -414,8 +424,10 @@
     wanted = pair_dev * nbr_count
     cap = 2 * wanted // groups
     count = pair_dev // 2
-    up = [(i + 1, i) for i in range(groups - 1)]
-    down = [(i, i + 1) for i in range(groups - 1)]
+    partners = [
+        [(i, j) for i in range(groups) for j in (i + 1 - 2 * ((i + r) % 2),) if 0 <= j < groups]
+        for r in range(2)
+    ]
     orbitals = pair_orbitals.T
 
     def swap(value, step=1):
@@ -423,16 +435,15 @@
 
     ints, here_s, aux_s = lax.optimization_barrier((ints, here.reshape(1), aux.reshape(1)))
 
-    above = lax.ppermute(ints, "pair", up)
-    below = lax.ppermute(ints, "pair", down)
+    near_one, near_two = (lax.ppermute(ints, "pair", pairs) for pairs in partners)
     first, second, ints, factor = prepare(
         aux_s, occ_energy.T, pno_count, virt_energy, proj_first, proj_second, ints
     )
-    above, first, second, ints, factor = lax.optimization_barrier(
-        (above, first, second, ints, factor)
+    near_one, first, second, ints, factor = lax.optimization_barrier(
+        (near_one, first, second, ints, factor)
     )
 
-    kept, sent = products(aux_s, ints, above, below)
+    kept, sent = products(aux_s, ints, near_one, near_two)
     total = kept + swap(sent)
     step = 2
     while 2 * step < aux_count:
@@ -480,10 +491,11 @@
             received = lax.all_to_all(outgoing, "pair", split_axis=0, concat_axis=0, tiled=True)
             return [received.reshape(groups * cap, width, width)[row_index]]
         one = lax.ppermute(part, "pair", rounds[0])
+        one_other = swap(one)
         cross = swap(one, 2)
-        others = swap(low)
-        two = joined(*(lax.ppermute(low, "pair", pairs) for pairs in rounds[1:]), token(one))
-        return [low, others, two, swap(two), one, swap(one), cross, swap(cross)]
+        two = (lax.ppermute(low, "pair", pairs) for pairs in rounds[1:])
+        two = joined(*two, token(one), one_other)
+        return [low, swap(low), two, swap(two), one, one_other, cross, swap(cross)]
 
     for it in range(ITERS):
         out = sweep(
@@ -502,12 +514,13 @@
         )
         if it < ITERS - 1:
             low, part = out
-    amps, terms = out
-
-    from_below = lax.ppermute(terms[2 * occ_dev :], "pair", down)
-    from_above = lax.ppermute(terms[:occ_dev], "pair", up)
+    amps, terms, *sent = out
+
+    near_one, near_two = (
+        lax.ppermute(value, "pair", pairs) for value, pairs in zip(sent, partners)
+    )
     whole, inner = first_terms(here_s, aux_s, orbitals, amps, swap(amps), first)
-    density = inner + terms[occ_dev : 2 * occ_dev] + from_below + from_above
+    density = inner + terms + near_one.astype(F32) + near_two.astype(F32)
     density = (density + swap(density)) / width
     return (whole, density)
 

time: 87.3 us -> 80.4 us (0.921)
  the two profiles are of different devices: /device:TPU:0 before, /device:TPU:15 now
where the time goes in v4:
time: 80.4 us; the launch traced here: 79.9 us
  starting transfers between devices  33.4 us (42%)
  waiting for transfers between devices  28.6 us (36%)
  Pallas kernels  11.1 us (14%)
  local copies, waits for them, and re-layouts  5.27 us (7%)
  between operations  0.83 us (1%)
    ppermute x4, starting transfers between devices, gathered(): two = (lax.ppermute(low, 'pair', pairs) for pairs in rounds[1:])  13.6 us
    ppermute x16, starting transfers between devices, swap(): return lax.ppermute(value, 'aux', [(i, i ^ step) for i in range(aux_count)])  11.8 us
    ppermute x2, waiting for transfers between devices, shards(): lax.ppermute(ints, 'pair', pairs)  11 us
    ppermute x16, waiting for transfers between devices, swap(): return lax.ppermute(value, 'aux', [(i, i ^ step) for i in range(aux_count)])  10.9 us
    ppermute x4, waiting for transfers between devices, gathered(): two = (lax.ppermute(low, 'pair', pairs) for pairs in rounds[1:])  6.64 us
    unnamed x20, local copies, waits for them, and re-layouts  5.27 us
    pallas_call x2, Pallas kernels, sweep(): pl.pallas_call(functools.partial(sweep_kernel, last, len(parts), rounds),...  5.14 us
    ppermute x2, starting transfers between devices, shards(): lax.ppermute(ints, 'pair', pairs)  4.55 us
  transfers between devices with their start and end apart: 26, of which 12 were waited for; matrix products, arithmetic and copies ran while one was open for 0% of the time, Pallas kernels for 5%

profile of v4, /device:TPU:15, one launch (start us, length us, event | category | flops | bytes accessed | tf_op | source)
XLA Modules:
  0.0 79.9 jit_solution(11899431280991162091)
XLA Ops:
  0.6 0.2 collective-permute-start
  0.9 4.3 %collective-permute-start.1 = (bf16[2,1536,128]{2,1,0:T(8,128)(2,1)}, bf16[2,1536,128]{2,1,0:T(8,128)(2,1)S(1)}, u32[]{:S(2)}, u32[]{:S(2)}) collective-permute-start(bf16[2,1536,128]{2,1,0:T(8,128)(2,1)} %ints_ref), channel_id=1, source_target_pairs={{4,8},{8,4},{5,9},{9,5},{6,10},{10,6},{7,11},{11,7},{20,24},{24,20... | collective-permute-start | bytes 2359304 | tf_op jit(solution)/shard_map/ppermute | solution.py:438
  5.2 1.1 %copy-done.1 = bf16[2,1536,128]{2,1,0:T(8,128)(2,1)S(1)} copy-done((bf16[2,1536,128]{2,1,0:T(8,128)(2,1)S(1)}, bf16[2,1536,128]{2,1,0:T(8,128)(2,1)}, u32[]{:S(2)}) %copy-start.1) | copy-done | bytes 786456
  6.3 1.0 %copy-done.2 = bf16[16,128,128]{2,1,0:T(8,128)(2,1)S(1)} copy-done((bf16[16,128,128]{2,1,0:T(8,128)(2,1)S(1)}, bf16[16,128,128]{2,1,0:T(8,128)(2,1)}, u32[]{:S(2)}) %copy-start.2) | copy-done | bytes 524312
  7.4 1.0 %copy-done.3 = bf16[16,128,128]{2,1,0:T(8,128)(2,1)S(1)} copy-done((bf16[16,128,128]{2,1,0:T(8,128)(2,1)S(1)}, bf16[16,128,128]{2,1,0:T(8,128)(2,1)}, u32[]{:S(2)}) %copy-start.3) | copy-done | bytes 524312
  8.4 0.7 copy-done.5
  9.1 0.7 copy-done.8
  9.8 0.7 copy-done.9
  10.5 0.9 %prepare.1 = (bf16[8,128,128]{2,1,0:T(8,128)(2,1)S(1)}, bf16[8,128,128]{2,1,0:T(8,128)(2,1)S(1)}, bf16[2,1536,128]{2,1,0:T(8,128)(2,1)S(1)}, f32[8,128,128]{2,1,0:T(8,128)S(1)}) custom-call(s32[1]{0:T(128)} %bitcast.1.aux_ref, f32[2,16]{1,0:T(2,128)S(1)} %bitcast.14, s32[16]{0:T(128)S(1)} %copy-done.9, f32[16,128]{1,0:T(8,128)S(1)} %copy-done.5, ...), custom_call_target="tpu_custom_call" | custom-call | bytes 2097152 | tf_op jit(solution)/shard_map/prepare/pallas_call | solution.py:74
  11.4 8.0 %collective-permute-done.one_ref = bf16[2,1536,128]{2,1,0:T(8,128)(2,1)S(1)} collective-permute-done((bf16[2,1536,128]{2,1,0:T(8,128)(2,1)}, bf16[2,1536,128]{2,1,0:T(8,128)(2,1)S(1)}, u32[]{:S(2)}, u32[]{:S(2)}) %collective-permute-start) | collective-permute-done | bytes 786464 | tf_op jit(solution)/shard_map/ppermute | solution.py:438
  19.3 3.0 %collective-permute-done.1.two_ref = bf16[2,1536,128]{2,1,0:T(8,128)(2,1)S(1)} collective-permute-done((bf16[2,1536,128]{2,1,0:T(8,128)(2,1)}, bf16[2,1536,128]{2,1,0:T(8,128)(2,1)S(1)}, u32[]{:S(2)}, u32[]{:S(2)}) %collective-permute-start.1) | collective-permute-done | bytes 786464 | tf_op jit(solution)/shard_map/ppermute | solution.py:438
  22.3 0.7 products.1
  23.1 1.6 %collective-permute-start.2 = (f32[576,128]{1,0:T(8,128)S(1)}, f32[576,128]{1,0:T(8,128)S(1)}, u32[]{:S(2)}, u32[]{:S(2)}) collective-permute-start(f32[576,128]{1,0:T(8,128)S(1)} %get-tuple-element.37), channel_id=1, source_target_pairs={{0,1},{1,0},{2,3},{3,2},{4,5},{5,4},{6,7},{7,6},{8,9},{9,8},{10,11... | collective-permute-start | bytes 884744 | tf_op jit(solution)/shard_map/ppermute | solution.py:434
  24.7 1.2 %collective-permute-done.2 = f32[576,128]{1,0:T(8,128)S(1)} collective-permute-done((f32[576,128]{1,0:T(8,128)S(1)}, f32[576,128]{1,0:T(8,128)S(1)}, u32[]{:S(2)}, u32[]{:S(2)}) %collective-permute-start.2) | collective-permute-done | bytes 294944 | tf_op jit(solution)/shard_map/ppermute | solution.py:434
  25.9 0.3 collective-permute-start.3
  26.2 0.7 collective-permute-start.4
  26.9 4.2 %collective-permute-done.3.far_ref = bf16[576,128]{1,0:T(8,128)(2,1)S(1)} collective-permute-done((bf16[576,128]{1,0:T(8,128)(2,1)S(1)}, bf16[576,128]{1,0:T(8,128)(2,1)S(1)}, u32[]{:S(2)}, u32[]{:S(2)}) %collective-permute-start.3) | collective-permute-done | bytes 147488 | tf_op jit(solution)/shard_map/ppermute | solution.py:434
  31.1 1.2 %collective-permute-start.5 = (bf16[576,128]{1,0:T(8,128)(2,1)S(1)}, bf16[576,128]{1,0:T(8,128)(2,1)S(1)}, u32[]{:S(2)}, u32[]{:S(2)}) collective-permute-start(bf16[576,128]{1,0:T(8,128)(2,1)S(1)} %collective-permute-done.3.far_ref), channel_id=1, source_target_pairs={{0,1},{1,0},{2,3},{3,2},{4,5},{5,4},{6,7},{7,6},{8,9},{9,8},{10,11... | collective-permute-start | bytes 442376 | tf_op jit(solution)/shard_map/ppermute | solution.py:434
  32.3 0.0 collective-permute-done.4.total_other
  32.3 1.0 %collective-permute-done.5.far_other = bf16[576,128]{1,0:T(8,128)(2,1)S(1)} collective-permute-done((bf16[576,128]{1,0:T(8,128)(2,1)S(1)}, bf16[576,128]{1,0:T(8,128)(2,1)S(1)}, u32[]{:S(2)}, u32[]{:S(2)}) %collective-permute-start.5) | collective-permute-done | bytes 147488 | tf_op jit(solution)/shard_map/ppermute | solution.py:434
  33.3 1.3 %exchange.1 = (f32[8,128,128]{2,1,0:T(8,128)S(1)}, bf16[8,128,128]{2,1,0:T(8,128)(2,1)S(1)}, bf16[4,128,128]{2,1,0:T(8,128)(2,1)S(1)}) custom-call(s32[1]{0:T(128)} %bitcast.here_ref, s32[1]{0:T(128)} %bitcast.1.aux_ref, s32[2,16]{1,0:T(2,128)S(1)} %bitcast.6, bf16[576,128]{1,0:T(8,128)(2,1)S(1)} %add_convert_fusion.total_ref, ...), custom_call_target="tpu_custom_call" | custom-call | flops 134217728 | bytes 2621440 | tf_op jit(solution)/shard_map/exchange/pallas_call | solution.py:172
  34.5 0.1 collective-permute-start.9
  34.6 0.0 copy-start.6
  34.6 0.0 copy-start.7
  34.6 3.5 %collective-permute-start.8 = (bf16[8,128,128]{2,1,0:T(8,128)(2,1)S(1)}, bf16[8,128,128]{2,1,0:T(8,128)(2,1)S(1)}, u32[]{:S(2)}, u32[]{:S(2)}) collective-permute-start(bf16[8,128,128]{2,1,0:T(8,128)(2,1)S(1)} %get-tuple-element.41.refs_0_), channel_id=1, source_target_pairs={{4,0},{8,12},{5,1},{9,13},{6,2},{10,14},{7,3},{11,15},{20,16},{24,... | collective-permute-start | bytes 786440 | tf_op jit(solution)/shard_map/ppermute | solution.py:496
  38.1 3.4 %collective-permute-start.7 = (bf16[8,128,128]{2,1,0:T(8,128)(2,1)S(1)}, bf16[8,128,128]{2,1,0:T(8,128)(2,1)S(1)}, u32[]{:S(2)}, u32[]{:S(2)}) collective-permute-start(bf16[8,128,128]{2,1,0:T(8,128)(2,1)S(1)} %get-tuple-element.41.refs_0_), channel_id=1, source_target_pairs={{4,8},{8,4},{5,9},{9,5},{6,10},{10,6},{7,11},{11,7},{20,24},{24,20... | collective-permute-start | bytes 786440 | tf_op jit(solution)/shard_map/ppermute | solution.py:496
  41.5 1.3 %collective-permute-start.6 = (bf16[8,128,128]{2,1,0:T(8,128)(2,1)S(1)}, bf16[8,128,128]{2,1,0:T(8,128)(2,1)S(1)}, u32[]{:S(2)}, u32[]{:S(2)}) collective-permute-start(bf16[8,128,128]{2,1,0:T(8,128)(2,1)S(1)} %get-tuple-element.41.refs_0_), channel_id=1, source_target_pairs={{0,1},{1,0},{2,3},{3,2},{4,5},{5,4},{6,7},{7,6},{8,9},{9,8},{10,11... | collective-permute-start | bytes 786440 | tf_op jit(solution)/shard_map/ppermute | solution.py:434
  42.8 0.1 collective-permute-start.10
  42.8 0.2 collective-permute-start.12
  43.1 1.0 %collective-permute-done.10.piece_ref.refs_5_ = bf16[4,128,128]{2,1,0:T(8,128)(2,1)S(1)} collective-permute-done((bf16[4,128,128]{2,1,0:T(8,128)(2,1)S(1)}, bf16[4,128,128]{2,1,0:T(8,128)(2,1)S(1)}, u32[]{:S(2)}, u32[]{:S(2)}) %collective-permute-start.10) | collective-permute-done | bytes 131104 | tf_op jit(solution)/shard_map/ppermute | solution.py:434
  44.1 0.0 collective-permute-done.8.right_ref
  44.1 2.8 %collective-permute-done.7.left_ref = bf16[8,128,128]{2,1,0:T(8,128)(2,1)S(1)} collective-permute-done((bf16[8,128,128]{2,1,0:T(8,128)(2,1)S(1)}, bf16[8,128,128]{2,1,0:T(8,128)(2,1)S(1)}, u32[]{:S(2)}, u32[]{:S(2)}) %collective-permute-start.7) | collective-permute-done | bytes 262176 | tf_op jit(solution)/shard_map/ppermute | solution.py:496
  46.9 0.1 joined.2.refs_2_
  47.0 1.9 %collective-permute-start.11 = (bf16[8,128,128]{2,1,0:T(8,128)(2,1)S(1)}, bf16[8,128,128]{2,1,0:T(8,128)(2,1)S(1)}, u32[]{:S(2)}, u32[]{:S(2)}) collective-permute-start(bf16[8,128,128]{2,1,0:T(8,128)(2,1)S(1)} %joined.2.refs_2_), channel_id=1, source_target_pairs={{0,1},{1,0},{2,3},{3,2},{4,5},{5,4},{6,7},{7,6},{8,9},{9,8},{10,11... | collective-permute-start | bytes 786440 | tf_op jit(solution)/shard_map/ppermute | solution.py:434
  48.9 0.0 collective-permute-done.12.refs_6_
  48.9 0.1 collective-permute-start.13
  48.9 0.0 collective-permute-done.6.refs_1_
  48.9 1.3 %collective-permute-done.13.refs_7_ = bf16[4,128,128]{2,1,0:T(8,128)(2,1)S(1)} collective-permute-done((bf16[4,128,128]{2,1,0:T(8,128)(2,1)S(1)}, bf16[4,128,128]{2,1,0:T(8,128)(2,1)S(1)}, u32[]{:S(2)}, u32[]{:S(2)}) %collective-permute-start.13) | collective-permute-done | bytes 131104 | tf_op jit(solution)/shard_map/ppermute | solution.py:434
  50.2 0.0 collective-permute-done.11.refs_3_
  50.2 1.9 %sweep.1 = (bf16[8,128,128]{2,1,0:T(8,128)(2,1)S(1)}, bf16[4,128,128]{2,1,0:T(8,128)(2,1)S(1)}) custom-call(s32[1]{0:T(128)} %bitcast.here_ref, s32[1]{0:T(128)} %bitcast.1.aux_ref, s32[2,16]{1,0:T(2,128)S(1)} %bitcast.7, s32[4,64]{1,0:T(4,128)S(1)} %bitcast.10, f32[4,16]{1,0:T(4,128)S(1)} %bitcast.12, bf16[8,128,128]{2,1,0:T(8,128)(2,1)S(1)} %get-tuple-element.41.refs_0_, ...), custom_call_target="tpu_custom_call" | custom-call | flops 268435456 | bytes 2883584 | tf_op jit(solution)/shard_map/sweep/pallas_call | solution.py:288
  52.1 0.1 collective-permute-start.17
  52.2 3.4 %collective-permute-start.16 = (bf16[8,128,128]{2,1,0:T(8,128)(2,1)S(1)}, bf16[8,128,128]{2,1,0:T(8,128)(2,1)S(1)}, u32[]{:S(2)}, u32[]{:S(2)}) collective-permute-start(bf16[8,128,128]{2,1,0:T(8,128)(2,1)S(1)} %get-tuple-element.44.refs_0_), channel_id=1, source_target_pairs={{4,0},{8,12},{5,1},{9,13},{6,2},{10,14},{7,3},{11,15},{20,16},{24,... | collective-permute-start | bytes 786440 | tf_op jit(solution)/shard_map/ppermute | solution.py:496
  55.6 3.4 %collective-permute-start.15 = (bf16[8,128,128]{2,1,0:T(8,128)(2,1)S(1)}, bf16[8,128,128]{2,1,0:T(8,128)(2,1)S(1)}, u32[]{:S(2)}, u32[]{:S(2)}) collective-permute-start(bf16[8,128,128]{2,1,0:T(8,128)(2,1)S(1)} %get-tuple-element.44.refs_0_), channel_id=1, source_target_pairs={{4,8},{8,4},{5,9},{9,5},{6,10},{10,6},{7,11},{11,7},{20,24},{24,20... | collective-permute-start | bytes 786440 | tf_op jit(solution)/shard_map/ppermute | solution.py:496
  58.9 1.3 %collective-permute-start.14 = (bf16[8,128,128]{2,1,0:T(8,128)(2,1)S(1)}, bf16[8,128,128]{2,1,0:T(8,128)(2,1)S(1)}, u32[]{:S(2)}, u32[]{:S(2)}) collective-permute-start(bf16[8,128,128]{2,1,0:T(8,128)(2,1)S(1)} %get-tuple-element.44.refs_0_), channel_id=1, source_target_pairs={{0,1},{1,0},{2,3},{3,2},{4,5},{5,4},{6,7},{7,6},{8,9},{9,8},{10,11... | collective-permute-start | bytes 786440 | tf_op jit(solution)/shard_map/ppermute | solution.py:434
  60.2 0.0 collective-permute-done.17.piece_ref.refs_4_
  60.2 0.1 collective-permute-start.18
  60.3 0.2 collective-permute-start.20
  60.5 1.3 %collective-permute-done.16.right_ref = bf16[8,128,128]{2,1,0:T(8,128)(2,1)S(1)} collective-permute-done((bf16[8,128,128]{2,1,0:T(8,128)(2,1)S(1)}, bf16[8,128,128]{2,1,0:T(8,128)(2,1)S(1)}, u32[]{:S(2)}, u32[]{:S(2)}) %collective-permute-start.16) | collective-permute-done | bytes 262176 | tf_op jit(solution)/shard_map/ppermute | solution.py:496
  61.8 2.5 %collective-permute-done.15.left_ref = bf16[8,128,128]{2,1,0:T(8,128)(2,1)S(1)} collective-permute-done((bf16[8,128,128]{2,1,0:T(8,128)(2,1)S(1)}, bf16[8,128,128]{2,1,0:T(8,128)(2,1)S(1)}, u32[]{:S(2)}, u32[]{:S(2)}) %collective-permute-start.15) | collective-permute-done | bytes 262176 | tf_op jit(solution)/shard_map/ppermute | solution.py:496
  64.3 0.0 collective-permute-done.18.piece_ref.refs_5_
  64.3 0.1 joined.3.refs_2_
  64.4 1.9 %collective-permute-start.19 = (bf16[8,128,128]{2,1,0:T(8,128)(2,1)S(1)}, bf16[8,128,128]{2,1,0:T(8,128)(2,1)S(1)}, u32[]{:S(2)}, u32[]{:S(2)}) collective-permute-start(bf16[8,128,128]{2,1,0:T(8,128)(2,1)S(1)} %joined.3.refs_2_), channel_id=1, source_target_pairs={{0,1},{1,0},{2,3},{3,2},{4,5},{5,4},{6,7},{7,6},{8,9},{9,8},{10,11... | collective-permute-start | bytes 786440 | tf_op jit(solution)/shard_map/ppermute | solution.py:434
  66.3 0.0 collective-permute-done.20.refs_6_
  66.3 0.1 collective-permute-start.21
  66.4 1.3 %collective-permute-done.21.refs_7_ = bf16[4,128,128]{2,1,0:T(8,128)(2,1)S(1)} collective-permute-done((bf16[4,128,128]{2,1,0:T(8,128)(2,1)S(1)}, bf16[4,128,128]{2,1,0:T(8,128)(2,1)S(1)}, u32[]{:S(2)}, u32[]{:S(2)}) %collective-permute-start.21) | collective-permute-done | bytes 131104 | tf_op jit(solution)/shard_map/ppermute | solution.py:434
  67.7 3.2 %last_sweep.1 = (f32[8,128,128]{2,1,0:T(8,128)S(1)}, f32[2,128,128]{2,1,0:T(8,128)S(1)}, bf16[2,128,128]{2,1,0:T(8,128)(2,1)S(1)}, bf16[2,128,128]{2,1,0:T(8,128)(2,1)S(1)}) custom-call(s32[1]{0:T(128)} %bitcast.here_ref, s32[1]{0:T(128)} %bitcast.1.aux_ref, s32[2,16]{1,0:T(2,128)S(1)} %bitcast.8, s32[4,64]{1,0:T(4,128)S(1)} %bitcast.11, ...), custom_call_target="tpu_custom_call" | custom-call | flops 268435456 | bytes 2883584 | tf_op jit(solution)/shard_map/last_sweep/pallas_call | solution.py:288
  70.9 0.4 collective-permute-start.22
  71.4 0.0 collective-permute-start.23
  71.4 3.4 %collective-permute-start.24 = (bf16[2,128,128]{2,1,0:T(8,128)(2,1)S(1)}, bf16[2,128,128]{2,1,0:T(8,128)(2,1)S(1)}, u32[]{:S(2)}, u32[]{:S(2)}) collective-permute-start(bf16[2,128,128]{2,1,0:T(8,128)(2,1)S(1)} %get-tuple-element.51), channel_id=1, source_target_pairs={{4,8},{8,4},{5,9},{9,5},{6,10},{10,6},{7,11},{11,7},{20,24},{24,20... | collective-permute-start | bytes 196616 | tf_op jit(solution)/shard_map/ppermute | solution.py:520
  74.7 0.0 collective-permute-done.22.others_ref
  74.7 3.0 %first_terms.1 = (f32[16,128,128]{2,1,0:T(8,128)}, f32[2,128,128]{2,1,0:T(8,128)S(1)}) custom-call(s32[1]{0:T(128)} %bitcast.here_ref, s32[1]{0:T(128)} %bitcast.1.aux_ref, s32[2,16]{1,0:T(2,128)S(1)} %bitcast.9, f32[8,128,128]{2,1,0:T(8,128)S(1)} %get-tuple-element.46.amps_ref, f32[8,128,128]{2,1,0:T(8,128)S(1)} %collective-permute-done.22.others_ref, ...), custom_call_target="tpu_custom_call" | custom-call | flops 201326592 | bytes 2097152 | tf_op jit(solution)/shard_map/first_terms/pallas_call | solution.py:364
  77.8 0.5 collective-permute-start.25
  78.3 1.0 %collective-permute-done.25 = f32[2,128,128]{2,1,0:T(8,128)S(1)} collective-permute-done((f32[2,128,128]{2,1,0:T(8,128)S(1)}, f32[2,128,128]{2,1,0:T(8,128)S(1)}, u32[]{:S(2)}, u32[]{:S(2)}) %collective-permute-start.25) | collective-permute-done | bytes 131104 | tf_op jit(solution)/shard_map/ppermute | solution.py:434
  79.2 0.7 add_multiply_fusion
  (21 shorter events, 0.1 us)
Async XLA Ops:
  0.6 18.7 %collective-permute-start = (bf16[2,1536,128]{2,1,0:T(8,128)(2,1)}, bf16[2,1536,128]{2,1,0:T(8,128)(2,1)S(1)}, u32[]{:S(2)}, u32[]{:S(2)}) collective-permute-start(bf16[2,1536,128]{2,1,0:T(8,128)(2,1)} %ints_ref), channel_id=1, source_target_pairs={{0,4},{4,0},{8,12},{12,8},{1,5},{5,1},{9,13},{13,9},{2,6},{6,2},{1... | collective-permute-start | bytes 2359304 | tf_op jit(solution)/shard_map/ppermute | solution.py:438
  0.9 21.5 %collective-permute-start.1 = (bf16[2,1536,128]{2,1,0:T(8,128)(2,1)}, bf16[2,1536,128]{2,1,0:T(8,128)(2,1)S(1)}, u32[]{:S(2)}, u32[]{:S(2)}) collective-permute-start(bf16[2,1536,128]{2,1,0:T(8,128)(2,1)} %ints_ref), channel_id=1, source_target_pairs={{4,8},{8,4},{5,9},{9,5},{6,10},{10,6},{7,11},{11,7},{20,24},{24,20... | collective-permute-start | bytes 2359304 | tf_op jit(solution)/shard_map/ppermute | solution.py:438
  5.2 1.1 %copy-start.1 = (bf16[2,1536,128]{2,1,0:T(8,128)(2,1)S(1)}, bf16[2,1536,128]{2,1,0:T(8,128)(2,1)}, u32[]{:S(2)}) copy-start(bf16[2,1536,128]{2,1,0:T(8,128)(2,1)} %ints_ref) | copy-start | bytes 2359300
  6.3 1.0 %copy-start.2 = (bf16[16,128,128]{2,1,0:T(8,128)(2,1)S(1)}, bf16[16,128,128]{2,1,0:T(8,128)(2,1)}, u32[]{:S(2)}) copy-start(bf16[16,128,128]{2,1,0:T(8,128)(2,1)} %first_ref.1) | copy-start | bytes 1572868
  7.4 1.0 %copy-start.3 = (bf16[16,128,128]{2,1,0:T(8,128)(2,1)S(1)}, bf16[16,128,128]{2,1,0:T(8,128)(2,1)}, u32[]{:S(2)}) copy-start(bf16[16,128,128]{2,1,0:T(8,128)(2,1)} %second_ref.1) | copy-start | bytes 1572868
  8.4 0.7 copy-start.5
  9.1 0.7 copy-start.8
  9.8 0.7 copy-start.9
  10.5 22.8 %copy-start.4 = (s32[16,2]{0,1:T(2,128)S(1)}, s32[16,2]{0,1:T(2,128)}, u32[]{:S(2)}) copy-start(s32[16,2]{0,1:T(2,128)} %param.18) | copy-start | bytes 388
  23.1 2.8 %collective-permute-start.2 = (f32[576,128]{1,0:T(8,128)S(1)}, f32[576,128]{1,0:T(8,128)S(1)}, u32[]{:S(2)}, u32[]{:S(2)}) collective-permute-start(f32[576,128]{1,0:T(8,128)S(1)} %get-tuple-element.37), channel_id=1, source_target_pairs={{0,1},{1,0},{2,3},{3,2},{4,5},{5,4},{6,7},{7,6},{8,9},{9,8},{10,11... | collective-permute-start | bytes 884744 | tf_op jit(solution)/shard_map/ppermute | solution.py:434
  25.9 5.1 %collective-permute-start.3 = (bf16[576,128]{1,0:T(8,128)(2,1)S(1)}, bf16[576,128]{1,0:T(8,128)(2,1)S(1)}, u32[]{:S(2)}, u32[]{:S(2)}) collective-permute-start(bf16[576,128]{1,0:T(8,128)(2,1)S(1)} %add_convert_fusion.total_ref), channel_id=1, source_target_pairs={{0,2},{1,3},{2,0},{3,1},{4,6},{5,7},{6,4},{7,5},{8,10},{9,11},{10,... | collective-permute-start | bytes 442376 | tf_op jit(solution)/shard_map/ppermute | solution.py:434
  26.2 6.0 %collective-permute-start.4 = (bf16[576,128]{1,0:T(8,128)(2,1)S(1)}, bf16[576,128]{1,0:T(8,128)(2,1)S(1)}, u32[]{:S(2)}, u32[]{:S(2)}) collective-permute-start(bf16[576,128]{1,0:T(8,128)(2,1)S(1)} %add_convert_fusion.total_ref), channel_id=1, source_target_pairs={{0,1},{1,0},{2,3},{3,2},{4,5},{5,4},{6,7},{7,6},{8,9},{9,8},{10,11... | collective-permute-start | bytes 442376 | tf_op jit(solution)/shard_map/ppermute | solution.py:434
  31.1 2.2 %collective-permute-start.5 = (bf16[576,128]{1,0:T(8,128)(2,1)S(1)}, bf16[576,128]{1,0:T(8,128)(2,1)S(1)}, u32[]{:S(2)}, u32[]{:S(2)}) collective-permute-start(bf16[576,128]{1,0:T(8,128)(2,1)S(1)} %collective-permute-done.3.far_ref), channel_id=1, source_target_pairs={{0,1},{1,0},{2,3},{3,2},{4,5},{5,4},{6,7},{7,6},{8,9},{9,8},{10,11... | collective-permute-start | bytes 442376 | tf_op jit(solution)/shard_map/ppermute | solution.py:434
  34.5 8.2 %collective-permute-start.9 = (bf16[4,128,128]{2,1,0:T(8,128)(2,1)S(1)}, bf16[4,128,128]{2,1,0:T(8,128)(2,1)S(1)}, u32[]{:S(2)}, u32[]{:S(2)}) collective-permute-start(bf16[4,128,128]{2,1,0:T(8,128)(2,1)S(1)} %get-tuple-element.42), channel_id=1, source_target_pairs={{4,12},{8,0},{0,4},{12,8},{5,13},{9,1},{1,5},{13,9},{6,14},{10,2},... | collective-permute-start | bytes 393224 | tf_op jit(solution)/shard_map/ppermute | solution.py:493
  34.6 15.6 %copy-start.6 = (s32[64,4]{0,1:T(4,128)S(1)}, s32[64,4]{0,1:T(4,128)}, u32[]{:S(2)}) copy-start(s32[64,4]{0,1:T(4,128)} %param.19) | copy-start | bytes 3076
  34.6 15.6 %copy-start.7 = (f32[16,4]{0,1:T(4,128)S(1)}, f32[16,4]{0,1:T(4,128)}, u32[]{:S(2)}) copy-start(f32[16,4]{0,1:T(4,128)} %param.14) | copy-start | bytes 772
  34.6 9.5 %collective-permute-start.8 = (bf16[8,128,128]{2,1,0:T(8,128)(2,1)S(1)}, bf16[8,128,128]{2,1,0:T(8,128)(2,1)S(1)}, u32[]{:S(2)}, u32[]{:S(2)}) collective-permute-start(bf16[8,128,128]{2,1,0:T(8,128)(2,1)S(1)} %get-tuple-element.41.refs_0_), channel_id=1, source_target_pairs={{4,0},{8,12},{5,1},{9,13},{6,2},{10,14},{7,3},{11,15},{20,16},{24,... | collective-permute-start | bytes 786440 | tf_op jit(solution)/shard_map/ppermute | solution.py:496
  38.1 8.8 %collective-permute-start.7 = (bf16[8,128,128]{2,1,0:T(8,128)(2,1)S(1)}, bf16[8,128,128]{2,1,0:T(8,128)(2,1)S(1)}, u32[]{:S(2)}, u32[]{:S(2)}) collective-permute-start(bf16[8,128,128]{2,1,0:T(8,128)(2,1)S(1)} %get-tuple-element.41.refs_0_), channel_id=1, source_target_pairs={{4,8},{8,4},{5,9},{9,5},{6,10},{10,6},{7,11},{11,7},{20,24},{24,20... | collective-permute-start | bytes 786440 | tf_op jit(solution)/shard_map/ppermute | solution.py:496
  41.5 7.5 %collective-permute-start.6 = (bf16[8,128,128]{2,1,0:T(8,128)(2,1)S(1)}, bf16[8,128,128]{2,1,0:T(8,128)(2,1)S(1)}, u32[]{:S(2)}, u32[]{:S(2)}) collective-permute-start(bf16[8,128,128]{2,1,0:T(8,128)(2,1)S(1)} %get-tuple-element.41.refs_0_), channel_id=1, source_target_pairs={{0,1},{1,0},{2,3},{3,2},{4,5},{5,4},{6,7},{7,6},{8,9},{9,8},{10,11... | collective-permute-start | bytes 786440 | tf_op jit(solution)/shard_map/ppermute | solution.py:434
  42.8 1.3 %collective-permute-start.10 = (bf16[4,128,128]{2,1,0:T(8,128)(2,1)S(1)}, bf16[4,128,128]{2,1,0:T(8,128)(2,1)S(1)}, u32[]{:S(2)}, u32[]{:S(2)}) collective-permute-start(bf16[4,128,128]{2,1,0:T(8,128)(2,1)S(1)} %collective-permute-done.9.piece_ref.refs_4_), channel_id=1, source_target_pairs={{0,1},{1,0},{2,3},{3,2},{4,5},{5,4},{6,7},{7,6},{8,9},{9,8},{10,11... | collective-permute-start | bytes 393224 | tf_op jit(solution)/shard_map/ppermute | solution.py:434
  42.8 7.4 %copy-start = (bf16[16,4,128,128]{3,2,1,0:T(8,128)(2,1)S(1)}, bf16[16,4,128,128]{3,2,1,0:T(8,128)(2,1)}, u32[]{:S(2)}) copy-start(bf16[16,4,128,128]{3,2,1,0:T(8,128)(2,1)} %refs_8_.3) | copy-start | bytes 6291460
  42.8 6.0 %collective-permute-start.12 = (bf16[4,128,128]{2,1,0:T(8,128)(2,1)S(1)}, bf16[4,128,128]{2,1,0:T(8,128)(2,1)S(1)}, u32[]{:S(2)}, u32[]{:S(2)}) collective-permute-start(bf16[4,128,128]{2,1,0:T(8,128)(2,1)S(1)} %collective-permute-done.9.piece_ref.refs_4_), channel_id=1, source_target_pairs={{0,2},{1,3},{2,0},{3,1},{4,6},{5,7},{6,4},{7,5},{8,10},{9,11},{10,... | collective-permute-start | bytes 393224 | tf_op jit(solution)/shard_map/ppermute | solution.py:434
  47.0 3.2 %collective-permute-start.11 = (bf16[8,128,128]{2,1,0:T(8,128)(2,1)S(1)}, bf16[8,128,128]{2,1,0:T(8,128)(2,1)S(1)}, u32[]{:S(2)}, u32[]{:S(2)}) collective-permute-start(bf16[8,128,128]{2,1,0:T(8,128)(2,1)S(1)} %joined.2.refs_2_), channel_id=1, source_target_pairs={{0,1},{1,0},{2,3},{3,2},{4,5},{5,4},{6,7},{7,6},{8,9},{9,8},{10,11... | collective-permute-start | bytes 786440 | tf_op jit(solution)/shard_map/ppermute | solution.py:434
  48.9 1.3 %collective-permute-start.13 = (bf16[4,128,128]{2,1,0:T(8,128)(2,1)S(1)}, bf16[4,128,128]{2,1,0:T(8,128)(2,1)S(1)}, u32[]{:S(2)}, u32[]{:S(2)}) collective-permute-start(bf16[4,128,128]{2,1,0:T(8,128)(2,1)S(1)} %collective-permute-done.12.refs_6_), channel_id=1, source_target_pairs={{0,1},{1,0},{2,3},{3,2},{4,5},{5,4},{6,7},{7,6},{8,9},{9,8},{10,11... | collective-permute-start | bytes 393224 | tf_op jit(solution)/shard_map/ppermute | solution.py:434
  52.1 8.1 %collective-permute-start.17 = (bf16[4,128,128]{2,1,0:T(8,128)(2,1)S(1)}, bf16[4,128,128]{2,1,0:T(8,128)(2,1)S(1)}, u32[]{:S(2)}, u32[]{:S(2)}) collective-permute-start(bf16[4,128,128]{2,1,0:T(8,128)(2,1)S(1)} %get-tuple-element.45), channel_id=1, source_target_pairs={{4,12},{8,0},{0,4},{12,8},{5,13},{9,1},{1,5},{13,9},{6,14},{10,2},... | collective-permute-start | bytes 393224 | tf_op jit(solution)/shard_map/ppermute | solution.py:493
  52.2 9.6 %collective-permute-start.16 = (bf16[8,128,128]{2,1,0:T(8,128)(2,1)S(1)}, bf16[8,128,128]{2,1,0:T(8,128)(2,1)S(1)}, u32[]{:S(2)}, u32[]{:S(2)}) collective-permute-start(bf16[8,128,128]{2,1,0:T(8,128)(2,1)S(1)} %get-tuple-element.44.refs_0_), channel_id=1, source_target_pairs={{4,0},{8,12},{5,1},{9,13},{6,2},{10,14},{7,3},{11,15},{20,16},{24,... | collective-permute-start | bytes 786440 | tf_op jit(solution)/shard_map/ppermute | solution.py:496
  55.6 8.8 %collective-permute-start.15 = (bf16[8,128,128]{2,1,0:T(8,128)(2,1)S(1)}, bf16[8,128,128]{2,1,0:T(8,128)(2,1)S(1)}, u32[]{:S(2)}, u32[]{:S(2)}) collective-permute-start(bf16[8,128,128]{2,1,0:T(8,128)(2,1)S(1)} %get-tuple-element.44.refs_0_), channel_id=1, source_target_pairs={{4,8},{8,4},{5,9},{9,5},{6,10},{10,6},{7,11},{11,7},{20,24},{24,20... | collective-permute-start | bytes 786440 | tf_op jit(solution)/shard_map/ppermute | solution.py:496
  58.9 7.5 %collective-permute-start.14 = (bf16[8,128,128]{2,1,0:T(8,128)(2,1)S(1)}, bf16[8,128,128]{2,1,0:T(8,128)(2,1)S(1)}, u32[]{:S(2)}, u32[]{:S(2)}) collective-permute-start(bf16[8,128,128]{2,1,0:T(8,128)(2,1)S(1)} %get-tuple-element.44.refs_0_), channel_id=1, source_target_pairs={{0,1},{1,0},{2,3},{3,2},{4,5},{5,4},{6,7},{7,6},{8,9},{9,8},{10,11... | collective-permute-start | bytes 786440 | tf_op jit(solution)/shard_map/ppermute | solution.py:434
  60.2 4.1 %collective-permute-start.18 = (bf16[4,128,128]{2,1,0:T(8,128)(2,1)S(1)}, bf16[4,128,128]{2,1,0:T(8,128)(2,1)S(1)}, u32[]{:S(2)}, u32[]{:S(2)}) collective-permute-start(bf16[4,128,128]{2,1,0:T(8,128)(2,1)S(1)} %collective-permute-done.17.piece_ref.refs_4_), channel_id=1, source_target_pairs={{0,1},{1,0},{2,3},{3,2},{4,5},{5,4},{6,7},{7,6},{8,9},{9,8},{10,11... | collective-permute-start | bytes 393224 | tf_op jit(solution)/shard_map/ppermute | solution.py:434
  60.3 6.0 %collective-permute-start.20 = (bf16[4,128,128]{2,1,0:T(8,128)(2,1)S(1)}, bf16[4,128,128]{2,1,0:T(8,128)(2,1)S(1)}, u32[]{:S(2)}, u32[]{:S(2)}) collective-permute-start(bf16[4,128,128]{2,1,0:T(8,128)(2,1)S(1)} %collective-permute-done.17.piece_ref.refs_4_), channel_id=1, source_target_pairs={{0,2},{1,3},{2,0},{3,1},{4,6},{5,7},{6,4},{7,5},{8,10},{9,11},{10,... | collective-permute-start | bytes 393224 | tf_op jit(solution)/shard_map/ppermute | solution.py:434
  64.4 3.3 %collective-permute-start.19 = (bf16[8,128,128]{2,1,0:T(8,128)(2,1)S(1)}, bf16[8,128,128]{2,1,0:T(8,128)(2,1)S(1)}, u32[]{:S(2)}, u32[]{:S(2)}) collective-permute-start(bf16[8,128,128]{2,1,0:T(8,128)(2,1)S(1)} %joined.3.refs_2_), channel_id=1, source_target_pairs={{0,1},{1,0},{2,3},{3,2},{4,5},{5,4},{6,7},{7,6},{8,9},{9,8},{10,11... | collective-permute-start | bytes 786440 | tf_op jit(solution)/shard_map/ppermute | solution.py:434
  66.3 1.3 %collective-permute-start.21 = (bf16[4,128,128]{2,1,0:T(8,128)(2,1)S(1)}, bf16[4,128,128]{2,1,0:T(8,128)(2,1)S(1)}, u32[]{:S(2)}, u32[]{:S(2)}) collective-permute-start(bf16[4,128,128]{2,1,0:T(8,128)(2,1)S(1)} %collective-permute-done.20.refs_6_), channel_id=1, source_target_pairs={{0,1},{1,0},{2,3},{3,2},{4,5},{5,4},{6,7},{7,6},{8,9},{9,8},{10,11... | collective-permute-start | bytes 393224 | tf_op jit(solution)/shard_map/ppermute | solution.py:434
  70.9 3.8 %collective-permute-start.22 = (f32[8,128,128]{2,1,0:T(8,128)S(1)}, f32[8,128,128]{2,1,0:T(8,128)S(1)}, u32[]{:S(2)}, u32[]{:S(2)}) collective-permute-start(f32[8,128,128]{2,1,0:T(8,128)S(1)} %get-tuple-element.46.amps_ref), channel_id=1, source_target_pairs={{0,1},{1,0},{2,3},{3,2},{4,5},{5,4},{6,7},{7,6},{8,9},{9,8},{10,11... | collective-permute-start | bytes 1572872 | tf_op jit(solution)/shard_map/ppermute | solution.py:434
  71.4 6.4 %collective-permute-start.23 = (bf16[2,128,128]{2,1,0:T(8,128)(2,1)S(1)}, bf16[2,128,128]{2,1,0:T(8,128)(2,1)S(1)}, u32[]{:S(2)}, u32[]{:S(2)}) collective-permute-start(bf16[2,128,128]{2,1,0:T(8,128)(2,1)S(1)} %get-tuple-element.50), channel_id=1, source_target_pairs={{0,4},{4,0},{8,12},{12,8},{1,5},{5,1},{9,13},{13,9},{2,6},{6,2},{1... | collective-permute-start | bytes 196616 | tf_op jit(solution)/shard_map/ppermute | solution.py:520
  71.4 6.4 %collective-permute-start.24 = (bf16[2,128,128]{2,1,0:T(8,128)(2,1)S(1)}, bf16[2,128,128]{2,1,0:T(8,128)(2,1)S(1)}, u32[]{:S(2)}, u32[]{:S(2)}) collective-permute-start(bf16[2,128,128]{2,1,0:T(8,128)(2,1)S(1)} %get-tuple-element.51), channel_id=1, source_target_pairs={{4,8},{8,4},{5,9},{9,5},{6,10},{10,6},{7,11},{11,7},{20,24},{24,20... | collective-permute-start | bytes 196616 | tf_op jit(solution)/shard_map/ppermute | solution.py:520
  77.8 1.5 %collective-permute-start.25 = (f32[2,128,128]{2,1,0:T(8,128)S(1)}, f32[2,128,128]{2,1,0:T(8,128)S(1)}, u32[]{:S(2)}, u32[]{:S(2)}) collective-permute-start(f32[2,128,128]{2,1,0:T(8,128)S(1)} %convert_add_fusion), channel_id=1, source_target_pairs={{0,1},{1,0},{2,3},{3,2},{4,5},{5,4},{6,7},{7,6},{8,9},{9,8},{10,11... | collective-permute-start | bytes 393224 | tf_op jit(solution)/shard_map/ppermute | solution.py:434

commit v5 on v4

--- a/solution.py
+++ b/solution.py
@@ -13,6 +13,7 @@
 VMEM = pl.BlockSpec(memory_space=pltpu.VMEM)
 SMEM = pl.BlockSpec(memory_space=pltpu.SMEM)
 ANY = pl.BlockSpec(memory_space=pl.ANY)
+HBM = pl.BlockSpec(memory_space=pltpu.HBM)
 
 
 def params(mib):
@@ -79,7 +80,7 @@
             jax.ShapeDtypeStruct(ints.shape, BF16),
             jax.ShapeDtypeStruct(shape, F32),
         ),
-        in_specs=[SMEM] * 3 + [VMEM] + [ANY] * 3,
+        in_specs=[SMEM] * 3 + [VMEM] + [HBM] * 3,
         out_specs=(VMEM,) * 4,
         scratch_shapes=[pltpu.SemaphoreType.DMA((3,))],
         compiler_params=params(8),
@@ -88,38 +89,125 @@
     )(aux, occupied, used, energy, first, second, ints)
 
 
-def product_kernel(aux_ref, own_ref, one_ref, two_ref, kept_ref, sent_ref, inner):
+def first_is_lower(here_ref, aux_ref):
+    return lax.rem(here_ref[0] + aux_ref[0], 2)
+
+
+def halves_kernel(here_ref, aux_ref, ints_ref, one_ref, two_ref, sems):
+    depth = one_ref.shape[1]
+    odd = first_is_lower(here_ref, aux_ref)
+    copies = [
+        pltpu.make_async_copy(ints_ref.at[:, pl.ds((1 - odd) * depth, depth)], one_ref, sems.at[0]),
+        pltpu.make_async_copy(ints_ref.at[:, pl.ds(odd * depth, depth)], two_ref, sems.at[1]),
+    ]
+    for copy in copies:
+        copy.start()
+    for copy in copies:
+        copy.wait()
+
+
+def halves(here, aux, ints):
+    count, depth, width = ints.shape
+    return pl.pallas_call(
+        halves_kernel,
+        out_shape=(jax.ShapeDtypeStruct((count, depth // 2, width), BF16),) * 2,
+        in_specs=[SMEM, SMEM, HBM],
+        out_specs=(VMEM, VMEM),
+        scratch_shapes=[pltpu.SemaphoreType.DMA((2,))],
+        compiler_params=params(4),
+        cost_estimate=cost(0, 4 * ints.size),
+        name="halves",
+    )(here, aux, ints)
+
+
+def product_kernel(
+    here_ref, aux_ref, own_ref, one_ref, two_ref, kept_ref, sent_ref, full_ref, inner_ref
+):
     count, _, width = own_ref.shape
+    depth = one_ref.shape[1]
+    odd = first_is_lower(here_ref, aux_ref)
     side = lax.rem(aux_ref[0], 2)
-    own = jnp.concatenate([own_ref[side], own_ref[1 - side]], axis=1)
-    at = 0
-    for near_ref in (one_ref, two_ref):
+    rows_each = count * width
+    for r, near_ref in enumerate((one_ref, two_ref)):
+        lower = odd if r == 0 else 1 - odd
+        rows = pl.ds(pl.multiple_of(lower * depth, depth), depth)
+        own = jnp.concatenate([own_ref[i, rows] for i in range(count)], axis=1)
         near = jnp.concatenate([near_ref[i] for i in range(count)], axis=1)
-        full = dot(own, near, ((0,), (0,)))
+        full_ref[...] = dot(
+            jnp.where(lower == 1, near, own), jnp.where(lower == 1, own, near), ((0,), (0,))
+        )
         for j in range(count):
             columns = slice(j * width, (j + 1) * width)
-            kept_ref[at : at + width] = full[:width, columns]
-            sent_ref[at : at + width] = full[width:, columns]
-            at += width
+            for out_ref, i in ((kept_ref, side), (sent_ref, 1 - side)):
+                at = pl.multiple_of((r ^ side) * rows_each + j * width, width)
+                out_ref[pl.ds(at, width)] = full_ref[
+                    pl.ds(pl.multiple_of(i * width, width), width), columns
+                ]
+    at = 2 * rows_each
     half = width // 2
-    inner[...] = dot(own_ref[0], own_ref[1], ((0,), (0,)))
-    kept_ref[at:] = inner[pl.ds(pl.multiple_of(side * half, half), half)]
-    sent_ref[at:] = inner[pl.ds(pl.multiple_of((1 - side) * half, half), half)]
-
-
-def products(aux, ints, one, two):
+    inner_ref[...] = dot(own_ref[0], own_ref[1], ((0,), (0,)))
+    kept_ref[at:] = inner_ref[pl.ds(pl.multiple_of(side * half, half), half)]
+    sent_ref[at:] = inner_ref[pl.ds(pl.multiple_of((1 - side) * half, half), half)]
+
+
+def products(here, aux, ints, one, two):
     count, depth, width = ints.shape
     rows = 2 * count * width + width // 2
     return pl.pallas_call(
         product_kernel,
         out_shape=(jax.ShapeDtypeStruct((rows, width), F32),) * 2,
-        in_specs=[SMEM] + [VMEM] * 3,
+        in_specs=[SMEM] * 2 + [VMEM] * 3,
         out_specs=(VMEM, VMEM),
-        scratch_shapes=[pltpu.VMEM((width, width), F32)],
+        scratch_shapes=[
+            pltpu.VMEM((count * width, count * width), F32),
+            pltpu.VMEM((width, width), F32),
+        ],
         compiler_params=params(12),
-        cost_estimate=cost(18 * depth * width * width, 12 * depth * width),
+        cost_estimate=cost(10 * depth * width * width, 8 * depth * width),
         name="products",
-    )(aux, ints, one, two)
+    )(here, aux, ints, one, two)
+
+
+def pair_kernel(kept_ref, received_ref, total_ref, one_ref, two_ref):
+    total = kept_ref[...] + received_ref[...]
+    total_ref[...] = total
+    rows = one_ref.shape[0]
+    one_ref[...] = total[:rows].astype(BF16)
+    two_ref[...] = total[rows : 2 * rows].astype(BF16)
+
+
+def pair_sum(kept, received, rows):
+    part = jax.ShapeDtypeStruct((rows, kept.shape[1]), BF16)
+    return pl.pallas_call(
+        pair_kernel,
+        out_shape=(jax.ShapeDtypeStruct(kept.shape, F32), part, part),
+        in_specs=[VMEM] * 2,
+        out_specs=(VMEM,) * 3,
+        compiler_params=params(4),
+        cost_estimate=cost(kept.size, 16 * kept.size),
+        name="pair_sum",
+    )(kept, received)
+
+
+def partner_kernel(total_ref, one_ref, two_ref, out_ref):
+    rows = one_ref.shape[0]
+    out_ref[:rows] = (total_ref[:rows] + one_ref[...].astype(F32)).astype(BF16)
+    out_ref[rows : 2 * rows] = (
+        total_ref[rows : 2 * rows] + two_ref[...].astype(F32)
+    ).astype(BF16)
+    out_ref[2 * rows :] = total_ref[2 * rows :].astype(BF16)
+
+
+def partner_sum(total, one, two):
+    return pl.pallas_call(
+        partner_kernel,
+        out_shape=jax.ShapeDtypeStruct(total.shape, BF16),
+        in_specs=[VMEM] * 3,
+        out_specs=VMEM,
+        compiler_params=params(4),
+        cost_estimate=cost(total.size, 8 * total.size),
+        name="partner_sum",
+    )(total, one, two)
 
 
 def own_part(aux_ref, low_ref, part_ref):
@@ -134,14 +222,16 @@
     count, width, _ = exch_ref.shape
     half = lax.rem(aux_ref[0], 2)
     base = here_ref[0] * 2 - 2
+    odd = lax.rem(here_ref[0], 2) == 1
     for i, total in (
         (half, total_ref[...].astype(F32) + far_ref[...].astype(F32)),
         (1 - half, total_other[...].astype(F32) + far_other[...].astype(F32)),
     ):
-        for at in range(4):
-            above = at // 2 == lax.rem(here_ref[0], 2)
-            slot = at % 2 + jnp.where(above, 4, 0)
-            table[i * 6 + slot] = total[at * width : (at + 1) * width]
+        for j in range(2):
+            one = total[j * width : (j + 1) * width]
+            two = total[(j + 2) * width : (j + 3) * width]
+            table[i * 6 + 4 + j] = jnp.where(odd, two, one)
+            table[j * 6 + i] = jnp.where(odd, one, two).T
         table[3, pl.ds(pl.multiple_of(i * (width // 2), width // 2), width // 2)] = total[4 * width :]
     table[6 + 2] = table[3].T
     for p in range(count):
@@ -435,7 +525,24 @@
 
     ints, here_s, aux_s = lax.optimization_barrier((ints, here.reshape(1), aux.reshape(1)))
 
-    near_one, near_two = (lax.ppermute(ints, "pair", pairs) for pairs in partners)
+    def both(one, two):
+        return [lax.ppermute(one, "pair", partners[0]), lax.ppermute(two, "pair", partners[1])]
+
+    def exchanged(one, two, rounds):
+        return [
+            lax.ppermute(
+                value,
+                ("pair", "aux"),
+                [
+                    (i * aux_count + a, j * aux_count + a)
+                    for a in range(aux_count)
+                    for i, j in rounds[(r + a) % 2]
+                ],
+            )
+            for r, value in enumerate((one, two))
+        ]
+
+    near_one, near_two = exchanged(*halves(here_s, aux_s, ints), partners)
     first, second, ints, factor = prepare(
         aux_s, occ_energy.T, pno_count, virt_energy, proj_first, proj_second, ints
     )
@@ -443,13 +550,13 @@
         (near_one, first, second, ints, factor)
     )
 
-    kept, sent = products(aux_s, ints, near_one, near_two)
-    total = kept + swap(sent)
+    kept, sent = products(here_s, aux_s, ints, near_one, near_two)
+    total, *sent = pair_sum(kept, swap(sent), occ_dev * width)
+    total = partner_sum(total, *both(*sent))
     step = 2
     while 2 * step < aux_count:
-        total = total + swap(total, step)
+        total = (total.astype(F32) + swap(total, step).astype(F32)).astype(BF16)
         step *= 2
-    total = total.astype(BF16)
     far = swap(total, step)
     exch, low, part = exchange(
         here_s, aux_s, orbitals, (total, far, swap(total), swap(far)), first, second, factor
@@ -493,8 +600,7 @@
         one = lax.ppermute(part, "pair", rounds[0])
         one_other = swap(one)
         cross = swap(one, 2)
-        two = (lax.ppermute(low, "pair", pairs) for pairs in rounds[1:])
-        two = joined(*two, token(one), one_other)
+        two = joined(*exchanged(low, low, rounds[1:]), token(one), one_other)
         return [low, swap(low), two, swap(two), one, one_other, cross, swap(cross)]
 
     for it in range(ITERS):
@@ -516,9 +622,7 @@
             low, part = out
     amps, terms, *sent = out
 
-    near_one, near_two = (
-        lax.ppermute(value, "pair", pairs) for value, pairs in zip(sent, partners)
-    )
+    near_one, near_two = both(*sent)
     whole, inner = first_terms(here_s, aux_s, orbitals, amps, swap(amps), first)
     density = inner + terms + near_one.astype(F32) + near_two.astype(F32)
     density = (density + swap(density)) / width

time: 80.4 us -> 77.7 us (0.966)
  waiting for transfers between devices: 28.6 us -> 16.5 us
  starting transfers between devices: 33.4 us -> 41.3 us
  local copies, waits for them, and re-layouts: 5.27 us -> 6.39 us
    ppermute x8 -> x10, waiting for transfers between devices: 17.6 us -> 6.59 us  [the longest x6 4.96 us: exchanged(): lax.ppermute(value, ('pair', 'aux'), [(i * aux_count + a, j * aux_count +...]
    ppermute x16, starting transfers between devices: 11.8 us -> 19.5 us  [swap(): return lax.ppermute(value, 'aux', [(i, i ^ step) for i in range(aux_count)])]
    unnamed x20 -> x22, local copies, waits for them, and re-layouts: 5.27 us -> 6.39 us
    ppermute x16, waiting for transfers between devices: 10.9 us -> 9.92 us  [swap(): return lax.ppermute(value, 'aux', [(i, i ^ step) for i in range(aux_count)])]
    ppermute x8 -> x10, starting transfers between devices: 21.5 us -> 21.3 us  [the longest x6 13.7 us: exchanged(): lax.ppermute(value, ('pair', 'aux'), [(i * aux_count + a, j * aux_count +...]
  transfers between devices with their start and end apart: 26 -> 28, of which waited for: 12 -> 13; matrix products, arithmetic and copies ran while one was open for 0% -> 0% of each run, Pallas kernels for 5% -> 5%
where the time goes in v5:
time: 77.7 us; the launch traced here: 77.2 us
  starting transfers between devices  41.3 us (53%)
  waiting for transfers between devices  16.5 us (21%)
  Pallas kernels  11.4 us (15%)
  local copies, waits for them, and re-layouts  6.39 us (8%)
  between operations  0.87 us (1%)
    ppermute x16, starting transfers between devices, swap(): return lax.ppermute(value, 'aux', [(i, i ^ step) for i in range(aux_count)])  19.5 us
    ppermute x6, starting transfers between devices, exchanged(): lax.ppermute(value, ('pair', 'aux'), [(i * aux_count + a, j * aux_count +...  13.7 us
    ppermute x16, waiting for transfers between devices, swap(): return lax.ppermute(value, 'aux', [(i, i ^ step) for i in range(aux_count)])  9.92 us
    ppermute x2, starting transfers between devices, both(): lax.ppermute(two, 'pair', partners[1])  7.14 us
    unnamed x22, local copies, waits for them, and re-layouts  6.39 us
    pallas_call x2, Pallas kernels, sweep(): pl.pallas_call(functools.partial(sweep_kernel, last, len(parts), rounds),...  5.14 us
    ppermute x6, waiting for transfers between devices, exchanged(): lax.ppermute(value, ('pair', 'aux'), [(i * aux_count + a, j * aux_count +...  4.96 us
    pallas_call x1, Pallas kernels, first_terms(): pl.pallas_call(first_kernel, out_shape=(jax.ShapeDtypeStruct((2 * count,...  2.97 us
  transfers between devices with their start and end apart: 28, of which 13 were waited for; matrix products, arithmetic and copies ran while one was open for 0% of the time, Pallas kernels for 5%

profile of v5, /device:TPU:15, one launch (start us, length us, event | category | flops | bytes accessed | tf_op | source)
XLA Modules:
  0.0 77.2 jit_solution(9306277957645903151)
XLA Ops:
  0.6 0.0 copy-start.1
  0.6 1.1 %copy-done.1 = bf16[2,1536,128]{2,1,0:T(8,128)(2,1)S(1)} copy-done((bf16[2,1536,128]{2,1,0:T(8,128)(2,1)S(1)}, bf16[2,1536,128]{2,1,0:T(8,128)(2,1)}, u32[]{:S(2)}) %copy-start.1) | copy-done | bytes 786456
  1.8 0.2 halves.1
  2.0 3.2 %collective-permute-start = (bf16[2,768,128]{2,1,0:T(8,128)(2,1)S(1)}, bf16[2,768,128]{2,1,0:T(8,128)(2,1)S(1)}, u32[]{:S(2)}, u32[]{:S(2)}) collective-permute-start(bf16[2,768,128]{2,1,0:T(8,128)(2,1)S(1)} %get-tuple-element.35), channel_id=1, source_target_pairs={{0,4},{4,0},{8,12},{12,8},{5,9},{9,5},{2,6},{6,2},{10,14},{14,10},... | collective-permute-start | bytes 1179656 | tf_op jit(solution)/shard_map/ppermute | solution.py:533
  5.2 1.9 %collective-permute-start.1 = (bf16[2,768,128]{2,1,0:T(8,128)(2,1)S(1)}, bf16[2,768,128]{2,1,0:T(8,128)(2,1)S(1)}, u32[]{:S(2)}, u32[]{:S(2)}) collective-permute-start(bf16[2,768,128]{2,1,0:T(8,128)(2,1)S(1)} %get-tuple-element.42), channel_id=1, source_target_pairs={{4,8},{8,4},{1,5},{5,1},{9,13},{13,9},{6,10},{10,6},{3,7},{7,3},{1... | collective-permute-start | bytes 1179656 | tf_op jit(solution)/shard_map/ppermute | solution.py:533
  7.1 0.0 copy-start.2
  7.2 1.1 %copy-done.2 = bf16[2,1536,128]{2,1,0:T(8,128)(2,1)S(1)} copy-done((bf16[2,1536,128]{2,1,0:T(8,128)(2,1)S(1)}, bf16[2,1536,128]{2,1,0:T(8,128)(2,1)}, u32[]{:S(2)}) %copy-start.2) | copy-done | bytes 786456
  8.3 1.0 %copy-done.3 = bf16[16,128,128]{2,1,0:T(8,128)(2,1)S(1)} copy-done((bf16[16,128,128]{2,1,0:T(8,128)(2,1)S(1)}, bf16[16,128,128]{2,1,0:T(8,128)(2,1)}, u32[]{:S(2)}) %copy-start.3) | copy-done | bytes 524312
  9.3 1.0 %copy-done.4 = bf16[16,128,128]{2,1,0:T(8,128)(2,1)S(1)} copy-done((bf16[16,128,128]{2,1,0:T(8,128)(2,1)S(1)}, bf16[16,128,128]{2,1,0:T(8,128)(2,1)}, u32[]{:S(2)}) %copy-start.4) | copy-done | bytes 524312
  10.4 0.7 copy-done.6
  11.1 0.7 copy-done.9
  11.7 0.7 copy-done.10
  12.4 0.9 %prepare.1 = (bf16[8,128,128]{2,1,0:T(8,128)(2,1)S(1)}, bf16[8,128,128]{2,1,0:T(8,128)(2,1)S(1)}, bf16[2,1536,128]{2,1,0:T(8,128)(2,1)S(1)}, f32[8,128,128]{2,1,0:T(8,128)S(1)}) custom-call(s32[1]{0:T(128)} %bitcast.1.aux_ref, f32[2,16]{1,0:T(2,128)S(1)} %bitcast.14, s32[16]{0:T(128)S(1)} %copy-done.10, f32[16,128]{1,0:T(8,128)S(1)} %copy-done.6, ...), custom_call_target="tpu_custom_call" | custom-call | bytes 2097152 | tf_op jit(solution)/shard_map/prepare/pallas_call | solution.py:75
  13.3 0.0 collective-permute-done.one_ref
  13.3 2.6 %collective-permute-done.1.two_ref = bf16[2,768,128]{2,1,0:T(8,128)(2,1)S(1)} collective-permute-done((bf16[2,768,128]{2,1,0:T(8,128)(2,1)S(1)}, bf16[2,768,128]{2,1,0:T(8,128)(2,1)S(1)}, u32[]{:S(2)}, u32[]{:S(2)}) %collective-permute-start.1) | collective-permute-done | bytes 393248 | tf_op jit(solution)/shard_map/ppermute | solution.py:533
  15.9 0.6 products.1
  16.5 0.1 collective-permute-start.2
  16.6 1.6 %collective-permute-done.2.received_ref = f32[576,128]{1,0:T(8,128)S(1)} collective-permute-done((f32[576,128]{1,0:T(8,128)S(1)}, f32[576,128]{1,0:T(8,128)S(1)}, u32[]{:S(2)}, u32[]{:S(2)}) %collective-permute-start.2) | collective-permute-done | bytes 294944 | tf_op jit(solution)/shard_map/ppermute | solution.py:524
  18.2 0.2 collective-permute-start.3
  18.4 4.3 %collective-permute-start.4 = (bf16[256,128]{1,0:T(8,128)(2,1)S(1)}, bf16[256,128]{1,0:T(8,128)(2,1)S(1)}, u32[]{:S(2)}, u32[]{:S(2)}) collective-permute-start(bf16[256,128]{1,0:T(8,128)(2,1)S(1)} %get-tuple-element.47), channel_id=1, source_target_pairs={{4,8},{8,4},{5,9},{9,5},{6,10},{10,6},{7,11},{11,7},{20,24},{24,20... | collective-permute-start | bytes 196616 | tf_op jit(solution)/shard_map/ppermute | solution.py:529
  22.7 0.0 collective-permute-done.3.one_ref
  22.7 1.6 %collective-permute-done.4.two_ref = bf16[256,128]{1,0:T(8,128)(2,1)S(1)} collective-permute-done((bf16[256,128]{1,0:T(8,128)(2,1)S(1)}, bf16[256,128]{1,0:T(8,128)(2,1)S(1)}, u32[]{:S(2)}, u32[]{:S(2)}) %collective-permute-start.4) | collective-permute-done | bytes 65568 | tf_op jit(solution)/shard_map/ppermute | solution.py:529
  24.4 0.3 collective-permute-start.5
  24.7 1.8 %collective-permute-start.6 = (bf16[576,128]{1,0:T(8,128)(2,1)S(1)}, bf16[576,128]{1,0:T(8,128)(2,1)S(1)}, u32[]{:S(2)}, u32[]{:S(2)}) collective-permute-start(bf16[576,128]{1,0:T(8,128)(2,1)S(1)} %partner_sum.1.total_ref), channel_id=1, source_target_pairs={{0,1},{1,0},{2,3},{3,2},{4,5},{5,4},{6,7},{7,6},{8,9},{9,8},{10,11... | collective-permute-start | bytes 442376 | tf_op jit(solution)/shard_map/ppermute | solution.py:524
  26.5 1.9 %collective-permute-done.5.far_ref = bf16[576,128]{1,0:T(8,128)(2,1)S(1)} collective-permute-done((bf16[576,128]{1,0:T(8,128)(2,1)S(1)}, bf16[576,128]{1,0:T(8,128)(2,1)S(1)}, u32[]{:S(2)}, u32[]{:S(2)}) %collective-permute-start.5) | collective-permute-done | bytes 147488 | tf_op jit(solution)/shard_map/ppermute | solution.py:524
  28.4 2.7 %collective-permute-start.7 = (bf16[576,128]{1,0:T(8,128)(2,1)S(1)}, bf16[576,128]{1,0:T(8,128)(2,1)S(1)}, u32[]{:S(2)}, u32[]{:S(2)}) collective-permute-start(bf16[576,128]{1,0:T(8,128)(2,1)S(1)} %collective-permute-done.5.far_ref), channel_id=1, source_target_pairs={{0,1},{1,0},{2,3},{3,2},{4,5},{5,4},{6,7},{7,6},{8,9},{9,8},{10,11... | collective-permute-start | bytes 442376 | tf_op jit(solution)/shard_map/ppermute | solution.py:524
  31.1 1.0 %collective-permute-done.7.far_other = bf16[576,128]{1,0:T(8,128)(2,1)S(1)} collective-permute-done((bf16[576,128]{1,0:T(8,128)(2,1)S(1)}, bf16[576,128]{1,0:T(8,128)(2,1)S(1)}, u32[]{:S(2)}, u32[]{:S(2)}) %collective-permute-start.7) | collective-permute-done | bytes 147488 | tf_op jit(solution)/shard_map/ppermute | solution.py:524
  32.1 1.4 %exchange.1 = (f32[8,128,128]{2,1,0:T(8,128)S(1)}, bf16[8,128,128]{2,1,0:T(8,128)(2,1)S(1)}, bf16[4,128,128]{2,1,0:T(8,128)(2,1)S(1)}) custom-call(s32[1]{0:T(128)} %bitcast.here_ref, s32[1]{0:T(128)} %bitcast.1.aux_ref, s32[2,16]{1,0:T(2,128)S(1)} %bitcast.6, bf16[576,128]{1,0:T(8,128)(2,1)S(1)} %partner_sum.1.total_ref, ...), custom_call_target="tpu_custom_call" | custom-call | flops 134217728 | bytes 2621440 | tf_op jit(solution)/shard_map/exchange/pallas_call | solution.py:262
  33.5 0.1 collective-permute-start.11
  33.5 0.0 copy-start.7
  33.6 0.0 copy-start.8
  33.6 3.6 %collective-permute-start.10 = (bf16[8,128,128]{2,1,0:T(8,128)(2,1)S(1)}, bf16[8,128,128]{2,1,0:T(8,128)(2,1)S(1)}, u32[]{:S(2)}, u32[]{:S(2)}) collective-permute-start(bf16[8,128,128]{2,1,0:T(8,128)(2,1)S(1)} %get-tuple-element.51.refs_0_), channel_id=1, source_target_pairs={{4,0},{8,12},{5,9},{9,5},{6,2},{10,14},{7,11},{11,7},{20,16},{24,2... | collective-permute-start | bytes 786440 | tf_op jit(solution)/shard_map/ppermute | solution.py:533
  37.2 1.3 %collective-permute-start.9 = (bf16[8,128,128]{2,1,0:T(8,128)(2,1)S(1)}, bf16[8,128,128]{2,1,0:T(8,128)(2,1)S(1)}, u32[]{:S(2)}, u32[]{:S(2)}) collective-permute-start(bf16[8,128,128]{2,1,0:T(8,128)(2,1)S(1)} %get-tuple-element.51.refs_0_), channel_id=1, source_target_pairs={{4,8},{8,4},{5,1},{9,13},{6,10},{10,6},{7,3},{11,15},{20,24},{24,2... | collective-permute-start | bytes 786440 | tf_op jit(solution)/shard_map/ppermute | solution.py:533
  38.5 3.4 %collective-permute-start.8 = (bf16[8,128,128]{2,1,0:T(8,128)(2,1)S(1)}, bf16[8,128,128]{2,1,0:T(8,128)(2,1)S(1)}, u32[]{:S(2)}, u32[]{:S(2)}) collective-permute-start(bf16[8,128,128]{2,1,0:T(8,128)(2,1)S(1)} %get-tuple-element.51.refs_0_), channel_id=1, source_target_pairs={{0,1},{1,0},{2,3},{3,2},{4,5},{5,4},{6,7},{7,6},{8,9},{9,8},{10,11... | collective-permute-start | bytes 786440 | tf_op jit(solution)/shard_map/ppermute | solution.py:524
  42.0 0.1 collective-permute-start.12
  42.1 0.2 collective-permute-start.14
  42.3 1.0 %collective-permute-done.12.piece_ref.refs_5_ = bf16[4,128,128]{2,1,0:T(8,128)(2,1)S(1)} collective-permute-done((bf16[4,128,128]{2,1,0:T(8,128)(2,1)S(1)}, bf16[4,128,128]{2,1,0:T(8,128)(2,1)S(1)}, u32[]{:S(2)}, u32[]{:S(2)}) %collective-permute-start.12) | collective-permute-done | bytes 131104 | tf_op jit(solution)/shard_map/ppermute | solution.py:524
  43.3 1.0 %collective-permute-done.9.left_ref = bf16[8,128,128]{2,1,0:T(8,128)(2,1)S(1)} collective-permute-done((bf16[8,128,128]{2,1,0:T(8,128)(2,1)S(1)}, bf16[8,128,128]{2,1,0:T(8,128)(2,1)S(1)}, u32[]{:S(2)}, u32[]{:S(2)}) %collective-permute-start.9) | collective-permute-done | bytes 262176 | tf_op jit(solution)/shard_map/ppermute | solution.py:533
  44.3 0.1 joined.2.refs_2_
  44.4 2.0 %collective-permute-start.13 = (bf16[8,128,128]{2,1,0:T(8,128)(2,1)S(1)}, bf16[8,128,128]{2,1,0:T(8,128)(2,1)S(1)}, u32[]{:S(2)}, u32[]{:S(2)}) collective-permute-start(bf16[8,128,128]{2,1,0:T(8,128)(2,1)S(1)} %joined.2.refs_2_), channel_id=1, source_target_pairs={{0,1},{1,0},{2,3},{3,2},{4,5},{5,4},{6,7},{7,6},{8,9},{9,8},{10,11... | collective-permute-start | bytes 786440 | tf_op jit(solution)/shard_map/ppermute | solution.py:524
  46.4 0.3 collective-permute-done.14.refs_6_
  46.7 1.3 %collective-permute-start.15 = (bf16[4,128,128]{2,1,0:T(8,128)(2,1)S(1)}, bf16[4,128,128]{2,1,0:T(8,128)(2,1)S(1)}, u32[]{:S(2)}, u32[]{:S(2)}) collective-permute-start(bf16[4,128,128]{2,1,0:T(8,128)(2,1)S(1)} %collective-permute-done.14.refs_6_), channel_id=1, source_target_pairs={{0,1},{1,0},{2,3},{3,2},{4,5},{5,4},{6,7},{7,6},{8,9},{9,8},{10,11... | collective-permute-start | bytes 393224 | tf_op jit(solution)/shard_map/ppermute | solution.py:524
  48.0 1.0 %collective-permute-done.15.refs_7_ = bf16[4,128,128]{2,1,0:T(8,128)(2,1)S(1)} collective-permute-done((bf16[4,128,128]{2,1,0:T(8,128)(2,1)S(1)}, bf16[4,128,128]{2,1,0:T(8,128)(2,1)S(1)}, u32[]{:S(2)}, u32[]{:S(2)}) %collective-permute-start.15) | collective-permute-done | bytes 131104 | tf_op jit(solution)/shard_map/ppermute | solution.py:524
  49.0 1.9 %sweep.1 = (bf16[8,128,128]{2,1,0:T(8,128)(2,1)S(1)}, bf16[4,128,128]{2,1,0:T(8,128)(2,1)S(1)}) custom-call(s32[1]{0:T(128)} %bitcast.here_ref, s32[1]{0:T(128)} %bitcast.1.aux_ref, s32[2,16]{1,0:T(2,128)S(1)} %bitcast.7, s32[4,64]{1,0:T(4,128)S(1)} %bitcast.10, f32[4,16]{1,0:T(4,128)S(1)} %bitcast.12, bf16[8,128,128]{2,1,0:T(8,128)(2,1)S(1)} %get-tuple-element.51.refs_0_, ...), custom_call_target="tpu_custom_call" | custom-call | flops 268435456 | bytes 2883584 | tf_op jit(solution)/shard_map/sweep/pallas_call | solution.py:378
  50.9 0.5 collective-permute-start.19
  51.3 2.1 %collective-permute-start.18 = (bf16[8,128,128]{2,1,0:T(8,128)(2,1)S(1)}, bf16[8,128,128]{2,1,0:T(8,128)(2,1)S(1)}, u32[]{:S(2)}, u32[]{:S(2)}) collective-permute-start(bf16[8,128,128]{2,1,0:T(8,128)(2,1)S(1)} %get-tuple-element.54.refs_0_), channel_id=1, source_target_pairs={{4,0},{8,12},{5,9},{9,5},{6,2},{10,14},{7,11},{11,7},{20,16},{24,2... | collective-permute-start | bytes 786440 | tf_op jit(solution)/shard_map/ppermute | solution.py:533
  53.4 1.6 %collective-permute-start.17 = (bf16[8,128,128]{2,1,0:T(8,128)(2,1)S(1)}, bf16[8,128,128]{2,1,0:T(8,128)(2,1)S(1)}, u32[]{:S(2)}, u32[]{:S(2)}) collective-permute-start(bf16[8,128,128]{2,1,0:T(8,128)(2,1)S(1)} %get-tuple-element.54.refs_0_), channel_id=1, source_target_pairs={{4,8},{8,4},{5,1},{9,13},{6,10},{10,6},{7,3},{11,15},{20,24},{24,2... | collective-permute-start | bytes 786440 | tf_op jit(solution)/shard_map/ppermute | solution.py:533
  55.0 3.0 %collective-permute-start.16 = (bf16[8,128,128]{2,1,0:T(8,128)(2,1)S(1)}, bf16[8,128,128]{2,1,0:T(8,128)(2,1)S(1)}, u32[]{:S(2)}, u32[]{:S(2)}) collective-permute-start(bf16[8,128,128]{2,1,0:T(8,128)(2,1)S(1)} %get-tuple-element.54.refs_0_), channel_id=1, source_target_pairs={{0,1},{1,0},{2,3},{3,2},{4,5},{5,4},{6,7},{7,6},{8,9},{9,8},{10,11... | collective-permute-start | bytes 786440 | tf_op jit(solution)/shard_map/ppermute | solution.py:524
  58.0 0.1 collective-permute-start.20
  58.1 0.2 collective-permute-start.22
  58.3 1.1 %collective-permute-done.20.piece_ref.refs_5_ = bf16[4,128,128]{2,1,0:T(8,128)(2,1)S(1)} collective-permute-done((bf16[4,128,128]{2,1,0:T(8,128)(2,1)S(1)}, bf16[4,128,128]{2,1,0:T(8,128)(2,1)S(1)}, u32[]{:S(2)}, u32[]{:S(2)}) %collective-permute-start.20) | collective-permute-done | bytes 131104 | tf_op jit(solution)/shard_map/ppermute | solution.py:524
  59.4 1.4 %collective-permute-done.17.left_ref = bf16[8,128,128]{2,1,0:T(8,128)(2,1)S(1)} collective-permute-done((bf16[8,128,128]{2,1,0:T(8,128)(2,1)S(1)}, bf16[8,128,128]{2,1,0:T(8,128)(2,1)S(1)}, u32[]{:S(2)}, u32[]{:S(2)}) %collective-permute-start.17) | collective-permute-done | bytes 262176 | tf_op jit(solution)/shard_map/ppermute | solution.py:533
  60.7 0.1 joined.3.refs_2_
  60.8 2.8 %collective-permute-start.21 = (bf16[8,128,128]{2,1,0:T(8,128)(2,1)S(1)}, bf16[8,128,128]{2,1,0:T(8,128)(2,1)S(1)}, u32[]{:S(2)}, u32[]{:S(2)}) collective-permute-start(bf16[8,128,128]{2,1,0:T(8,128)(2,1)S(1)} %joined.3.refs_2_), channel_id=1, source_target_pairs={{0,1},{1,0},{2,3},{3,2},{4,5},{5,4},{6,7},{7,6},{8,9},{9,8},{10,11... | collective-permute-start | bytes 786440 | tf_op jit(solution)/shard_map/ppermute | solution.py:524
  63.6 0.4 collective-permute-start.23
  64.0 1.0 %collective-permute-done.23.refs_7_ = bf16[4,128,128]{2,1,0:T(8,128)(2,1)S(1)} collective-permute-done((bf16[4,128,128]{2,1,0:T(8,128)(2,1)S(1)}, bf16[4,128,128]{2,1,0:T(8,128)(2,1)S(1)}, u32[]{:S(2)}, u32[]{:S(2)}) %collective-permute-start.23) | collective-permute-done | bytes 131104 | tf_op jit(solution)/shard_map/ppermute | solution.py:524
  65.0 3.2 %last_sweep.1 = (f32[8,128,128]{2,1,0:T(8,128)S(1)}, f32[2,128,128]{2,1,0:T(8,128)S(1)}, bf16[2,128,128]{2,1,0:T(8,128)(2,1)S(1)}, bf16[2,128,128]{2,1,0:T(8,128)(2,1)S(1)}) custom-call(s32[1]{0:T(128)} %bitcast.here_ref, s32[1]{0:T(128)} %bitcast.1.aux_ref, s32[2,16]{1,0:T(2,128)S(1)} %bitcast.8, s32[4,64]{1,0:T(4,128)S(1)} %bitcast.11, ...), custom_call_target="tpu_custom_call" | custom-call | flops 268435456 | bytes 2883584 | tf_op jit(solution)/shard_map/last_sweep/pallas_call | solution.py:378
  68.2 0.4 collective-permute-start.24
  68.7 0.2 collective-permute-start.25
  68.9 2.8 %collective-permute-start.26 = (bf16[2,128,128]{2,1,0:T(8,128)(2,1)S(1)}, bf16[2,128,128]{2,1,0:T(8,128)(2,1)S(1)}, u32[]{:S(2)}, u32[]{:S(2)}) collective-permute-start(bf16[2,128,128]{2,1,0:T(8,128)(2,1)S(1)} %get-tuple-element.61), channel_id=1, source_target_pairs={{4,8},{8,4},{5,9},{9,5},{6,10},{10,6},{7,11},{11,7},{20,24},{24,20... | collective-permute-start | bytes 196616 | tf_op jit(solution)/shard_map/ppermute | solution.py:529
  71.7 3.0 %first_terms.1 = (f32[16,128,128]{2,1,0:T(8,128)}, f32[2,128,128]{2,1,0:T(8,128)S(1)}) custom-call(s32[1]{0:T(128)} %bitcast.here_ref, s32[1]{0:T(128)} %bitcast.1.aux_ref, s32[2,16]{1,0:T(2,128)S(1)} %bitcast.9, f32[8,128,128]{2,1,0:T(8,128)S(1)} %get-tuple-element.56.amps_ref, f32[8,128,128]{2,1,0:T(8,128)S(1)} %collective-permute-done.24.others_ref, ...), custom_call_target="tpu_custom_call" | custom-call | flops 201326592 | bytes 2097152 | tf_op jit(solution)/shard_map/first_terms/pallas_call | solution.py:454
  74.8 0.8 %collective-permute-start.27 = (f32[2,128,128]{2,1,0:T(8,128)S(1)}, f32[2,128,128]{2,1,0:T(8,128)S(1)}, u32[]{:S(2)}, u32[]{:S(2)}) collective-permute-start(f32[2,128,128]{2,1,0:T(8,128)S(1)} %convert_add_fusion), channel_id=1, source_target_pairs={{0,1},{1,0},{2,3},{3,2},{4,5},{5,4},{6,7},{7,6},{8,9},{9,8},{10,11... | collective-permute-start | bytes 393224 | tf_op jit(solution)/shard_map/ppermute | solution.py:524
  75.5 1.0 %collective-permute-done.27 = f32[2,128,128]{2,1,0:T(8,128)S(1)} collective-permute-done((f32[2,128,128]{2,1,0:T(8,128)S(1)}, f32[2,128,128]{2,1,0:T(8,128)S(1)}, u32[]{:S(2)}, u32[]{:S(2)}) %collective-permute-start.27) | collective-permute-done | bytes 131104 | tf_op jit(solution)/shard_map/ppermute | solution.py:524
  76.5 0.7 add_multiply_fusion
  (29 shorter events, 0.2 us)
Async XLA Ops:
  0.6 1.1 %copy-start.1 = (bf16[2,1536,128]{2,1,0:T(8,128)(2,1)S(1)}, bf16[2,1536,128]{2,1,0:T(8,128)(2,1)}, u32[]{:S(2)}) copy-start(bf16[2,1536,128]{2,1,0:T(8,128)(2,1)} %ints_ref.1) | copy-start | bytes 2359300
  2.0 11.3 %collective-permute-start = (bf16[2,768,128]{2,1,0:T(8,128)(2,1)S(1)}, bf16[2,768,128]{2,1,0:T(8,128)(2,1)S(1)}, u32[]{:S(2)}, u32[]{:S(2)}) collective-permute-start(bf16[2,768,128]{2,1,0:T(8,128)(2,1)S(1)} %get-tuple-element.35), channel_id=1, source_target_pairs={{0,4},{4,0},{8,12},{12,8},{5,9},{9,5},{2,6},{6,2},{10,14},{14,10},... | collective-permute-start | bytes 1179656 | tf_op jit(solution)/shard_map/ppermute | solution.py:533
  5.2 10.7 %collective-permute-start.1 = (bf16[2,768,128]{2,1,0:T(8,128)(2,1)S(1)}, bf16[2,768,128]{2,1,0:T(8,128)(2,1)S(1)}, u32[]{:S(2)}, u32[]{:S(2)}) collective-permute-start(bf16[2,768,128]{2,1,0:T(8,128)(2,1)S(1)} %get-tuple-element.42), channel_id=1, source_target_pairs={{4,8},{8,4},{1,5},{5,1},{9,13},{13,9},{6,10},{10,6},{3,7},{7,3},{1... | collective-permute-start | bytes 1179656 | tf_op jit(solution)/shard_map/ppermute | solution.py:533
  7.1 1.1 %copy-start.2 = (bf16[2,1536,128]{2,1,0:T(8,128)(2,1)S(1)}, bf16[2,1536,128]{2,1,0:T(8,128)(2,1)}, u32[]{:S(2)}) copy-start(bf16[2,1536,128]{2,1,0:T(8,128)(2,1)} %ints_ref.1) | copy-start | bytes 2359300
  8.3 1.0 %copy-start.3 = (bf16[16,128,128]{2,1,0:T(8,128)(2,1)S(1)}, bf16[16,128,128]{2,1,0:T(8,128)(2,1)}, u32[]{:S(2)}) copy-start(bf16[16,128,128]{2,1,0:T(8,128)(2,1)} %first_ref.1) | copy-start | bytes 1572868
  9.3 1.0 %copy-start.4 = (bf16[16,128,128]{2,1,0:T(8,128)(2,1)S(1)}, bf16[16,128,128]{2,1,0:T(8,128)(2,1)}, u32[]{:S(2)}) copy-start(bf16[16,128,128]{2,1,0:T(8,128)(2,1)} %second_ref.1) | copy-start | bytes 1572868
  10.4 0.7 copy-start.6
  11.1 0.7 copy-start.9
  11.7 0.7 copy-start.10
  12.4 19.7 %copy-start.5 = (s32[16,2]{0,1:T(2,128)S(1)}, s32[16,2]{0,1:T(2,128)}, u32[]{:S(2)}) copy-start(s32[16,2]{0,1:T(2,128)} %param.18) | copy-start | bytes 388
  16.5 1.6 %collective-permute-start.2 = (f32[576,128]{1,0:T(8,128)S(1)}, f32[576,128]{1,0:T(8,128)S(1)}, u32[]{:S(2)}, u32[]{:S(2)}) collective-permute-start(f32[576,128]{1,0:T(8,128)S(1)} %get-tuple-element.44), channel_id=1, source_target_pairs={{0,1},{1,0},{2,3},{3,2},{4,5},{5,4},{6,7},{7,6},{8,9},{9,8},{10,11... | collective-permute-start | bytes 884744 | tf_op jit(solution)/shard_map/ppermute | solution.py:524
  18.2 4.5 %collective-permute-start.3 = (bf16[256,128]{1,0:T(8,128)(2,1)S(1)}, bf16[256,128]{1,0:T(8,128)(2,1)S(1)}, u32[]{:S(2)}, u32[]{:S(2)}) collective-permute-start(bf16[256,128]{1,0:T(8,128)(2,1)S(1)} %get-tuple-element.46), channel_id=1, source_target_pairs={{0,4},{4,0},{8,12},{12,8},{1,5},{5,1},{9,13},{13,9},{2,6},{6,2},{1... | collective-permute-start | bytes 196616 | tf_op jit(solution)/shard_map/ppermute | solution.py:529
  18.4 6.0 %collective-permute-start.4 = (bf16[256,128]{1,0:T(8,128)(2,1)S(1)}, bf16[256,128]{1,0:T(8,128)(2,1)S(1)}, u32[]{:S(2)}, u32[]{:S(2)}) collective-permute-start(bf16[256,128]{1,0:T(8,128)(2,1)S(1)} %get-tuple-element.47), channel_id=1, source_target_pairs={{4,8},{8,4},{5,9},{9,5},{6,10},{10,6},{7,11},{11,7},{20,24},{24,20... | collective-permute-start | bytes 196616 | tf_op jit(solution)/shard_map/ppermute | solution.py:529
  24.4 4.1 %collective-permute-start.5 = (bf16[576,128]{1,0:T(8,128)(2,1)S(1)}, bf16[576,128]{1,0:T(8,128)(2,1)S(1)}, u32[]{:S(2)}, u32[]{:S(2)}) collective-permute-start(bf16[576,128]{1,0:T(8,128)(2,1)S(1)} %partner_sum.1.total_ref), channel_id=1, source_target_pairs={{0,2},{1,3},{2,0},{3,1},{4,6},{5,7},{6,4},{7,5},{8,10},{9,11},{10,... | collective-permute-start | bytes 442376 | tf_op jit(solution)/shard_map/ppermute | solution.py:524
  24.7 6.4 %collective-permute-start.6 = (bf16[576,128]{1,0:T(8,128)(2,1)S(1)}, bf16[576,128]{1,0:T(8,128)(2,1)S(1)}, u32[]{:S(2)}, u32[]{:S(2)}) collective-permute-start(bf16[576,128]{1,0:T(8,128)(2,1)S(1)} %partner_sum.1.total_ref), channel_id=1, source_target_pairs={{0,1},{1,0},{2,3},{3,2},{4,5},{5,4},{6,7},{7,6},{8,9},{9,8},{10,11... | collective-permute-start | bytes 442376 | tf_op jit(solution)/shard_map/ppermute | solution.py:524
  28.4 3.7 %collective-permute-start.7 = (bf16[576,128]{1,0:T(8,128)(2,1)S(1)}, bf16[576,128]{1,0:T(8,128)(2,1)S(1)}, u32[]{:S(2)}, u32[]{:S(2)}) collective-permute-start(bf16[576,128]{1,0:T(8,128)(2,1)S(1)} %collective-permute-done.5.far_ref), channel_id=1, source_target_pairs={{0,1},{1,0},{2,3},{3,2},{4,5},{5,4},{6,7},{7,6},{8,9},{9,8},{10,11... | collective-permute-start | bytes 442376 | tf_op jit(solution)/shard_map/ppermute | solution.py:524
  33.5 8.5 %collective-permute-start.11 = (bf16[4,128,128]{2,1,0:T(8,128)(2,1)S(1)}, bf16[4,128,128]{2,1,0:T(8,128)(2,1)S(1)}, u32[]{:S(2)}, u32[]{:S(2)}) collective-permute-start(bf16[4,128,128]{2,1,0:T(8,128)(2,1)S(1)} %get-tuple-element.52), channel_id=1, source_target_pairs={{4,12},{8,0},{0,4},{12,8},{5,13},{9,1},{1,5},{13,9},{6,14},{10,2},... | collective-permute-start | bytes 393224 | tf_op jit(solution)/shard_map/ppermute | solution.py:600
  33.5 15.4 %copy-start.7 = (s32[64,4]{0,1:T(4,128)S(1)}, s32[64,4]{0,1:T(4,128)}, u32[]{:S(2)}) copy-start(s32[64,4]{0,1:T(4,128)} %param.19) | copy-start | bytes 3076
  33.6 15.4 %copy-start.8 = (f32[16,4]{0,1:T(4,128)S(1)}, f32[16,4]{0,1:T(4,128)}, u32[]{:S(2)}) copy-start(f32[16,4]{0,1:T(4,128)} %param.14) | copy-start | bytes 772
  33.6 9.8 %collective-permute-start.10 = (bf16[8,128,128]{2,1,0:T(8,128)(2,1)S(1)}, bf16[8,128,128]{2,1,0:T(8,128)(2,1)S(1)}, u32[]{:S(2)}, u32[]{:S(2)}) collective-permute-start(bf16[8,128,128]{2,1,0:T(8,128)(2,1)S(1)} %get-tuple-element.51.refs_0_), channel_id=1, source_target_pairs={{4,0},{8,12},{5,9},{9,5},{6,2},{10,14},{7,11},{11,7},{20,16},{24,2... | collective-permute-start | bytes 786440 | tf_op jit(solution)/shard_map/ppermute | solution.py:533
  37.2 7.1 %collective-permute-start.9 = (bf16[8,128,128]{2,1,0:T(8,128)(2,1)S(1)}, bf16[8,128,128]{2,1,0:T(8,128)(2,1)S(1)}, u32[]{:S(2)}, u32[]{:S(2)}) collective-permute-start(bf16[8,128,128]{2,1,0:T(8,128)(2,1)S(1)} %get-tuple-element.51.refs_0_), channel_id=1, source_target_pairs={{4,8},{8,4},{5,1},{9,13},{6,10},{10,6},{7,3},{11,15},{20,24},{24,2... | collective-permute-start | bytes 786440 | tf_op jit(solution)/shard_map/ppermute | solution.py:533
  38.5 9.4 %collective-permute-start.8 = (bf16[8,128,128]{2,1,0:T(8,128)(2,1)S(1)}, bf16[8,128,128]{2,1,0:T(8,128)(2,1)S(1)}, u32[]{:S(2)}, u32[]{:S(2)}) collective-permute-start(bf16[8,128,128]{2,1,0:T(8,128)(2,1)S(1)} %get-tuple-element.51.refs_0_), channel_id=1, source_target_pairs={{0,1},{1,0},{2,3},{3,2},{4,5},{5,4},{6,7},{7,6},{8,9},{9,8},{10,11... | collective-permute-start | bytes 786440 | tf_op jit(solution)/shard_map/ppermute | solution.py:524
  42.0 1.3 %collective-permute-start.12 = (bf16[4,128,128]{2,1,0:T(8,128)(2,1)S(1)}, bf16[4,128,128]{2,1,0:T(8,128)(2,1)S(1)}, u32[]{:S(2)}, u32[]{:S(2)}) collective-permute-start(bf16[4,128,128]{2,1,0:T(8,128)(2,1)S(1)} %collective-permute-done.11.piece_ref.refs_4_), channel_id=1, source_target_pairs={{0,1},{1,0},{2,3},{3,2},{4,5},{5,4},{6,7},{7,6},{8,9},{9,8},{10,11... | collective-permute-start | bytes 393224 | tf_op jit(solution)/shard_map/ppermute | solution.py:524
  42.1 6.9 %copy-start = (bf16[16,4,128,128]{3,2,1,0:T(8,128)(2,1)S(1)}, bf16[16,4,128,128]{3,2,1,0:T(8,128)(2,1)}, u32[]{:S(2)}) copy-start(bf16[16,4,128,128]{3,2,1,0:T(8,128)(2,1)} %refs_8_.3) | copy-start | bytes 6291460
  42.1 4.6 %collective-permute-start.14 = (bf16[4,128,128]{2,1,0:T(8,128)(2,1)S(1)}, bf16[4,128,128]{2,1,0:T(8,128)(2,1)S(1)}, u32[]{:S(2)}, u32[]{:S(2)}) collective-permute-start(bf16[4,128,128]{2,1,0:T(8,128)(2,1)S(1)} %collective-permute-done.11.piece_ref.refs_4_), channel_id=1, source_target_pairs={{0,2},{1,3},{2,0},{3,1},{4,6},{5,7},{6,4},{7,5},{8,10},{9,11},{10,... | collective-permute-start | bytes 393224 | tf_op jit(solution)/shard_map/ppermute | solution.py:524
  44.4 4.6 %collective-permute-start.13 = (bf16[8,128,128]{2,1,0:T(8,128)(2,1)S(1)}, bf16[8,128,128]{2,1,0:T(8,128)(2,1)S(1)}, u32[]{:S(2)}, u32[]{:S(2)}) collective-permute-start(bf16[8,128,128]{2,1,0:T(8,128)(2,1)S(1)} %joined.2.refs_2_), channel_id=1, source_target_pairs={{0,1},{1,0},{2,3},{3,2},{4,5},{5,4},{6,7},{7,6},{8,9},{9,8},{10,11... | collective-permute-start | bytes 786440 | tf_op jit(solution)/shard_map/ppermute | solution.py:524
  46.7 2.3 %collective-permute-start.15 = (bf16[4,128,128]{2,1,0:T(8,128)(2,1)S(1)}, bf16[4,128,128]{2,1,0:T(8,128)(2,1)S(1)}, u32[]{:S(2)}, u32[]{:S(2)}) collective-permute-start(bf16[4,128,128]{2,1,0:T(8,128)(2,1)S(1)} %collective-permute-done.14.refs_6_), channel_id=1, source_target_pairs={{0,1},{1,0},{2,3},{3,2},{4,5},{5,4},{6,7},{7,6},{8,9},{9,8},{10,11... | collective-permute-start | bytes 393224 | tf_op jit(solution)/shard_map/ppermute | solution.py:524
  50.9 7.1 %collective-permute-start.19 = (bf16[4,128,128]{2,1,0:T(8,128)(2,1)S(1)}, bf16[4,128,128]{2,1,0:T(8,128)(2,1)S(1)}, u32[]{:S(2)}, u32[]{:S(2)}) collective-permute-start(bf16[4,128,128]{2,1,0:T(8,128)(2,1)S(1)} %get-tuple-element.55), channel_id=1, source_target_pairs={{4,12},{8,0},{0,4},{12,8},{5,13},{9,1},{1,5},{13,9},{6,14},{10,2},... | collective-permute-start | bytes 393224 | tf_op jit(solution)/shard_map/ppermute | solution.py:600
  51.3 8.0 %collective-permute-start.18 = (bf16[8,128,128]{2,1,0:T(8,128)(2,1)S(1)}, bf16[8,128,128]{2,1,0:T(8,128)(2,1)S(1)}, u32[]{:S(2)}, u32[]{:S(2)}) collective-permute-start(bf16[8,128,128]{2,1,0:T(8,128)(2,1)S(1)} %get-tuple-element.54.refs_0_), channel_id=1, source_target_pairs={{4,0},{8,12},{5,9},{9,5},{6,2},{10,14},{7,11},{11,7},{20,16},{24,2... | collective-permute-start | bytes 786440 | tf_op jit(solution)/shard_map/ppermute | solution.py:533
  53.4 7.3 %collective-permute-start.17 = (bf16[8,128,128]{2,1,0:T(8,128)(2,1)S(1)}, bf16[8,128,128]{2,1,0:T(8,128)(2,1)S(1)}, u32[]{:S(2)}, u32[]{:S(2)}) collective-permute-start(bf16[8,128,128]{2,1,0:T(8,128)(2,1)S(1)} %get-tuple-element.54.refs_0_), channel_id=1, source_target_pairs={{4,8},{8,4},{5,1},{9,13},{6,10},{10,6},{7,3},{11,15},{20,24},{24,2... | collective-permute-start | bytes 786440 | tf_op jit(solution)/shard_map/ppermute | solution.py:533
  55.0 9.0 %collective-permute-start.16 = (bf16[8,128,128]{2,1,0:T(8,128)(2,1)S(1)}, bf16[8,128,128]{2,1,0:T(8,128)(2,1)S(1)}, u32[]{:S(2)}, u32[]{:S(2)}) collective-permute-start(bf16[8,128,128]{2,1,0:T(8,128)(2,1)S(1)} %get-tuple-element.54.refs_0_), channel_id=1, source_target_pairs={{0,1},{1,0},{2,3},{3,2},{4,5},{5,4},{6,7},{7,6},{8,9},{9,8},{10,11... | collective-permute-start | bytes 786440 | tf_op jit(solution)/shard_map/ppermute | solution.py:524
  58.0 1.3 %collective-permute-start.20 = (bf16[4,128,128]{2,1,0:T(8,128)(2,1)S(1)}, bf16[4,128,128]{2,1,0:T(8,128)(2,1)S(1)}, u32[]{:S(2)}, u32[]{:S(2)}) collective-permute-start(bf16[4,128,128]{2,1,0:T(8,128)(2,1)S(1)} %collective-permute-done.19.piece_ref.refs_4_), channel_id=1, source_target_pairs={{0,1},{1,0},{2,3},{3,2},{4,5},{5,4},{6,7},{7,6},{8,9},{9,8},{10,11... | collective-permute-start | bytes 393224 | tf_op jit(solution)/shard_map/ppermute | solution.py:524
  58.1 5.5 %collective-permute-start.22 = (bf16[4,128,128]{2,1,0:T(8,128)(2,1)S(1)}, bf16[4,128,128]{2,1,0:T(8,128)(2,1)S(1)}, u32[]{:S(2)}, u32[]{:S(2)}) collective-permute-start(bf16[4,128,128]{2,1,0:T(8,128)(2,1)S(1)} %collective-permute-done.19.piece_ref.refs_4_), channel_id=1, source_target_pairs={{0,2},{1,3},{2,0},{3,1},{4,6},{5,7},{6,4},{7,5},{8,10},{9,11},{10,... | collective-permute-start | bytes 393224 | tf_op jit(solution)/shard_map/ppermute | solution.py:524
  60.8 4.2 %collective-permute-start.21 = (bf16[8,128,128]{2,1,0:T(8,128)(2,1)S(1)}, bf16[8,128,128]{2,1,0:T(8,128)(2,1)S(1)}, u32[]{:S(2)}, u32[]{:S(2)}) collective-permute-start(bf16[8,128,128]{2,1,0:T(8,128)(2,1)S(1)} %joined.3.refs_2_), channel_id=1, source_target_pairs={{0,1},{1,0},{2,3},{3,2},{4,5},{5,4},{6,7},{7,6},{8,9},{9,8},{10,11... | collective-permute-start | bytes 786440 | tf_op jit(solution)/shard_map/ppermute | solution.py:524
  63.6 1.4 %collective-permute-start.23 = (bf16[4,128,128]{2,1,0:T(8,128)(2,1)S(1)}, bf16[4,128,128]{2,1,0:T(8,128)(2,1)S(1)}, u32[]{:S(2)}, u32[]{:S(2)}) collective-permute-start(bf16[4,128,128]{2,1,0:T(8,128)(2,1)S(1)} %collective-permute-done.22.refs_6_), channel_id=1, source_target_pairs={{0,1},{1,0},{2,3},{3,2},{4,5},{5,4},{6,7},{7,6},{8,9},{9,8},{10,11... | collective-permute-start | bytes 393224 | tf_op jit(solution)/shard_map/ppermute | solution.py:524
  68.2 3.5 %collective-permute-start.24 = (f32[8,128,128]{2,1,0:T(8,128)S(1)}, f32[8,128,128]{2,1,0:T(8,128)S(1)}, u32[]{:S(2)}, u32[]{:S(2)}) collective-permute-start(f32[8,128,128]{2,1,0:T(8,128)S(1)} %get-tuple-element.56.amps_ref), channel_id=1, source_target_pairs={{0,1},{1,0},{2,3},{3,2},{4,5},{5,4},{6,7},{7,6},{8,9},{9,8},{10,11... | collective-permute-start | bytes 1572872 | tf_op jit(solution)/shard_map/ppermute | solution.py:524
  68.7 6.0 %collective-permute-start.25 = (bf16[2,128,128]{2,1,0:T(8,128)(2,1)S(1)}, bf16[2,128,128]{2,1,0:T(8,128)(2,1)S(1)}, u32[]{:S(2)}, u32[]{:S(2)}) collective-permute-start(bf16[2,128,128]{2,1,0:T(8,128)(2,1)S(1)} %get-tuple-element.60), channel_id=1, source_target_pairs={{0,4},{4,0},{8,12},{12,8},{1,5},{5,1},{9,13},{13,9},{2,6},{6,2},{1... | collective-permute-start | bytes 196616 | tf_op jit(solution)/shard_map/ppermute | solution.py:529
  68.9 5.8 %collective-permute-start.26 = (bf16[2,128,128]{2,1,0:T(8,128)(2,1)S(1)}, bf16[2,128,128]{2,1,0:T(8,128)(2,1)S(1)}, u32[]{:S(2)}, u32[]{:S(2)}) collective-permute-start(bf16[2,128,128]{2,1,0:T(8,128)(2,1)S(1)} %get-tuple-element.61), channel_id=1, source_target_pairs={{4,8},{8,4},{5,9},{9,5},{6,10},{10,6},{7,11},{11,7},{20,24},{24,20... | collective-permute-start | bytes 196616 | tf_op jit(solution)/shard_map/ppermute | solution.py:529
  74.8 1.8 %collective-permute-start.27 = (f32[2,128,128]{2,1,0:T(8,128)S(1)}, f32[2,128,128]{2,1,0:T(8,128)S(1)}, u32[]{:S(2)}, u32[]{:S(2)}) collective-permute-start(f32[2,128,128]{2,1,0:T(8,128)S(1)} %convert_add_fusion), channel_id=1, source_target_pairs={{0,1},{1,0},{2,3},{3,2},{4,5},{5,4},{6,7},{7,6},{8,9},{9,8},{10,11... | collective-permute-start | bytes 393224 | tf_op jit(solution)/shard_map/ppermute | solution.py:524

commit v6 on v5

--- a/solution.py
+++ b/solution.py
@@ -43,8 +43,8 @@
 
 
 def prepare_kernel(
-    aux_ref, occ_ref, used_ref, energy_ref, first_ref, second_ref, ints_ref,
-    first_out, second_out, ints_out, factor_ref, sems,
+    aux_ref, occ_ref, used_ref, energy_ref, first_ref, second_ref,
+    first_out, second_out, factor_ref, sems,
 ):
     count, width, _ = factor_ref.shape
     half = lax.rem(aux_ref[0], 2)
@@ -52,7 +52,6 @@
     copies = [
         pltpu.make_async_copy(first_ref.at[rows], first_out, sems.at[0]),
         pltpu.make_async_copy(second_ref.at[rows], second_out, sems.at[1]),
-        pltpu.make_async_copy(ints_ref, ints_out, sems.at[2]),
     ]
     for copy in copies:
         copy.start()
@@ -69,7 +68,7 @@
         copy.wait()
 
 
-def prepare(aux, occupied, used, energy, first, second, ints):
+def prepare(aux, occupied, used, energy, first, second):
     pair_dev, width, _ = first.shape
     shape = (pair_dev // 2, width, width)
     return pl.pallas_call(
@@ -77,16 +76,15 @@
         out_shape=(
             jax.ShapeDtypeStruct(shape, BF16),
             jax.ShapeDtypeStruct(shape, BF16),
-            jax.ShapeDtypeStruct(ints.shape, BF16),
             jax.ShapeDtypeStruct(shape, F32),
         ),
-        in_specs=[SMEM] * 3 + [VMEM] + [HBM] * 3,
-        out_specs=(VMEM,) * 4,
-        scratch_shapes=[pltpu.SemaphoreType.DMA((3,))],
+        in_specs=[SMEM] * 3 + [VMEM] + [HBM] * 2,
+        out_specs=(VMEM,) * 3,
+        scratch_shapes=[pltpu.SemaphoreType.DMA((2,))],
         compiler_params=params(8),
         cost_estimate=cost(0, 8 * pair_dev * width * width),
         name="prepare",
-    )(aux, occupied, used, energy, first, second, ints)
+    )(aux, occupied, used, energy, first, second)
 
 
 def first_is_lower(here_ref, aux_ref):
@@ -120,176 +118,16 @@
     )(here, aux, ints)
 
 
-def product_kernel(
-    here_ref, aux_ref, own_ref, one_ref, two_ref, kept_ref, sent_ref, full_ref, inner_ref
+PRODUCT, FIRST, SECOND = 4, 5, 6
+
+
+def index_kernel(
+    rounds, here_ref, aux_ref, orbitals_ref, near_ref, couple_ref, index_ref, weight_ref
 ):
-    count, _, width = own_ref.shape
-    depth = one_ref.shape[1]
-    odd = first_is_lower(here_ref, aux_ref)
-    side = lax.rem(aux_ref[0], 2)
-    rows_each = count * width
-    for r, near_ref in enumerate((one_ref, two_ref)):
-        lower = odd if r == 0 else 1 - odd
-        rows = pl.ds(pl.multiple_of(lower * depth, depth), depth)
-        own = jnp.concatenate([own_ref[i, rows] for i in range(count)], axis=1)
-        near = jnp.concatenate([near_ref[i] for i in range(count)], axis=1)
-        full_ref[...] = dot(
-            jnp.where(lower == 1, near, own), jnp.where(lower == 1, own, near), ((0,), (0,))
-        )
-        for j in range(count):
-            columns = slice(j * width, (j + 1) * width)
-            for out_ref, i in ((kept_ref, side), (sent_ref, 1 - side)):
-                at = pl.multiple_of((r ^ side) * rows_each + j * width, width)
-                out_ref[pl.ds(at, width)] = full_ref[
-                    pl.ds(pl.multiple_of(i * width, width), width), columns
-                ]
-    at = 2 * rows_each
-    half = width // 2
-    inner_ref[...] = dot(own_ref[0], own_ref[1], ((0,), (0,)))
-    kept_ref[at:] = inner_ref[pl.ds(pl.multiple_of(side * half, half), half)]
-    sent_ref[at:] = inner_ref[pl.ds(pl.multiple_of((1 - side) * half, half), half)]
-
-
-def products(here, aux, ints, one, two):
-    count, depth, width = ints.shape
-    rows = 2 * count * width + width // 2
-    return pl.pallas_call(
-        product_kernel,
-        out_shape=(jax.ShapeDtypeStruct((rows, width), F32),) * 2,
-        in_specs=[SMEM] * 2 + [VMEM] * 3,
-        out_specs=(VMEM, VMEM),
-        scratch_shapes=[
-            pltpu.VMEM((count * width, count * width), F32),
-            pltpu.VMEM((width, width), F32),
-        ],
-        compiler_params=params(12),
-        cost_estimate=cost(10 * depth * width * width, 8 * depth * width),
-        name="products",
-    )(here, aux, ints, one, two)
-
-
-def pair_kernel(kept_ref, received_ref, total_ref, one_ref, two_ref):
-    total = kept_ref[...] + received_ref[...]
-    total_ref[...] = total
-    rows = one_ref.shape[0]
-    one_ref[...] = total[:rows].astype(BF16)
-    two_ref[...] = total[rows : 2 * rows].astype(BF16)
-
-
-def pair_sum(kept, received, rows):
-    part = jax.ShapeDtypeStruct((rows, kept.shape[1]), BF16)
-    return pl.pallas_call(
-        pair_kernel,
-        out_shape=(jax.ShapeDtypeStruct(kept.shape, F32), part, part),
-        in_specs=[VMEM] * 2,
-        out_specs=(VMEM,) * 3,
-        compiler_params=params(4),
-        cost_estimate=cost(kept.size, 16 * kept.size),
-        name="pair_sum",
-    )(kept, received)
-
-
-def partner_kernel(total_ref, one_ref, two_ref, out_ref):
-    rows = one_ref.shape[0]
-    out_ref[:rows] = (total_ref[:rows] + one_ref[...].astype(F32)).astype(BF16)
-    out_ref[rows : 2 * rows] = (
-        total_ref[rows : 2 * rows] + two_ref[...].astype(F32)
-    ).astype(BF16)
-    out_ref[2 * rows :] = total_ref[2 * rows :].astype(BF16)
-
-
-def partner_sum(total, one, two):
-    return pl.pallas_call(
-        partner_kernel,
-        out_shape=jax.ShapeDtypeStruct(total.shape, BF16),
-        in_specs=[VMEM] * 3,
-        out_specs=VMEM,
-        compiler_params=params(4),
-        cost_estimate=cost(total.size, 8 * total.size),
-        name="partner_sum",
-    )(total, one, two)
-
-
-def own_part(aux_ref, low_ref, part_ref):
-    count = part_ref.shape[0]
-    part_ref[...] = low_ref[pl.ds(lax.rem(aux_ref[0] // 2, 2) * count, count)]
-
-
-def exchange_kernel(
-    here_ref, aux_ref, orbitals_ref, total_ref, far_ref, total_other, far_other,
-    first_ref, second_ref, factor_ref, exch_ref, low_ref, part_ref, table,
-):
-    count, width, _ = exch_ref.shape
-    half = lax.rem(aux_ref[0], 2)
-    base = here_ref[0] * 2 - 2
-    odd = lax.rem(here_ref[0], 2) == 1
-    for i, total in (
-        (half, total_ref[...].astype(F32) + far_ref[...].astype(F32)),
-        (1 - half, total_other[...].astype(F32) + far_other[...].astype(F32)),
-    ):
-        for j in range(2):
-            one = total[j * width : (j + 1) * width]
-            two = total[(j + 2) * width : (j + 3) * width]
-            table[i * 6 + 4 + j] = jnp.where(odd, two, one)
-            table[j * 6 + i] = jnp.where(odd, one, two).T
-        table[3, pl.ds(pl.multiple_of(i * (width // 2), width // 2), width // 2)] = total[4 * width :]
-    table[6 + 2] = table[3].T
-    for p in range(count):
-        row = half * count + p
-        slot = (orbitals_ref[0, row] - base - 2) * 6 + orbitals_ref[1, row] - base
-        right = second_ref[p]
-        left = first_ref[p]
-        high, rest = split(table[slot])
-        inner = dot(
-            jnp.concatenate([high, rest], axis=1),
-            jnp.concatenate([right, right], axis=0),
-            ((1,), (0,)),
-        )
-        high, rest = split(inner)
-        exch = dot(
-            jnp.concatenate([left, left], axis=0),
-            jnp.concatenate([high, rest], axis=0),
-            ((0,), (0,)),
-        )
-        exch_ref[p] = exch
-        low_ref[p] = (factor_ref[p] * exch).astype(BF16)
-    own_part(aux_ref, low_ref, part_ref)
-
-
-def exchange(here, aux, orbitals, sums, first, second, factor):
-    shape = first.shape
-    count, width, _ = shape
-    return pl.pallas_call(
-        exchange_kernel,
-        out_shape=(
-            jax.ShapeDtypeStruct(shape, F32),
-            jax.ShapeDtypeStruct(shape, BF16),
-            jax.ShapeDtypeStruct((count // 2, width, width), BF16),
-        ),
-        in_specs=[SMEM] * 3 + [VMEM] * (len(sums) + 3),
-        out_specs=(VMEM,) * 3,
-        scratch_shapes=[pltpu.VMEM((12, width, width), F32)],
-        compiler_params=params(12),
-        cost_estimate=cost(8 * count * width**3, 20 * count * width * width),
-        name="exchange",
-    )(here, aux, orbitals, *sums, first, second, factor)
-
-
-def sweep_kernel(last, pieces, rounds, here_ref, aux_ref, orbitals_ref, near_ref, couple_ref, *refs):
-    parts = refs[:pieces]
-    over_ref, exch_ref, factor_ref, second_ref = refs[pieces : pieces + 4]
-    if last:
-        amps_ref, terms_ref, one_ref, two_ref, all_terms, table = refs[pieces + 4 :]
-    else:
-        low_ref, part_ref, table = refs[pieces + 4 :]
-    count, width, _ = exch_ref.shape
-    pair_dev, nbr_count = over_ref.shape[:2]
+    nbr_count, pair_dev = couple_ref.shape
+    count = pair_dev // 2
     here = here_ref[0]
     half = lax.rem(aux_ref[0], 2)
-    at = 0
-    for part in parts:
-        table[at : at + part.shape[0]] = part[...]
-        at += part.shape[0]
     across = lax.rem(aux_ref[0] // 2, 2)
     near_block = -1
     for start, end in rounds[0] if rounds else ():
@@ -315,13 +153,211 @@
         spot = other * count + local + jnp.where(owner == here, 0, 2 * count)
         return jnp.where(owner == near_block, halved, spot)
 
+    lane = lax.broadcasted_iota(jnp.int32, (1, index_ref.shape[1]), 1)
+    for p in range(count):
+        row = half * count + p
+        first = orbitals_ref[0, row] - here * 2
+        second = orbitals_ref[1, row] - here * 2 + 2
+        values = {PRODUCT: first * 6 + second, FIRST: first, SECOND: second}
+        values.update((n, place(p, n)) for n in range(nbr_count))
+        index_ref[p : p + 1] = sum(jnp.where(lane == at, v, 0) for at, v in values.items())
+        weight_ref[p : p + 1] = sum(
+            jnp.where(lane == n, couple_ref[n, row], 0.0) for n in range(nbr_count)
+        )
+
+
+def indices(rounds, here, aux, orbitals, near, couple):
+    nbr_count, pair_dev = couple.shape
+    assert nbr_count <= PRODUCT
+    return pl.pallas_call(
+        functools.partial(index_kernel, rounds),
+        out_shape=(
+            jax.ShapeDtypeStruct((pair_dev // 2, 128), jnp.int32),
+            jax.ShapeDtypeStruct((pair_dev // 2, 128), F32),
+        ),
+        in_specs=[SMEM] * 5,
+        out_specs=(VMEM, VMEM),
+        compiler_params=params(4),
+        cost_estimate=cost(10**6, 2**16),
+        name="indices",
+    )(here, aux, orbitals, near, couple)
+
+
+def product_kernel(
+    here_ref, aux_ref, own_one_ref, own_two_ref, one_ref, two_ref, kept_ref, sent_ref, full_ref,
+    inner_ref,
+):
+    count, _, width = one_ref.shape
+    odd = first_is_lower(here_ref, aux_ref)
+    side = lax.rem(aux_ref[0], 2)
+    rows_each = count * width
+    for r, (own_ref, near_ref) in enumerate(((own_two_ref, one_ref), (own_one_ref, two_ref))):
+        lower = odd if r == 0 else 1 - odd
+        own = jnp.concatenate([own_ref[i] for i in range(count)], axis=1)
+        near = jnp.concatenate([near_ref[i] for i in range(count)], axis=1)
+        full_ref[...] = dot(
+            jnp.where(lower == 1, near, own), jnp.where(lower == 1, own, near), ((0,), (0,))
+        )
+        for j in range(count):
+            columns = slice(j * width, (j + 1) * width)
+            for out_ref, i in ((kept_ref, side), (sent_ref, 1 - side)):
+                at = pl.multiple_of((r ^ side) * rows_each + j * width, width)
+                out_ref[pl.ds(at, width)] = full_ref[
+                    pl.ds(pl.multiple_of(i * width, width), width), columns
+                ]
+    at = 2 * rows_each
+    half = width // 2
+    inner_ref[...] = dot(own_one_ref[0], own_one_ref[1], ((0,), (0,))) + dot(
+        own_two_ref[0], own_two_ref[1], ((0,), (0,))
+    )
+    kept_ref[at:] = inner_ref[pl.ds(pl.multiple_of(side * half, half), half)]
+    sent_ref[at:] = inner_ref[pl.ds(pl.multiple_of((1 - side) * half, half), half)]
+
+
+def products(here, aux, own_one, own_two, one, two):
+    count, depth, width = one.shape
+    rows = 2 * count * width + width // 2
+    return pl.pallas_call(
+        product_kernel,
+        out_shape=(jax.ShapeDtypeStruct((rows, width), F32),) * 2,
+        in_specs=[SMEM] * 2 + [VMEM] * 4,
+        out_specs=(VMEM, VMEM),
+        scratch_shapes=[
+            pltpu.VMEM((count * width, count * width), F32),
+            pltpu.VMEM((width, width), F32),
+        ],
+        compiler_params=params(12),
+        cost_estimate=cost(20 * depth * width * width, 16 * depth * width),
+        name="products",
+    )(here, aux, own_one, own_two, one, two)
+
+
+def pair_kernel(kept_ref, received_ref, total_ref, one_ref, two_ref):
+    total = kept_ref[...] + received_ref[...]
+    total_ref[...] = total
+    rows = one_ref.shape[0]
+    one_ref[...] = total[:rows].astype(BF16)
+    two_ref[...] = total[rows : 2 * rows].astype(BF16)
+
+
+def pair_sum(kept, received, rows):
+    part = jax.ShapeDtypeStruct((rows, kept.shape[1]), BF16)
+    return pl.pallas_call(
+        pair_kernel,
+        out_shape=(jax.ShapeDtypeStruct(kept.shape, F32), part, part),
+        in_specs=[VMEM] * 2,
+        out_specs=(VMEM,) * 3,
+        compiler_params=params(4),
+        cost_estimate=cost(kept.size, 16 * kept.size),
+        name="pair_sum",
+    )(kept, received)
+
+
+def partner_kernel(total_ref, one_ref, two_ref, out_ref):
+    rows = one_ref.shape[0]
+    out_ref[:rows] = (total_ref[:rows] + one_ref[...].astype(F32)).astype(BF16)
+    out_ref[rows : 2 * rows] = (
+        total_ref[rows : 2 * rows] + two_ref[...].astype(F32)
+    ).astype(BF16)
+    out_ref[2 * rows :] = total_ref[2 * rows :].astype(BF16)
+
+
+def partner_sum(total, one, two):
+    return pl.pallas_call(
+        partner_kernel,
+        out_shape=jax.ShapeDtypeStruct(total.shape, BF16),
+        in_specs=[VMEM] * 3,
+        out_specs=VMEM,
+        compiler_params=params(4),
+        cost_estimate=cost(total.size, 8 * total.size),
+        name="partner_sum",
+    )(total, one, two)
+
+
+def own_part(aux_ref, low_ref, part_ref):
+    count = part_ref.shape[0]
+    part_ref[...] = low_ref[pl.ds(lax.rem(aux_ref[0] // 2, 2) * count, count)]
+
+
+def exchange_kernel(
+    here_ref, aux_ref, index_ref, total_ref, far_ref, total_other, far_other,
+    first_ref, second_ref, factor_ref, exch_ref, low_ref, part_ref, table,
+):
+    count, width, _ = exch_ref.shape
+    half = lax.rem(aux_ref[0], 2)
+    odd = lax.rem(here_ref[0], 2) == 1
+    for i, total in (
+        (half, total_ref[...].astype(F32) + far_ref[...].astype(F32)),
+        (1 - half, total_other[...].astype(F32) + far_other[...].astype(F32)),
+    ):
+        for j in range(2):
+            one = total[j * width : (j + 1) * width]
+            two = total[(j + 2) * width : (j + 3) * width]
+            table[i * 6 + 4 + j] = jnp.where(odd, two, one)
+            table[j * 6 + i] = jnp.where(odd, one, two).T
+        table[3, pl.ds(pl.multiple_of(i * (width // 2), width // 2), width // 2)] = total[4 * width :]
+    table[6 + 2] = table[3].T
+    for p in range(count):
+        right = second_ref[p]
+        left = first_ref[p]
+        high, rest = split(table[index_ref[p, PRODUCT]])
+        inner = dot(
+            jnp.concatenate([high, rest], axis=1),
+            jnp.concatenate([right, right], axis=0),
+            ((1,), (0,)),
+        )
+        high, rest = split(inner)
+        exch = dot(
+            jnp.concatenate([left, left], axis=0),
+            jnp.concatenate([high, rest], axis=0),
+            ((0,), (0,)),
+        )
+        exch_ref[p] = exch
+        low_ref[p] = (factor_ref[p] * exch).astype(BF16)
+    own_part(aux_ref, low_ref, part_ref)
+
+
+def exchange(here, aux, index, sums, first, second, factor):
+    shape = first.shape
+    count, width, _ = shape
+    return pl.pallas_call(
+        exchange_kernel,
+        out_shape=(
+            jax.ShapeDtypeStruct(shape, F32),
+            jax.ShapeDtypeStruct(shape, BF16),
+            jax.ShapeDtypeStruct((count // 2, width, width), BF16),
+        ),
+        in_specs=[SMEM] * 2 + [VMEM] * (len(sums) + 4),
+        out_specs=(VMEM,) * 3,
+        scratch_shapes=[pltpu.VMEM((12, width, width), F32)],
+        compiler_params=params(12),
+        cost_estimate=cost(8 * count * width**3, 20 * count * width * width),
+        name="exchange",
+    )(here, aux, index, *sums, first, second, factor)
+
+
+def sweep_kernel(last, pieces, here_ref, aux_ref, index_ref, weight_ref, *refs):
+    parts = refs[:pieces]
+    over_ref, exch_ref, factor_ref, second_ref = refs[pieces : pieces + 4]
+    if last:
+        amps_ref, terms_ref, one_ref, two_ref, all_terms, table = refs[pieces + 4 :]
+    else:
+        low_ref, part_ref, table = refs[pieces + 4 :]
+    count, width, _ = exch_ref.shape
+    nbr_count = over_ref.shape[1]
+    here = here_ref[0]
+    half = lax.rem(aux_ref[0], 2)
+    at = 0
+    for part in parts:
+        table[at : at + part.shape[0]] = part[...]
+        at += part.shape[0]
     done = []
     for p in range(count):
         row = half * count + p
         halves = []
         for n in range(nbr_count):
-            moved = dot(over_ref[row, n], table[place(p, n)], ((1,), (0,)))
-            halves.append((couple_ref[n, row] * moved).astype(BF16))
+            moved = dot(over_ref[row, n], table[index_ref[p, n]], ((1,), (0,)))
+            halves.append((weight_ref[p, n] * moved).astype(BF16))
         coupled = dot(
             jnp.concatenate(halves, axis=1),
             jnp.concatenate([over_ref[row, n] for n in range(nbr_count)], axis=1),
@@ -348,7 +384,7 @@
             terms.append(square(moved))
         all_terms[...] = jnp.zeros_like(all_terms)
         for p in range(count):
-            spot = orbitals_ref[1, half * count + p] - here * 2 + 2
+            spot = index_ref[p, SECOND]
             all_terms[spot] += terms[p]
         terms_ref[...] = all_terms[2:4]
         below = lax.rem(here, 2) * 4
@@ -356,7 +392,7 @@
         two_ref[...] = all_terms[pl.ds(below, 2)].astype(BF16)
 
 
-def sweep(last, rounds, here, aux, orbitals, near, couple, parts, over, exch, factor, second):
+def sweep(last, here, aux, index, weight, parts, over, exch, factor, second):
     count, width, _ = exch.shape
     rows = sum(part.shape[0] for part in parts)
     if last:
@@ -376,15 +412,15 @@
         out_specs = (VMEM, VMEM)
         scratch = []
     return pl.pallas_call(
-        functools.partial(sweep_kernel, last, len(parts), rounds),
+        functools.partial(sweep_kernel, last, len(parts)),
         out_shape=out_shape,
-        in_specs=[SMEM] * 5 + [VMEM] * (len(parts) + 4),
+        in_specs=[SMEM] * 2 + [VMEM] * (len(parts) + 6),
         out_specs=out_specs,
         scratch_shapes=scratch + [pltpu.VMEM((rows, width, width), BF16)],
         compiler_params=params(16),
         cost_estimate=cost(16 * count * width**3, (rows + 16 * count) * width * width),
         name="last_sweep" if last else "sweep",
-    )(here, aux, orbitals, near, couple, *parts, over, exch, factor, second)
+    )(here, aux, index, weight, *parts, over, exch, factor, second)
 
 
 def token_kernel(piece_ref, out_ref):
@@ -421,7 +457,7 @@
 
 
 def first_kernel(
-    here_ref, aux_ref, orbitals_ref, amps_ref, others_ref, first_ref, whole_ref, terms_ref, sems
+    aux_ref, index_ref, amps_ref, others_ref, first_ref, whole_ref, terms_ref, sems
 ):
     count = amps_ref.shape[0]
     half = lax.rem(aux_ref[0], 2)
@@ -443,13 +479,13 @@
         terms.append(square(moved))
     terms_ref[...] = jnp.zeros_like(terms_ref)
     for p in range(count):
-        spot = orbitals_ref[0, half * count + p] - here_ref[0] * 2
+        spot = index_ref[p, FIRST]
         terms_ref[spot] += terms[p]
     for copy in copies:
         copy.wait()
 
 
-def first_terms(here, aux, orbitals, amps, others, first):
+def first_terms(aux, index, amps, others, first):
     count, width, _ = amps.shape
     return pl.pallas_call(
         first_kernel,
@@ -457,13 +493,13 @@
             jax.ShapeDtypeStruct((2 * count, width, width), F32),
             jax.ShapeDtypeStruct((2, width, width), F32),
         ),
-        in_specs=[SMEM] * 3 + [VMEM] * 3,
+        in_specs=[SMEM] + [VMEM] * 4,
         out_specs=(ANY, VMEM),
         scratch_shapes=[pltpu.SemaphoreType.DMA((2,))],
         compiler_params=params(12),
         cost_estimate=cost(12 * count * width**3, 16 * count * width * width),
         name="first_terms",
-    )(here, aux, orbitals, amps, others, first)
+    )(aux, index, amps, others, first)
 
 
 def window_rounds(groups):
@@ -518,7 +554,6 @@
         [(i, j) for i in range(groups) for j in (i + 1 - 2 * ((i + r) % 2),) if 0 <= j < groups]
         for r in range(2)
     ]
-    orbitals = pair_orbitals.T
 
     def swap(value, step=1):
         return lax.ppermute(value, "aux", [(i, i ^ step) for i in range(aux_count)])
@@ -542,25 +577,12 @@
             for r, value in enumerate((one, two))
         ]
 
-    near_one, near_two = exchanged(*halves(here_s, aux_s, ints), partners)
-    first, second, ints, factor = prepare(
-        aux_s, occ_energy.T, pno_count, virt_energy, proj_first, proj_second, ints
+    own_halves = halves(here_s, aux_s, ints)
+    near_one, near_two = exchanged(*own_halves, partners)
+    first, second, factor = prepare(
+        aux_s, occ_energy.T, pno_count, virt_energy, proj_first, proj_second
     )
-    near_one, first, second, ints, factor = lax.optimization_barrier(
-        (near_one, first, second, ints, factor)
-    )
-
-    kept, sent = products(here_s, aux_s, ints, near_one, near_two)
-    total, *sent = pair_sum(kept, swap(sent), occ_dev * width)
-    total = partner_sum(total, *both(*sent))
-    step = 2
-    while 2 * step < aux_count:
-        total = (total.astype(F32) + swap(total, step).astype(F32)).astype(BF16)
-        step *= 2
-    far = swap(total, step)
-    exch, low, part = exchange(
-        here_s, aux_s, orbitals, (total, far, swap(total), swap(far)), first, second, factor
-    )
+    near_one, first, second, factor = lax.optimization_barrier((near_one, first, second, factor))
 
     if cap < pair_dev or groups // 4 != 1 or aux_count != 4:
         rounds = None
@@ -586,6 +608,19 @@
         )
     else:
         rounds = window_rounds(groups)
+    index, weight = indices(rounds, here_s, aux_s, pair_orbitals.T, neighbours.T, couple.T)
+
+    kept, sent = products(here_s, aux_s, *own_halves, near_one, near_two)
+    total, *sent = pair_sum(kept, swap(sent), occ_dev * width)
+    total = partner_sum(total, *both(*sent))
+    step = 2
+    while 2 * step < aux_count:
+        total = (total.astype(F32) + swap(total, step).astype(F32)).astype(BF16)
+        step *= 2
+    far = swap(total, step)
+    exch, low, part = exchange(
+        here_s, aux_s, index, (total, far, swap(total), swap(far)), first, second, factor
+    )
 
     def gathered(low, part):
         if rounds is None:
@@ -606,12 +641,10 @@
     for it in range(ITERS):
         out = sweep(
             it == ITERS - 1,
-            rounds,
             here_s,
             aux_s,
-            orbitals,
-            neighbours.T,
-            couple.T,
+            index,
+            weight,
             gathered(low, part),
             intersections,
             exch,
@@ -623,7 +656,7 @@
     amps, terms, *sent = out
 
     near_one, near_two = both(*sent)
-    whole, inner = first_terms(here_s, aux_s, orbitals, amps, swap(amps), first)
+    whole, inner = first_terms(aux_s, index, amps, swap(amps), first)
     density = inner + terms + near_one.astype(F32) + near_two.astype(F32)
     density = (density + swap(density)) / width
     return (whole, density)

time: 77.7 us -> 75.8 us (0.976)
  Pallas kernels: 11.4 us -> 10.1 us
  local copies, waits for them, and re-layouts: 6.39 us -> 5.26 us
    ppermute x6, waiting for transfers between devices: 4.96 us -> 6.27 us  [exchanged(): lax.ppermute(value, ('pair', 'aux'), [(i * aux_count + a, j * aux_count +...]
    unnamed x22 -> x20, local copies, waits for them, and re-layouts: 6.39 us -> 5.26 us
    ppermute x16, waiting for transfers between devices: 9.92 us -> 8.97 us  [swap(): return lax.ppermute(value, 'aux', [(i, i ^ step) for i in range(aux_count)])]
    pallas_call x2 -> x3, Pallas kernels: 5.14 us -> 5.04 us  [the longest x2 3.71 us: sweep(): pl.pallas_call(functools.partial(sweep_kernel, last, len(parts)), out_sha...]
  transfers between devices with their start and end apart: 28 -> 28, of which waited for: 13 -> 12; matrix products, arithmetic and copies ran while one was open for 0% -> 0% of each run, Pallas kernels for 5% -> 6%
where the time goes in v6:
time: 75.8 us; the launch traced here: 75.3 us
  starting transfers between devices  41.5 us (55%)
  waiting for transfers between devices  16.9 us (22%)
  Pallas kernels  10.1 us (13%)
  local copies, waits for them, and re-layouts  5.26 us (7%)
  between operations  0.9 us (1%)
    ppermute x16, starting transfers between devices, swap(): return lax.ppermute(value, 'aux', [(i, i ^ step) for i in range(aux_count)])  19.2 us
    ppermute x6, starting transfers between devices, exchanged(): lax.ppermute(value, ('pair', 'aux'), [(i * aux_count + a, j * aux_count +...  13.5 us
    ppermute x16, waiting for transfers between devices, swap(): return lax.ppermute(value, 'aux', [(i, i ^ step) for i in range(aux_count)])  8.97 us
    ppermute x2, starting transfers between devices, both(): lax.ppermute(two, 'pair', partners[1])  7.48 us
    ppermute x6, waiting for transfers between devices, exchanged(): lax.ppermute(value, ('pair', 'aux'), [(i * aux_count + a, j * aux_count +...  6.27 us
    unnamed x20, local copies, waits for them, and re-layouts  5.26 us
    pallas_call x2, Pallas kernels, sweep(): pl.pallas_call(functools.partial(sweep_kernel, last, len(parts)), out_sha...  3.71 us
    pallas_call x1, Pallas kernels, first_terms(): pl.pallas_call(first_kernel, out_shape=(jax.ShapeDtypeStruct((2 * count,...  2.35 us
  transfers between devices with their start and end apart: 28, of which 12 were waited for; matrix products, arithmetic and copies ran while one was open for 0% of the time, Pallas kernels for 6%

profile of v6, /device:TPU:15, one launch (start us, length us, event | category | flops | bytes accessed | tf_op | source)
XLA Modules:
  0.0 75.3 jit_solution(7724647629370934185)
XLA Ops:
  0.6 1.1 %copy-done.1 = bf16[2,1536,128]{2,1,0:T(8,128)(2,1)S(1)} copy-done((bf16[2,1536,128]{2,1,0:T(8,128)(2,1)S(1)}, bf16[2,1536,128]{2,1,0:T(8,128)(2,1)}, u32[]{:S(2)}) %copy-start.1) | copy-done | bytes 786456
  1.8 0.2 halves.1
  2.0 0.0 copy-start.5
  2.0 0.0 copy-start.6
  2.0 0.0 copy-start.7
  2.0 3.3 %collective-permute-start = (bf16[2,768,128]{2,1,0:T(8,128)(2,1)S(1)}, bf16[2,768,128]{2,1,0:T(8,128)(2,1)S(1)}, u32[]{:S(2)}, u32[]{:S(2)}) collective-permute-start(bf16[2,768,128]{2,1,0:T(8,128)(2,1)S(1)} %get-tuple-element.37.own_one_ref), channel_id=1, source_target_pairs={{0,4},{4,0},{8,12},{12,8},{5,9},{9,5},{2,6},{6,2},{10,14},{14,10},... | collective-permute-start | bytes 1179656 | tf_op jit(solution)/shard_map/ppermute | solution.py:568
  5.4 1.9 %collective-permute-start.1 = (bf16[2,768,128]{2,1,0:T(8,128)(2,1)S(1)}, bf16[2,768,128]{2,1,0:T(8,128)(2,1)S(1)}, u32[]{:S(2)}, u32[]{:S(2)}) collective-permute-start(bf16[2,768,128]{2,1,0:T(8,128)(2,1)S(1)} %get-tuple-element.38.own_two_ref), channel_id=1, source_target_pairs={{4,8},{8,4},{1,5},{5,1},{9,13},{13,9},{6,10},{10,6},{3,7},{7,3},{1... | collective-permute-start | bytes 1179656 | tf_op jit(solution)/shard_map/ppermute | solution.py:568
  7.3 0.0 copy-start.2
  7.3 1.0 %copy-done.2 = bf16[16,128,128]{2,1,0:T(8,128)(2,1)S(1)} copy-done((bf16[16,128,128]{2,1,0:T(8,128)(2,1)S(1)}, bf16[16,128,128]{2,1,0:T(8,128)(2,1)}, u32[]{:S(2)}) %copy-start.2) | copy-done | bytes 524312
  8.4 1.0 %copy-done.3 = bf16[16,128,128]{2,1,0:T(8,128)(2,1)S(1)} copy-done((bf16[16,128,128]{2,1,0:T(8,128)(2,1)S(1)}, bf16[16,128,128]{2,1,0:T(8,128)(2,1)}, u32[]{:S(2)}) %copy-start.3) | copy-done | bytes 524312
  9.4 0.7 copy-done.4
  10.1 0.7 copy-done.8
  10.8 0.7 copy-done.9
  11.4 0.8 %prepare.1 = (bf16[8,128,128]{2,1,0:T(8,128)(2,1)S(1)}, bf16[8,128,128]{2,1,0:T(8,128)(2,1)S(1)}, f32[8,128,128]{2,1,0:T(8,128)S(1)}) custom-call(s32[1]{0:T(128)} %bitcast.1.aux_ref, f32[2,16]{1,0:T(2,128)S(1)} %bitcast.9, s32[16]{0:T(128)S(1)} %copy-done.9, f32[16,128]{1,0:T(8,128)S(1)} %copy-done.4, bf16[16,128,128]{2,1,0:T(8,128)(2,1)S(1)} %copy-done.2, ...), custom_call_target="tpu_custom_call" | custom-call | bytes 2097152 | tf_op jit(solution)/shard_map/prepare/pallas_call | solution.py:74
  12.3 0.0 collective-permute-done.one_ref
  12.3 3.8 %collective-permute-done.1.two_ref = bf16[2,768,128]{2,1,0:T(8,128)(2,1)S(1)} collective-permute-done((bf16[2,768,128]{2,1,0:T(8,128)(2,1)S(1)}, bf16[2,768,128]{2,1,0:T(8,128)(2,1)S(1)}, u32[]{:S(2)}, u32[]{:S(2)}) %collective-permute-start.1) | collective-permute-done | bytes 393248 | tf_op jit(solution)/shard_map/ppermute | solution.py:568
  16.0 0.6 products.1
  16.6 0.1 collective-permute-start.2
  16.7 1.6 %collective-permute-done.2.received_ref = f32[576,128]{1,0:T(8,128)S(1)} collective-permute-done((f32[576,128]{1,0:T(8,128)S(1)}, f32[576,128]{1,0:T(8,128)S(1)}, u32[]{:S(2)}, u32[]{:S(2)}) %collective-permute-start.2) | collective-permute-done | bytes 294944 | tf_op jit(solution)/shard_map/ppermute | solution.py:559
  18.3 0.2 collective-permute-start.3
  18.6 4.3 %collective-permute-start.4 = (bf16[256,128]{1,0:T(8,128)(2,1)S(1)}, bf16[256,128]{1,0:T(8,128)(2,1)S(1)}, u32[]{:S(2)}, u32[]{:S(2)}) collective-permute-start(bf16[256,128]{1,0:T(8,128)(2,1)S(1)} %get-tuple-element.47), channel_id=1, source_target_pairs={{4,8},{8,4},{5,9},{9,5},{6,10},{10,6},{7,11},{11,7},{20,24},{24,20... | collective-permute-start | bytes 196616 | tf_op jit(solution)/shard_map/ppermute | solution.py:564
  22.9 0.0 collective-permute-done.3.one_ref
  22.9 1.6 %collective-permute-done.4.two_ref = bf16[256,128]{1,0:T(8,128)(2,1)S(1)} collective-permute-done((bf16[256,128]{1,0:T(8,128)(2,1)S(1)}, bf16[256,128]{1,0:T(8,128)(2,1)S(1)}, u32[]{:S(2)}, u32[]{:S(2)}) %collective-permute-start.4) | collective-permute-done | bytes 65568 | tf_op jit(solution)/shard_map/ppermute | solution.py:564
  24.6 0.3 collective-permute-start.5
  24.9 1.8 %collective-permute-start.6 = (bf16[576,128]{1,0:T(8,128)(2,1)S(1)}, bf16[576,128]{1,0:T(8,128)(2,1)S(1)}, u32[]{:S(2)}, u32[]{:S(2)}) collective-permute-start(bf16[576,128]{1,0:T(8,128)(2,1)S(1)} %partner_sum.1.total_ref), channel_id=1, source_target_pairs={{0,1},{1,0},{2,3},{3,2},{4,5},{5,4},{6,7},{7,6},{8,9},{9,8},{10,11... | collective-permute-start | bytes 442376 | tf_op jit(solution)/shard_map/ppermute | solution.py:559
  26.7 1.9 %collective-permute-done.5.far_ref = bf16[576,128]{1,0:T(8,128)(2,1)S(1)} collective-permute-done((bf16[576,128]{1,0:T(8,128)(2,1)S(1)}, bf16[576,128]{1,0:T(8,128)(2,1)S(1)}, u32[]{:S(2)}, u32[]{:S(2)}) %collective-permute-start.5) | collective-permute-done | bytes 147488 | tf_op jit(solution)/shard_map/ppermute | solution.py:559
  28.6 2.7 %collective-permute-start.7 = (bf16[576,128]{1,0:T(8,128)(2,1)S(1)}, bf16[576,128]{1,0:T(8,128)(2,1)S(1)}, u32[]{:S(2)}, u32[]{:S(2)}) collective-permute-start(bf16[576,128]{1,0:T(8,128)(2,1)S(1)} %collective-permute-done.5.far_ref), channel_id=1, source_target_pairs={{0,1},{1,0},{2,3},{3,2},{4,5},{5,4},{6,7},{7,6},{8,9},{9,8},{10,11... | collective-permute-start | bytes 442376 | tf_op jit(solution)/shard_map/ppermute | solution.py:559
  31.3 1.3 %indices.1 = (s32[8,128]{1,0:T(8,128)S(1)}, f32[8,128]{1,0:T(8,128)S(1)}) custom-call(s32[1]{0:T(128)} %bitcast.here_ref, s32[1]{0:T(128)} %bitcast.1.aux_ref, s32[2,16]{1,0:T(2,128)S(1)} %bitcast.8, s32[4,64]{1,0:T(4,128)S(1)} %bitcast.6, f32[4,16]{1,0:T(4,128)S(1)} %bitcast.7), custom_call_target="tpu_custom_call" | custom-call | flops 1000000 | bytes 65536 | tf_op jit(solution)/shard_map/indices/pallas_call | solution.py:172
  32.6 0.0 collective-permute-done.6.total_other
  32.6 0.8 %exchange.1 = (f32[8,128,128]{2,1,0:T(8,128)S(1)}, bf16[8,128,128]{2,1,0:T(8,128)(2,1)S(1)}, bf16[4,128,128]{2,1,0:T(8,128)(2,1)S(1)}) custom-call(s32[1]{0:T(128)} %bitcast.here_ref, s32[1]{0:T(128)} %bitcast.1.aux_ref, s32[8,128]{1,0:T(8,128)S(1)} %get-tuple-element.34.index_ref, bf16[576,128]{1,0:T(8,128)(2,1)S(1)} %partner_sum.1.total_ref, ...), custom_call_target="tpu_custom_call" | custom-call | flops 134217728 | bytes 2621440 | tf_op jit(solution)/shard_map/exchange/pallas_call | solution.py:323
  33.5 0.1 collective-permute-start.11
  33.5 3.6 %collective-permute-start.10 = (bf16[8,128,128]{2,1,0:T(8,128)(2,1)S(1)}, bf16[8,128,128]{2,1,0:T(8,128)(2,1)S(1)}, u32[]{:S(2)}, u32[]{:S(2)}) collective-permute-start(bf16[8,128,128]{2,1,0:T(8,128)(2,1)S(1)} %get-tuple-element.51.refs_0_), channel_id=1, source_target_pairs={{4,0},{8,12},{5,9},{9,5},{6,2},{10,14},{7,11},{11,7},{20,16},{24,2... | collective-permute-start | bytes 786440 | tf_op jit(solution)/shard_map/ppermute | solution.py:568
  37.2 1.3 %collective-permute-start.9 = (bf16[8,128,128]{2,1,0:T(8,128)(2,1)S(1)}, bf16[8,128,128]{2,1,0:T(8,128)(2,1)S(1)}, u32[]{:S(2)}, u32[]{:S(2)}) collective-permute-start(bf16[8,128,128]{2,1,0:T(8,128)(2,1)S(1)} %get-tuple-element.51.refs_0_), channel_id=1, source_target_pairs={{4,8},{8,4},{5,1},{9,13},{6,10},{10,6},{7,3},{11,15},{20,24},{24,2... | collective-permute-start | bytes 786440 | tf_op jit(solution)/shard_map/ppermute | solution.py:568
  38.5 3.0 %collective-permute-start.8 = (bf16[8,128,128]{2,1,0:T(8,128)(2,1)S(1)}, bf16[8,128,128]{2,1,0:T(8,128)(2,1)S(1)}, u32[]{:S(2)}, u32[]{:S(2)}) collective-permute-start(bf16[8,128,128]{2,1,0:T(8,128)(2,1)S(1)} %get-tuple-element.51.refs_0_), channel_id=1, source_target_pairs={{0,1},{1,0},{2,3},{3,2},{4,5},{5,4},{6,7},{7,6},{8,9},{9,8},{10,11... | collective-permute-start | bytes 786440 | tf_op jit(solution)/shard_map/ppermute | solution.py:559
  41.5 0.1 collective-permute-start.12
  41.6 0.2 collective-permute-start.14
  41.8 1.1 %collective-permute-done.12.piece_ref.refs_5_ = bf16[4,128,128]{2,1,0:T(8,128)(2,1)S(1)} collective-permute-done((bf16[4,128,128]{2,1,0:T(8,128)(2,1)S(1)}, bf16[4,128,128]{2,1,0:T(8,128)(2,1)S(1)}, u32[]{:S(2)}, u32[]{:S(2)}) %collective-permute-start.12) | collective-permute-done | bytes 131104 | tf_op jit(solution)/shard_map/ppermute | solution.py:559
  42.8 1.1 %collective-permute-done.9.left_ref = bf16[8,128,128]{2,1,0:T(8,128)(2,1)S(1)} collective-permute-done((bf16[8,128,128]{2,1,0:T(8,128)(2,1)S(1)}, bf16[8,128,128]{2,1,0:T(8,128)(2,1)S(1)}, u32[]{:S(2)}, u32[]{:S(2)}) %collective-permute-start.9) | collective-permute-done | bytes 262176 | tf_op jit(solution)/shard_map/ppermute | solution.py:568
  43.9 0.1 joined.2.refs_2_
  44.0 1.9 %collective-permute-start.13 = (bf16[8,128,128]{2,1,0:T(8,128)(2,1)S(1)}, bf16[8,128,128]{2,1,0:T(8,128)(2,1)S(1)}, u32[]{:S(2)}, u32[]{:S(2)}) collective-permute-start(bf16[8,128,128]{2,1,0:T(8,128)(2,1)S(1)} %joined.2.refs_2_), channel_id=1, source_target_pairs={{0,1},{1,0},{2,3},{3,2},{4,5},{5,4},{6,7},{7,6},{8,9},{9,8},{10,11... | collective-permute-start | bytes 786440 | tf_op jit(solution)/shard_map/ppermute | solution.py:559
  45.9 0.3 collective-permute-done.14.refs_6_
  46.2 1.3 %collective-permute-start.15 = (bf16[4,128,128]{2,1,0:T(8,128)(2,1)S(1)}, bf16[4,128,128]{2,1,0:T(8,128)(2,1)S(1)}, u32[]{:S(2)}, u32[]{:S(2)}) collective-permute-start(bf16[4,128,128]{2,1,0:T(8,128)(2,1)S(1)} %collective-permute-done.14.refs_6_), channel_id=1, source_target_pairs={{0,1},{1,0},{2,3},{3,2},{4,5},{5,4},{6,7},{7,6},{8,9},{9,8},{10,11... | collective-permute-start | bytes 393224 | tf_op jit(solution)/shard_map/ppermute | solution.py:559
  47.5 1.0 %collective-permute-done.15.refs_7_ = bf16[4,128,128]{2,1,0:T(8,128)(2,1)S(1)} collective-permute-done((bf16[4,128,128]{2,1,0:T(8,128)(2,1)S(1)}, bf16[4,128,128]{2,1,0:T(8,128)(2,1)S(1)}, u32[]{:S(2)}, u32[]{:S(2)}) %collective-permute-start.15) | collective-permute-done | bytes 131104 | tf_op jit(solution)/shard_map/ppermute | solution.py:559
  48.5 1.2 %sweep.1 = (bf16[8,128,128]{2,1,0:T(8,128)(2,1)S(1)}, bf16[4,128,128]{2,1,0:T(8,128)(2,1)S(1)}) custom-call(s32[1]{0:T(128)} %bitcast.here_ref, s32[1]{0:T(128)} %bitcast.1.aux_ref, s32[8,128]{1,0:T(8,128)S(1)} %get-tuple-element.34.index_ref, f32[8,128]{1,0:T(8,128)S(1)} %get-tuple-element.35.weight_ref, ...), custom_call_target="tpu_custom_call" | custom-call | flops 268435456 | bytes 2883584 | tf_op jit(solution)/shard_map/sweep/pallas_call | solution.py:414
  49.7 0.8 %collective-permute-start.19 = (bf16[4,128,128]{2,1,0:T(8,128)(2,1)S(1)}, bf16[4,128,128]{2,1,0:T(8,128)(2,1)S(1)}, u32[]{:S(2)}, u32[]{:S(2)}) collective-permute-start(bf16[4,128,128]{2,1,0:T(8,128)(2,1)S(1)} %get-tuple-element.55), channel_id=1, source_target_pairs={{4,12},{8,0},{0,4},{12,8},{5,13},{9,1},{1,5},{13,9},{6,14},{10,2},... | collective-permute-start | bytes 393224 | tf_op jit(solution)/shard_map/ppermute | solution.py:635
  50.4 1.9 %collective-permute-start.18 = (bf16[8,128,128]{2,1,0:T(8,128)(2,1)S(1)}, bf16[8,128,128]{2,1,0:T(8,128)(2,1)S(1)}, u32[]{:S(2)}, u32[]{:S(2)}) collective-permute-start(bf16[8,128,128]{2,1,0:T(8,128)(2,1)S(1)} %get-tuple-element.54.refs_0_), channel_id=1, source_target_pairs={{4,0},{8,12},{5,9},{9,5},{6,2},{10,14},{7,11},{11,7},{20,16},{24,2... | collective-permute-start | bytes 786440 | tf_op jit(solution)/shard_map/ppermute | solution.py:568
  52.4 1.4 %collective-permute-start.17 = (bf16[8,128,128]{2,1,0:T(8,128)(2,1)S(1)}, bf16[8,128,128]{2,1,0:T(8,128)(2,1)S(1)}, u32[]{:S(2)}, u32[]{:S(2)}) collective-permute-start(bf16[8,128,128]{2,1,0:T(8,128)(2,1)S(1)} %get-tuple-element.54.refs_0_), channel_id=1, source_target_pairs={{4,8},{8,4},{5,1},{9,13},{6,10},{10,6},{7,3},{11,15},{20,24},{24,2... | collective-permute-start | bytes 786440 | tf_op jit(solution)/shard_map/ppermute | solution.py:568
  53.8 3.0 %collective-permute-start.16 = (bf16[8,128,128]{2,1,0:T(8,128)(2,1)S(1)}, bf16[8,128,128]{2,1,0:T(8,128)(2,1)S(1)}, u32[]{:S(2)}, u32[]{:S(2)}) collective-permute-start(bf16[8,128,128]{2,1,0:T(8,128)(2,1)S(1)} %get-tuple-element.54.refs_0_), channel_id=1, source_target_pairs={{0,1},{1,0},{2,3},{3,2},{4,5},{5,4},{6,7},{7,6},{8,9},{9,8},{10,11... | collective-permute-start | bytes 786440 | tf_op jit(solution)/shard_map/ppermute | solution.py:559
  56.8 0.1 collective-permute-start.20
  56.9 0.2 collective-permute-start.22
  57.0 1.1 %collective-permute-done.20.piece_ref.refs_5_ = bf16[4,128,128]{2,1,0:T(8,128)(2,1)S(1)} collective-permute-done((bf16[4,128,128]{2,1,0:T(8,128)(2,1)S(1)}, bf16[4,128,128]{2,1,0:T(8,128)(2,1)S(1)}, u32[]{:S(2)}, u32[]{:S(2)}) %collective-permute-start.20) | collective-permute-done | bytes 131104 | tf_op jit(solution)/shard_map/ppermute | solution.py:559
  58.1 1.4 %collective-permute-done.17.left_ref = bf16[8,128,128]{2,1,0:T(8,128)(2,1)S(1)} collective-permute-done((bf16[8,128,128]{2,1,0:T(8,128)(2,1)S(1)}, bf16[8,128,128]{2,1,0:T(8,128)(2,1)S(1)}, u32[]{:S(2)}, u32[]{:S(2)}) %collective-permute-start.17) | collective-permute-done | bytes 262176 | tf_op jit(solution)/shard_map/ppermute | solution.py:568
  59.5 0.1 joined.3.refs_2_
  59.6 2.8 %collective-permute-start.21 = (bf16[8,128,128]{2,1,0:T(8,128)(2,1)S(1)}, bf16[8,128,128]{2,1,0:T(8,128)(2,1)S(1)}, u32[]{:S(2)}, u32[]{:S(2)}) collective-permute-start(bf16[8,128,128]{2,1,0:T(8,128)(2,1)S(1)} %joined.3.refs_2_), channel_id=1, source_target_pairs={{0,1},{1,0},{2,3},{3,2},{4,5},{5,4},{6,7},{7,6},{8,9},{9,8},{10,11... | collective-permute-start | bytes 786440 | tf_op jit(solution)/shard_map/ppermute | solution.py:559
  62.4 0.4 collective-permute-start.23
  62.8 1.0 %collective-permute-done.23.refs_7_ = bf16[4,128,128]{2,1,0:T(8,128)(2,1)S(1)} collective-permute-done((bf16[4,128,128]{2,1,0:T(8,128)(2,1)S(1)}, bf16[4,128,128]{2,1,0:T(8,128)(2,1)S(1)}, u32[]{:S(2)}, u32[]{:S(2)}) %collective-permute-start.23) | collective-permute-done | bytes 131104 | tf_op jit(solution)/shard_map/ppermute | solution.py:559
  63.8 2.5 %last_sweep.1 = (f32[8,128,128]{2,1,0:T(8,128)S(1)}, f32[2,128,128]{2,1,0:T(8,128)S(1)}, bf16[2,128,128]{2,1,0:T(8,128)(2,1)S(1)}, bf16[2,128,128]{2,1,0:T(8,128)(2,1)S(1)}) custom-call(s32[1]{0:T(128)} %bitcast.here_ref, s32[1]{0:T(128)} %bitcast.1.aux_ref, s32[8,128]{1,0:T(8,128)S(1)} %get-tuple-element.34.index_ref, ...), custom_call_target="tpu_custom_call" | custom-call | flops 268435456 | bytes 2883584 | tf_op jit(solution)/shard_map/last_sweep/pallas_call | solution.py:414
  66.3 0.4 collective-permute-start.24
  66.8 0.2 collective-permute-start.25
  67.0 3.2 %collective-permute-start.26 = (bf16[2,128,128]{2,1,0:T(8,128)(2,1)S(1)}, bf16[2,128,128]{2,1,0:T(8,128)(2,1)S(1)}, u32[]{:S(2)}, u32[]{:S(2)}) collective-permute-start(bf16[2,128,128]{2,1,0:T(8,128)(2,1)S(1)} %get-tuple-element.61), channel_id=1, source_target_pairs={{4,8},{8,4},{5,9},{9,5},{6,10},{10,6},{7,11},{11,7},{20,24},{24,20... | collective-permute-start | bytes 196616 | tf_op jit(solution)/shard_map/ppermute | solution.py:564
  70.1 2.4 %first_terms.1 = (f32[16,128,128]{2,1,0:T(8,128)}, f32[2,128,128]{2,1,0:T(8,128)S(1)}) custom-call(s32[1]{0:T(128)} %bitcast.1.aux_ref, s32[8,128]{1,0:T(8,128)S(1)} %get-tuple-element.34.index_ref, f32[8,128,128]{2,1,0:T(8,128)S(1)} %get-tuple-element.56.amps_ref, f32[8,128,128]{2,1,0:T(8,128)S(1)} %collective-permute-done.24.others_ref, ...), custom_call_target="tpu_custom_call" | custom-call | flops 201326592 | bytes 2097152 | tf_op jit(solution)/shard_map/first_terms/pallas_call | solution.py:490
  72.6 1.1 %collective-permute-start.27 = (f32[2,128,128]{2,1,0:T(8,128)S(1)}, f32[2,128,128]{2,1,0:T(8,128)S(1)}, u32[]{:S(2)}, u32[]{:S(2)}) collective-permute-start(f32[2,128,128]{2,1,0:T(8,128)S(1)} %convert_add_fusion), channel_id=1, source_target_pairs={{0,1},{1,0},{2,3},{3,2},{4,5},{5,4},{6,7},{7,6},{8,9},{9,8},{10,11... | collective-permute-start | bytes 393224 | tf_op jit(solution)/shard_map/ppermute | solution.py:559
  73.6 1.0 %collective-permute-done.27 = f32[2,128,128]{2,1,0:T(8,128)S(1)} collective-permute-done((f32[2,128,128]{2,1,0:T(8,128)S(1)}, f32[2,128,128]{2,1,0:T(8,128)S(1)}, u32[]{:S(2)}, u32[]{:S(2)}) %collective-permute-start.27) | collective-permute-done | bytes 131104 | tf_op jit(solution)/shard_map/ppermute | solution.py:559
  74.6 0.7 add_multiply_fusion
  (28 shorter events, 0.2 us)
Async XLA Ops:
  0.6 1.1 %copy-start.1 = (bf16[2,1536,128]{2,1,0:T(8,128)(2,1)S(1)}, bf16[2,1536,128]{2,1,0:T(8,128)(2,1)}, u32[]{:S(2)}) copy-start(bf16[2,1536,128]{2,1,0:T(8,128)(2,1)} %ints_ref) | copy-start | bytes 2359300
  2.0 29.3 %copy-start.5 = (s32[64,4]{0,1:T(4,128)S(1)}, s32[64,4]{0,1:T(4,128)}, u32[]{:S(2)}) copy-start(s32[64,4]{0,1:T(4,128)} %param.19) | copy-start | bytes 3076
  2.0 29.3 %copy-start.6 = (f32[16,4]{0,1:T(4,128)S(1)}, f32[16,4]{0,1:T(4,128)}, u32[]{:S(2)}) copy-start(f32[16,4]{0,1:T(4,128)} %param.14) | copy-start | bytes 772
  2.0 29.3 %copy-start.7 = (s32[16,2]{0,1:T(2,128)S(1)}, s32[16,2]{0,1:T(2,128)}, u32[]{:S(2)}) copy-start(s32[16,2]{0,1:T(2,128)} %param.18) | copy-start | bytes 388
  2.0 10.2 %collective-permute-start = (bf16[2,768,128]{2,1,0:T(8,128)(2,1)S(1)}, bf16[2,768,128]{2,1,0:T(8,128)(2,1)S(1)}, u32[]{:S(2)}, u32[]{:S(2)}) collective-permute-start(bf16[2,768,128]{2,1,0:T(8,128)(2,1)S(1)} %get-tuple-element.37.own_one_ref), channel_id=1, source_target_pairs={{0,4},{4,0},{8,12},{12,8},{5,9},{9,5},{2,6},{6,2},{10,14},{14,10},... | collective-permute-start | bytes 1179656 | tf_op jit(solution)/shard_map/ppermute | solution.py:568
  5.4 10.7 %collective-permute-start.1 = (bf16[2,768,128]{2,1,0:T(8,128)(2,1)S(1)}, bf16[2,768,128]{2,1,0:T(8,128)(2,1)S(1)}, u32[]{:S(2)}, u32[]{:S(2)}) collective-permute-start(bf16[2,768,128]{2,1,0:T(8,128)(2,1)S(1)} %get-tuple-element.38.own_two_ref), channel_id=1, source_target_pairs={{4,8},{8,4},{1,5},{5,1},{9,13},{13,9},{6,10},{10,6},{3,7},{7,3},{1... | collective-permute-start | bytes 1179656 | tf_op jit(solution)/shard_map/ppermute | solution.py:568
  7.3 1.0 %copy-start.2 = (bf16[16,128,128]{2,1,0:T(8,128)(2,1)S(1)}, bf16[16,128,128]{2,1,0:T(8,128)(2,1)}, u32[]{:S(2)}) copy-start(bf16[16,128,128]{2,1,0:T(8,128)(2,1)} %first_ref.1) | copy-start | bytes 1572868
  8.4 1.0 %copy-start.3 = (bf16[16,128,128]{2,1,0:T(8,128)(2,1)S(1)}, bf16[16,128,128]{2,1,0:T(8,128)(2,1)}, u32[]{:S(2)}) copy-start(bf16[16,128,128]{2,1,0:T(8,128)(2,1)} %second_ref.1) | copy-start | bytes 1572868
  9.4 0.7 copy-start.4
  10.1 0.7 copy-start.8
  10.8 0.7 copy-start.9
  16.6 1.6 %collective-permute-start.2 = (f32[576,128]{1,0:T(8,128)S(1)}, f32[576,128]{1,0:T(8,128)S(1)}, u32[]{:S(2)}, u32[]{:S(2)}) collective-permute-start(f32[576,128]{1,0:T(8,128)S(1)} %get-tuple-element.44), channel_id=1, source_target_pairs={{0,1},{1,0},{2,3},{3,2},{4,5},{5,4},{6,7},{7,6},{8,9},{9,8},{10,11... | collective-permute-start | bytes 884744 | tf_op jit(solution)/shard_map/ppermute | solution.py:559
  18.3 4.5 %collective-permute-start.3 = (bf16[256,128]{1,0:T(8,128)(2,1)S(1)}, bf16[256,128]{1,0:T(8,128)(2,1)S(1)}, u32[]{:S(2)}, u32[]{:S(2)}) collective-permute-start(bf16[256,128]{1,0:T(8,128)(2,1)S(1)} %get-tuple-element.46), channel_id=1, source_target_pairs={{0,4},{4,0},{8,12},{12,8},{1,5},{5,1},{9,13},{13,9},{2,6},{6,2},{1... | collective-permute-start | bytes 196616 | tf_op jit(solution)/shard_map/ppermute | solution.py:564
  18.6 6.0 %collective-permute-start.4 = (bf16[256,128]{1,0:T(8,128)(2,1)S(1)}, bf16[256,128]{1,0:T(8,128)(2,1)S(1)}, u32[]{:S(2)}, u32[]{:S(2)}) collective-permute-start(bf16[256,128]{1,0:T(8,128)(2,1)S(1)} %get-tuple-element.47), channel_id=1, source_target_pairs={{4,8},{8,4},{5,9},{9,5},{6,10},{10,6},{7,11},{11,7},{20,24},{24,20... | collective-permute-start | bytes 196616 | tf_op jit(solution)/shard_map/ppermute | solution.py:564
  24.6 4.1 %collective-permute-start.5 = (bf16[576,128]{1,0:T(8,128)(2,1)S(1)}, bf16[576,128]{1,0:T(8,128)(2,1)S(1)}, u32[]{:S(2)}, u32[]{:S(2)}) collective-permute-start(bf16[576,128]{1,0:T(8,128)(2,1)S(1)} %partner_sum.1.total_ref), channel_id=1, source_target_pairs={{0,2},{1,3},{2,0},{3,1},{4,6},{5,7},{6,4},{7,5},{8,10},{9,11},{10,... | collective-permute-start | bytes 442376 | tf_op jit(solution)/shard_map/ppermute | solution.py:559
  24.9 7.8 %collective-permute-start.6 = (bf16[576,128]{1,0:T(8,128)(2,1)S(1)}, bf16[576,128]{1,0:T(8,128)(2,1)S(1)}, u32[]{:S(2)}, u32[]{:S(2)}) collective-permute-start(bf16[576,128]{1,0:T(8,128)(2,1)S(1)} %partner_sum.1.total_ref), channel_id=1, source_target_pairs={{0,1},{1,0},{2,3},{3,2},{4,5},{5,4},{6,7},{7,6},{8,9},{9,8},{10,11... | collective-permute-start | bytes 442376 | tf_op jit(solution)/shard_map/ppermute | solution.py:559
  28.6 4.0 %collective-permute-start.7 = (bf16[576,128]{1,0:T(8,128)(2,1)S(1)}, bf16[576,128]{1,0:T(8,128)(2,1)S(1)}, u32[]{:S(2)}, u32[]{:S(2)}) collective-permute-start(bf16[576,128]{1,0:T(8,128)(2,1)S(1)} %collective-permute-done.5.far_ref), channel_id=1, source_target_pairs={{0,1},{1,0},{2,3},{3,2},{4,5},{5,4},{6,7},{7,6},{8,9},{9,8},{10,11... | collective-permute-start | bytes 442376 | tf_op jit(solution)/shard_map/ppermute | solution.py:559
  33.5 8.0 %collective-permute-start.11 = (bf16[4,128,128]{2,1,0:T(8,128)(2,1)S(1)}, bf16[4,128,128]{2,1,0:T(8,128)(2,1)S(1)}, u32[]{:S(2)}, u32[]{:S(2)}) collective-permute-start(bf16[4,128,128]{2,1,0:T(8,128)(2,1)S(1)} %get-tuple-element.52), channel_id=1, source_target_pairs={{4,12},{8,0},{0,4},{12,8},{5,13},{9,1},{1,5},{13,9},{6,14},{10,2},... | collective-permute-start | bytes 393224 | tf_op jit(solution)/shard_map/ppermute | solution.py:635
  33.5 9.3 %collective-permute-start.10 = (bf16[8,128,128]{2,1,0:T(8,128)(2,1)S(1)}, bf16[8,128,128]{2,1,0:T(8,128)(2,1)S(1)}, u32[]{:S(2)}, u32[]{:S(2)}) collective-permute-start(bf16[8,128,128]{2,1,0:T(8,128)(2,1)S(1)} %get-tuple-element.51.refs_0_), channel_id=1, source_target_pairs={{4,0},{8,12},{5,9},{9,5},{6,2},{10,14},{7,11},{11,7},{20,16},{24,2... | collective-permute-start | bytes 786440 | tf_op jit(solution)/shard_map/ppermute | solution.py:568
  37.2 6.7 %collective-permute-start.9 = (bf16[8,128,128]{2,1,0:T(8,128)(2,1)S(1)}, bf16[8,128,128]{2,1,0:T(8,128)(2,1)S(1)}, u32[]{:S(2)}, u32[]{:S(2)}) collective-permute-start(bf16[8,128,128]{2,1,0:T(8,128)(2,1)S(1)} %get-tuple-element.51.refs_0_), channel_id=1, source_target_pairs={{4,8},{8,4},{5,1},{9,13},{6,10},{10,6},{7,3},{11,15},{20,24},{24,2... | collective-permute-start | bytes 786440 | tf_op jit(solution)/shard_map/ppermute | solution.py:568
  38.5 9.0 %collective-permute-start.8 = (bf16[8,128,128]{2,1,0:T(8,128)(2,1)S(1)}, bf16[8,128,128]{2,1,0:T(8,128)(2,1)S(1)}, u32[]{:S(2)}, u32[]{:S(2)}) collective-permute-start(bf16[8,128,128]{2,1,0:T(8,128)(2,1)S(1)} %get-tuple-element.51.refs_0_), channel_id=1, source_target_pairs={{0,1},{1,0},{2,3},{3,2},{4,5},{5,4},{6,7},{7,6},{8,9},{9,8},{10,11... | collective-permute-start | bytes 786440 | tf_op jit(solution)/shard_map/ppermute | solution.py:559
  41.5 1.3 %collective-permute-start.12 = (bf16[4,128,128]{2,1,0:T(8,128)(2,1)S(1)}, bf16[4,128,128]{2,1,0:T(8,128)(2,1)S(1)}, u32[]{:S(2)}, u32[]{:S(2)}) collective-permute-start(bf16[4,128,128]{2,1,0:T(8,128)(2,1)S(1)} %collective-permute-done.11.piece_ref.refs_4_), channel_id=1, source_target_pairs={{0,1},{1,0},{2,3},{3,2},{4,5},{5,4},{6,7},{7,6},{8,9},{9,8},{10,11... | collective-permute-start | bytes 393224 | tf_op jit(solution)/shard_map/ppermute | solution.py:559
  41.6 6.9 %copy-start = (bf16[16,4,128,128]{3,2,1,0:T(8,128)(2,1)S(1)}, bf16[16,4,128,128]{3,2,1,0:T(8,128)(2,1)}, u32[]{:S(2)}) copy-start(bf16[16,4,128,128]{3,2,1,0:T(8,128)(2,1)} %refs_8_.3) | copy-start | bytes 6291460
  41.6 4.6 %collective-permute-start.14 = (bf16[4,128,128]{2,1,0:T(8,128)(2,1)S(1)}, bf16[4,128,128]{2,1,0:T(8,128)(2,1)S(1)}, u32[]{:S(2)}, u32[]{:S(2)}) collective-permute-start(bf16[4,128,128]{2,1,0:T(8,128)(2,1)S(1)} %collective-permute-done.11.piece_ref.refs_4_), channel_id=1, source_target_pairs={{0,2},{1,3},{2,0},{3,1},{4,6},{5,7},{6,4},{7,5},{8,10},{9,11},{10,... | collective-permute-start | bytes 393224 | tf_op jit(solution)/shard_map/ppermute | solution.py:559
  44.0 4.5 %collective-permute-start.13 = (bf16[8,128,128]{2,1,0:T(8,128)(2,1)S(1)}, bf16[8,128,128]{2,1,0:T(8,128)(2,1)S(1)}, u32[]{:S(2)}, u32[]{:S(2)}) collective-permute-start(bf16[8,128,128]{2,1,0:T(8,128)(2,1)S(1)} %joined.2.refs_2_), channel_id=1, source_target_pairs={{0,1},{1,0},{2,3},{3,2},{4,5},{5,4},{6,7},{7,6},{8,9},{9,8},{10,11... | collective-permute-start | bytes 786440 | tf_op jit(solution)/shard_map/ppermute | solution.py:559
  46.2 2.3 %collective-permute-start.15 = (bf16[4,128,128]{2,1,0:T(8,128)(2,1)S(1)}, bf16[4,128,128]{2,1,0:T(8,128)(2,1)S(1)}, u32[]{:S(2)}, u32[]{:S(2)}) collective-permute-start(bf16[4,128,128]{2,1,0:T(8,128)(2,1)S(1)} %collective-permute-done.14.refs_6_), channel_id=1, source_target_pairs={{0,1},{1,0},{2,3},{3,2},{4,5},{5,4},{6,7},{7,6},{8,9},{9,8},{10,11... | collective-permute-start | bytes 393224 | tf_op jit(solution)/shard_map/ppermute | solution.py:559
  49.7 7.1 %collective-permute-start.19 = (bf16[4,128,128]{2,1,0:T(8,128)(2,1)S(1)}, bf16[4,128,128]{2,1,0:T(8,128)(2,1)S(1)}, u32[]{:S(2)}, u32[]{:S(2)}) collective-permute-start(bf16[4,128,128]{2,1,0:T(8,128)(2,1)S(1)} %get-tuple-element.55), channel_id=1, source_target_pairs={{4,12},{8,0},{0,4},{12,8},{5,13},{9,1},{1,5},{13,9},{6,14},{10,2},... | collective-permute-start | bytes 393224 | tf_op jit(solution)/shard_map/ppermute | solution.py:635
  50.4 7.7 %collective-permute-start.18 = (bf16[8,128,128]{2,1,0:T(8,128)(2,1)S(1)}, bf16[8,128,128]{2,1,0:T(8,128)(2,1)S(1)}, u32[]{:S(2)}, u32[]{:S(2)}) collective-permute-start(bf16[8,128,128]{2,1,0:T(8,128)(2,1)S(1)} %get-tuple-element.54.refs_0_), channel_id=1, source_target_pairs={{4,0},{8,12},{5,9},{9,5},{6,2},{10,14},{7,11},{11,7},{20,16},{24,2... | collective-permute-start | bytes 786440 | tf_op jit(solution)/shard_map/ppermute | solution.py:568
  52.4 7.2 %collective-permute-start.17 = (bf16[8,128,128]{2,1,0:T(8,128)(2,1)S(1)}, bf16[8,128,128]{2,1,0:T(8,128)(2,1)S(1)}, u32[]{:S(2)}, u32[]{:S(2)}) collective-permute-start(bf16[8,128,128]{2,1,0:T(8,128)(2,1)S(1)} %get-tuple-element.54.refs_0_), channel_id=1, source_target_pairs={{4,8},{8,4},{5,1},{9,13},{6,10},{10,6},{7,3},{11,15},{20,24},{24,2... | collective-permute-start | bytes 786440 | tf_op jit(solution)/shard_map/ppermute | solution.py:568
  53.8 9.0 %collective-permute-start.16 = (bf16[8,128,128]{2,1,0:T(8,128)(2,1)S(1)}, bf16[8,128,128]{2,1,0:T(8,128)(2,1)S(1)}, u32[]{:S(2)}, u32[]{:S(2)}) collective-permute-start(bf16[8,128,128]{2,1,0:T(8,128)(2,1)S(1)} %get-tuple-element.54.refs_0_), channel_id=1, source_target_pairs={{0,1},{1,0},{2,3},{3,2},{4,5},{5,4},{6,7},{7,6},{8,9},{9,8},{10,11... | collective-permute-start | bytes 786440 | tf_op jit(solution)/shard_map/ppermute | solution.py:559
  56.8 1.3 %collective-permute-start.20 = (bf16[4,128,128]{2,1,0:T(8,128)(2,1)S(1)}, bf16[4,128,128]{2,1,0:T(8,128)(2,1)S(1)}, u32[]{:S(2)}, u32[]{:S(2)}) collective-permute-start(bf16[4,128,128]{2,1,0:T(8,128)(2,1)S(1)} %collective-permute-done.19.piece_ref.refs_4_), channel_id=1, source_target_pairs={{0,1},{1,0},{2,3},{3,2},{4,5},{5,4},{6,7},{7,6},{8,9},{9,8},{10,11... | collective-permute-start | bytes 393224 | tf_op jit(solution)/shard_map/ppermute | solution.py:559
  56.9 5.5 %collective-permute-start.22 = (bf16[4,128,128]{2,1,0:T(8,128)(2,1)S(1)}, bf16[4,128,128]{2,1,0:T(8,128)(2,1)S(1)}, u32[]{:S(2)}, u32[]{:S(2)}) collective-permute-start(bf16[4,128,128]{2,1,0:T(8,128)(2,1)S(1)} %collective-permute-done.19.piece_ref.refs_4_), channel_id=1, source_target_pairs={{0,2},{1,3},{2,0},{3,1},{4,6},{5,7},{6,4},{7,5},{8,10},{9,11},{10,... | collective-permute-start | bytes 393224 | tf_op jit(solution)/shard_map/ppermute | solution.py:559
  59.6 4.2 %collective-permute-start.21 = (bf16[8,128,128]{2,1,0:T(8,128)(2,1)S(1)}, bf16[8,128,128]{2,1,0:T(8,128)(2,1)S(1)}, u32[]{:S(2)}, u32[]{:S(2)}) collective-permute-start(bf16[8,128,128]{2,1,0:T(8,128)(2,1)S(1)} %joined.3.refs_2_), channel_id=1, source_target_pairs={{0,1},{1,0},{2,3},{3,2},{4,5},{5,4},{6,7},{7,6},{8,9},{9,8},{10,11... | collective-permute-start | bytes 786440 | tf_op jit(solution)/shard_map/ppermute | solution.py:559
  62.4 1.4 %collective-permute-start.23 = (bf16[4,128,128]{2,1,0:T(8,128)(2,1)S(1)}, bf16[4,128,128]{2,1,0:T(8,128)(2,1)S(1)}, u32[]{:S(2)}, u32[]{:S(2)}) collective-permute-start(bf16[4,128,128]{2,1,0:T(8,128)(2,1)S(1)} %collective-permute-done.22.refs_6_), channel_id=1, source_target_pairs={{0,1},{1,0},{2,3},{3,2},{4,5},{5,4},{6,7},{7,6},{8,9},{9,8},{10,11... | collective-permute-start | bytes 393224 | tf_op jit(solution)/shard_map/ppermute | solution.py:559
  66.3 3.8 %collective-permute-start.24 = (f32[8,128,128]{2,1,0:T(8,128)S(1)}, f32[8,128,128]{2,1,0:T(8,128)S(1)}, u32[]{:S(2)}, u32[]{:S(2)}) collective-permute-start(f32[8,128,128]{2,1,0:T(8,128)S(1)} %get-tuple-element.56.amps_ref), channel_id=1, source_target_pairs={{0,1},{1,0},{2,3},{3,2},{4,5},{5,4},{6,7},{7,6},{8,9},{9,8},{10,11... | collective-permute-start | bytes 1572872 | tf_op jit(solution)/shard_map/ppermute | solution.py:559
  66.8 5.8 %collective-permute-start.25 = (bf16[2,128,128]{2,1,0:T(8,128)(2,1)S(1)}, bf16[2,128,128]{2,1,0:T(8,128)(2,1)S(1)}, u32[]{:S(2)}, u32[]{:S(2)}) collective-permute-start(bf16[2,128,128]{2,1,0:T(8,128)(2,1)S(1)} %get-tuple-element.60), channel_id=1, source_target_pairs={{0,4},{4,0},{8,12},{12,8},{1,5},{5,1},{9,13},{13,9},{2,6},{6,2},{1... | collective-permute-start | bytes 196616 | tf_op jit(solution)/shard_map/ppermute | solution.py:564
  67.0 5.6 %collective-permute-start.26 = (bf16[2,128,128]{2,1,0:T(8,128)(2,1)S(1)}, bf16[2,128,128]{2,1,0:T(8,128)(2,1)S(1)}, u32[]{:S(2)}, u32[]{:S(2)}) collective-permute-start(bf16[2,128,128]{2,1,0:T(8,128)(2,1)S(1)} %get-tuple-element.61), channel_id=1, source_target_pairs={{4,8},{8,4},{5,9},{9,5},{6,10},{10,6},{7,11},{11,7},{20,24},{24,20... | collective-permute-start | bytes 196616 | tf_op jit(solution)/shard_map/ppermute | solution.py:564
  72.6 2.1 %collective-permute-start.27 = (f32[2,128,128]{2,1,0:T(8,128)S(1)}, f32[2,128,128]{2,1,0:T(8,128)S(1)}, u32[]{:S(2)}, u32[]{:S(2)}) collective-permute-start(f32[2,128,128]{2,1,0:T(8,128)S(1)} %convert_add_fusion), channel_id=1, source_target_pairs={{0,1},{1,0},{2,3},{3,2},{4,5},{5,4},{6,7},{7,6},{8,9},{9,8},{10,11... | collective-permute-start | bytes 393224 | tf_op jit(solution)/shard_map/ppermute | solution.py:559

commit v7 on v6

--- a/solution.py
+++ b/solution.py
@@ -43,8 +43,8 @@
 
 
 def prepare_kernel(
-    aux_ref, occ_ref, used_ref, energy_ref, first_ref, second_ref,
-    first_out, second_out, factor_ref, sems,
+    aux_ref, occ_ref, used_ref, energy_ref, first_ref, second_ref, ints_ref,
+    first_out, second_out, ints_out, factor_ref, sems,
 ):
     count, width, _ = factor_ref.shape
     half = lax.rem(aux_ref[0], 2)
@@ -52,6 +52,7 @@
     copies = [
         pltpu.make_async_copy(first_ref.at[rows], first_out, sems.at[0]),
         pltpu.make_async_copy(second_ref.at[rows], second_out, sems.at[1]),
+        pltpu.make_async_copy(ints_ref, ints_out, sems.at[2]),
     ]
     for copy in copies:
         copy.start()
@@ -68,7 +69,7 @@
         copy.wait()
 
 
-def prepare(aux, occupied, used, energy, first, second):
+def prepare(aux, occupied, used, energy, first, second, ints):
     pair_dev, width, _ = first.shape
     shape = (pair_dev // 2, width, width)
     return pl.pallas_call(
@@ -76,46 +77,16 @@
         out_shape=(
             jax.ShapeDtypeStruct(shape, BF16),
             jax.ShapeDtypeStruct(shape, BF16),
+            jax.ShapeDtypeStruct(ints.shape, BF16),
             jax.ShapeDtypeStruct(shape, F32),
         ),
-        in_specs=[SMEM] * 3 + [VMEM] + [HBM] * 2,
-        out_specs=(VMEM,) * 3,
-        scratch_shapes=[pltpu.SemaphoreType.DMA((2,))],
+        in_specs=[SMEM] * 3 + [VMEM] + [HBM] * 3,
+        out_specs=(VMEM,) * 4,
+        scratch_shapes=[pltpu.SemaphoreType.DMA((3,))],
         compiler_params=params(8),
         cost_estimate=cost(0, 8 * pair_dev * width * width),
         name="prepare",
-    )(aux, occupied, used, energy, first, second)
-
-
-def first_is_lower(here_ref, aux_ref):
-    return lax.rem(here_ref[0] + aux_ref[0], 2)
-
-
-def halves_kernel(here_ref, aux_ref, ints_ref, one_ref, two_ref, sems):
-    depth = one_ref.shape[1]
-    odd = first_is_lower(here_ref, aux_ref)
-    copies = [
-        pltpu.make_async_copy(ints_ref.at[:, pl.ds((1 - odd) * depth, depth)], one_ref, sems.at[0]),
-        pltpu.make_async_copy(ints_ref.at[:, pl.ds(odd * depth, depth)], two_ref, sems.at[1]),
-    ]
-    for copy in copies:
-        copy.start()
-    for copy in copies:
-        copy.wait()
-
-
-def halves(here, aux, ints):
-    count, depth, width = ints.shape
-    return pl.pallas_call(
-        halves_kernel,
-        out_shape=(jax.ShapeDtypeStruct((count, depth // 2, width), BF16),) * 2,
-        in_specs=[SMEM, SMEM, HBM],
-        out_specs=(VMEM, VMEM),
-        scratch_shapes=[pltpu.SemaphoreType.DMA((2,))],
-        compiler_params=params(4),
-        cost_estimate=cost(0, 4 * ints.size),
-        name="halves",
-    )(here, aux, ints)
+    )(aux, occupied, used, energy, first, second, ints)
 
 
 PRODUCT, FIRST, SECOND = 4, 5, 6
@@ -183,95 +154,55 @@
     )(here, aux, orbitals, near, couple)
 
 
-def product_kernel(
-    here_ref, aux_ref, own_one_ref, own_two_ref, one_ref, two_ref, kept_ref, sent_ref, full_ref,
-    inner_ref,
-):
-    count, _, width = one_ref.shape
-    odd = first_is_lower(here_ref, aux_ref)
-    side = lax.rem(aux_ref[0], 2)
-    rows_each = count * width
-    for r, (own_ref, near_ref) in enumerate(((own_two_ref, one_ref), (own_one_ref, two_ref))):
-        lower = odd if r == 0 else 1 - odd
-        own = jnp.concatenate([own_ref[i] for i in range(count)], axis=1)
-        near = jnp.concatenate([near_ref[i] for i in range(count)], axis=1)
-        full_ref[...] = dot(
-            jnp.where(lower == 1, near, own), jnp.where(lower == 1, own, near), ((0,), (0,))
-        )
+def product_kernel(aux_ref, own_ref, near_ref, total_ref, sent_ref):
+    count, _, width = own_ref.shape
+    second = lax.rem(aux_ref[0], 2) == 1
+    own = jnp.concatenate([own_ref[i] for i in range(count)], axis=1)
+    near = jnp.concatenate([near_ref[i] for i in range(count)], axis=1)
+    full = dot(jnp.where(second, near, own), jnp.where(second, own, near), ((0,), (0,)))
+    at = 0
+    for i in range(count):
         for j in range(count):
-            columns = slice(j * width, (j + 1) * width)
-            for out_ref, i in ((kept_ref, side), (sent_ref, 1 - side)):
-                at = pl.multiple_of((r ^ side) * rows_each + j * width, width)
-                out_ref[pl.ds(at, width)] = full_ref[
-                    pl.ds(pl.multiple_of(i * width, width), width), columns
-                ]
-    at = 2 * rows_each
-    half = width // 2
-    inner_ref[...] = dot(own_one_ref[0], own_one_ref[1], ((0,), (0,))) + dot(
-        own_two_ref[0], own_two_ref[1], ((0,), (0,))
-    )
-    kept_ref[at:] = inner_ref[pl.ds(pl.multiple_of(side * half, half), half)]
-    sent_ref[at:] = inner_ref[pl.ds(pl.multiple_of((1 - side) * half, half), half)]
-
-
-def products(here, aux, own_one, own_two, one, two):
-    count, depth, width = one.shape
-    rows = 2 * count * width + width // 2
+            block = full[i * width : (i + 1) * width, j * width : (j + 1) * width]
+            total_ref[at : at + width] = block
+            sent_ref[at : at + width] = block.astype(BF16)
+            at += width
+    total_ref[at:] = dot(own_ref[0], own_ref[1], ((0,), (0,)))
+
+
+def products(aux, ints, near):
+    count, depth, width = ints.shape
+    rows = count * count * width
     return pl.pallas_call(
         product_kernel,
-        out_shape=(jax.ShapeDtypeStruct((rows, width), F32),) * 2,
-        in_specs=[SMEM] * 2 + [VMEM] * 4,
+        out_shape=(
+            jax.ShapeDtypeStruct((rows + width, width), F32),
+            jax.ShapeDtypeStruct((rows, width), BF16),
+        ),
+        in_specs=[SMEM] + [VMEM] * 2,
         out_specs=(VMEM, VMEM),
-        scratch_shapes=[
-            pltpu.VMEM((count * width, count * width), F32),
-            pltpu.VMEM((width, width), F32),
-        ],
         compiler_params=params(12),
-        cost_estimate=cost(20 * depth * width * width, 16 * depth * width),
+        cost_estimate=cost(10 * depth * width * width, 8 * depth * width),
         name="products",
-    )(here, aux, own_one, own_two, one, two)
-
-
-def pair_kernel(kept_ref, received_ref, total_ref, one_ref, two_ref):
-    total = kept_ref[...] + received_ref[...]
-    total_ref[...] = total
-    rows = one_ref.shape[0]
-    one_ref[...] = total[:rows].astype(BF16)
-    two_ref[...] = total[rows : 2 * rows].astype(BF16)
-
-
-def pair_sum(kept, received, rows):
-    part = jax.ShapeDtypeStruct((rows, kept.shape[1]), BF16)
-    return pl.pallas_call(
-        pair_kernel,
-        out_shape=(jax.ShapeDtypeStruct(kept.shape, F32), part, part),
-        in_specs=[VMEM] * 2,
-        out_specs=(VMEM,) * 3,
-        compiler_params=params(4),
-        cost_estimate=cost(kept.size, 16 * kept.size),
-        name="pair_sum",
-    )(kept, received)
-
-
-def partner_kernel(total_ref, one_ref, two_ref, out_ref):
-    rows = one_ref.shape[0]
-    out_ref[:rows] = (total_ref[:rows] + one_ref[...].astype(F32)).astype(BF16)
-    out_ref[rows : 2 * rows] = (
-        total_ref[rows : 2 * rows] + two_ref[...].astype(F32)
-    ).astype(BF16)
-    out_ref[2 * rows :] = total_ref[2 * rows :].astype(BF16)
-
-
-def partner_sum(total, one, two):
+    )(aux, ints, near)
+
+
+def partner_kernel(total_ref, received_ref, out_ref):
+    rows = received_ref.shape[0]
+    out_ref[:rows] = (total_ref[:rows] + received_ref[...].astype(F32)).astype(BF16)
+    out_ref[rows:] = total_ref[rows:].astype(BF16)
+
+
+def partner_sum(total, received):
     return pl.pallas_call(
         partner_kernel,
         out_shape=jax.ShapeDtypeStruct(total.shape, BF16),
-        in_specs=[VMEM] * 3,
+        in_specs=[VMEM] * 2,
         out_specs=VMEM,
         compiler_params=params(4),
         cost_estimate=cost(total.size, 8 * total.size),
         name="partner_sum",
-    )(total, one, two)
+    )(total, received)
 
 
 def own_part(aux_ref, low_ref, part_ref):
@@ -280,23 +211,23 @@
 
 
 def exchange_kernel(
-    here_ref, aux_ref, index_ref, total_ref, far_ref, total_other, far_other,
+    aux_ref, index_ref, total_ref, far_ref, total_other, far_other,
     first_ref, second_ref, factor_ref, exch_ref, low_ref, part_ref, table,
 ):
     count, width, _ = exch_ref.shape
-    half = lax.rem(aux_ref[0], 2)
-    odd = lax.rem(here_ref[0], 2) == 1
-    for i, total in (
-        (half, total_ref[...].astype(F32) + far_ref[...].astype(F32)),
-        (1 - half, total_other[...].astype(F32) + far_other[...].astype(F32)),
-    ):
+    second = lax.rem(aux_ref[0], 2) == 1
+    mine = total_ref[...].astype(F32) + far_ref[...].astype(F32)
+    others = total_other[...].astype(F32) + far_other[...].astype(F32)
+    for i in range(2):
         for j in range(2):
-            one = total[j * width : (j + 1) * width]
-            two = total[(j + 2) * width : (j + 3) * width]
-            table[i * 6 + 4 + j] = jnp.where(odd, two, one)
-            table[j * 6 + i] = jnp.where(odd, one, two).T
-        table[3, pl.ds(pl.multiple_of(i * (width // 2), width // 2), width // 2)] = total[4 * width :]
-    table[6 + 2] = table[3].T
+            at = (2 * i + j) * width
+            one = mine[at : at + width]
+            two = others[at : at + width]
+            table[i * 6 + 4 + j] = jnp.where(second, two, one)
+            table[j * 6 + i] = jnp.where(second, one, two).T
+    inner = mine[4 * width :] + others[4 * width :]
+    table[3] = inner
+    table[6 + 2] = inner.T
     for p in range(count):
         right = second_ref[p]
         left = first_ref[p]
@@ -317,7 +248,7 @@
     own_part(aux_ref, low_ref, part_ref)
 
 
-def exchange(here, aux, index, sums, first, second, factor):
+def exchange(aux, index, sums, first, second, factor):
     shape = first.shape
     count, width, _ = shape
     return pl.pallas_call(
@@ -327,13 +258,13 @@
             jax.ShapeDtypeStruct(shape, BF16),
             jax.ShapeDtypeStruct((count // 2, width, width), BF16),
         ),
-        in_specs=[SMEM] * 2 + [VMEM] * (len(sums) + 4),
+        in_specs=[SMEM] + [VMEM] * (len(sums) + 4),
         out_specs=(VMEM,) * 3,
         scratch_shapes=[pltpu.VMEM((12, width, width), F32)],
         compiler_params=params(12),
         cost_estimate=cost(8 * count * width**3, 20 * count * width * width),
         name="exchange",
-    )(here, aux, index, *sums, first, second, factor)
+    )(aux, index, *sums, first, second, factor)
 
 
 def sweep_kernel(last, pieces, here_ref, aux_ref, index_ref, weight_ref, *refs):
@@ -577,12 +508,29 @@
             for r, value in enumerate((one, two))
         ]
 
-    own_halves = halves(here_s, aux_s, ints)
-    near_one, near_two = exchanged(*own_halves, partners)
-    first, second, factor = prepare(
-        aux_s, occ_energy.T, pno_count, virt_energy, proj_first, proj_second
+    def joint(rounds):
+        return [
+            (i * aux_count + a, j * aux_count + (a ^ turn))
+            for a in range(aux_count)
+            for i, j, turn in rounds[a % 2]
+        ]
+
+    near = lax.ppermute(
+        ints,
+        ("pair", "aux"),
+        joint(
+            [
+                [(i + 1, i, 0) for i in range(groups - 1)],
+                [(i, i + 1, 0) for i in range(groups - 1)],
+            ]
+        ),
     )
-    near_one, first, second, factor = lax.optimization_barrier((near_one, first, second, factor))
+    first, second, ints, factor = prepare(
+        aux_s, occ_energy.T, pno_count, virt_energy, proj_first, proj_second, ints
+    )
+    near, first, second, ints, factor = lax.optimization_barrier(
+        (near, first, second, ints, factor)
+    )
 
     if cap < pair_dev or groups // 4 != 1 or aux_count != 4:
         rounds = None
@@ -610,16 +558,25 @@
         rounds = window_rounds(groups)
     index, weight = indices(rounds, here_s, aux_s, pair_orbitals.T, neighbours.T, couple.T)
 
-    kept, sent = products(here_s, aux_s, *own_halves, near_one, near_two)
-    total, *sent = pair_sum(kept, swap(sent), occ_dev * width)
-    total = partner_sum(total, *both(*sent))
+    total, sent = products(aux_s, ints, near)
+    received = lax.ppermute(
+        sent,
+        ("pair", "aux"),
+        joint(
+            [
+                [(i, i + 1, 1) for i in range(groups - 1)],
+                [(i + 1, i, 1) for i in range(groups - 1)],
+            ]
+        ),
+    )
+    total = partner_sum(total, received)
     step = 2
     while 2 * step < aux_count:
         total = (total.astype(F32) + swap(total, step).astype(F32)).astype(BF16)
         step *= 2
     far = swap(total, step)
     exch, low, part = exchange(
-        here_s, aux_s, index, (total, far, swap(total), swap(far)), first, second, factor
+        aux_s, index, (total, far, swap(total), swap(far)), first, second, factor
     )
 
     def gathered(low, part):

time: 75.8 us -> 72 us (0.950)
  starting transfers between devices: 41.5 us -> 37.5 us
    ppermute x0 -> x2, waiting for transfers between devices: none -> 6.94 us  [the longest x1 3.86 us: shards(): lax.ppermute(ints, ('pair', 'aux'), joint([[(i + 1, i, 0) for i in range(...]
    ppermute x0 -> x2, starting transfers between devices: none -> 6.83 us  [the longest x1 3.49 us: shards(): lax.ppermute(sent, ('pair', 'aux'), joint([[(i, i + 1, 1) for i in range(...]
    ppermute x6 -> x4, starting transfers between devices: 13.5 us -> 7.99 us  [exchanged(): lax.ppermute(value, ('pair', 'aux'), [(i * aux_count + a, j * aux_count +...]
    ppermute x2 -> x1, starting transfers between devices: 7.48 us -> 2.82 us  [both(): lax.ppermute(two, 'pair', partners[1])]
    ppermute x16 -> x15, waiting for transfers between devices: 8.97 us -> 6.43 us  [swap(): return lax.ppermute(value, 'aux', [(i, i ^ step) for i in range(aux_count)])]
    ppermute x6 -> x4, waiting for transfers between devices: 6.27 us -> 4.14 us  [exchanged(): lax.ppermute(value, ('pair', 'aux'), [(i * aux_count + a, j * aux_count +...]
    ppermute x2 -> x1, waiting for transfers between devices: 1.63 us -> 0.01 us  [both(): lax.ppermute(two, 'pair', partners[1])]
    ppermute x16 -> x15, starting transfers between devices: 19.2 us -> 18.6 us  [swap(): return lax.ppermute(value, 'aux', [(i, i ^ step) for i in range(aux_count)])]
  transfers between devices with their start and end apart: 28 -> 25, of which waited for: 12 -> 10; matrix products, arithmetic and copies ran while one was open for 0% -> 0% of each run, Pallas kernels for 6% -> 7%
where the time goes in v7:
time: 72 us; the launch traced here: 71.6 us
  starting transfers between devices  37.5 us (52%)
  waiting for transfers between devices  17.5 us (24%)
  Pallas kernels  9.75 us (14%)
  local copies, waits for them, and re-layouts  5.26 us (7%)
  between operations  0.86 us (1%)
    ppermute x15, starting transfers between devices, swap(): return lax.ppermute(value, 'aux', [(i, i ^ step) for i in range(aux_count)])  18.6 us
    ppermute x4, starting transfers between devices, exchanged(): lax.ppermute(value, ('pair', 'aux'), [(i * aux_count + a, j * aux_count +...  7.99 us
    ppermute x15, waiting for transfers between devices, swap(): return lax.ppermute(value, 'aux', [(i, i ^ step) for i in range(aux_count)])  6.43 us
    unnamed x20, local copies, waits for them, and re-layouts  5.26 us
    ppermute x4, waiting for transfers between devices, exchanged(): lax.ppermute(value, ('pair', 'aux'), [(i * aux_count + a, j * aux_count +...  4.14 us
    ppermute x1, waiting for transfers between devices, shards(): lax.ppermute(ints, ('pair', 'aux'), joint([[(i + 1, i, 0) for i in range(...  3.86 us
    pallas_call x2, Pallas kernels, sweep(): pl.pallas_call(functools.partial(sweep_kernel, last, len(parts)), out_sha...  3.71 us
    ppermute x1, starting transfers between devices, shards(): lax.ppermute(sent, ('pair', 'aux'), joint([[(i, i + 1, 1) for i in range(...  3.49 us
  transfers between devices with their start and end apart: 25, of which 10 were waited for; matrix products, arithmetic and copies ran while one was open for 0% of the time, Pallas kernels for 7%

profile of v7, /device:TPU:15, one launch (start us, length us, event | category | flops | bytes accessed | tf_op | source)
XLA Modules:
  0.0 71.6 jit_solution(4680864260006665020)
XLA Ops:
  0.7 3.3 %collective-permute-start = (bf16[2,1536,128]{2,1,0:T(8,128)(2,1)}, bf16[2,1536,128]{2,1,0:T(8,128)(2,1)S(1)}, u32[]{:S(2)}, u32[]{:S(2)}) collective-permute-start(bf16[2,1536,128]{2,1,0:T(8,128)(2,1)} %ints_ref), channel_id=1, source_target_pairs={{4,0},{8,4},{12,8},{1,5},{5,9},{9,13},{6,2},{10,6},{14,10},{3,7},{... | collective-permute-start | bytes 2359304 | tf_op jit(solution)/shard_map/ppermute | solution.py:518
  4.0 1.1 %copy-done.1 = bf16[2,1536,128]{2,1,0:T(8,128)(2,1)S(1)} copy-done((bf16[2,1536,128]{2,1,0:T(8,128)(2,1)S(1)}, bf16[2,1536,128]{2,1,0:T(8,128)(2,1)}, u32[]{:S(2)}) %copy-start.1) | copy-done | bytes 786456
  5.2 1.0 %copy-done.2 = bf16[16,128,128]{2,1,0:T(8,128)(2,1)S(1)} copy-done((bf16[16,128,128]{2,1,0:T(8,128)(2,1)S(1)}, bf16[16,128,128]{2,1,0:T(8,128)(2,1)}, u32[]{:S(2)}) %copy-start.2) | copy-done | bytes 524312
  6.2 1.0 %copy-done.3 = bf16[16,128,128]{2,1,0:T(8,128)(2,1)S(1)} copy-done((bf16[16,128,128]{2,1,0:T(8,128)(2,1)S(1)}, bf16[16,128,128]{2,1,0:T(8,128)(2,1)}, u32[]{:S(2)}) %copy-start.3) | copy-done | bytes 524312
  7.2 0.7 copy-done.4
  7.9 0.7 copy-done.7
  8.6 0.7 copy-done.9
  9.3 0.9 %prepare.1 = (bf16[8,128,128]{2,1,0:T(8,128)(2,1)S(1)}, bf16[8,128,128]{2,1,0:T(8,128)(2,1)S(1)}, bf16[2,1536,128]{2,1,0:T(8,128)(2,1)S(1)}, f32[8,128,128]{2,1,0:T(8,128)S(1)}) custom-call(s32[1]{0:T(128)} %bitcast.1.aux_ref, f32[2,16]{1,0:T(2,128)S(1)} %bitcast.8, s32[16]{0:T(128)S(1)} %copy-done.9, f32[16,128]{1,0:T(8,128)S(1)} %copy-done.4, ...), custom_call_target="tpu_custom_call" | custom-call | bytes 2097152 | tf_op jit(solution)/shard_map/prepare/pallas_call | solution.py:75
  10.2 3.9 %collective-permute-done.near_ref = bf16[2,1536,128]{2,1,0:T(8,128)(2,1)S(1)} collective-permute-done((bf16[2,1536,128]{2,1,0:T(8,128)(2,1)}, bf16[2,1536,128]{2,1,0:T(8,128)(2,1)S(1)}, u32[]{:S(2)}, u32[]{:S(2)}) %collective-permute-start) | collective-permute-done | bytes 786464 | tf_op jit(solution)/shard_map/ppermute | solution.py:518
  14.0 0.5 products.1
  14.6 3.5 %collective-permute-start.1 = (bf16[512,128]{1,0:T(8,128)(2,1)S(1)}, bf16[512,128]{1,0:T(8,128)(2,1)S(1)}, u32[]{:S(2)}, u32[]{:S(2)}) collective-permute-start(bf16[512,128]{1,0:T(8,128)(2,1)S(1)} %get-tuple-element.41), channel_id=1, source_target_pairs={{0,5},{4,9},{8,13},{5,0},{9,4},{13,8},{2,7},{6,11},{10,15},{7,2},{... | collective-permute-start | bytes 393224 | tf_op jit(solution)/shard_map/ppermute | solution.py:562
  18.1 3.1 %collective-permute-done.1.received_ref = bf16[512,128]{1,0:T(8,128)(2,1)S(1)} collective-permute-done((bf16[512,128]{1,0:T(8,128)(2,1)S(1)}, bf16[512,128]{1,0:T(8,128)(2,1)S(1)}, u32[]{:S(2)}, u32[]{:S(2)}) %collective-permute-start.1) | collective-permute-done | bytes 131104 | tf_op jit(solution)/shard_map/ppermute | solution.py:562
  21.2 0.3 collective-permute-start.2
  21.5 1.5 %collective-permute-start.3 = (bf16[640,128]{1,0:T(8,128)(2,1)S(1)}, bf16[640,128]{1,0:T(8,128)(2,1)S(1)}, u32[]{:S(2)}, u32[]{:S(2)}) collective-permute-start(bf16[640,128]{1,0:T(8,128)(2,1)S(1)} %partner_sum.1.total_ref), channel_id=1, source_target_pairs={{0,1},{1,0},{2,3},{3,2},{4,5},{5,4},{6,7},{7,6},{8,9},{9,8},{10,11... | collective-permute-start | bytes 491528 | tf_op jit(solution)/shard_map/ppermute | solution.py:490
  23.0 2.4 %collective-permute-done.2.far_ref = bf16[640,128]{1,0:T(8,128)(2,1)S(1)} collective-permute-done((bf16[640,128]{1,0:T(8,128)(2,1)S(1)}, bf16[640,128]{1,0:T(8,128)(2,1)S(1)}, u32[]{:S(2)}, u32[]{:S(2)}) %collective-permute-start.2) | collective-permute-done | bytes 163872 | tf_op jit(solution)/shard_map/ppermute | solution.py:490
  25.4 2.4 %collective-permute-start.4 = (bf16[640,128]{1,0:T(8,128)(2,1)S(1)}, bf16[640,128]{1,0:T(8,128)(2,1)S(1)}, u32[]{:S(2)}, u32[]{:S(2)}) collective-permute-start(bf16[640,128]{1,0:T(8,128)(2,1)S(1)} %collective-permute-done.2.far_ref), channel_id=1, source_target_pairs={{0,1},{1,0},{2,3},{3,2},{4,5},{5,4},{6,7},{7,6},{8,9},{9,8},{10,11... | collective-permute-start | bytes 491528 | tf_op jit(solution)/shard_map/ppermute | solution.py:490
  27.9 1.3 %indices.1 = (s32[8,128]{1,0:T(8,128)S(1)}, f32[8,128]{1,0:T(8,128)S(1)}) custom-call(s32[1]{0:T(128)} %bitcast.here_ref, s32[1]{0:T(128)} %bitcast.1.aux_ref, s32[2,16]{1,0:T(2,128)S(1)} %bitcast.9, s32[4,64]{1,0:T(4,128)S(1)} %bitcast.6, f32[4,16]{1,0:T(4,128)S(1)} %bitcast.7), custom_call_target="tpu_custom_call" | custom-call | flops 1000000 | bytes 65536 | tf_op jit(solution)/shard_map/indices/pallas_call | solution.py:143
  29.2 0.0 collective-permute-done.3.total_other
  29.2 0.0 collective-permute-done.4.far_other
  29.2 0.8 %exchange.1 = (f32[8,128,128]{2,1,0:T(8,128)S(1)}, bf16[8,128,128]{2,1,0:T(8,128)(2,1)S(1)}, bf16[4,128,128]{2,1,0:T(8,128)(2,1)S(1)}) custom-call(s32[1]{0:T(128)} %bitcast.1.aux_ref, s32[8,128]{1,0:T(8,128)S(1)} %get-tuple-element.31.index_ref, bf16[640,128]{1,0:T(8,128)(2,1)S(1)} %partner_sum.1.total_ref, ...), custom_call_target="tpu_custom_call" | custom-call | flops 134217728 | bytes 2621440 | tf_op jit(solution)/shard_map/exchange/pallas_call | solution.py:254
  30.0 0.1 collective-permute-start.8
  30.1 3.2 %collective-permute-start.7 = (bf16[8,128,128]{2,1,0:T(8,128)(2,1)S(1)}, bf16[8,128,128]{2,1,0:T(8,128)(2,1)S(1)}, u32[]{:S(2)}, u32[]{:S(2)}) collective-permute-start(bf16[8,128,128]{2,1,0:T(8,128)(2,1)S(1)} %get-tuple-element.45.refs_0_), channel_id=1, source_target_pairs={{4,0},{8,12},{5,9},{9,5},{6,2},{10,14},{7,11},{11,7},{20,16},{24,2... | collective-permute-start | bytes 786440 | tf_op jit(solution)/shard_map/ppermute | solution.py:499
  33.3 1.3 %collective-permute-start.6 = (bf16[8,128,128]{2,1,0:T(8,128)(2,1)S(1)}, bf16[8,128,128]{2,1,0:T(8,128)(2,1)S(1)}, u32[]{:S(2)}, u32[]{:S(2)}) collective-permute-start(bf16[8,128,128]{2,1,0:T(8,128)(2,1)S(1)} %get-tuple-element.45.refs_0_), channel_id=1, source_target_pairs={{4,8},{8,4},{5,1},{9,13},{6,10},{10,6},{7,3},{11,15},{20,24},{24,2... | collective-permute-start | bytes 786440 | tf_op jit(solution)/shard_map/ppermute | solution.py:499
  34.6 3.0 %collective-permute-start.5 = (bf16[8,128,128]{2,1,0:T(8,128)(2,1)S(1)}, bf16[8,128,128]{2,1,0:T(8,128)(2,1)S(1)}, u32[]{:S(2)}, u32[]{:S(2)}) collective-permute-start(bf16[8,128,128]{2,1,0:T(8,128)(2,1)S(1)} %get-tuple-element.45.refs_0_), channel_id=1, source_target_pairs={{0,1},{1,0},{2,3},{3,2},{4,5},{5,4},{6,7},{7,6},{8,9},{9,8},{10,11... | collective-permute-start | bytes 786440 | tf_op jit(solution)/shard_map/ppermute | solution.py:490
  37.6 0.0 collective-permute-done.8.piece_ref.refs_4_
  37.6 0.1 collective-permute-start.9
  37.7 0.2 collective-permute-start.11
  37.9 1.0 %collective-permute-done.9.piece_ref.refs_5_ = bf16[4,128,128]{2,1,0:T(8,128)(2,1)S(1)} collective-permute-done((bf16[4,128,128]{2,1,0:T(8,128)(2,1)S(1)}, bf16[4,128,128]{2,1,0:T(8,128)(2,1)S(1)}, u32[]{:S(2)}, u32[]{:S(2)}) %collective-permute-start.9) | collective-permute-done | bytes 131104 | tf_op jit(solution)/shard_map/ppermute | solution.py:490
  39.0 0.0 collective-permute-done.7.right_ref
  39.0 1.4 %collective-permute-done.6.left_ref = bf16[8,128,128]{2,1,0:T(8,128)(2,1)S(1)} collective-permute-done((bf16[8,128,128]{2,1,0:T(8,128)(2,1)S(1)}, bf16[8,128,128]{2,1,0:T(8,128)(2,1)S(1)}, u32[]{:S(2)}, u32[]{:S(2)}) %collective-permute-start.6) | collective-permute-done | bytes 262176 | tf_op jit(solution)/shard_map/ppermute | solution.py:499
  40.4 0.1 joined.2.refs_2_
  40.4 2.0 %collective-permute-start.10 = (bf16[8,128,128]{2,1,0:T(8,128)(2,1)S(1)}, bf16[8,128,128]{2,1,0:T(8,128)(2,1)S(1)}, u32[]{:S(2)}, u32[]{:S(2)}) collective-permute-start(bf16[8,128,128]{2,1,0:T(8,128)(2,1)S(1)} %joined.2.refs_2_), channel_id=1, source_target_pairs={{0,1},{1,0},{2,3},{3,2},{4,5},{5,4},{6,7},{7,6},{8,9},{9,8},{10,11... | collective-permute-start | bytes 786440 | tf_op jit(solution)/shard_map/ppermute | solution.py:490
  42.4 0.0 collective-permute-done.11.refs_6_
  42.4 1.2 %collective-permute-start.12 = (bf16[4,128,128]{2,1,0:T(8,128)(2,1)S(1)}, bf16[4,128,128]{2,1,0:T(8,128)(2,1)S(1)}, u32[]{:S(2)}, u32[]{:S(2)}) collective-permute-start(bf16[4,128,128]{2,1,0:T(8,128)(2,1)S(1)} %collective-permute-done.11.refs_6_), channel_id=1, source_target_pairs={{0,1},{1,0},{2,3},{3,2},{4,5},{5,4},{6,7},{7,6},{8,9},{9,8},{10,11... | collective-permute-start | bytes 393224 | tf_op jit(solution)/shard_map/ppermute | solution.py:490
  43.6 0.0 collective-permute-done.5.refs_1_
  43.6 1.0 %collective-permute-done.12.refs_7_ = bf16[4,128,128]{2,1,0:T(8,128)(2,1)S(1)} collective-permute-done((bf16[4,128,128]{2,1,0:T(8,128)(2,1)S(1)}, bf16[4,128,128]{2,1,0:T(8,128)(2,1)S(1)}, u32[]{:S(2)}, u32[]{:S(2)}) %collective-permute-start.12) | collective-permute-done | bytes 131104 | tf_op jit(solution)/shard_map/ppermute | solution.py:490
  44.6 0.0 collective-permute-done.10.refs_3_
  44.6 1.2 %sweep.1 = (bf16[8,128,128]{2,1,0:T(8,128)(2,1)S(1)}, bf16[4,128,128]{2,1,0:T(8,128)(2,1)S(1)}) custom-call(s32[1]{0:T(128)} %bitcast.here_ref, s32[1]{0:T(128)} %bitcast.1.aux_ref, s32[8,128]{1,0:T(8,128)S(1)} %get-tuple-element.31.index_ref, f32[8,128]{1,0:T(8,128)S(1)} %get-tuple-element.32.weight_ref, ...), custom_call_target="tpu_custom_call" | custom-call | flops 268435456 | bytes 2883584 | tf_op jit(solution)/shard_map/sweep/pallas_call | solution.py:345
  45.8 0.8 %collective-permute-start.16 = (bf16[4,128,128]{2,1,0:T(8,128)(2,1)S(1)}, bf16[4,128,128]{2,1,0:T(8,128)(2,1)S(1)}, u32[]{:S(2)}, u32[]{:S(2)}) collective-permute-start(bf16[4,128,128]{2,1,0:T(8,128)(2,1)S(1)} %get-tuple-element.49), channel_id=1, source_target_pairs={{4,12},{8,0},{0,4},{12,8},{5,13},{9,1},{1,5},{13,9},{6,14},{10,2},... | collective-permute-start | bytes 393224 | tf_op jit(solution)/shard_map/ppermute | solution.py:592
  46.5 2.2 %collective-permute-start.15 = (bf16[8,128,128]{2,1,0:T(8,128)(2,1)S(1)}, bf16[8,128,128]{2,1,0:T(8,128)(2,1)S(1)}, u32[]{:S(2)}, u32[]{:S(2)}) collective-permute-start(bf16[8,128,128]{2,1,0:T(8,128)(2,1)S(1)} %get-tuple-element.48.refs_0_), channel_id=1, source_target_pairs={{4,0},{8,12},{5,9},{9,5},{6,2},{10,14},{7,11},{11,7},{20,16},{24,2... | collective-permute-start | bytes 786440 | tf_op jit(solution)/shard_map/ppermute | solution.py:499
  48.7 1.3 %collective-permute-start.14 = (bf16[8,128,128]{2,1,0:T(8,128)(2,1)S(1)}, bf16[8,128,128]{2,1,0:T(8,128)(2,1)S(1)}, u32[]{:S(2)}, u32[]{:S(2)}) collective-permute-start(bf16[8,128,128]{2,1,0:T(8,128)(2,1)S(1)} %get-tuple-element.48.refs_0_), channel_id=1, source_target_pairs={{4,8},{8,4},{5,1},{9,13},{6,10},{10,6},{7,3},{11,15},{20,24},{24,2... | collective-permute-start | bytes 786440 | tf_op jit(solution)/shard_map/ppermute | solution.py:499
  50.0 2.8 %collective-permute-start.13 = (bf16[8,128,128]{2,1,0:T(8,128)(2,1)S(1)}, bf16[8,128,128]{2,1,0:T(8,128)(2,1)S(1)}, u32[]{:S(2)}, u32[]{:S(2)}) collective-permute-start(bf16[8,128,128]{2,1,0:T(8,128)(2,1)S(1)} %get-tuple-element.48.refs_0_), channel_id=1, source_target_pairs={{0,1},{1,0},{2,3},{3,2},{4,5},{5,4},{6,7},{7,6},{8,9},{9,8},{10,11... | collective-permute-start | bytes 786440 | tf_op jit(solution)/shard_map/ppermute | solution.py:490
  52.9 0.0 collective-permute-done.16.piece_ref.refs_4_
  52.9 0.1 collective-permute-start.17
  53.0 0.2 collective-permute-start.19
  53.2 0.5 collective-permute-done.15.right_ref
  53.7 2.2 %collective-permute-done.14.left_ref = bf16[8,128,128]{2,1,0:T(8,128)(2,1)S(1)} collective-permute-done((bf16[8,128,128]{2,1,0:T(8,128)(2,1)S(1)}, bf16[8,128,128]{2,1,0:T(8,128)(2,1)S(1)}, u32[]{:S(2)}, u32[]{:S(2)}) %collective-permute-start.14) | collective-permute-done | bytes 262176 | tf_op jit(solution)/shard_map/ppermute | solution.py:499
  55.9 0.0 collective-permute-done.17.piece_ref.refs_5_
  55.9 0.1 joined.3.refs_2_
  55.9 2.6 %collective-permute-start.18 = (bf16[8,128,128]{2,1,0:T(8,128)(2,1)S(1)}, bf16[8,128,128]{2,1,0:T(8,128)(2,1)S(1)}, u32[]{:S(2)}, u32[]{:S(2)}) collective-permute-start(bf16[8,128,128]{2,1,0:T(8,128)(2,1)S(1)} %joined.3.refs_2_), channel_id=1, source_target_pairs={{0,1},{1,0},{2,3},{3,2},{4,5},{5,4},{6,7},{7,6},{8,9},{9,8},{10,11... | collective-permute-start | bytes 786440 | tf_op jit(solution)/shard_map/ppermute | solution.py:490
  58.5 0.0 collective-permute-done.19.refs_6_
  58.5 0.4 collective-permute-start.20
  58.9 0.0 collective-permute-done.13.refs_1_
  58.9 1.0 %collective-permute-done.20.refs_7_ = bf16[4,128,128]{2,1,0:T(8,128)(2,1)S(1)} collective-permute-done((bf16[4,128,128]{2,1,0:T(8,128)(2,1)S(1)}, bf16[4,128,128]{2,1,0:T(8,128)(2,1)S(1)}, u32[]{:S(2)}, u32[]{:S(2)}) %collective-permute-start.20) | collective-permute-done | bytes 131104 | tf_op jit(solution)/shard_map/ppermute | solution.py:490
  59.9 0.0 collective-permute-done.18.refs_3_
  59.9 2.5 %last_sweep.1 = (f32[8,128,128]{2,1,0:T(8,128)S(1)}, f32[2,128,128]{2,1,0:T(8,128)S(1)}, bf16[2,128,128]{2,1,0:T(8,128)(2,1)S(1)}, bf16[2,128,128]{2,1,0:T(8,128)(2,1)S(1)}) custom-call(s32[1]{0:T(128)} %bitcast.here_ref, s32[1]{0:T(128)} %bitcast.1.aux_ref, s32[8,128]{1,0:T(8,128)S(1)} %get-tuple-element.31.index_ref, ...), custom_call_target="tpu_custom_call" | custom-call | flops 268435456 | bytes 2883584 | tf_op jit(solution)/shard_map/last_sweep/pallas_call | solution.py:345
  62.4 0.4 collective-permute-start.21
  62.9 0.3 collective-permute-start.22
  63.2 2.8 %collective-permute-start.23 = (bf16[2,128,128]{2,1,0:T(8,128)(2,1)S(1)}, bf16[2,128,128]{2,1,0:T(8,128)(2,1)S(1)}, u32[]{:S(2)}, u32[]{:S(2)}) collective-permute-start(bf16[2,128,128]{2,1,0:T(8,128)(2,1)S(1)} %get-tuple-element.55), channel_id=1, source_target_pairs={{4,8},{8,4},{5,9},{9,5},{6,10},{10,6},{7,11},{11,7},{20,24},{24,20... | collective-permute-start | bytes 196616 | tf_op jit(solution)/shard_map/ppermute | solution.py:495
  66.0 0.0 collective-permute-done.21.others_ref
  66.1 2.3 %first_terms.1 = (f32[16,128,128]{2,1,0:T(8,128)}, f32[2,128,128]{2,1,0:T(8,128)S(1)}) custom-call(s32[1]{0:T(128)} %bitcast.1.aux_ref, s32[8,128]{1,0:T(8,128)S(1)} %get-tuple-element.31.index_ref, f32[8,128,128]{2,1,0:T(8,128)S(1)} %get-tuple-element.50.amps_ref, f32[8,128,128]{2,1,0:T(8,128)S(1)} %collective-permute-done.21.others_ref, ...), custom_call_target="tpu_custom_call" | custom-call | flops 201326592 | bytes 2097152 | tf_op jit(solution)/shard_map/first_terms/pallas_call | solution.py:421
  68.5 1.4 %collective-permute-start.24 = (f32[2,128,128]{2,1,0:T(8,128)S(1)}, f32[2,128,128]{2,1,0:T(8,128)S(1)}, u32[]{:S(2)}, u32[]{:S(2)}) collective-permute-start(f32[2,128,128]{2,1,0:T(8,128)S(1)} %convert_add_fusion), channel_id=1, source_target_pairs={{0,1},{1,0},{2,3},{3,2},{4,5},{5,4},{6,7},{7,6},{8,9},{9,8},{10,11... | collective-permute-start | bytes 393224 | tf_op jit(solution)/shard_map/ppermute | solution.py:490
  69.9 1.0 %collective-permute-done.24 = f32[2,128,128]{2,1,0:T(8,128)S(1)} collective-permute-done((f32[2,128,128]{2,1,0:T(8,128)S(1)}, f32[2,128,128]{2,1,0:T(8,128)S(1)}, u32[]{:S(2)}, u32[]{:S(2)}) %collective-permute-start.24) | collective-permute-done | bytes 131104 | tf_op jit(solution)/shard_map/ppermute | solution.py:490
  70.9 0.7 add_multiply_fusion
  (20 shorter events, 0.1 us)
Async XLA Ops:
  0.6 27.2 %copy-start.5 = (s32[64,4]{0,1:T(4,128)S(1)}, s32[64,4]{0,1:T(4,128)}, u32[]{:S(2)}) copy-start(s32[64,4]{0,1:T(4,128)} %param.19) | copy-start | bytes 3076
  0.6 27.2 %copy-start.8 = (s32[16,2]{0,1:T(2,128)S(1)}, s32[16,2]{0,1:T(2,128)}, u32[]{:S(2)}) copy-start(s32[16,2]{0,1:T(2,128)} %param.18) | copy-start | bytes 388
  0.7 27.2 %copy-start.6 = (f32[16,4]{0,1:T(4,128)S(1)}, f32[16,4]{0,1:T(4,128)}, u32[]{:S(2)}) copy-start(f32[16,4]{0,1:T(4,128)} %param.14) | copy-start | bytes 772
  0.7 13.4 %collective-permute-start = (bf16[2,1536,128]{2,1,0:T(8,128)(2,1)}, bf16[2,1536,128]{2,1,0:T(8,128)(2,1)S(1)}, u32[]{:S(2)}, u32[]{:S(2)}) collective-permute-start(bf16[2,1536,128]{2,1,0:T(8,128)(2,1)} %ints_ref), channel_id=1, source_target_pairs={{4,0},{8,4},{12,8},{1,5},{5,9},{9,13},{6,2},{10,6},{14,10},{3,7},{... | collective-permute-start | bytes 2359304 | tf_op jit(solution)/shard_map/ppermute | solution.py:518
  4.0 1.1 %copy-start.1 = (bf16[2,1536,128]{2,1,0:T(8,128)(2,1)S(1)}, bf16[2,1536,128]{2,1,0:T(8,128)(2,1)}, u32[]{:S(2)}) copy-start(bf16[2,1536,128]{2,1,0:T(8,128)(2,1)} %ints_ref) | copy-start | bytes 2359300
  5.2 1.0 %copy-start.2 = (bf16[16,128,128]{2,1,0:T(8,128)(2,1)S(1)}, bf16[16,128,128]{2,1,0:T(8,128)(2,1)}, u32[]{:S(2)}) copy-start(bf16[16,128,128]{2,1,0:T(8,128)(2,1)} %first_ref.1) | copy-start | bytes 1572868
  6.2 1.0 %copy-start.3 = (bf16[16,128,128]{2,1,0:T(8,128)(2,1)S(1)}, bf16[16,128,128]{2,1,0:T(8,128)(2,1)}, u32[]{:S(2)}) copy-start(bf16[16,128,128]{2,1,0:T(8,128)(2,1)} %second_ref.1) | copy-start | bytes 1572868
  7.2 0.7 copy-start.4
  7.9 0.7 copy-start.7
  8.6 0.7 copy-start.9
  14.6 6.6 %collective-permute-start.1 = (bf16[512,128]{1,0:T(8,128)(2,1)S(1)}, bf16[512,128]{1,0:T(8,128)(2,1)S(1)}, u32[]{:S(2)}, u32[]{:S(2)}) collective-permute-start(bf16[512,128]{1,0:T(8,128)(2,1)S(1)} %get-tuple-element.41), channel_id=1, source_target_pairs={{0,5},{4,9},{8,13},{5,0},{9,4},{13,8},{2,7},{6,11},{10,15},{7,2},{... | collective-permute-start | bytes 393224 | tf_op jit(solution)/shard_map/ppermute | solution.py:562
  21.2 4.2 %collective-permute-start.2 = (bf16[640,128]{1,0:T(8,128)(2,1)S(1)}, bf16[640,128]{1,0:T(8,128)(2,1)S(1)}, u32[]{:S(2)}, u32[]{:S(2)}) collective-permute-start(bf16[640,128]{1,0:T(8,128)(2,1)S(1)} %partner_sum.1.total_ref), channel_id=1, source_target_pairs={{0,2},{1,3},{2,0},{3,1},{4,6},{5,7},{6,4},{7,5},{8,10},{9,11},{10,... | collective-permute-start | bytes 491528 | tf_op jit(solution)/shard_map/ppermute | solution.py:490
  21.5 7.7 %collective-permute-start.3 = (bf16[640,128]{1,0:T(8,128)(2,1)S(1)}, bf16[640,128]{1,0:T(8,128)(2,1)S(1)}, u32[]{:S(2)}, u32[]{:S(2)}) collective-permute-start(bf16[640,128]{1,0:T(8,128)(2,1)S(1)} %partner_sum.1.total_ref), channel_id=1, source_target_pairs={{0,1},{1,0},{2,3},{3,2},{4,5},{5,4},{6,7},{7,6},{8,9},{9,8},{10,11... | collective-permute-start | bytes 491528 | tf_op jit(solution)/shard_map/ppermute | solution.py:490
  25.4 3.8 %collective-permute-start.4 = (bf16[640,128]{1,0:T(8,128)(2,1)S(1)}, bf16[640,128]{1,0:T(8,128)(2,1)S(1)}, u32[]{:S(2)}, u32[]{:S(2)}) collective-permute-start(bf16[640,128]{1,0:T(8,128)(2,1)S(1)} %collective-permute-done.2.far_ref), channel_id=1, source_target_pairs={{0,1},{1,0},{2,3},{3,2},{4,5},{5,4},{6,7},{7,6},{8,9},{9,8},{10,11... | collective-permute-start | bytes 491528 | tf_op jit(solution)/shard_map/ppermute | solution.py:490
  30.0 7.6 %collective-permute-start.8 = (bf16[4,128,128]{2,1,0:T(8,128)(2,1)S(1)}, bf16[4,128,128]{2,1,0:T(8,128)(2,1)S(1)}, u32[]{:S(2)}, u32[]{:S(2)}) collective-permute-start(bf16[4,128,128]{2,1,0:T(8,128)(2,1)S(1)} %get-tuple-element.46), channel_id=1, source_target_pairs={{4,12},{8,0},{0,4},{12,8},{5,13},{9,1},{1,5},{13,9},{6,14},{10,2},... | collective-permute-start | bytes 393224 | tf_op jit(solution)/shard_map/ppermute | solution.py:592
  30.1 8.9 %collective-permute-start.7 = (bf16[8,128,128]{2,1,0:T(8,128)(2,1)S(1)}, bf16[8,128,128]{2,1,0:T(8,128)(2,1)S(1)}, u32[]{:S(2)}, u32[]{:S(2)}) collective-permute-start(bf16[8,128,128]{2,1,0:T(8,128)(2,1)S(1)} %get-tuple-element.45.refs_0_), channel_id=1, source_target_pairs={{4,0},{8,12},{5,9},{9,5},{6,2},{10,14},{7,11},{11,7},{20,16},{24,2... | collective-permute-start | bytes 786440 | tf_op jit(solution)/shard_map/ppermute | solution.py:499
  33.3 7.1 %collective-permute-start.6 = (bf16[8,128,128]{2,1,0:T(8,128)(2,1)S(1)}, bf16[8,128,128]{2,1,0:T(8,128)(2,1)S(1)}, u32[]{:S(2)}, u32[]{:S(2)}) collective-permute-start(bf16[8,128,128]{2,1,0:T(8,128)(2,1)S(1)} %get-tuple-element.45.refs_0_), channel_id=1, source_target_pairs={{4,8},{8,4},{5,1},{9,13},{6,10},{10,6},{7,3},{11,15},{20,24},{24,2... | collective-permute-start | bytes 786440 | tf_op jit(solution)/shard_map/ppermute | solution.py:499
  34.6 9.0 %collective-permute-start.5 = (bf16[8,128,128]{2,1,0:T(8,128)(2,1)S(1)}, bf16[8,128,128]{2,1,0:T(8,128)(2,1)S(1)}, u32[]{:S(2)}, u32[]{:S(2)}) collective-permute-start(bf16[8,128,128]{2,1,0:T(8,128)(2,1)S(1)} %get-tuple-element.45.refs_0_), channel_id=1, source_target_pairs={{0,1},{1,0},{2,3},{3,2},{4,5},{5,4},{6,7},{7,6},{8,9},{9,8},{10,11... | collective-permute-start | bytes 786440 | tf_op jit(solution)/shard_map/ppermute | solution.py:490
  37.6 1.3 %collective-permute-start.9 = (bf16[4,128,128]{2,1,0:T(8,128)(2,1)S(1)}, bf16[4,128,128]{2,1,0:T(8,128)(2,1)S(1)}, u32[]{:S(2)}, u32[]{:S(2)}) collective-permute-start(bf16[4,128,128]{2,1,0:T(8,128)(2,1)S(1)} %collective-permute-done.8.piece_ref.refs_4_), channel_id=1, source_target_pairs={{0,1},{1,0},{2,3},{3,2},{4,5},{5,4},{6,7},{7,6},{8,9},{9,8},{10,11... | collective-permute-start | bytes 393224 | tf_op jit(solution)/shard_map/ppermute | solution.py:490
  37.7 6.9 %copy-start = (bf16[16,4,128,128]{3,2,1,0:T(8,128)(2,1)S(1)}, bf16[16,4,128,128]{3,2,1,0:T(8,128)(2,1)}, u32[]{:S(2)}) copy-start(bf16[16,4,128,128]{3,2,1,0:T(8,128)(2,1)} %refs_8_.3) | copy-start | bytes 6291460
  37.7 4.7 %collective-permute-start.11 = (bf16[4,128,128]{2,1,0:T(8,128)(2,1)S(1)}, bf16[4,128,128]{2,1,0:T(8,128)(2,1)S(1)}, u32[]{:S(2)}, u32[]{:S(2)}) collective-permute-start(bf16[4,128,128]{2,1,0:T(8,128)(2,1)S(1)} %collective-permute-done.8.piece_ref.refs_4_), channel_id=1, source_target_pairs={{0,2},{1,3},{2,0},{3,1},{4,6},{5,7},{6,4},{7,5},{8,10},{9,11},{10,... | collective-permute-start | bytes 393224 | tf_op jit(solution)/shard_map/ppermute | solution.py:490
  40.4 4.2 %collective-permute-start.10 = (bf16[8,128,128]{2,1,0:T(8,128)(2,1)S(1)}, bf16[8,128,128]{2,1,0:T(8,128)(2,1)S(1)}, u32[]{:S(2)}, u32[]{:S(2)}) collective-permute-start(bf16[8,128,128]{2,1,0:T(8,128)(2,1)S(1)} %joined.2.refs_2_), channel_id=1, source_target_pairs={{0,1},{1,0},{2,3},{3,2},{4,5},{5,4},{6,7},{7,6},{8,9},{9,8},{10,11... | collective-permute-start | bytes 786440 | tf_op jit(solution)/shard_map/ppermute | solution.py:490
  42.4 2.2 %collective-permute-start.12 = (bf16[4,128,128]{2,1,0:T(8,128)(2,1)S(1)}, bf16[4,128,128]{2,1,0:T(8,128)(2,1)S(1)}, u32[]{:S(2)}, u32[]{:S(2)}) collective-permute-start(bf16[4,128,128]{2,1,0:T(8,128)(2,1)S(1)} %collective-permute-done.11.refs_6_), channel_id=1, source_target_pairs={{0,1},{1,0},{2,3},{3,2},{4,5},{5,4},{6,7},{7,6},{8,9},{9,8},{10,11... | collective-permute-start | bytes 393224 | tf_op jit(solution)/shard_map/ppermute | solution.py:490
  45.8 7.1 %collective-permute-start.16 = (bf16[4,128,128]{2,1,0:T(8,128)(2,1)S(1)}, bf16[4,128,128]{2,1,0:T(8,128)(2,1)S(1)}, u32[]{:S(2)}, u32[]{:S(2)}) collective-permute-start(bf16[4,128,128]{2,1,0:T(8,128)(2,1)S(1)} %get-tuple-element.49), channel_id=1, source_target_pairs={{4,12},{8,0},{0,4},{12,8},{5,13},{9,1},{1,5},{13,9},{6,14},{10,2},... | collective-permute-start | bytes 393224 | tf_op jit(solution)/shard_map/ppermute | solution.py:592
  46.5 7.1 %collective-permute-start.15 = (bf16[8,128,128]{2,1,0:T(8,128)(2,1)S(1)}, bf16[8,128,128]{2,1,0:T(8,128)(2,1)S(1)}, u32[]{:S(2)}, u32[]{:S(2)}) collective-permute-start(bf16[8,128,128]{2,1,0:T(8,128)(2,1)S(1)} %get-tuple-element.48.refs_0_), channel_id=1, source_target_pairs={{4,0},{8,12},{5,9},{9,5},{6,2},{10,14},{7,11},{11,7},{20,16},{24,2... | collective-permute-start | bytes 786440 | tf_op jit(solution)/shard_map/ppermute | solution.py:499
  48.7 7.1 %collective-permute-start.14 = (bf16[8,128,128]{2,1,0:T(8,128)(2,1)S(1)}, bf16[8,128,128]{2,1,0:T(8,128)(2,1)S(1)}, u32[]{:S(2)}, u32[]{:S(2)}) collective-permute-start(bf16[8,128,128]{2,1,0:T(8,128)(2,1)S(1)} %get-tuple-element.48.refs_0_), channel_id=1, source_target_pairs={{4,8},{8,4},{5,1},{9,13},{6,10},{10,6},{7,3},{11,15},{20,24},{24,2... | collective-permute-start | bytes 786440 | tf_op jit(solution)/shard_map/ppermute | solution.py:499
  50.0 8.8 %collective-permute-start.13 = (bf16[8,128,128]{2,1,0:T(8,128)(2,1)S(1)}, bf16[8,128,128]{2,1,0:T(8,128)(2,1)S(1)}, u32[]{:S(2)}, u32[]{:S(2)}) collective-permute-start(bf16[8,128,128]{2,1,0:T(8,128)(2,1)S(1)} %get-tuple-element.48.refs_0_), channel_id=1, source_target_pairs={{0,1},{1,0},{2,3},{3,2},{4,5},{5,4},{6,7},{7,6},{8,9},{9,8},{10,11... | collective-permute-start | bytes 786440 | tf_op jit(solution)/shard_map/ppermute | solution.py:490
  52.9 3.0 %collective-permute-start.17 = (bf16[4,128,128]{2,1,0:T(8,128)(2,1)S(1)}, bf16[4,128,128]{2,1,0:T(8,128)(2,1)S(1)}, u32[]{:S(2)}, u32[]{:S(2)}) collective-permute-start(bf16[4,128,128]{2,1,0:T(8,128)(2,1)S(1)} %collective-permute-done.16.piece_ref.refs_4_), channel_id=1, source_target_pairs={{0,1},{1,0},{2,3},{3,2},{4,5},{5,4},{6,7},{7,6},{8,9},{9,8},{10,11... | collective-permute-start | bytes 393224 | tf_op jit(solution)/shard_map/ppermute | solution.py:490
  53.0 5.5 %collective-permute-start.19 = (bf16[4,128,128]{2,1,0:T(8,128)(2,1)S(1)}, bf16[4,128,128]{2,1,0:T(8,128)(2,1)S(1)}, u32[]{:S(2)}, u32[]{:S(2)}) collective-permute-start(bf16[4,128,128]{2,1,0:T(8,128)(2,1)S(1)} %collective-permute-done.16.piece_ref.refs_4_), channel_id=1, source_target_pairs={{0,2},{1,3},{2,0},{3,1},{4,6},{5,7},{6,4},{7,5},{8,10},{9,11},{10,... | collective-permute-start | bytes 393224 | tf_op jit(solution)/shard_map/ppermute | solution.py:490
  55.9 3.9 %collective-permute-start.18 = (bf16[8,128,128]{2,1,0:T(8,128)(2,1)S(1)}, bf16[8,128,128]{2,1,0:T(8,128)(2,1)S(1)}, u32[]{:S(2)}, u32[]{:S(2)}) collective-permute-start(bf16[8,128,128]{2,1,0:T(8,128)(2,1)S(1)} %joined.3.refs_2_), channel_id=1, source_target_pairs={{0,1},{1,0},{2,3},{3,2},{4,5},{5,4},{6,7},{7,6},{8,9},{9,8},{10,11... | collective-permute-start | bytes 786440 | tf_op jit(solution)/shard_map/ppermute | solution.py:490
  58.5 1.4 %collective-permute-start.20 = (bf16[4,128,128]{2,1,0:T(8,128)(2,1)S(1)}, bf16[4,128,128]{2,1,0:T(8,128)(2,1)S(1)}, u32[]{:S(2)}, u32[]{:S(2)}) collective-permute-start(bf16[4,128,128]{2,1,0:T(8,128)(2,1)S(1)} %collective-permute-done.19.refs_6_), channel_id=1, source_target_pairs={{0,1},{1,0},{2,3},{3,2},{4,5},{5,4},{6,7},{7,6},{8,9},{9,8},{10,11... | collective-permute-start | bytes 393224 | tf_op jit(solution)/shard_map/ppermute | solution.py:490
  62.4 3.6 %collective-permute-start.21 = (f32[8,128,128]{2,1,0:T(8,128)S(1)}, f32[8,128,128]{2,1,0:T(8,128)S(1)}, u32[]{:S(2)}, u32[]{:S(2)}) collective-permute-start(f32[8,128,128]{2,1,0:T(8,128)S(1)} %get-tuple-element.50.amps_ref), channel_id=1, source_target_pairs={{0,1},{1,0},{2,3},{3,2},{4,5},{5,4},{6,7},{7,6},{8,9},{9,8},{10,11... | collective-permute-start | bytes 1572872 | tf_op jit(solution)/shard_map/ppermute | solution.py:490
  62.9 5.5 %collective-permute-start.22 = (bf16[2,128,128]{2,1,0:T(8,128)(2,1)S(1)}, bf16[2,128,128]{2,1,0:T(8,128)(2,1)S(1)}, u32[]{:S(2)}, u32[]{:S(2)}) collective-permute-start(bf16[2,128,128]{2,1,0:T(8,128)(2,1)S(1)} %get-tuple-element.54), channel_id=1, source_target_pairs={{0,4},{4,0},{8,12},{12,8},{1,5},{5,1},{9,13},{13,9},{2,6},{6,2},{1... | collective-permute-start | bytes 196616 | tf_op jit(solution)/shard_map/ppermute | solution.py:495
  63.2 5.2 %collective-permute-start.23 = (bf16[2,128,128]{2,1,0:T(8,128)(2,1)S(1)}, bf16[2,128,128]{2,1,0:T(8,128)(2,1)S(1)}, u32[]{:S(2)}, u32[]{:S(2)}) collective-permute-start(bf16[2,128,128]{2,1,0:T(8,128)(2,1)S(1)} %get-tuple-element.55), channel_id=1, source_target_pairs={{4,8},{8,4},{5,9},{9,5},{6,10},{10,6},{7,11},{11,7},{20,24},{24,20... | collective-permute-start | bytes 196616 | tf_op jit(solution)/shard_map/ppermute | solution.py:495
  68.5 2.4 %collective-permute-start.24 = (f32[2,128,128]{2,1,0:T(8,128)S(1)}, f32[2,128,128]{2,1,0:T(8,128)S(1)}, u32[]{:S(2)}, u32[]{:S(2)}) collective-permute-start(f32[2,128,128]{2,1,0:T(8,128)S(1)} %convert_add_fusion), channel_id=1, source_target_pairs={{0,1},{1,0},{2,3},{3,2},{4,5},{5,4},{6,7},{7,6},{8,9},{9,8},{10,11... | collective-permute-start | bytes 393224 | tf_op jit(solution)/shard_map/ppermute | solution.py:490

commit v8 on v7

--- a/solution.py
+++ b/solution.py
@@ -154,7 +154,7 @@
     )(here, aux, orbitals, near, couple)
 
 
-def product_kernel(aux_ref, own_ref, near_ref, total_ref, sent_ref):
+def product_kernel(aux_ref, own_ref, near_ref, all_ref, sent_ref):
     count, _, width = own_ref.shape
     second = lax.rem(aux_ref[0], 2) == 1
     own = jnp.concatenate([own_ref[i] for i in range(count)], axis=1)
@@ -163,11 +163,11 @@
     at = 0
     for i in range(count):
         for j in range(count):
-            block = full[i * width : (i + 1) * width, j * width : (j + 1) * width]
-            total_ref[at : at + width] = block
-            sent_ref[at : at + width] = block.astype(BF16)
+            block = full[i * width : (i + 1) * width, j * width : (j + 1) * width].astype(BF16)
+            all_ref[at : at + width] = block
+            sent_ref[at : at + width] = block
             at += width
-    total_ref[at:] = dot(own_ref[0], own_ref[1], ((0,), (0,)))
+    all_ref[at:] = dot(own_ref[0], own_ref[1], ((0,), (0,))).astype(BF16)
 
 
 def products(aux, ints, near):
@@ -176,7 +176,7 @@
     return pl.pallas_call(
         product_kernel,
         out_shape=(
-            jax.ShapeDtypeStruct((rows + width, width), F32),
+            jax.ShapeDtypeStruct((rows + width, width), BF16),
             jax.ShapeDtypeStruct((rows, width), BF16),
         ),
         in_specs=[SMEM] + [VMEM] * 2,
@@ -187,37 +187,25 @@
     )(aux, ints, near)
 
 
-def partner_kernel(total_ref, received_ref, out_ref):
-    rows = received_ref.shape[0]
-    out_ref[:rows] = (total_ref[:rows] + received_ref[...].astype(F32)).astype(BF16)
-    out_ref[rows:] = total_ref[rows:].astype(BF16)
-
-
-def partner_sum(total, received):
-    return pl.pallas_call(
-        partner_kernel,
-        out_shape=jax.ShapeDtypeStruct(total.shape, BF16),
-        in_specs=[VMEM] * 2,
-        out_specs=VMEM,
-        compiler_params=params(4),
-        cost_estimate=cost(total.size, 8 * total.size),
-        name="partner_sum",
-    )(total, received)
-
-
 def own_part(aux_ref, low_ref, part_ref):
     count = part_ref.shape[0]
     part_ref[...] = low_ref[pl.ds(lax.rem(aux_ref[0] // 2, 2) * count, count)]
 
 
-def exchange_kernel(
-    aux_ref, index_ref, total_ref, far_ref, total_other, far_other,
-    first_ref, second_ref, factor_ref, exch_ref, low_ref, part_ref, table,
-):
+def exchange_kernel(aux_ref, index_ref, *refs):
+    mine_refs, other_refs, refs = refs[:4], refs[4:8], refs[8:]
+    first_ref, second_ref, factor_ref, exch_ref, low_ref, part_ref, table = refs
     count, width, _ = exch_ref.shape
     second = lax.rem(aux_ref[0], 2) == 1
-    mine = total_ref[...].astype(F32) + far_ref[...].astype(F32)
-    others = total_other[...].astype(F32) + far_other[...].astype(F32)
+    rows = 4 * width
+
+    def summed(refs):
+        whole, cross, near, near_cross = (ref[...].astype(F32) for ref in refs)
+        both = whole + cross
+        return both[:rows] + (near + near_cross), both[rows:]
+
+    mine, inner = summed(mine_refs)
+    others, inner_other = summed(other_refs)
     for i in range(2):
         for j in range(2):
             at = (2 * i + j) * width
@@ -225,7 +213,7 @@
             two = others[at : at + width]
             table[i * 6 + 4 + j] = jnp.where(second, two, one)
             table[j * 6 + i] = jnp.where(second, one, two).T
-    inner = mine[4 * width :] + others[4 * width :]
+    inner = inner + inner_other
     table[3] = inner
     table[6 + 2] = inner.T
     for p in range(count):
@@ -532,7 +520,8 @@
         (near, first, second, ints, factor)
     )
 
-    if cap < pair_dev or groups // 4 != 1 or aux_count != 4:
+    assert aux_count == 4
+    if cap < pair_dev or groups // 4 != 1:
         rounds = None
         requests = neighbours.reshape(groups, wanted)
         owners = requests // pair_dev
@@ -558,25 +547,23 @@
         rounds = window_rounds(groups)
     index, weight = indices(rounds, here_s, aux_s, pair_orbitals.T, neighbours.T, couple.T)
 
-    total, sent = products(aux_s, ints, near)
-    received = lax.ppermute(
-        sent,
-        ("pair", "aux"),
-        joint(
-            [
-                [(i, i + 1, 1) for i in range(groups - 1)],
-                [(i + 1, i, 1) for i in range(groups - 1)],
-            ]
-        ),
-    )
-    total = partner_sum(total, received)
-    step = 2
-    while 2 * step < aux_count:
-        total = (total.astype(F32) + swap(total, step).astype(F32)).astype(BF16)
-        step *= 2
-    far = swap(total, step)
+    everything, sent = products(aux_s, ints, near)
+
+    def over_z(turn):
+        return lax.ppermute(
+            sent,
+            ("pair", "aux"),
+            joint(
+                [
+                    [(i, i + 1, turn) for i in range(groups - 1)],
+                    [(i + 1, i, turn) for i in range(groups - 1)],
+                ]
+            ),
+        )
+
+    sums = [everything, swap(everything, 2), over_z(1), over_z(3)]
     exch, low, part = exchange(
-        aux_s, index, (total, far, swap(total), swap(far)), first, second, factor
+        aux_s, index, sums + [swap(value) for value in sums], first, second, factor
     )
 
     def gathered(low, part):

time: 72 us -> 71.7 us (level)
  waiting for transfers between devices: 17.5 us -> 14 us
  starting transfers between devices: 37.5 us -> 40.2 us
    ppermute x15 -> x17, starting transfers between devices: 18.6 us -> 14.9 us  [swap(): return lax.ppermute(value, 'aux', [(i, i ^ step) for i in range(aux_count)])]
    ppermute x2, starting transfers between devices: 0.83 us -> 4.38 us  [gathered(): one = lax.ppermute(part, 'pair', rounds[0])]
    ppermute x1 -> x2, starting transfers between devices: 3.49 us -> 6.61 us  [over_z(): lax.ppermute(sent, ('pair', 'aux'), joint([[(i, i + 1, turn) for i in ran...]
    ppermute x15 -> x17, waiting for transfers between devices: 6.43 us -> 4.03 us  [swap(): return lax.ppermute(value, 'aux', [(i, i ^ step) for i in range(aux_count)])]
    ppermute x1, starting transfers between devices: 2.82 us -> 4.53 us  [both(): lax.ppermute(two, 'pair', partners[1])]
    ppermute x4, starting transfers between devices: 7.99 us -> 6.43 us  [exchanged(): lax.ppermute(value, ('pair', 'aux'), [(i * aux_count + a, j * aux_count +...]
    ppermute x1 -> x2, waiting for transfers between devices: 3.08 us -> 1.56 us  [over_z(): lax.ppermute(sent, ('pair', 'aux'), joint([[(i, i + 1, turn) for i in ran...]
  transfers between devices with their start and end apart: 25 -> 28, of which waited for: 10 -> 10; matrix products, arithmetic and copies ran while one was open for 0% -> 0% of each run, Pallas kernels for 7% -> 7%
where the time goes in v8:
time: 71.7 us; the launch traced here: 70.9 us
  starting transfers between devices  40.2 us (56%)
  waiting for transfers between devices  14 us (20%)
  Pallas kernels  9.77 us (14%)
  local copies, waits for them, and re-layouts  5.26 us (7%)
  between operations  0.89 us (1%)
    ppermute x17, starting transfers between devices, swap(): return lax.ppermute(value, 'aux', [(i, i ^ step) for i in range(aux_count)])  14.9 us
    ppermute x2, starting transfers between devices, over_z(): lax.ppermute(sent, ('pair', 'aux'), joint([[(i, i + 1, turn) for i in ran...  6.61 us
    ppermute x4, starting transfers between devices, exchanged(): lax.ppermute(value, ('pair', 'aux'), [(i * aux_count + a, j * aux_count +...  6.43 us
    unnamed x20, local copies, waits for them, and re-layouts  5.26 us
    ppermute x4, waiting for transfers between devices, exchanged(): lax.ppermute(value, ('pair', 'aux'), [(i * aux_count + a, j * aux_count +...  4.57 us
    ppermute x1, starting transfers between devices, both(): lax.ppermute(two, 'pair', partners[1])  4.53 us
    ppermute x2, starting transfers between devices, gathered(): one = lax.ppermute(part, 'pair', rounds[0])  4.38 us
    ppermute x17, waiting for transfers between devices, swap(): return lax.ppermute(value, 'aux', [(i, i ^ step) for i in range(aux_count)])  4.03 us
  transfers between devices with their start and end apart: 28, of which 10 were waited for; matrix products, arithmetic and copies ran while one was open for 0% of the time, Pallas kernels for 7%

profile of v8, /device:TPU:15, one launch (start us, length us, event | category | flops | bytes accessed | tf_op | source)
XLA Modules:
  0.0 70.9 jit_solution(16108414020008242397)
XLA Ops:
  0.7 3.3 %collective-permute-start = (bf16[2,1536,128]{2,1,0:T(8,128)(2,1)}, bf16[2,1536,128]{2,1,0:T(8,128)(2,1)S(1)}, u32[]{:S(2)}, u32[]{:S(2)}) collective-permute-start(bf16[2,1536,128]{2,1,0:T(8,128)(2,1)} %ints_ref), channel_id=1, source_target_pairs={{4,0},{8,4},{12,8},{1,5},{5,9},{9,13},{6,2},{10,6},{14,10},{3,7},{... | collective-permute-start | bytes 2359304 | tf_op jit(solution)/shard_map/ppermute | solution.py:506
  4.0 1.1 %copy-done.1 = bf16[2,1536,128]{2,1,0:T(8,128)(2,1)S(1)} copy-done((bf16[2,1536,128]{2,1,0:T(8,128)(2,1)S(1)}, bf16[2,1536,128]{2,1,0:T(8,128)(2,1)}, u32[]{:S(2)}) %copy-start.1) | copy-done | bytes 786456
  5.2 1.0 %copy-done.2 = bf16[16,128,128]{2,1,0:T(8,128)(2,1)S(1)} copy-done((bf16[16,128,128]{2,1,0:T(8,128)(2,1)S(1)}, bf16[16,128,128]{2,1,0:T(8,128)(2,1)}, u32[]{:S(2)}) %copy-start.2) | copy-done | bytes 524312
  6.2 1.0 %copy-done.3 = bf16[16,128,128]{2,1,0:T(8,128)(2,1)S(1)} copy-done((bf16[16,128,128]{2,1,0:T(8,128)(2,1)S(1)}, bf16[16,128,128]{2,1,0:T(8,128)(2,1)}, u32[]{:S(2)}) %copy-start.3) | copy-done | bytes 524312
  7.2 0.7 copy-done.4
  7.9 0.7 copy-done.7
  8.6 0.7 copy-done.9
  9.3 0.9 %prepare.1 = (bf16[8,128,128]{2,1,0:T(8,128)(2,1)S(1)}, bf16[8,128,128]{2,1,0:T(8,128)(2,1)S(1)}, bf16[2,1536,128]{2,1,0:T(8,128)(2,1)S(1)}, f32[8,128,128]{2,1,0:T(8,128)S(1)}) custom-call(s32[1]{0:T(128)} %bitcast.1.aux_ref, f32[2,16]{1,0:T(2,128)S(1)} %bitcast.8, s32[16]{0:T(128)S(1)} %copy-done.9, f32[16,128]{1,0:T(8,128)S(1)} %copy-done.4, ...), custom_call_target="tpu_custom_call" | custom-call | bytes 2097152 | tf_op jit(solution)/shard_map/prepare/pallas_call | solution.py:75
  10.2 3.9 %collective-permute-done.near_ref = bf16[2,1536,128]{2,1,0:T(8,128)(2,1)S(1)} collective-permute-done((bf16[2,1536,128]{2,1,0:T(8,128)(2,1)}, bf16[2,1536,128]{2,1,0:T(8,128)(2,1)S(1)}, u32[]{:S(2)}, u32[]{:S(2)}) %collective-permute-start) | collective-permute-done | bytes 786464 | tf_op jit(solution)/shard_map/ppermute | solution.py:506
  14.0 0.5 products.1
  14.6 0.3 collective-permute-start.1
  14.9 4.7 %collective-permute-start.3 = (bf16[512,128]{1,0:T(8,128)(2,1)S(1)}, bf16[512,128]{1,0:T(8,128)(2,1)S(1)}, u32[]{:S(2)}, u32[]{:S(2)}) collective-permute-start(bf16[512,128]{1,0:T(8,128)(2,1)S(1)} %get-tuple-element.41), channel_id=1, source_target_pairs={{0,7},{4,11},{8,15},{5,2},{9,6},{13,10},{2,5},{6,9},{10,13},{7,0},... | collective-permute-start | bytes 393224 | tf_op jit(solution)/shard_map/ppermute | solution.py:553
  19.6 1.9 %collective-permute-start.2 = (bf16[512,128]{1,0:T(8,128)(2,1)S(1)}, bf16[512,128]{1,0:T(8,128)(2,1)S(1)}, u32[]{:S(2)}, u32[]{:S(2)}) collective-permute-start(bf16[512,128]{1,0:T(8,128)(2,1)S(1)} %get-tuple-element.41), channel_id=1, source_target_pairs={{0,5},{4,9},{8,13},{5,0},{9,4},{13,8},{2,7},{6,11},{10,15},{7,2},{... | collective-permute-start | bytes 393224 | tf_op jit(solution)/shard_map/ppermute | solution.py:553
  21.5 1.7 %collective-permute-start.4 = (bf16[640,128]{1,0:T(8,128)(2,1)S(1)}, bf16[640,128]{1,0:T(8,128)(2,1)S(1)}, u32[]{:S(2)}, u32[]{:S(2)}) collective-permute-start(bf16[640,128]{1,0:T(8,128)(2,1)S(1)} %get-tuple-element.40.refs_0_), channel_id=1, source_target_pairs={{0,1},{1,0},{2,3},{3,2},{4,5},{5,4},{6,7},{7,6},{8,9},{9,8},{10,11... | collective-permute-start | bytes 491528 | tf_op jit(solution)/shard_map/ppermute | solution.py:478
  23.2 0.0 collective-permute-done.1.refs_1_
  23.3 0.1 collective-permute-start.5
  23.3 0.0 collective-permute-done.3.refs_3_
  23.3 1.0 %collective-permute-start.7 = (bf16[512,128]{1,0:T(8,128)(2,1)S(1)}, bf16[512,128]{1,0:T(8,128)(2,1)S(1)}, u32[]{:S(2)}, u32[]{:S(2)}) collective-permute-start(bf16[512,128]{1,0:T(8,128)(2,1)S(1)} %collective-permute-done.3.refs_3_), channel_id=1, source_target_pairs={{0,1},{1,0},{2,3},{3,2},{4,5},{5,4},{6,7},{7,6},{8,9},{9,8},{10,11... | collective-permute-start | bytes 393224 | tf_op jit(solution)/shard_map/ppermute | solution.py:478
  24.3 1.6 %collective-permute-done.2.refs_2_ = bf16[512,128]{1,0:T(8,128)(2,1)S(1)} collective-permute-done((bf16[512,128]{1,0:T(8,128)(2,1)S(1)}, bf16[512,128]{1,0:T(8,128)(2,1)S(1)}, u32[]{:S(2)}, u32[]{:S(2)}) %collective-permute-start.2) | collective-permute-done | bytes 131104 | tf_op jit(solution)/shard_map/ppermute | solution.py:553
  25.9 1.3 %indices.1 = (s32[8,128]{1,0:T(8,128)S(1)}, f32[8,128]{1,0:T(8,128)S(1)}) custom-call(s32[1]{0:T(128)} %bitcast.here_ref, s32[1]{0:T(128)} %bitcast.1.aux_ref, s32[2,16]{1,0:T(2,128)S(1)} %bitcast.9, s32[4,64]{1,0:T(4,128)S(1)} %bitcast.6, f32[4,16]{1,0:T(4,128)S(1)} %bitcast.7), custom_call_target="tpu_custom_call" | custom-call | flops 1000000 | bytes 65536 | tf_op jit(solution)/shard_map/indices/pallas_call | solution.py:143
  27.2 0.0 collective-permute-done.4.refs_4_
  27.2 0.0 collective-permute-done.7.refs_7_
  27.3 0.0 collective-permute-done.5.refs_5_
  27.3 0.9 %exchange.1 = (f32[8,128,128]{2,1,0:T(8,128)S(1)}, bf16[8,128,128]{2,1,0:T(8,128)(2,1)S(1)}, bf16[4,128,128]{2,1,0:T(8,128)(2,1)S(1)}) custom-call(s32[1]{0:T(128)} %bitcast.1.aux_ref, s32[8,128]{1,0:T(8,128)S(1)} %get-tuple-element.31.index_ref, bf16[640,128]{1,0:T(8,128)(2,1)S(1)} %get-tuple-element.40.refs_0_, ...), custom_call_target="tpu_custom_call" | custom-call | flops 134217728 | bytes 2621440 | tf_op jit(solution)/shard_map/exchange/pallas_call | solution.py:242
  28.1 2.4 %collective-permute-start.11 = (bf16[4,128,128]{2,1,0:T(8,128)(2,1)S(1)}, bf16[4,128,128]{2,1,0:T(8,128)(2,1)S(1)}, u32[]{:S(2)}, u32[]{:S(2)}) collective-permute-start(bf16[4,128,128]{2,1,0:T(8,128)(2,1)S(1)} %get-tuple-element.46), channel_id=1, source_target_pairs={{4,12},{8,0},{0,4},{12,8},{5,13},{9,1},{1,5},{13,9},{6,14},{10,2},... | collective-permute-start | bytes 393224 | tf_op jit(solution)/shard_map/ppermute | solution.py:579
  30.5 1.9 %collective-permute-start.10 = (bf16[8,128,128]{2,1,0:T(8,128)(2,1)S(1)}, bf16[8,128,128]{2,1,0:T(8,128)(2,1)S(1)}, u32[]{:S(2)}, u32[]{:S(2)}) collective-permute-start(bf16[8,128,128]{2,1,0:T(8,128)(2,1)S(1)} %get-tuple-element.45.refs_0_), channel_id=1, source_target_pairs={{4,0},{8,12},{5,9},{9,5},{6,2},{10,14},{7,11},{11,7},{20,16},{24,2... | collective-permute-start | bytes 786440 | tf_op jit(solution)/shard_map/ppermute | solution.py:487
  32.4 1.3 %collective-permute-start.9 = (bf16[8,128,128]{2,1,0:T(8,128)(2,1)S(1)}, bf16[8,128,128]{2,1,0:T(8,128)(2,1)S(1)}, u32[]{:S(2)}, u32[]{:S(2)}) collective-permute-start(bf16[8,128,128]{2,1,0:T(8,128)(2,1)S(1)} %get-tuple-element.45.refs_0_), channel_id=1, source_target_pairs={{4,8},{8,4},{5,1},{9,13},{6,10},{10,6},{7,3},{11,15},{20,24},{24,2... | collective-permute-start | bytes 786440 | tf_op jit(solution)/shard_map/ppermute | solution.py:487
  33.7 2.5 %collective-permute-start.8 = (bf16[8,128,128]{2,1,0:T(8,128)(2,1)S(1)}, bf16[8,128,128]{2,1,0:T(8,128)(2,1)S(1)}, u32[]{:S(2)}, u32[]{:S(2)}) collective-permute-start(bf16[8,128,128]{2,1,0:T(8,128)(2,1)S(1)} %get-tuple-element.45.refs_0_), channel_id=1, source_target_pairs={{0,1},{1,0},{2,3},{3,2},{4,5},{5,4},{6,7},{7,6},{8,9},{9,8},{10,11... | collective-permute-start | bytes 786440 | tf_op jit(solution)/shard_map/ppermute | solution.py:478
  36.2 0.1 collective-permute-start.12
  36.3 0.2 collective-permute-start.14
  36.5 1.0 %collective-permute-done.12.piece_ref.refs_5_ = bf16[4,128,128]{2,1,0:T(8,128)(2,1)S(1)} collective-permute-done((bf16[4,128,128]{2,1,0:T(8,128)(2,1)S(1)}, bf16[4,128,128]{2,1,0:T(8,128)(2,1)S(1)}, u32[]{:S(2)}, u32[]{:S(2)}) %collective-permute-start.12) | collective-permute-done | bytes 131104 | tf_op jit(solution)/shard_map/ppermute | solution.py:478
  37.5 0.5 collective-permute-done.10.right_ref
  38.0 0.9 %collective-permute-done.9.left_ref = bf16[8,128,128]{2,1,0:T(8,128)(2,1)S(1)} collective-permute-done((bf16[8,128,128]{2,1,0:T(8,128)(2,1)S(1)}, bf16[8,128,128]{2,1,0:T(8,128)(2,1)S(1)}, u32[]{:S(2)}, u32[]{:S(2)}) %collective-permute-start.9) | collective-permute-done | bytes 262176 | tf_op jit(solution)/shard_map/ppermute | solution.py:487
  38.9 0.1 joined.2.refs_2_
  38.9 2.3 %collective-permute-start.13 = (bf16[8,128,128]{2,1,0:T(8,128)(2,1)S(1)}, bf16[8,128,128]{2,1,0:T(8,128)(2,1)S(1)}, u32[]{:S(2)}, u32[]{:S(2)}) collective-permute-start(bf16[8,128,128]{2,1,0:T(8,128)(2,1)S(1)} %joined.2.refs_2_), channel_id=1, source_target_pairs={{0,1},{1,0},{2,3},{3,2},{4,5},{5,4},{6,7},{7,6},{8,9},{9,8},{10,11... | collective-permute-start | bytes 786440 | tf_op jit(solution)/shard_map/ppermute | solution.py:478
  41.2 1.0 %collective-permute-start.15 = (bf16[4,128,128]{2,1,0:T(8,128)(2,1)S(1)}, bf16[4,128,128]{2,1,0:T(8,128)(2,1)S(1)}, u32[]{:S(2)}, u32[]{:S(2)}) collective-permute-start(bf16[4,128,128]{2,1,0:T(8,128)(2,1)S(1)} %collective-permute-done.14.refs_6_), channel_id=1, source_target_pairs={{0,1},{1,0},{2,3},{3,2},{4,5},{5,4},{6,7},{7,6},{8,9},{9,8},{10,11... | collective-permute-start | bytes 393224 | tf_op jit(solution)/shard_map/ppermute | solution.py:478
  42.2 1.0 %collective-permute-done.15.refs_7_ = bf16[4,128,128]{2,1,0:T(8,128)(2,1)S(1)} collective-permute-done((bf16[4,128,128]{2,1,0:T(8,128)(2,1)S(1)}, bf16[4,128,128]{2,1,0:T(8,128)(2,1)S(1)}, u32[]{:S(2)}, u32[]{:S(2)}) %collective-permute-start.15) | collective-permute-done | bytes 131104 | tf_op jit(solution)/shard_map/ppermute | solution.py:478
  43.2 1.2 %sweep.1 = (bf16[8,128,128]{2,1,0:T(8,128)(2,1)S(1)}, bf16[4,128,128]{2,1,0:T(8,128)(2,1)S(1)}) custom-call(s32[1]{0:T(128)} %bitcast.here_ref, s32[1]{0:T(128)} %bitcast.1.aux_ref, s32[8,128]{1,0:T(8,128)S(1)} %get-tuple-element.31.index_ref, f32[8,128]{1,0:T(8,128)S(1)} %get-tuple-element.32.weight_ref, ...), custom_call_target="tpu_custom_call" | custom-call | flops 268435456 | bytes 2883584 | tf_op jit(solution)/shard_map/sweep/pallas_call | solution.py:333
  44.3 2.0 %collective-permute-start.19 = (bf16[4,128,128]{2,1,0:T(8,128)(2,1)S(1)}, bf16[4,128,128]{2,1,0:T(8,128)(2,1)S(1)}, u32[]{:S(2)}, u32[]{:S(2)}) collective-permute-start(bf16[4,128,128]{2,1,0:T(8,128)(2,1)S(1)} %get-tuple-element.49), channel_id=1, source_target_pairs={{4,12},{8,0},{0,4},{12,8},{5,13},{9,1},{1,5},{13,9},{6,14},{10,2},... | collective-permute-start | bytes 393224 | tf_op jit(solution)/shard_map/ppermute | solution.py:579
  46.3 1.9 %collective-permute-start.18 = (bf16[8,128,128]{2,1,0:T(8,128)(2,1)S(1)}, bf16[8,128,128]{2,1,0:T(8,128)(2,1)S(1)}, u32[]{:S(2)}, u32[]{:S(2)}) collective-permute-start(bf16[8,128,128]{2,1,0:T(8,128)(2,1)S(1)} %get-tuple-element.48.refs_0_), channel_id=1, source_target_pairs={{4,0},{8,12},{5,9},{9,5},{6,2},{10,14},{7,11},{11,7},{20,16},{24,2... | collective-permute-start | bytes 786440 | tf_op jit(solution)/shard_map/ppermute | solution.py:487
  48.3 1.3 %collective-permute-start.17 = (bf16[8,128,128]{2,1,0:T(8,128)(2,1)S(1)}, bf16[8,128,128]{2,1,0:T(8,128)(2,1)S(1)}, u32[]{:S(2)}, u32[]{:S(2)}) collective-permute-start(bf16[8,128,128]{2,1,0:T(8,128)(2,1)S(1)} %get-tuple-element.48.refs_0_), channel_id=1, source_target_pairs={{4,8},{8,4},{5,1},{9,13},{6,10},{10,6},{7,3},{11,15},{20,24},{24,2... | collective-permute-start | bytes 786440 | tf_op jit(solution)/shard_map/ppermute | solution.py:487
  49.6 1.9 %collective-permute-start.16 = (bf16[8,128,128]{2,1,0:T(8,128)(2,1)S(1)}, bf16[8,128,128]{2,1,0:T(8,128)(2,1)S(1)}, u32[]{:S(2)}, u32[]{:S(2)}) collective-permute-start(bf16[8,128,128]{2,1,0:T(8,128)(2,1)S(1)} %get-tuple-element.48.refs_0_), channel_id=1, source_target_pairs={{0,1},{1,0},{2,3},{3,2},{4,5},{5,4},{6,7},{7,6},{8,9},{9,8},{10,11... | collective-permute-start | bytes 786440 | tf_op jit(solution)/shard_map/ppermute | solution.py:478
  51.5 0.0 collective-permute-done.19.piece_ref.refs_4_
  51.5 0.1 collective-permute-start.20
  51.6 0.2 collective-permute-start.22
  51.7 1.7 %collective-permute-done.18.right_ref = bf16[8,128,128]{2,1,0:T(8,128)(2,1)S(1)} collective-permute-done((bf16[8,128,128]{2,1,0:T(8,128)(2,1)S(1)}, bf16[8,128,128]{2,1,0:T(8,128)(2,1)S(1)}, u32[]{:S(2)}, u32[]{:S(2)}) %collective-permute-start.18) | collective-permute-done | bytes 262176 | tf_op jit(solution)/shard_map/ppermute | solution.py:487
  53.5 1.5 %collective-permute-done.17.left_ref = bf16[8,128,128]{2,1,0:T(8,128)(2,1)S(1)} collective-permute-done((bf16[8,128,128]{2,1,0:T(8,128)(2,1)S(1)}, bf16[8,128,128]{2,1,0:T(8,128)(2,1)S(1)}, u32[]{:S(2)}, u32[]{:S(2)}) %collective-permute-start.17) | collective-permute-done | bytes 262176 | tf_op jit(solution)/shard_map/ppermute | solution.py:487
  55.0 0.0 collective-permute-done.20.piece_ref.refs_5_
  55.0 0.1 joined.3.refs_2_
  55.0 2.1 %collective-permute-start.21 = (bf16[8,128,128]{2,1,0:T(8,128)(2,1)S(1)}, bf16[8,128,128]{2,1,0:T(8,128)(2,1)S(1)}, u32[]{:S(2)}, u32[]{:S(2)}) collective-permute-start(bf16[8,128,128]{2,1,0:T(8,128)(2,1)S(1)} %joined.3.refs_2_), channel_id=1, source_target_pairs={{0,1},{1,0},{2,3},{3,2},{4,5},{5,4},{6,7},{7,6},{8,9},{9,8},{10,11... | collective-permute-start | bytes 786440 | tf_op jit(solution)/shard_map/ppermute | solution.py:478
  57.1 0.0 collective-permute-done.22.refs_6_
  57.1 0.4 collective-permute-start.23
  57.5 1.0 %collective-permute-done.23.refs_7_ = bf16[4,128,128]{2,1,0:T(8,128)(2,1)S(1)} collective-permute-done((bf16[4,128,128]{2,1,0:T(8,128)(2,1)S(1)}, bf16[4,128,128]{2,1,0:T(8,128)(2,1)S(1)}, u32[]{:S(2)}, u32[]{:S(2)}) %collective-permute-start.23) | collective-permute-done | bytes 131104 | tf_op jit(solution)/shard_map/ppermute | solution.py:478
  58.5 0.0 collective-permute-done.21.refs_3_
  58.5 2.5 %last_sweep.1 = (f32[8,128,128]{2,1,0:T(8,128)S(1)}, f32[2,128,128]{2,1,0:T(8,128)S(1)}, bf16[2,128,128]{2,1,0:T(8,128)(2,1)S(1)}, bf16[2,128,128]{2,1,0:T(8,128)(2,1)S(1)}) custom-call(s32[1]{0:T(128)} %bitcast.here_ref, s32[1]{0:T(128)} %bitcast.1.aux_ref, s32[8,128]{1,0:T(8,128)S(1)} %get-tuple-element.31.index_ref, ...), custom_call_target="tpu_custom_call" | custom-call | flops 268435456 | bytes 2883584 | tf_op jit(solution)/shard_map/last_sweep/pallas_call | solution.py:333
  61.0 0.4 collective-permute-start.24
  61.4 0.0 collective-permute-start.25
  61.5 4.5 %collective-permute-start.26 = (bf16[2,128,128]{2,1,0:T(8,128)(2,1)S(1)}, bf16[2,128,128]{2,1,0:T(8,128)(2,1)S(1)}, u32[]{:S(2)}, u32[]{:S(2)}) collective-permute-start(bf16[2,128,128]{2,1,0:T(8,128)(2,1)S(1)} %get-tuple-element.55), channel_id=1, source_target_pairs={{4,8},{8,4},{5,9},{9,5},{6,10},{10,6},{7,11},{11,7},{20,24},{24,20... | collective-permute-start | bytes 196616 | tf_op jit(solution)/shard_map/ppermute | solution.py:483
  66.0 0.0 collective-permute-done.24.others_ref
  66.0 2.4 %first_terms.1 = (f32[16,128,128]{2,1,0:T(8,128)}, f32[2,128,128]{2,1,0:T(8,128)S(1)}) custom-call(s32[1]{0:T(128)} %bitcast.1.aux_ref, s32[8,128]{1,0:T(8,128)S(1)} %get-tuple-element.31.index_ref, f32[8,128,128]{2,1,0:T(8,128)S(1)} %get-tuple-element.50.amps_ref, f32[8,128,128]{2,1,0:T(8,128)S(1)} %collective-permute-done.24.others_ref, ...), custom_call_target="tpu_custom_call" | custom-call | flops 201326592 | bytes 2097152 | tf_op jit(solution)/shard_map/first_terms/pallas_call | solution.py:409
  68.4 0.0 collective-permute-done.25
  68.4 0.8 %collective-permute-start.27 = (f32[2,128,128]{2,1,0:T(8,128)S(1)}, f32[2,128,128]{2,1,0:T(8,128)S(1)}, u32[]{:S(2)}, u32[]{:S(2)}) collective-permute-start(f32[2,128,128]{2,1,0:T(8,128)S(1)} %convert_add_fusion), channel_id=1, source_target_pairs={{0,1},{1,0},{2,3},{3,2},{4,5},{5,4},{6,7},{7,6},{8,9},{9,8},{10,11... | collective-permute-start | bytes 393224 | tf_op jit(solution)/shard_map/ppermute | solution.py:478
  69.2 1.0 %collective-permute-done.27 = f32[2,128,128]{2,1,0:T(8,128)S(1)} collective-permute-done((f32[2,128,128]{2,1,0:T(8,128)S(1)}, f32[2,128,128]{2,1,0:T(8,128)S(1)}, u32[]{:S(2)}, u32[]{:S(2)}) %collective-permute-start.27) | collective-permute-done | bytes 131104 | tf_op jit(solution)/shard_map/ppermute | solution.py:478
  70.2 0.7 add_multiply_fusion
  (25 shorter events, 0.1 us)
Async XLA Ops:
  0.6 25.2 %copy-start.5 = (s32[64,4]{0,1:T(4,128)S(1)}, s32[64,4]{0,1:T(4,128)}, u32[]{:S(2)}) copy-start(s32[64,4]{0,1:T(4,128)} %param.19) | copy-start | bytes 3076
  0.6 25.2 %copy-start.8 = (s32[16,2]{0,1:T(2,128)S(1)}, s32[16,2]{0,1:T(2,128)}, u32[]{:S(2)}) copy-start(s32[16,2]{0,1:T(2,128)} %param.18) | copy-start | bytes 388
  0.7 25.2 %copy-start.6 = (f32[16,4]{0,1:T(4,128)S(1)}, f32[16,4]{0,1:T(4,128)}, u32[]{:S(2)}) copy-start(f32[16,4]{0,1:T(4,128)} %param.14) | copy-start | bytes 772
  0.7 13.4 %collective-permute-start = (bf16[2,1536,128]{2,1,0:T(8,128)(2,1)}, bf16[2,1536,128]{2,1,0:T(8,128)(2,1)S(1)}, u32[]{:S(2)}, u32[]{:S(2)}) collective-permute-start(bf16[2,1536,128]{2,1,0:T(8,128)(2,1)} %ints_ref), channel_id=1, source_target_pairs={{4,0},{8,4},{12,8},{1,5},{5,9},{9,13},{6,2},{10,6},{14,10},{3,7},{... | collective-permute-start | bytes 2359304 | tf_op jit(solution)/shard_map/ppermute | solution.py:506
  4.0 1.1 %copy-start.1 = (bf16[2,1536,128]{2,1,0:T(8,128)(2,1)S(1)}, bf16[2,1536,128]{2,1,0:T(8,128)(2,1)}, u32[]{:S(2)}) copy-start(bf16[2,1536,128]{2,1,0:T(8,128)(2,1)} %ints_ref) | copy-start | bytes 2359300
  5.2 1.0 %copy-start.2 = (bf16[16,128,128]{2,1,0:T(8,128)(2,1)S(1)}, bf16[16,128,128]{2,1,0:T(8,128)(2,1)}, u32[]{:S(2)}) copy-start(bf16[16,128,128]{2,1,0:T(8,128)(2,1)} %first_ref.1) | copy-start | bytes 1572868
  6.2 1.0 %copy-start.3 = (bf16[16,128,128]{2,1,0:T(8,128)(2,1)S(1)}, bf16[16,128,128]{2,1,0:T(8,128)(2,1)}, u32[]{:S(2)}) copy-start(bf16[16,128,128]{2,1,0:T(8,128)(2,1)} %second_ref.1) | copy-start | bytes 1572868
  7.2 0.7 copy-start.4
  7.9 0.7 copy-start.7
  8.6 0.7 copy-start.9
  14.6 8.7 %collective-permute-start.1 = (bf16[640,128]{1,0:T(8,128)(2,1)S(1)}, bf16[640,128]{1,0:T(8,128)(2,1)S(1)}, u32[]{:S(2)}, u32[]{:S(2)}) collective-permute-start(bf16[640,128]{1,0:T(8,128)(2,1)S(1)} %get-tuple-element.40.refs_0_), channel_id=1, source_target_pairs={{0,2},{1,3},{2,0},{3,1},{4,6},{5,7},{6,4},{7,5},{8,10},{9,11},{10,... | collective-permute-start | bytes 491528 | tf_op jit(solution)/shard_map/ppermute | solution.py:478
  14.9 8.5 %collective-permute-start.3 = (bf16[512,128]{1,0:T(8,128)(2,1)S(1)}, bf16[512,128]{1,0:T(8,128)(2,1)S(1)}, u32[]{:S(2)}, u32[]{:S(2)}) collective-permute-start(bf16[512,128]{1,0:T(8,128)(2,1)S(1)} %get-tuple-element.41), channel_id=1, source_target_pairs={{0,7},{4,11},{8,15},{5,2},{9,6},{13,10},{2,5},{6,9},{10,13},{7,0},... | collective-permute-start | bytes 393224 | tf_op jit(solution)/shard_map/ppermute | solution.py:553
  19.6 6.3 %collective-permute-start.2 = (bf16[512,128]{1,0:T(8,128)(2,1)S(1)}, bf16[512,128]{1,0:T(8,128)(2,1)S(1)}, u32[]{:S(2)}, u32[]{:S(2)}) collective-permute-start(bf16[512,128]{1,0:T(8,128)(2,1)S(1)} %get-tuple-element.41), channel_id=1, source_target_pairs={{0,5},{4,9},{8,13},{5,0},{9,4},{13,8},{2,7},{6,11},{10,15},{7,2},{... | collective-permute-start | bytes 393224 | tf_op jit(solution)/shard_map/ppermute | solution.py:553
  21.5 5.7 %collective-permute-start.4 = (bf16[640,128]{1,0:T(8,128)(2,1)S(1)}, bf16[640,128]{1,0:T(8,128)(2,1)S(1)}, u32[]{:S(2)}, u32[]{:S(2)}) collective-permute-start(bf16[640,128]{1,0:T(8,128)(2,1)S(1)} %get-tuple-element.40.refs_0_), channel_id=1, source_target_pairs={{0,1},{1,0},{2,3},{3,2},{4,5},{5,4},{6,7},{7,6},{8,9},{9,8},{10,11... | collective-permute-start | bytes 491528 | tf_op jit(solution)/shard_map/ppermute | solution.py:478
  23.3 4.0 %collective-permute-start.5 = (bf16[640,128]{1,0:T(8,128)(2,1)S(1)}, bf16[640,128]{1,0:T(8,128)(2,1)S(1)}, u32[]{:S(2)}, u32[]{:S(2)}) collective-permute-start(bf16[640,128]{1,0:T(8,128)(2,1)S(1)} %collective-permute-done.1.refs_1_), channel_id=1, source_target_pairs={{0,1},{1,0},{2,3},{3,2},{4,5},{5,4},{6,7},{7,6},{8,9},{9,8},{10,11... | collective-permute-start | bytes 491528 | tf_op jit(solution)/shard_map/ppermute | solution.py:478
  23.3 3.9 %collective-permute-start.7 = (bf16[512,128]{1,0:T(8,128)(2,1)S(1)}, bf16[512,128]{1,0:T(8,128)(2,1)S(1)}, u32[]{:S(2)}, u32[]{:S(2)}) collective-permute-start(bf16[512,128]{1,0:T(8,128)(2,1)S(1)} %collective-permute-done.3.refs_3_), channel_id=1, source_target_pairs={{0,1},{1,0},{2,3},{3,2},{4,5},{5,4},{6,7},{7,6},{8,9},{9,8},{10,11... | collective-permute-start | bytes 393224 | tf_op jit(solution)/shard_map/ppermute | solution.py:478
  25.9 1.4 %collective-permute-start.6 = (bf16[512,128]{1,0:T(8,128)(2,1)S(1)}, bf16[512,128]{1,0:T(8,128)(2,1)S(1)}, u32[]{:S(2)}, u32[]{:S(2)}) collective-permute-start(bf16[512,128]{1,0:T(8,128)(2,1)S(1)} %collective-permute-done.2.refs_2_), channel_id=1, source_target_pairs={{0,1},{1,0},{2,3},{3,2},{4,5},{5,4},{6,7},{7,6},{8,9},{9,8},{10,11... | collective-permute-start | bytes 393224 | tf_op jit(solution)/shard_map/ppermute | solution.py:478
  28.1 8.0 %collective-permute-start.11 = (bf16[4,128,128]{2,1,0:T(8,128)(2,1)S(1)}, bf16[4,128,128]{2,1,0:T(8,128)(2,1)S(1)}, u32[]{:S(2)}, u32[]{:S(2)}) collective-permute-start(bf16[4,128,128]{2,1,0:T(8,128)(2,1)S(1)} %get-tuple-element.46), channel_id=1, source_target_pairs={{4,12},{8,0},{0,4},{12,8},{5,13},{9,1},{1,5},{13,9},{6,14},{10,2},... | collective-permute-start | bytes 393224 | tf_op jit(solution)/shard_map/ppermute | solution.py:579
  30.5 7.5 %collective-permute-start.10 = (bf16[8,128,128]{2,1,0:T(8,128)(2,1)S(1)}, bf16[8,128,128]{2,1,0:T(8,128)(2,1)S(1)}, u32[]{:S(2)}, u32[]{:S(2)}) collective-permute-start(bf16[8,128,128]{2,1,0:T(8,128)(2,1)S(1)} %get-tuple-element.45.refs_0_), channel_id=1, source_target_pairs={{4,0},{8,12},{5,9},{9,5},{6,2},{10,14},{7,11},{11,7},{20,16},{24,2... | collective-permute-start | bytes 786440 | tf_op jit(solution)/shard_map/ppermute | solution.py:487
  32.4 6.5 %collective-permute-start.9 = (bf16[8,128,128]{2,1,0:T(8,128)(2,1)S(1)}, bf16[8,128,128]{2,1,0:T(8,128)(2,1)S(1)}, u32[]{:S(2)}, u32[]{:S(2)}) collective-permute-start(bf16[8,128,128]{2,1,0:T(8,128)(2,1)S(1)} %get-tuple-element.45.refs_0_), channel_id=1, source_target_pairs={{4,8},{8,4},{5,1},{9,13},{6,10},{10,6},{7,3},{11,15},{20,24},{24,2... | collective-permute-start | bytes 786440 | tf_op jit(solution)/shard_map/ppermute | solution.py:487
  33.7 8.5 %collective-permute-start.8 = (bf16[8,128,128]{2,1,0:T(8,128)(2,1)S(1)}, bf16[8,128,128]{2,1,0:T(8,128)(2,1)S(1)}, u32[]{:S(2)}, u32[]{:S(2)}) collective-permute-start(bf16[8,128,128]{2,1,0:T(8,128)(2,1)S(1)} %get-tuple-element.45.refs_0_), channel_id=1, source_target_pairs={{0,1},{1,0},{2,3},{3,2},{4,5},{5,4},{6,7},{7,6},{8,9},{9,8},{10,11... | collective-permute-start | bytes 786440 | tf_op jit(solution)/shard_map/ppermute | solution.py:478
  36.2 1.3 %collective-permute-start.12 = (bf16[4,128,128]{2,1,0:T(8,128)(2,1)S(1)}, bf16[4,128,128]{2,1,0:T(8,128)(2,1)S(1)}, u32[]{:S(2)}, u32[]{:S(2)}) collective-permute-start(bf16[4,128,128]{2,1,0:T(8,128)(2,1)S(1)} %collective-permute-done.11.piece_ref.refs_4_), channel_id=1, source_target_pairs={{0,1},{1,0},{2,3},{3,2},{4,5},{5,4},{6,7},{7,6},{8,9},{9,8},{10,11... | collective-permute-start | bytes 393224 | tf_op jit(solution)/shard_map/ppermute | solution.py:478
  36.2 6.9 %copy-start = (bf16[16,4,128,128]{3,2,1,0:T(8,128)(2,1)S(1)}, bf16[16,4,128,128]{3,2,1,0:T(8,128)(2,1)}, u32[]{:S(2)}) copy-start(bf16[16,4,128,128]{3,2,1,0:T(8,128)(2,1)} %refs_8_.3) | copy-start | bytes 6291460
  36.3 5.0 %collective-permute-start.14 = (bf16[4,128,128]{2,1,0:T(8,128)(2,1)S(1)}, bf16[4,128,128]{2,1,0:T(8,128)(2,1)S(1)}, u32[]{:S(2)}, u32[]{:S(2)}) collective-permute-start(bf16[4,128,128]{2,1,0:T(8,128)(2,1)S(1)} %collective-permute-done.11.piece_ref.refs_4_), channel_id=1, source_target_pairs={{0,2},{1,3},{2,0},{3,1},{4,6},{5,7},{6,4},{7,5},{8,10},{9,11},{10,... | collective-permute-start | bytes 393224 | tf_op jit(solution)/shard_map/ppermute | solution.py:478
  38.9 4.2 %collective-permute-start.13 = (bf16[8,128,128]{2,1,0:T(8,128)(2,1)S(1)}, bf16[8,128,128]{2,1,0:T(8,128)(2,1)S(1)}, u32[]{:S(2)}, u32[]{:S(2)}) collective-permute-start(bf16[8,128,128]{2,1,0:T(8,128)(2,1)S(1)} %joined.2.refs_2_), channel_id=1, source_target_pairs={{0,1},{1,0},{2,3},{3,2},{4,5},{5,4},{6,7},{7,6},{8,9},{9,8},{10,11... | collective-permute-start | bytes 786440 | tf_op jit(solution)/shard_map/ppermute | solution.py:478
  41.2 1.9 %collective-permute-start.15 = (bf16[4,128,128]{2,1,0:T(8,128)(2,1)S(1)}, bf16[4,128,128]{2,1,0:T(8,128)(2,1)S(1)}, u32[]{:S(2)}, u32[]{:S(2)}) collective-permute-start(bf16[4,128,128]{2,1,0:T(8,128)(2,1)S(1)} %collective-permute-done.14.refs_6_), channel_id=1, source_target_pairs={{0,1},{1,0},{2,3},{3,2},{4,5},{5,4},{6,7},{7,6},{8,9},{9,8},{10,11... | collective-permute-start | bytes 393224 | tf_op jit(solution)/shard_map/ppermute | solution.py:478
  44.3 7.2 %collective-permute-start.19 = (bf16[4,128,128]{2,1,0:T(8,128)(2,1)S(1)}, bf16[4,128,128]{2,1,0:T(8,128)(2,1)S(1)}, u32[]{:S(2)}, u32[]{:S(2)}) collective-permute-start(bf16[4,128,128]{2,1,0:T(8,128)(2,1)S(1)} %get-tuple-element.49), channel_id=1, source_target_pairs={{4,12},{8,0},{0,4},{12,8},{5,13},{9,1},{1,5},{13,9},{6,14},{10,2},... | collective-permute-start | bytes 393224 | tf_op jit(solution)/shard_map/ppermute | solution.py:579
  46.3 7.1 %collective-permute-start.18 = (bf16[8,128,128]{2,1,0:T(8,128)(2,1)S(1)}, bf16[8,128,128]{2,1,0:T(8,128)(2,1)S(1)}, u32[]{:S(2)}, u32[]{:S(2)}) collective-permute-start(bf16[8,128,128]{2,1,0:T(8,128)(2,1)S(1)} %get-tuple-element.48.refs_0_), channel_id=1, source_target_pairs={{4,0},{8,12},{5,9},{9,5},{6,2},{10,14},{7,11},{11,7},{20,16},{24,2... | collective-permute-start | bytes 786440 | tf_op jit(solution)/shard_map/ppermute | solution.py:487
  48.3 6.7 %collective-permute-start.17 = (bf16[8,128,128]{2,1,0:T(8,128)(2,1)S(1)}, bf16[8,128,128]{2,1,0:T(8,128)(2,1)S(1)}, u32[]{:S(2)}, u32[]{:S(2)}) collective-permute-start(bf16[8,128,128]{2,1,0:T(8,128)(2,1)S(1)} %get-tuple-element.48.refs_0_), channel_id=1, source_target_pairs={{4,8},{8,4},{5,1},{9,13},{6,10},{10,6},{7,3},{11,15},{20,24},{24,2... | collective-permute-start | bytes 786440 | tf_op jit(solution)/shard_map/ppermute | solution.py:487
  49.6 7.9 %collective-permute-start.16 = (bf16[8,128,128]{2,1,0:T(8,128)(2,1)S(1)}, bf16[8,128,128]{2,1,0:T(8,128)(2,1)S(1)}, u32[]{:S(2)}, u32[]{:S(2)}) collective-permute-start(bf16[8,128,128]{2,1,0:T(8,128)(2,1)S(1)} %get-tuple-element.48.refs_0_), channel_id=1, source_target_pairs={{0,1},{1,0},{2,3},{3,2},{4,5},{5,4},{6,7},{7,6},{8,9},{9,8},{10,11... | collective-permute-start | bytes 786440 | tf_op jit(solution)/shard_map/ppermute | solution.py:478
  51.5 3.5 %collective-permute-start.20 = (bf16[4,128,128]{2,1,0:T(8,128)(2,1)S(1)}, bf16[4,128,128]{2,1,0:T(8,128)(2,1)S(1)}, u32[]{:S(2)}, u32[]{:S(2)}) collective-permute-start(bf16[4,128,128]{2,1,0:T(8,128)(2,1)S(1)} %collective-permute-done.19.piece_ref.refs_4_), channel_id=1, source_target_pairs={{0,1},{1,0},{2,3},{3,2},{4,5},{5,4},{6,7},{7,6},{8,9},{9,8},{10,11... | collective-permute-start | bytes 393224 | tf_op jit(solution)/shard_map/ppermute | solution.py:478
  51.6 5.5 %collective-permute-start.22 = (bf16[4,128,128]{2,1,0:T(8,128)(2,1)S(1)}, bf16[4,128,128]{2,1,0:T(8,128)(2,1)S(1)}, u32[]{:S(2)}, u32[]{:S(2)}) collective-permute-start(bf16[4,128,128]{2,1,0:T(8,128)(2,1)S(1)} %collective-permute-done.19.piece_ref.refs_4_), channel_id=1, source_target_pairs={{0,2},{1,3},{2,0},{3,1},{4,6},{5,7},{6,4},{7,5},{8,10},{9,11},{10,... | collective-permute-start | bytes 393224 | tf_op jit(solution)/shard_map/ppermute | solution.py:478
  55.0 3.4 %collective-permute-start.21 = (bf16[8,128,128]{2,1,0:T(8,128)(2,1)S(1)}, bf16[8,128,128]{2,1,0:T(8,128)(2,1)S(1)}, u32[]{:S(2)}, u32[]{:S(2)}) collective-permute-start(bf16[8,128,128]{2,1,0:T(8,128)(2,1)S(1)} %joined.3.refs_2_), channel_id=1, source_target_pairs={{0,1},{1,0},{2,3},{3,2},{4,5},{5,4},{6,7},{7,6},{8,9},{9,8},{10,11... | collective-permute-start | bytes 786440 | tf_op jit(solution)/shard_map/ppermute | solution.py:478
  57.1 1.4 %collective-permute-start.23 = (bf16[4,128,128]{2,1,0:T(8,128)(2,1)S(1)}, bf16[4,128,128]{2,1,0:T(8,128)(2,1)S(1)}, u32[]{:S(2)}, u32[]{:S(2)}) collective-permute-start(bf16[4,128,128]{2,1,0:T(8,128)(2,1)S(1)} %collective-permute-done.22.refs_6_), channel_id=1, source_target_pairs={{0,1},{1,0},{2,3},{3,2},{4,5},{5,4},{6,7},{7,6},{8,9},{9,8},{10,11... | collective-permute-start | bytes 393224 | tf_op jit(solution)/shard_map/ppermute | solution.py:478
  61.0 5.0 %collective-permute-start.24 = (f32[8,128,128]{2,1,0:T(8,128)S(1)}, f32[8,128,128]{2,1,0:T(8,128)S(1)}, u32[]{:S(2)}, u32[]{:S(2)}) collective-permute-start(f32[8,128,128]{2,1,0:T(8,128)S(1)} %get-tuple-element.50.amps_ref), channel_id=1, source_target_pairs={{0,1},{1,0},{2,3},{3,2},{4,5},{5,4},{6,7},{7,6},{8,9},{9,8},{10,11... | collective-permute-start | bytes 1572872 | tf_op jit(solution)/shard_map/ppermute | solution.py:478
  61.4 6.9 %collective-permute-start.25 = (bf16[2,128,128]{2,1,0:T(8,128)(2,1)S(1)}, bf16[2,128,128]{2,1,0:T(8,128)(2,1)S(1)}, u32[]{:S(2)}, u32[]{:S(2)}) collective-permute-start(bf16[2,128,128]{2,1,0:T(8,128)(2,1)S(1)} %get-tuple-element.54), channel_id=1, source_target_pairs={{0,4},{4,0},{8,12},{12,8},{1,5},{5,1},{9,13},{13,9},{2,6},{6,2},{1... | collective-permute-start | bytes 196616 | tf_op jit(solution)/shard_map/ppermute | solution.py:483
  61.5 6.9 %collective-permute-start.26 = (bf16[2,128,128]{2,1,0:T(8,128)(2,1)S(1)}, bf16[2,128,128]{2,1,0:T(8,128)(2,1)S(1)}, u32[]{:S(2)}, u32[]{:S(2)}) collective-permute-start(bf16[2,128,128]{2,1,0:T(8,128)(2,1)S(1)} %get-tuple-element.55), channel_id=1, source_target_pairs={{4,8},{8,4},{5,9},{9,5},{6,10},{10,6},{7,11},{11,7},{20,24},{24,20... | collective-permute-start | bytes 196616 | tf_op jit(solution)/shard_map/ppermute | solution.py:483
  68.4 1.8 %collective-permute-start.27 = (f32[2,128,128]{2,1,0:T(8,128)S(1)}, f32[2,128,128]{2,1,0:T(8,128)S(1)}, u32[]{:S(2)}, u32[]{:S(2)}) collective-permute-start(f32[2,128,128]{2,1,0:T(8,128)S(1)} %convert_add_fusion), channel_id=1, source_target_pairs={{0,1},{1,0},{2,3},{3,2},{4,5},{5,4},{6,7},{7,6},{8,9},{9,8},{10,11... | collective-permute-start | bytes 393224 | tf_op jit(solution)/shard_map/ppermute | solution.py:478

commit v9 on v8

--- a/solution.py
+++ b/solution.py
@@ -255,23 +255,33 @@
     )(aux, index, *sums, first, second, factor)
 
 
-def sweep_kernel(last, pieces, here_ref, aux_ref, index_ref, weight_ref, *refs):
+def sweep_kernel(step, pieces, here_ref, aux_ref, index_ref, weight_ref, *refs):
     parts = refs[:pieces]
     over_ref, exch_ref, factor_ref, second_ref = refs[pieces : pieces + 4]
-    if last:
-        amps_ref, terms_ref, one_ref, two_ref, all_terms, table = refs[pieces + 4 :]
-    else:
-        low_ref, part_ref, table = refs[pieces + 4 :]
+    last = step == "last"
+    refs = refs[pieces + 4 :]
     count, width, _ = exch_ref.shape
     nbr_count = over_ref.shape[1]
     here = here_ref[0]
     half = lax.rem(aux_ref[0], 2)
-    at = 0
-    for part in parts:
-        table[at : at + part.shape[0]] = part[...]
-        at += part.shape[0]
+    across = lax.rem(aux_ref[0] // 2, 2) * (count // 2)
+    if step == "rest":
+        table, part_ref = parts
+        (low_ref,) = refs
+        low_ref[pl.ds(across, count // 2)] = part_ref[...]
+        pairs = [count // 2 - across + k for k in range(count // 2)]
+    else:
+        table = refs[-1]
+        at = 0
+        for part in parts:
+            table[at : at + part.shape[0]] = part[...]
+            at += part.shape[0]
+        pairs = [across + k for k in range(count // 2)]
+    if last:
+        amps_ref, terms_ref, one_ref, two_ref, all_terms, table = refs
+        pairs = range(count)
     done = []
-    for p in range(count):
+    for k, p in enumerate(pairs):
         row = half * count + p
         halves = []
         for n in range(nbr_count):
@@ -286,11 +296,11 @@
         if last:
             amps_ref[p] = amps
             done.append(amps)
+        elif step == "part":
+            refs[0][k] = amps.astype(BF16)
         else:
             low_ref[p] = amps.astype(BF16)
-    if not last:
-        own_part(aux_ref, low_ref, part_ref)
-    else:
+    if last:
         terms = []
         for p in range(count):
             right = second_ref[p]
@@ -313,33 +323,43 @@
 
 def sweep(last, here, aux, index, weight, parts, over, exch, factor, second):
     count, width, _ = exch.shape
-    rows = sum(part.shape[0] for part in parts)
+    table = (sum(part.shape[0] for part in parts), width, width)
+
+    def call(step, parts, out_shape, scratch):
+        return pl.pallas_call(
+            functools.partial(sweep_kernel, step, len(parts)),
+            out_shape=out_shape,
+            in_specs=[SMEM] * 2 + [VMEM] * (len(parts) + 6),
+            out_specs=(VMEM,) * len(out_shape),
+            scratch_shapes=scratch,
+            compiler_params=params(16),
+            cost_estimate=cost(16 * count * width**3, (table[0] + 16 * count) * width * width),
+            name="sweep_" + step,
+        )(here, aux, index, weight, *parts, over, exch, factor, second)
+
     if last:
-        out_shape = (
-            jax.ShapeDtypeStruct(exch.shape, F32),
-            jax.ShapeDtypeStruct((2, width, width), F32),
-            jax.ShapeDtypeStruct((2, width, width), BF16),
-            jax.ShapeDtypeStruct((2, width, width), BF16),
-        )
-        out_specs = (VMEM,) * 4
-        scratch = [pltpu.VMEM((6, width, width), F32)]
-    else:
-        out_shape = (
-            jax.ShapeDtypeStruct(exch.shape, BF16),
+        return call(
+            "last",
+            parts,
+            (
+                jax.ShapeDtypeStruct(exch.shape, F32),
+                jax.ShapeDtypeStruct((2, width, width), F32),
+                jax.ShapeDtypeStruct((2, width, width), BF16),
+                jax.ShapeDtypeStruct((2, width, width), BF16),
+            ),
+            [pltpu.VMEM((6, width, width), F32), pltpu.VMEM(table, BF16)],
+        )
+    part, whole = call(
+        "part",
+        parts,
+        (
             jax.ShapeDtypeStruct((count // 2, width, width), BF16),
-        )
-        out_specs = (VMEM, VMEM)
-        scratch = []
-    return pl.pallas_call(
-        functools.partial(sweep_kernel, last, len(parts)),
-        out_shape=out_shape,
-        in_specs=[SMEM] * 2 + [VMEM] * (len(parts) + 6),
-        out_specs=out_specs,
-        scratch_shapes=scratch + [pltpu.VMEM((rows, width, width), BF16)],
-        compiler_params=params(16),
-        cost_estimate=cost(16 * count * width**3, (rows + 16 * count) * width * width),
-        name="last_sweep" if last else "sweep",
-    )(here, aux, index, weight, *parts, over, exch, factor, second)
+            jax.ShapeDtypeStruct(table, BF16),
+        ),
+        [],
+    )
+    (low,) = call("rest", (whole, part), (jax.ShapeDtypeStruct(exch.shape, BF16),), [])
+    return low, part
 
 
 def token_kernel(piece_ref, out_ref):

time: 71.7 us -> 70.9 us (0.989)
  starting transfers between devices: 40.2 us -> 39.4 us
    ppermute x1, starting transfers between devices: 4.53 us -> 3.03 us  [both(): lax.ppermute(two, 'pair', partners[1])]
    pallas_call x2 -> x3, Pallas kernels: 3.71 us -> 4.09 us  [call(): pl.pallas_call(functools.partial(sweep_kernel, step, len(parts)), out_sha...]
  transfers between devices with their start and end apart: 28 -> 28, of which waited for: 10 -> 10; matrix products, arithmetic and copies ran while one was open for 0% -> 0% of each run, Pallas kernels for 7% -> 8%
where the time goes in v9:
time: 70.9 us; the launch traced here: 70.4 us
  starting transfers between devices  39.4 us (56%)
  waiting for transfers between devices  14 us (20%)
  Pallas kernels  10.2 us (14%)
  local copies, waits for them, and re-layouts  5.26 us (7%)
  between operations  0.9 us (1%)
    ppermute x17, starting transfers between devices, swap(): return lax.ppermute(value, 'aux', [(i, i ^ step) for i in range(aux_count)])  15.6 us
    ppermute x2, starting transfers between devices, over_z(): lax.ppermute(sent, ('pair', 'aux'), joint([[(i, i + 1, turn) for i in ran...  6.61 us
    ppermute x4, starting transfers between devices, exchanged(): lax.ppermute(value, ('pair', 'aux'), [(i * aux_count + a, j * aux_count +...  6.44 us
    unnamed x20, local copies, waits for them, and re-layouts  5.26 us
    ppermute x4, waiting for transfers between devices, exchanged(): lax.ppermute(value, ('pair', 'aux'), [(i * aux_count + a, j * aux_count +...  4.54 us
    ppermute x2, starting transfers between devices, gathered(): one = lax.ppermute(part, 'pair', rounds[0])  4.38 us
    pallas_call x3, Pallas kernels, call(): pl.pallas_call(functools.partial(sweep_kernel, step, len(parts)), out_sha...  4.09 us
    ppermute x17, waiting for transfers between devices, swap(): return lax.ppermute(value, 'aux', [(i, i ^ step) for i in range(aux_count)])  4.04 us
  transfers between devices with their start and end apart: 28, of which 10 were waited for; matrix products, arithmetic and copies ran while one was open for 0% of the time, Pallas kernels for 8%

profile of v9, /device:TPU:15, one launch (start us, length us, event | category | flops | bytes accessed | tf_op | source)
XLA Modules:
  0.0 70.4 jit_solution(4854495655300876237)
XLA Ops:
  0.7 3.3 %collective-permute-start = (bf16[2,1536,128]{2,1,0:T(8,128)(2,1)}, bf16[2,1536,128]{2,1,0:T(8,128)(2,1)S(1)}, u32[]{:S(2)}, u32[]{:S(2)}) collective-permute-start(bf16[2,1536,128]{2,1,0:T(8,128)(2,1)} %ints_ref), channel_id=1, source_target_pairs={{4,0},{8,4},{12,8},{1,5},{5,9},{9,13},{6,2},{10,6},{14,10},{3,7},{... | collective-permute-start | bytes 2359304 | tf_op jit(solution)/shard_map/ppermute | solution.py:526
  4.0 1.1 %copy-done.1 = bf16[2,1536,128]{2,1,0:T(8,128)(2,1)S(1)} copy-done((bf16[2,1536,128]{2,1,0:T(8,128)(2,1)S(1)}, bf16[2,1536,128]{2,1,0:T(8,128)(2,1)}, u32[]{:S(2)}) %copy-start.1) | copy-done | bytes 786456
  5.2 1.0 %copy-done.2 = bf16[16,128,128]{2,1,0:T(8,128)(2,1)S(1)} copy-done((bf16[16,128,128]{2,1,0:T(8,128)(2,1)S(1)}, bf16[16,128,128]{2,1,0:T(8,128)(2,1)}, u32[]{:S(2)}) %copy-start.2) | copy-done | bytes 524312
  6.2 1.0 %copy-done.3 = bf16[16,128,128]{2,1,0:T(8,128)(2,1)S(1)} copy-done((bf16[16,128,128]{2,1,0:T(8,128)(2,1)S(1)}, bf16[16,128,128]{2,1,0:T(8,128)(2,1)}, u32[]{:S(2)}) %copy-start.3) | copy-done | bytes 524312
  7.2 0.7 copy-done.4
  7.9 0.7 copy-done.7
  8.6 0.7 copy-done.9
  9.3 0.9 %prepare.1 = (bf16[8,128,128]{2,1,0:T(8,128)(2,1)S(1)}, bf16[8,128,128]{2,1,0:T(8,128)(2,1)S(1)}, bf16[2,1536,128]{2,1,0:T(8,128)(2,1)S(1)}, f32[8,128,128]{2,1,0:T(8,128)S(1)}) custom-call(s32[1]{0:T(128)} %bitcast.1.aux_ref, f32[2,16]{1,0:T(2,128)S(1)} %bitcast.8, s32[16]{0:T(128)S(1)} %copy-done.9, f32[16,128]{1,0:T(8,128)S(1)} %copy-done.4, ...), custom_call_target="tpu_custom_call" | custom-call | bytes 2097152 | tf_op jit(solution)/shard_map/prepare/pallas_call | solution.py:75
  10.2 3.9 %collective-permute-done.near_ref = bf16[2,1536,128]{2,1,0:T(8,128)(2,1)S(1)} collective-permute-done((bf16[2,1536,128]{2,1,0:T(8,128)(2,1)}, bf16[2,1536,128]{2,1,0:T(8,128)(2,1)S(1)}, u32[]{:S(2)}, u32[]{:S(2)}) %collective-permute-start) | collective-permute-done | bytes 786464 | tf_op jit(solution)/shard_map/ppermute | solution.py:526
  14.0 0.5 products.1
  14.6 0.3 collective-permute-start.1
  14.9 4.7 %collective-permute-start.3 = (bf16[512,128]{1,0:T(8,128)(2,1)S(1)}, bf16[512,128]{1,0:T(8,128)(2,1)S(1)}, u32[]{:S(2)}, u32[]{:S(2)}) collective-permute-start(bf16[512,128]{1,0:T(8,128)(2,1)S(1)} %get-tuple-element.41), channel_id=1, source_target_pairs={{0,7},{4,11},{8,15},{5,2},{9,6},{13,10},{2,5},{6,9},{10,13},{7,0},... | collective-permute-start | bytes 393224 | tf_op jit(solution)/shard_map/ppermute | solution.py:573
  19.6 1.9 %collective-permute-start.2 = (bf16[512,128]{1,0:T(8,128)(2,1)S(1)}, bf16[512,128]{1,0:T(8,128)(2,1)S(1)}, u32[]{:S(2)}, u32[]{:S(2)}) collective-permute-start(bf16[512,128]{1,0:T(8,128)(2,1)S(1)} %get-tuple-element.41), channel_id=1, source_target_pairs={{0,5},{4,9},{8,13},{5,0},{9,4},{13,8},{2,7},{6,11},{10,15},{7,2},{... | collective-permute-start | bytes 393224 | tf_op jit(solution)/shard_map/ppermute | solution.py:573
  21.5 1.7 %collective-permute-start.4 = (bf16[640,128]{1,0:T(8,128)(2,1)S(1)}, bf16[640,128]{1,0:T(8,128)(2,1)S(1)}, u32[]{:S(2)}, u32[]{:S(2)}) collective-permute-start(bf16[640,128]{1,0:T(8,128)(2,1)S(1)} %get-tuple-element.40.refs_0_), channel_id=1, source_target_pairs={{0,1},{1,0},{2,3},{3,2},{4,5},{5,4},{6,7},{7,6},{8,9},{9,8},{10,11... | collective-permute-start | bytes 491528 | tf_op jit(solution)/shard_map/ppermute | solution.py:498
  23.3 0.0 collective-permute-done.1.refs_1_
  23.3 0.1 collective-permute-start.5
  23.3 0.0 collective-permute-done.3.refs_3_
  23.3 1.0 %collective-permute-start.7 = (bf16[512,128]{1,0:T(8,128)(2,1)S(1)}, bf16[512,128]{1,0:T(8,128)(2,1)S(1)}, u32[]{:S(2)}, u32[]{:S(2)}) collective-permute-start(bf16[512,128]{1,0:T(8,128)(2,1)S(1)} %collective-permute-done.3.refs_3_), channel_id=1, source_target_pairs={{0,1},{1,0},{2,3},{3,2},{4,5},{5,4},{6,7},{7,6},{8,9},{9,8},{10,11... | collective-permute-start | bytes 393224 | tf_op jit(solution)/shard_map/ppermute | solution.py:498
  24.3 1.6 %collective-permute-done.2.refs_2_ = bf16[512,128]{1,0:T(8,128)(2,1)S(1)} collective-permute-done((bf16[512,128]{1,0:T(8,128)(2,1)S(1)}, bf16[512,128]{1,0:T(8,128)(2,1)S(1)}, u32[]{:S(2)}, u32[]{:S(2)}) %collective-permute-start.2) | collective-permute-done | bytes 131104 | tf_op jit(solution)/shard_map/ppermute | solution.py:573
  25.9 0.0 collective-permute-start.6
  25.9 1.3 %indices.1 = (s32[8,128]{1,0:T(8,128)S(1)}, f32[8,128]{1,0:T(8,128)S(1)}) custom-call(s32[1]{0:T(128)} %bitcast.here_ref, s32[1]{0:T(128)} %bitcast.1.aux_ref, s32[2,16]{1,0:T(2,128)S(1)} %bitcast.9, s32[4,64]{1,0:T(4,128)S(1)} %bitcast.6, f32[4,16]{1,0:T(4,128)S(1)} %bitcast.7), custom_call_target="tpu_custom_call" | custom-call | flops 1000000 | bytes 65536 | tf_op jit(solution)/shard_map/indices/pallas_call | solution.py:143
  27.2 0.0 collective-permute-done.4.refs_4_
  27.3 0.0 collective-permute-done.6.refs_6_
  27.3 0.0 collective-permute-done.5.refs_5_
  27.3 0.9 %exchange.1 = (f32[8,128,128]{2,1,0:T(8,128)S(1)}, bf16[8,128,128]{2,1,0:T(8,128)(2,1)S(1)}, bf16[4,128,128]{2,1,0:T(8,128)(2,1)S(1)}) custom-call(s32[1]{0:T(128)} %bitcast.1.aux_ref, s32[8,128]{1,0:T(8,128)S(1)} %get-tuple-element.31.index_ref, bf16[640,128]{1,0:T(8,128)(2,1)S(1)} %get-tuple-element.40.refs_0_, ...), custom_call_target="tpu_custom_call" | custom-call | flops 134217728 | bytes 2621440 | tf_op jit(solution)/shard_map/exchange/pallas_call | solution.py:242
  28.1 2.4 %collective-permute-start.11 = (bf16[4,128,128]{2,1,0:T(8,128)(2,1)S(1)}, bf16[4,128,128]{2,1,0:T(8,128)(2,1)S(1)}, u32[]{:S(2)}, u32[]{:S(2)}) collective-permute-start(bf16[4,128,128]{2,1,0:T(8,128)(2,1)S(1)} %get-tuple-element.46), channel_id=1, source_target_pairs={{4,12},{8,0},{0,4},{12,8},{5,13},{9,1},{1,5},{13,9},{6,14},{10,2},... | collective-permute-start | bytes 393224 | tf_op jit(solution)/shard_map/ppermute | solution.py:599
  30.5 1.9 %collective-permute-start.10 = (bf16[8,128,128]{2,1,0:T(8,128)(2,1)S(1)}, bf16[8,128,128]{2,1,0:T(8,128)(2,1)S(1)}, u32[]{:S(2)}, u32[]{:S(2)}) collective-permute-start(bf16[8,128,128]{2,1,0:T(8,128)(2,1)S(1)} %get-tuple-element.45.refs_0_), channel_id=1, source_target_pairs={{4,0},{8,12},{5,9},{9,5},{6,2},{10,14},{7,11},{11,7},{20,16},{24,2... | collective-permute-start | bytes 786440 | tf_op jit(solution)/shard_map/ppermute | solution.py:507
  32.4 1.3 %collective-permute-start.9 = (bf16[8,128,128]{2,1,0:T(8,128)(2,1)S(1)}, bf16[8,128,128]{2,1,0:T(8,128)(2,1)S(1)}, u32[]{:S(2)}, u32[]{:S(2)}) collective-permute-start(bf16[8,128,128]{2,1,0:T(8,128)(2,1)S(1)} %get-tuple-element.45.refs_0_), channel_id=1, source_target_pairs={{4,8},{8,4},{5,1},{9,13},{6,10},{10,6},{7,3},{11,15},{20,24},{24,2... | collective-permute-start | bytes 786440 | tf_op jit(solution)/shard_map/ppermute | solution.py:507
  33.7 2.5 %collective-permute-start.8 = (bf16[8,128,128]{2,1,0:T(8,128)(2,1)S(1)}, bf16[8,128,128]{2,1,0:T(8,128)(2,1)S(1)}, u32[]{:S(2)}, u32[]{:S(2)}) collective-permute-start(bf16[8,128,128]{2,1,0:T(8,128)(2,1)S(1)} %get-tuple-element.45.refs_0_), channel_id=1, source_target_pairs={{0,1},{1,0},{2,3},{3,2},{4,5},{5,4},{6,7},{7,6},{8,9},{9,8},{10,11... | collective-permute-start | bytes 786440 | tf_op jit(solution)/shard_map/ppermute | solution.py:498
  36.2 0.1 collective-permute-start.12
  36.3 0.2 collective-permute-start.14
  36.5 1.1 %collective-permute-done.12.piece_ref.refs_5_ = bf16[4,128,128]{2,1,0:T(8,128)(2,1)S(1)} collective-permute-done((bf16[4,128,128]{2,1,0:T(8,128)(2,1)S(1)}, bf16[4,128,128]{2,1,0:T(8,128)(2,1)S(1)}, u32[]{:S(2)}, u32[]{:S(2)}) %collective-permute-start.12) | collective-permute-done | bytes 131104 | tf_op jit(solution)/shard_map/ppermute | solution.py:498
  37.5 0.5 collective-permute-done.10.right_ref
  38.0 0.9 %collective-permute-done.9.left_ref = bf16[8,128,128]{2,1,0:T(8,128)(2,1)S(1)} collective-permute-done((bf16[8,128,128]{2,1,0:T(8,128)(2,1)S(1)}, bf16[8,128,128]{2,1,0:T(8,128)(2,1)S(1)}, u32[]{:S(2)}, u32[]{:S(2)}) %collective-permute-start.9) | collective-permute-done | bytes 262176 | tf_op jit(solution)/shard_map/ppermute | solution.py:507
  38.9 0.1 joined.2.refs_2_
  39.0 2.3 %collective-permute-start.13 = (bf16[8,128,128]{2,1,0:T(8,128)(2,1)S(1)}, bf16[8,128,128]{2,1,0:T(8,128)(2,1)S(1)}, u32[]{:S(2)}, u32[]{:S(2)}) collective-permute-start(bf16[8,128,128]{2,1,0:T(8,128)(2,1)S(1)} %joined.2.refs_2_), channel_id=1, source_target_pairs={{0,1},{1,0},{2,3},{3,2},{4,5},{5,4},{6,7},{7,6},{8,9},{9,8},{10,11... | collective-permute-start | bytes 786440 | tf_op jit(solution)/shard_map/ppermute | solution.py:498
  41.2 0.0 collective-permute-done.14.refs_6_
  41.2 1.0 %collective-permute-start.15 = (bf16[4,128,128]{2,1,0:T(8,128)(2,1)S(1)}, bf16[4,128,128]{2,1,0:T(8,128)(2,1)S(1)}, u32[]{:S(2)}, u32[]{:S(2)}) collective-permute-start(bf16[4,128,128]{2,1,0:T(8,128)(2,1)S(1)} %collective-permute-done.14.refs_6_), channel_id=1, source_target_pairs={{0,1},{1,0},{2,3},{3,2},{4,5},{5,4},{6,7},{7,6},{8,9},{9,8},{10,11... | collective-permute-start | bytes 393224 | tf_op jit(solution)/shard_map/ppermute | solution.py:498
  42.2 1.0 %collective-permute-done.15.refs_7_ = bf16[4,128,128]{2,1,0:T(8,128)(2,1)S(1)} collective-permute-done((bf16[4,128,128]{2,1,0:T(8,128)(2,1)S(1)}, bf16[4,128,128]{2,1,0:T(8,128)(2,1)S(1)}, u32[]{:S(2)}, u32[]{:S(2)}) %collective-permute-start.15) | collective-permute-done | bytes 131104 | tf_op jit(solution)/shard_map/ppermute | solution.py:498
  43.2 0.8 %sweep_part.1 = (bf16[4,128,128]{2,1,0:T(8,128)(2,1)S(1)}, bf16[48,128,128]{2,1,0:T(8,128)(2,1)S(1)}) custom-call(s32[1]{0:T(128)} %bitcast.here_ref, s32[1]{0:T(128)} %bitcast.1.aux_ref, s32[8,128]{1,0:T(8,128)S(1)} %get-tuple-element.31.index_ref, f32[8,128]{1,0:T(8,128)S(1)} %get-tuple-element.32.weight_ref, ...), custom_call_target="tpu_custom_call" | custom-call | flops 268435456 | bytes 2883584 | tf_op jit(solution)/shard_map/sweep_part/pallas_call | solution.py:329
  44.0 2.0 %collective-permute-start.19 = (bf16[4,128,128]{2,1,0:T(8,128)(2,1)S(1)}, bf16[4,128,128]{2,1,0:T(8,128)(2,1)S(1)}, u32[]{:S(2)}, u32[]{:S(2)}) collective-permute-start(bf16[4,128,128]{2,1,0:T(8,128)(2,1)S(1)} %get-tuple-element.49.refs_1_), channel_id=1, source_target_pairs={{4,12},{8,0},{0,4},{12,8},{5,13},{9,1},{1,5},{13,9},{6,14},{10,2},... | collective-permute-start | bytes 393224 | tf_op jit(solution)/shard_map/ppermute | solution.py:599
  46.0 0.8 %sweep_rest.1.refs_0_ = bf16[8,128,128]{2,1,0:T(8,128)(2,1)S(1)} custom-call(s32[1]{0:T(128)} %bitcast.here_ref, s32[1]{0:T(128)} %bitcast.1.aux_ref, s32[8,128]{1,0:T(8,128)S(1)} %get-tuple-element.31.index_ref, f32[8,128]{1,0:T(8,128)S(1)} %get-tuple-element.32.weight_ref, bf16[48,128,128]{2,1,0:T(8,128)(2,1)S(1)} %get-tuple-element.48.refs_0_, ...), custom_call_target="tpu_custom_call" | custom-call | flops 268435456 | bytes 2883584 | tf_op jit(solution)/shard_map/sweep_rest/pallas_call | solution.py:329
  46.8 1.9 %collective-permute-start.18 = (bf16[8,128,128]{2,1,0:T(8,128)(2,1)S(1)}, bf16[8,128,128]{2,1,0:T(8,128)(2,1)S(1)}, u32[]{:S(2)}, u32[]{:S(2)}) collective-permute-start(bf16[8,128,128]{2,1,0:T(8,128)(2,1)S(1)} %sweep_rest.1.refs_0_), channel_id=1, source_target_pairs={{4,0},{8,12},{5,9},{9,5},{6,2},{10,14},{7,11},{11,7},{20,16},{24,2... | collective-permute-start | bytes 786440 | tf_op jit(solution)/shard_map/ppermute | solution.py:507
  48.7 1.3 %collective-permute-start.17 = (bf16[8,128,128]{2,1,0:T(8,128)(2,1)S(1)}, bf16[8,128,128]{2,1,0:T(8,128)(2,1)S(1)}, u32[]{:S(2)}, u32[]{:S(2)}) collective-permute-start(bf16[8,128,128]{2,1,0:T(8,128)(2,1)S(1)} %sweep_rest.1.refs_0_), channel_id=1, source_target_pairs={{4,8},{8,4},{5,1},{9,13},{6,10},{10,6},{7,3},{11,15},{20,24},{24,2... | collective-permute-start | bytes 786440 | tf_op jit(solution)/shard_map/ppermute | solution.py:507
  50.0 1.9 %collective-permute-start.16 = (bf16[8,128,128]{2,1,0:T(8,128)(2,1)S(1)}, bf16[8,128,128]{2,1,0:T(8,128)(2,1)S(1)}, u32[]{:S(2)}, u32[]{:S(2)}) collective-permute-start(bf16[8,128,128]{2,1,0:T(8,128)(2,1)S(1)} %sweep_rest.1.refs_0_), channel_id=1, source_target_pairs={{0,1},{1,0},{2,3},{3,2},{4,5},{5,4},{6,7},{7,6},{8,9},{9,8},{10,11... | collective-permute-start | bytes 786440 | tf_op jit(solution)/shard_map/ppermute | solution.py:498
  51.9 0.1 collective-permute-start.20
  52.0 0.2 collective-permute-start.22
  52.2 1.7 %collective-permute-done.18.right_ref = bf16[8,128,128]{2,1,0:T(8,128)(2,1)S(1)} collective-permute-done((bf16[8,128,128]{2,1,0:T(8,128)(2,1)S(1)}, bf16[8,128,128]{2,1,0:T(8,128)(2,1)S(1)}, u32[]{:S(2)}, u32[]{:S(2)}) %collective-permute-start.18) | collective-permute-done | bytes 262176 | tf_op jit(solution)/shard_map/ppermute | solution.py:507
  53.9 1.5 %collective-permute-done.17.left_ref = bf16[8,128,128]{2,1,0:T(8,128)(2,1)S(1)} collective-permute-done((bf16[8,128,128]{2,1,0:T(8,128)(2,1)S(1)}, bf16[8,128,128]{2,1,0:T(8,128)(2,1)S(1)}, u32[]{:S(2)}, u32[]{:S(2)}) %collective-permute-start.17) | collective-permute-done | bytes 262176 | tf_op jit(solution)/shard_map/ppermute | solution.py:507
  55.4 0.1 joined.3.refs_2_
  55.4 2.1 %collective-permute-start.21 = (bf16[8,128,128]{2,1,0:T(8,128)(2,1)S(1)}, bf16[8,128,128]{2,1,0:T(8,128)(2,1)S(1)}, u32[]{:S(2)}, u32[]{:S(2)}) collective-permute-start(bf16[8,128,128]{2,1,0:T(8,128)(2,1)S(1)} %joined.3.refs_2_), channel_id=1, source_target_pairs={{0,1},{1,0},{2,3},{3,2},{4,5},{5,4},{6,7},{7,6},{8,9},{9,8},{10,11... | collective-permute-start | bytes 786440 | tf_op jit(solution)/shard_map/ppermute | solution.py:498
  57.5 0.0 collective-permute-done.22.refs_6_
  57.5 0.4 collective-permute-start.23
  57.9 1.0 %collective-permute-done.23.refs_7_ = bf16[4,128,128]{2,1,0:T(8,128)(2,1)S(1)} collective-permute-done((bf16[4,128,128]{2,1,0:T(8,128)(2,1)S(1)}, bf16[4,128,128]{2,1,0:T(8,128)(2,1)S(1)}, u32[]{:S(2)}, u32[]{:S(2)}) %collective-permute-start.23) | collective-permute-done | bytes 131104 | tf_op jit(solution)/shard_map/ppermute | solution.py:498
  58.9 2.5 %sweep_last.1 = (f32[8,128,128]{2,1,0:T(8,128)S(1)}, f32[2,128,128]{2,1,0:T(8,128)S(1)}, bf16[2,128,128]{2,1,0:T(8,128)(2,1)S(1)}, bf16[2,128,128]{2,1,0:T(8,128)(2,1)S(1)}) custom-call(s32[1]{0:T(128)} %bitcast.here_ref, s32[1]{0:T(128)} %bitcast.1.aux_ref, s32[8,128]{1,0:T(8,128)S(1)} %get-tuple-element.31.index_ref, ...), custom_call_target="tpu_custom_call" | custom-call | flops 268435456 | bytes 2883584 | tf_op jit(solution)/shard_map/sweep_last/pallas_call | solution.py:329
  61.4 0.4 collective-permute-start.24
  61.9 0.0 collective-permute-start.25
  61.9 3.0 %collective-permute-start.26 = (bf16[2,128,128]{2,1,0:T(8,128)(2,1)S(1)}, bf16[2,128,128]{2,1,0:T(8,128)(2,1)S(1)}, u32[]{:S(2)}, u32[]{:S(2)}) collective-permute-start(bf16[2,128,128]{2,1,0:T(8,128)(2,1)S(1)} %get-tuple-element.55), channel_id=1, source_target_pairs={{4,8},{8,4},{5,9},{9,5},{6,10},{10,6},{7,11},{11,7},{20,24},{24,20... | collective-permute-start | bytes 196616 | tf_op jit(solution)/shard_map/ppermute | solution.py:503
  64.9 0.0 collective-permute-done.24.others_ref
  65.0 2.3 %first_terms.1 = (f32[16,128,128]{2,1,0:T(8,128)}, f32[2,128,128]{2,1,0:T(8,128)S(1)}) custom-call(s32[1]{0:T(128)} %bitcast.1.aux_ref, s32[8,128]{1,0:T(8,128)S(1)} %get-tuple-element.31.index_ref, f32[8,128,128]{2,1,0:T(8,128)S(1)} %get-tuple-element.50.amps_ref, f32[8,128,128]{2,1,0:T(8,128)S(1)} %collective-permute-done.24.others_ref, ...), custom_call_target="tpu_custom_call" | custom-call | flops 201326592 | bytes 2097152 | tf_op jit(solution)/shard_map/first_terms/pallas_call | solution.py:429
  67.3 0.0 collective-permute-done.25
  67.4 1.4 %collective-permute-start.27 = (f32[2,128,128]{2,1,0:T(8,128)S(1)}, f32[2,128,128]{2,1,0:T(8,128)S(1)}, u32[]{:S(2)}, u32[]{:S(2)}) collective-permute-start(f32[2,128,128]{2,1,0:T(8,128)S(1)} %convert_add_fusion), channel_id=1, source_target_pairs={{0,1},{1,0},{2,3},{3,2},{4,5},{5,4},{6,7},{7,6},{8,9},{9,8},{10,11... | collective-permute-start | bytes 393224 | tf_op jit(solution)/shard_map/ppermute | solution.py:498
  68.8 1.0 %collective-permute-done.27 = f32[2,128,128]{2,1,0:T(8,128)S(1)} collective-permute-done((f32[2,128,128]{2,1,0:T(8,128)S(1)}, f32[2,128,128]{2,1,0:T(8,128)S(1)}, u32[]{:S(2)}, u32[]{:S(2)}) %collective-permute-start.27) | collective-permute-done | bytes 131104 | tf_op jit(solution)/shard_map/ppermute | solution.py:498
  69.8 0.7 add_multiply_fusion
  (26 shorter events, 0.1 us)
Async XLA Ops:
  0.6 25.2 %copy-start.5 = (s32[64,4]{0,1:T(4,128)S(1)}, s32[64,4]{0,1:T(4,128)}, u32[]{:S(2)}) copy-start(s32[64,4]{0,1:T(4,128)} %param.19) | copy-start | bytes 3076
  0.6 25.2 %copy-start.8 = (s32[16,2]{0,1:T(2,128)S(1)}, s32[16,2]{0,1:T(2,128)}, u32[]{:S(2)}) copy-start(s32[16,2]{0,1:T(2,128)} %param.18) | copy-start | bytes 388
  0.7 25.2 %copy-start.6 = (f32[16,4]{0,1:T(4,128)S(1)}, f32[16,4]{0,1:T(4,128)}, u32[]{:S(2)}) copy-start(f32[16,4]{0,1:T(4,128)} %param.14) | copy-start | bytes 772
  0.7 13.4 %collective-permute-start = (bf16[2,1536,128]{2,1,0:T(8,128)(2,1)}, bf16[2,1536,128]{2,1,0:T(8,128)(2,1)S(1)}, u32[]{:S(2)}, u32[]{:S(2)}) collective-permute-start(bf16[2,1536,128]{2,1,0:T(8,128)(2,1)} %ints_ref), channel_id=1, source_target_pairs={{4,0},{8,4},{12,8},{1,5},{5,9},{9,13},{6,2},{10,6},{14,10},{3,7},{... | collective-permute-start | bytes 2359304 | tf_op jit(solution)/shard_map/ppermute | solution.py:526
  4.0 1.1 %copy-start.1 = (bf16[2,1536,128]{2,1,0:T(8,128)(2,1)S(1)}, bf16[2,1536,128]{2,1,0:T(8,128)(2,1)}, u32[]{:S(2)}) copy-start(bf16[2,1536,128]{2,1,0:T(8,128)(2,1)} %ints_ref) | copy-start | bytes 2359300
  5.2 1.0 %copy-start.2 = (bf16[16,128,128]{2,1,0:T(8,128)(2,1)S(1)}, bf16[16,128,128]{2,1,0:T(8,128)(2,1)}, u32[]{:S(2)}) copy-start(bf16[16,128,128]{2,1,0:T(8,128)(2,1)} %first_ref.1) | copy-start | bytes 1572868
  6.2 1.0 %copy-start.3 = (bf16[16,128,128]{2,1,0:T(8,128)(2,1)S(1)}, bf16[16,128,128]{2,1,0:T(8,128)(2,1)}, u32[]{:S(2)}) copy-start(bf16[16,128,128]{2,1,0:T(8,128)(2,1)} %second_ref.1) | copy-start | bytes 1572868
  7.2 0.7 copy-start.4
  7.9 0.7 copy-start.7
  8.6 0.7 copy-start.9
  14.6 8.7 %collective-permute-start.1 = (bf16[640,128]{1,0:T(8,128)(2,1)S(1)}, bf16[640,128]{1,0:T(8,128)(2,1)S(1)}, u32[]{:S(2)}, u32[]{:S(2)}) collective-permute-start(bf16[640,128]{1,0:T(8,128)(2,1)S(1)} %get-tuple-element.40.refs_0_), channel_id=1, source_target_pairs={{0,2},{1,3},{2,0},{3,1},{4,6},{5,7},{6,4},{7,5},{8,10},{9,11},{10,... | collective-permute-start | bytes 491528 | tf_op jit(solution)/shard_map/ppermute | solution.py:498
  14.9 8.5 %collective-permute-start.3 = (bf16[512,128]{1,0:T(8,128)(2,1)S(1)}, bf16[512,128]{1,0:T(8,128)(2,1)S(1)}, u32[]{:S(2)}, u32[]{:S(2)}) collective-permute-start(bf16[512,128]{1,0:T(8,128)(2,1)S(1)} %get-tuple-element.41), channel_id=1, source_target_pairs={{0,7},{4,11},{8,15},{5,2},{9,6},{13,10},{2,5},{6,9},{10,13},{7,0},... | collective-permute-start | bytes 393224 | tf_op jit(solution)/shard_map/ppermute | solution.py:573
  19.6 6.3 %collective-permute-start.2 = (bf16[512,128]{1,0:T(8,128)(2,1)S(1)}, bf16[512,128]{1,0:T(8,128)(2,1)S(1)}, u32[]{:S(2)}, u32[]{:S(2)}) collective-permute-start(bf16[512,128]{1,0:T(8,128)(2,1)S(1)} %get-tuple-element.41), channel_id=1, source_target_pairs={{0,5},{4,9},{8,13},{5,0},{9,4},{13,8},{2,7},{6,11},{10,15},{7,2},{... | collective-permute-start | bytes 393224 | tf_op jit(solution)/shard_map/ppermute | solution.py:573
  21.5 5.7 %collective-permute-start.4 = (bf16[640,128]{1,0:T(8,128)(2,1)S(1)}, bf16[640,128]{1,0:T(8,128)(2,1)S(1)}, u32[]{:S(2)}, u32[]{:S(2)}) collective-permute-start(bf16[640,128]{1,0:T(8,128)(2,1)S(1)} %get-tuple-element.40.refs_0_), channel_id=1, source_target_pairs={{0,1},{1,0},{2,3},{3,2},{4,5},{5,4},{6,7},{7,6},{8,9},{9,8},{10,11... | collective-permute-start | bytes 491528 | tf_op jit(solution)/shard_map/ppermute | solution.py:498
  23.3 4.0 %collective-permute-start.5 = (bf16[640,128]{1,0:T(8,128)(2,1)S(1)}, bf16[640,128]{1,0:T(8,128)(2,1)S(1)}, u32[]{:S(2)}, u32[]{:S(2)}) collective-permute-start(bf16[640,128]{1,0:T(8,128)(2,1)S(1)} %collective-permute-done.1.refs_1_), channel_id=1, source_target_pairs={{0,1},{1,0},{2,3},{3,2},{4,5},{5,4},{6,7},{7,6},{8,9},{9,8},{10,11... | collective-permute-start | bytes 491528 | tf_op jit(solution)/shard_map/ppermute | solution.py:498
  23.3 3.9 %collective-permute-start.7 = (bf16[512,128]{1,0:T(8,128)(2,1)S(1)}, bf16[512,128]{1,0:T(8,128)(2,1)S(1)}, u32[]{:S(2)}, u32[]{:S(2)}) collective-permute-start(bf16[512,128]{1,0:T(8,128)(2,1)S(1)} %collective-permute-done.3.refs_3_), channel_id=1, source_target_pairs={{0,1},{1,0},{2,3},{3,2},{4,5},{5,4},{6,7},{7,6},{8,9},{9,8},{10,11... | collective-permute-start | bytes 393224 | tf_op jit(solution)/shard_map/ppermute | solution.py:498
  25.9 1.4 %collective-permute-start.6 = (bf16[512,128]{1,0:T(8,128)(2,1)S(1)}, bf16[512,128]{1,0:T(8,128)(2,1)S(1)}, u32[]{:S(2)}, u32[]{:S(2)}) collective-permute-start(bf16[512,128]{1,0:T(8,128)(2,1)S(1)} %collective-permute-done.2.refs_2_), channel_id=1, source_target_pairs={{0,1},{1,0},{2,3},{3,2},{4,5},{5,4},{6,7},{7,6},{8,9},{9,8},{10,11... | collective-permute-start | bytes 393224 | tf_op jit(solution)/shard_map/ppermute | solution.py:498
  28.1 8.0 %collective-permute-start.11 = (bf16[4,128,128]{2,1,0:T(8,128)(2,1)S(1)}, bf16[4,128,128]{2,1,0:T(8,128)(2,1)S(1)}, u32[]{:S(2)}, u32[]{:S(2)}) collective-permute-start(bf16[4,128,128]{2,1,0:T(8,128)(2,1)S(1)} %get-tuple-element.46), channel_id=1, source_target_pairs={{4,12},{8,0},{0,4},{12,8},{5,13},{9,1},{1,5},{13,9},{6,14},{10,2},... | collective-permute-start | bytes 393224 | tf_op jit(solution)/shard_map/ppermute | solution.py:599
  30.5 7.5 %collective-permute-start.10 = (bf16[8,128,128]{2,1,0:T(8,128)(2,1)S(1)}, bf16[8,128,128]{2,1,0:T(8,128)(2,1)S(1)}, u32[]{:S(2)}, u32[]{:S(2)}) collective-permute-start(bf16[8,128,128]{2,1,0:T(8,128)(2,1)S(1)} %get-tuple-element.45.refs_0_), channel_id=1, source_target_pairs={{4,0},{8,12},{5,9},{9,5},{6,2},{10,14},{7,11},{11,7},{20,16},{24,2... | collective-permute-start | bytes 786440 | tf_op jit(solution)/shard_map/ppermute | solution.py:507
  32.4 6.5 %collective-permute-start.9 = (bf16[8,128,128]{2,1,0:T(8,128)(2,1)S(1)}, bf16[8,128,128]{2,1,0:T(8,128)(2,1)S(1)}, u32[]{:S(2)}, u32[]{:S(2)}) collective-permute-start(bf16[8,128,128]{2,1,0:T(8,128)(2,1)S(1)} %get-tuple-element.45.refs_0_), channel_id=1, source_target_pairs={{4,8},{8,4},{5,1},{9,13},{6,10},{10,6},{7,3},{11,15},{20,24},{24,2... | collective-permute-start | bytes 786440 | tf_op jit(solution)/shard_map/ppermute | solution.py:507
  33.7 8.5 %collective-permute-start.8 = (bf16[8,128,128]{2,1,0:T(8,128)(2,1)S(1)}, bf16[8,128,128]{2,1,0:T(8,128)(2,1)S(1)}, u32[]{:S(2)}, u32[]{:S(2)}) collective-permute-start(bf16[8,128,128]{2,1,0:T(8,128)(2,1)S(1)} %get-tuple-element.45.refs_0_), channel_id=1, source_target_pairs={{0,1},{1,0},{2,3},{3,2},{4,5},{5,4},{6,7},{7,6},{8,9},{9,8},{10,11... | collective-permute-start | bytes 786440 | tf_op jit(solution)/shard_map/ppermute | solution.py:498
  36.2 1.3 %collective-permute-start.12 = (bf16[4,128,128]{2,1,0:T(8,128)(2,1)S(1)}, bf16[4,128,128]{2,1,0:T(8,128)(2,1)S(1)}, u32[]{:S(2)}, u32[]{:S(2)}) collective-permute-start(bf16[4,128,128]{2,1,0:T(8,128)(2,1)S(1)} %collective-permute-done.11.piece_ref.refs_4_), channel_id=1, source_target_pairs={{0,1},{1,0},{2,3},{3,2},{4,5},{5,4},{6,7},{7,6},{8,9},{9,8},{10,11... | collective-permute-start | bytes 393224 | tf_op jit(solution)/shard_map/ppermute | solution.py:498
  36.3 6.9 %copy-start = (bf16[16,4,128,128]{3,2,1,0:T(8,128)(2,1)S(1)}, bf16[16,4,128,128]{3,2,1,0:T(8,128)(2,1)}, u32[]{:S(2)}) copy-start(bf16[16,4,128,128]{3,2,1,0:T(8,128)(2,1)} %refs_8_.3) | copy-start | bytes 6291460
  36.3 5.0 %collective-permute-start.14 = (bf16[4,128,128]{2,1,0:T(8,128)(2,1)S(1)}, bf16[4,128,128]{2,1,0:T(8,128)(2,1)S(1)}, u32[]{:S(2)}, u32[]{:S(2)}) collective-permute-start(bf16[4,128,128]{2,1,0:T(8,128)(2,1)S(1)} %collective-permute-done.11.piece_ref.refs_4_), channel_id=1, source_target_pairs={{0,2},{1,3},{2,0},{3,1},{4,6},{5,7},{6,4},{7,5},{8,10},{9,11},{10,... | collective-permute-start | bytes 393224 | tf_op jit(solution)/shard_map/ppermute | solution.py:498
  39.0 4.2 %collective-permute-start.13 = (bf16[8,128,128]{2,1,0:T(8,128)(2,1)S(1)}, bf16[8,128,128]{2,1,0:T(8,128)(2,1)S(1)}, u32[]{:S(2)}, u32[]{:S(2)}) collective-permute-start(bf16[8,128,128]{2,1,0:T(8,128)(2,1)S(1)} %joined.2.refs_2_), channel_id=1, source_target_pairs={{0,1},{1,0},{2,3},{3,2},{4,5},{5,4},{6,7},{7,6},{8,9},{9,8},{10,11... | collective-permute-start | bytes 786440 | tf_op jit(solution)/shard_map/ppermute | solution.py:498
  41.2 1.9 %collective-permute-start.15 = (bf16[4,128,128]{2,1,0:T(8,128)(2,1)S(1)}, bf16[4,128,128]{2,1,0:T(8,128)(2,1)S(1)}, u32[]{:S(2)}, u32[]{:S(2)}) collective-permute-start(bf16[4,128,128]{2,1,0:T(8,128)(2,1)S(1)} %collective-permute-done.14.refs_6_), channel_id=1, source_target_pairs={{0,1},{1,0},{2,3},{3,2},{4,5},{5,4},{6,7},{7,6},{8,9},{9,8},{10,11... | collective-permute-start | bytes 393224 | tf_op jit(solution)/shard_map/ppermute | solution.py:498
  44.0 7.9 %collective-permute-start.19 = (bf16[4,128,128]{2,1,0:T(8,128)(2,1)S(1)}, bf16[4,128,128]{2,1,0:T(8,128)(2,1)S(1)}, u32[]{:S(2)}, u32[]{:S(2)}) collective-permute-start(bf16[4,128,128]{2,1,0:T(8,128)(2,1)S(1)} %get-tuple-element.49.refs_1_), channel_id=1, source_target_pairs={{4,12},{8,0},{0,4},{12,8},{5,13},{9,1},{1,5},{13,9},{6,14},{10,2},... | collective-permute-start | bytes 393224 | tf_op jit(solution)/shard_map/ppermute | solution.py:599
  46.8 7.1 %collective-permute-start.18 = (bf16[8,128,128]{2,1,0:T(8,128)(2,1)S(1)}, bf16[8,128,128]{2,1,0:T(8,128)(2,1)S(1)}, u32[]{:S(2)}, u32[]{:S(2)}) collective-permute-start(bf16[8,128,128]{2,1,0:T(8,128)(2,1)S(1)} %sweep_rest.1.refs_0_), channel_id=1, source_target_pairs={{4,0},{8,12},{5,9},{9,5},{6,2},{10,14},{7,11},{11,7},{20,16},{24,2... | collective-permute-start | bytes 786440 | tf_op jit(solution)/shard_map/ppermute | solution.py:507
  48.7 6.7 %collective-permute-start.17 = (bf16[8,128,128]{2,1,0:T(8,128)(2,1)S(1)}, bf16[8,128,128]{2,1,0:T(8,128)(2,1)S(1)}, u32[]{:S(2)}, u32[]{:S(2)}) collective-permute-start(bf16[8,128,128]{2,1,0:T(8,128)(2,1)S(1)} %sweep_rest.1.refs_0_), channel_id=1, source_target_pairs={{4,8},{8,4},{5,1},{9,13},{6,10},{10,6},{7,3},{11,15},{20,24},{24,2... | collective-permute-start | bytes 786440 | tf_op jit(solution)/shard_map/ppermute | solution.py:507
  50.0 7.9 %collective-permute-start.16 = (bf16[8,128,128]{2,1,0:T(8,128)(2,1)S(1)}, bf16[8,128,128]{2,1,0:T(8,128)(2,1)S(1)}, u32[]{:S(2)}, u32[]{:S(2)}) collective-permute-start(bf16[8,128,128]{2,1,0:T(8,128)(2,1)S(1)} %sweep_rest.1.refs_0_), channel_id=1, source_target_pairs={{0,1},{1,0},{2,3},{3,2},{4,5},{5,4},{6,7},{7,6},{8,9},{9,8},{10,11... | collective-permute-start | bytes 786440 | tf_op jit(solution)/shard_map/ppermute | solution.py:498
  51.9 3.5 %collective-permute-start.20 = (bf16[4,128,128]{2,1,0:T(8,128)(2,1)S(1)}, bf16[4,128,128]{2,1,0:T(8,128)(2,1)S(1)}, u32[]{:S(2)}, u32[]{:S(2)}) collective-permute-start(bf16[4,128,128]{2,1,0:T(8,128)(2,1)S(1)} %collective-permute-done.19.piece_ref.refs_4_), channel_id=1, source_target_pairs={{0,1},{1,0},{2,3},{3,2},{4,5},{5,4},{6,7},{7,6},{8,9},{9,8},{10,11... | collective-permute-start | bytes 393224 | tf_op jit(solution)/shard_map/ppermute | solution.py:498
  52.0 5.5 %collective-permute-start.22 = (bf16[4,128,128]{2,1,0:T(8,128)(2,1)S(1)}, bf16[4,128,128]{2,1,0:T(8,128)(2,1)S(1)}, u32[]{:S(2)}, u32[]{:S(2)}) collective-permute-start(bf16[4,128,128]{2,1,0:T(8,128)(2,1)S(1)} %collective-permute-done.19.piece_ref.refs_4_), channel_id=1, source_target_pairs={{0,2},{1,3},{2,0},{3,1},{4,6},{5,7},{6,4},{7,5},{8,10},{9,11},{10,... | collective-permute-start | bytes 393224 | tf_op jit(solution)/shard_map/ppermute | solution.py:498
  55.4 3.4 %collective-permute-start.21 = (bf16[8,128,128]{2,1,0:T(8,128)(2,1)S(1)}, bf16[8,128,128]{2,1,0:T(8,128)(2,1)S(1)}, u32[]{:S(2)}, u32[]{:S(2)}) collective-permute-start(bf16[8,128,128]{2,1,0:T(8,128)(2,1)S(1)} %joined.3.refs_2_), channel_id=1, source_target_pairs={{0,1},{1,0},{2,3},{3,2},{4,5},{5,4},{6,7},{7,6},{8,9},{9,8},{10,11... | collective-permute-start | bytes 786440 | tf_op jit(solution)/shard_map/ppermute | solution.py:498
  57.5 1.4 %collective-permute-start.23 = (bf16[4,128,128]{2,1,0:T(8,128)(2,1)S(1)}, bf16[4,128,128]{2,1,0:T(8,128)(2,1)S(1)}, u32[]{:S(2)}, u32[]{:S(2)}) collective-permute-start(bf16[4,128,128]{2,1,0:T(8,128)(2,1)S(1)} %collective-permute-done.22.refs_6_), channel_id=1, source_target_pairs={{0,1},{1,0},{2,3},{3,2},{4,5},{5,4},{6,7},{7,6},{8,9},{9,8},{10,11... | collective-permute-start | bytes 393224 | tf_op jit(solution)/shard_map/ppermute | solution.py:498
  61.4 3.5 %collective-permute-start.24 = (f32[8,128,128]{2,1,0:T(8,128)S(1)}, f32[8,128,128]{2,1,0:T(8,128)S(1)}, u32[]{:S(2)}, u32[]{:S(2)}) collective-permute-start(f32[8,128,128]{2,1,0:T(8,128)S(1)} %get-tuple-element.50.amps_ref), channel_id=1, source_target_pairs={{0,1},{1,0},{2,3},{3,2},{4,5},{5,4},{6,7},{7,6},{8,9},{9,8},{10,11... | collective-permute-start | bytes 1572872 | tf_op jit(solution)/shard_map/ppermute | solution.py:498
  61.9 5.4 %collective-permute-start.25 = (bf16[2,128,128]{2,1,0:T(8,128)(2,1)S(1)}, bf16[2,128,128]{2,1,0:T(8,128)(2,1)S(1)}, u32[]{:S(2)}, u32[]{:S(2)}) collective-permute-start(bf16[2,128,128]{2,1,0:T(8,128)(2,1)S(1)} %get-tuple-element.54), channel_id=1, source_target_pairs={{0,4},{4,0},{8,12},{12,8},{1,5},{5,1},{9,13},{13,9},{2,6},{6,2},{1... | collective-permute-start | bytes 196616 | tf_op jit(solution)/shard_map/ppermute | solution.py:503
  61.9 5.4 %collective-permute-start.26 = (bf16[2,128,128]{2,1,0:T(8,128)(2,1)S(1)}, bf16[2,128,128]{2,1,0:T(8,128)(2,1)S(1)}, u32[]{:S(2)}, u32[]{:S(2)}) collective-permute-start(bf16[2,128,128]{2,1,0:T(8,128)(2,1)S(1)} %get-tuple-element.55), channel_id=1, source_target_pairs={{4,8},{8,4},{5,9},{9,5},{6,10},{10,6},{7,11},{11,7},{20,24},{24,20... | collective-permute-start | bytes 196616 | tf_op jit(solution)/shard_map/ppermute | solution.py:503
  67.4 2.4 %collective-permute-start.27 = (f32[2,128,128]{2,1,0:T(8,128)S(1)}, f32[2,128,128]{2,1,0:T(8,128)S(1)}, u32[]{:S(2)}, u32[]{:S(2)}) collective-permute-start(f32[2,128,128]{2,1,0:T(8,128)S(1)} %convert_add_fusion), channel_id=1, source_target_pairs={{0,1},{1,0},{2,3},{3,2},{4,5},{5,4},{6,7},{7,6},{8,9},{9,8},{10,11... | collective-permute-start | bytes 393224 | tf_op jit(solution)/shard_map/ppermute | solution.py:498

commit v10 on v9

--- a/solution.py
+++ b/solution.py
@@ -599,7 +599,7 @@
         one = lax.ppermute(part, "pair", rounds[0])
         one_other = swap(one)
         cross = swap(one, 2)
-        two = joined(*exchanged(low, low, rounds[1:]), token(one), one_other)
+        two = joined(*exchanged(low, low, rounds[:0:-1]), token(one), one_other)
         return [low, swap(low), two, swap(two), one, one_other, cross, swap(cross)]
 
     for it in range(ITERS):

time: 70.9 us -> 70.7 us (level)
  starting transfers between devices: 39.4 us -> 32.4 us
  waiting for transfers between devices: 14 us -> 20.8 us
    ppermute x17, starting transfers between devices: 15.6 us -> 7.68 us  [swap(): return lax.ppermute(value, 'aux', [(i, i ^ step) for i in range(aux_count)])]
    ppermute x4, waiting for transfers between devices: 4.54 us -> 10.9 us  [exchanged(): lax.ppermute(value, ('pair', 'aux'), [(i * aux_count + a, j * aux_count +...]
    ppermute x4, starting transfers between devices: 6.44 us -> 8.9 us  [exchanged(): lax.ppermute(value, ('pair', 'aux'), [(i * aux_count + a, j * aux_count +...]
    ppermute x2, starting transfers between devices: 4.38 us -> 3.08 us  [gathered(): one = lax.ppermute(part, 'pair', rounds[0])]
  transfers between devices with their start and end apart: 28 -> 28, of which waited for: 10 -> 9; matrix products, arithmetic and copies ran while one was open for 0% -> 0% of each run, Pallas kernels for 8% -> 8%
where the time goes in v10:
time: 70.7 us; the launch traced here: 70.2 us
  starting transfers between devices  32.4 us (46%)
  waiting for transfers between devices  20.8 us (29%)
  Pallas kernels  10.2 us (14%)
  local copies, waits for them, and re-layouts  5.26 us (7%)
  between operations  0.93 us (1%)
    ppermute x4, waiting for transfers between devices, exchanged(): lax.ppermute(value, ('pair', 'aux'), [(i * aux_count + a, j * aux_count +...  10.9 us
    ppermute x4, starting transfers between devices, exchanged(): lax.ppermute(value, ('pair', 'aux'), [(i * aux_count + a, j * aux_count +...  8.9 us
    ppermute x17, starting transfers between devices, swap(): return lax.ppermute(value, 'aux', [(i, i ^ step) for i in range(aux_count)])  7.68 us
    ppermute x2, starting transfers between devices, over_z(): lax.ppermute(sent, ('pair', 'aux'), joint([[(i, i + 1, turn) for i in ran...  6.61 us
    unnamed x20, local copies, waits for them, and re-layouts  5.26 us
    ppermute x17, waiting for transfers between devices, swap(): return lax.ppermute(value, 'aux', [(i, i ^ step) for i in range(aux_count)])  4.44 us
    pallas_call x3, Pallas kernels, call(): pl.pallas_call(functools.partial(sweep_kernel, step, len(parts)), out_sha...  4.08 us
    ppermute x1, waiting for transfers between devices, shards(): lax.ppermute(ints, ('pair', 'aux'), joint([[(i + 1, i, 0) for i in range(...  3.86 us
  transfers between devices with their start and end apart: 28, of which 9 were waited for; matrix products, arithmetic and copies ran while one was open for 0% of the time, Pallas kernels for 8%

profile of v10, /device:TPU:15, one launch (start us, length us, event | category | flops | bytes accessed | tf_op | source)
XLA Modules:
  0.0 70.2 jit_solution(10602910461844603727)
XLA Ops:
  0.7 3.3 %collective-permute-start = (bf16[2,1536,128]{2,1,0:T(8,128)(2,1)}, bf16[2,1536,128]{2,1,0:T(8,128)(2,1)S(1)}, u32[]{:S(2)}, u32[]{:S(2)}) collective-permute-start(bf16[2,1536,128]{2,1,0:T(8,128)(2,1)} %ints_ref), channel_id=1, source_target_pairs={{4,0},{8,4},{12,8},{1,5},{5,9},{9,13},{6,2},{10,6},{14,10},{3,7},{... | collective-permute-start | bytes 2359304 | tf_op jit(solution)/shard_map/ppermute | solution.py:526
  4.0 1.1 %copy-done.1 = bf16[2,1536,128]{2,1,0:T(8,128)(2,1)S(1)} copy-done((bf16[2,1536,128]{2,1,0:T(8,128)(2,1)S(1)}, bf16[2,1536,128]{2,1,0:T(8,128)(2,1)}, u32[]{:S(2)}) %copy-start.1) | copy-done | bytes 786456
  5.2 1.0 %copy-done.2 = bf16[16,128,128]{2,1,0:T(8,128)(2,1)S(1)} copy-done((bf16[16,128,128]{2,1,0:T(8,128)(2,1)S(1)}, bf16[16,128,128]{2,1,0:T(8,128)(2,1)}, u32[]{:S(2)}) %copy-start.2) | copy-done | bytes 524312
  6.2 1.0 %copy-done.3 = bf16[16,128,128]{2,1,0:T(8,128)(2,1)S(1)} copy-done((bf16[16,128,128]{2,1,0:T(8,128)(2,1)S(1)}, bf16[16,128,128]{2,1,0:T(8,128)(2,1)}, u32[]{:S(2)}) %copy-start.3) | copy-done | bytes 524312
  7.2 0.7 copy-done.4
  7.9 0.7 copy-done.7
  8.6 0.7 copy-done.9
  9.3 0.9 %prepare.1 = (bf16[8,128,128]{2,1,0:T(8,128)(2,1)S(1)}, bf16[8,128,128]{2,1,0:T(8,128)(2,1)S(1)}, bf16[2,1536,128]{2,1,0:T(8,128)(2,1)S(1)}, f32[8,128,128]{2,1,0:T(8,128)S(1)}) custom-call(s32[1]{0:T(128)} %bitcast.1.aux_ref, f32[2,16]{1,0:T(2,128)S(1)} %bitcast.8, s32[16]{0:T(128)S(1)} %copy-done.9, f32[16,128]{1,0:T(8,128)S(1)} %copy-done.4, ...), custom_call_target="tpu_custom_call" | custom-call | bytes 2097152 | tf_op jit(solution)/shard_map/prepare/pallas_call | solution.py:75
  10.2 3.9 %collective-permute-done.near_ref = bf16[2,1536,128]{2,1,0:T(8,128)(2,1)S(1)} collective-permute-done((bf16[2,1536,128]{2,1,0:T(8,128)(2,1)}, bf16[2,1536,128]{2,1,0:T(8,128)(2,1)S(1)}, u32[]{:S(2)}, u32[]{:S(2)}) %collective-permute-start) | collective-permute-done | bytes 786464 | tf_op jit(solution)/shard_map/ppermute | solution.py:526
  14.0 0.5 products.1
  14.6 0.3 collective-permute-start.1
  14.9 4.7 %collective-permute-start.3 = (bf16[512,128]{1,0:T(8,128)(2,1)S(1)}, bf16[512,128]{1,0:T(8,128)(2,1)S(1)}, u32[]{:S(2)}, u32[]{:S(2)}) collective-permute-start(bf16[512,128]{1,0:T(8,128)(2,1)S(1)} %get-tuple-element.41), channel_id=1, source_target_pairs={{0,7},{4,11},{8,15},{5,2},{9,6},{13,10},{2,5},{6,9},{10,13},{7,0},... | collective-permute-start | bytes 393224 | tf_op jit(solution)/shard_map/ppermute | solution.py:573
  19.6 1.9 %collective-permute-start.2 = (bf16[512,128]{1,0:T(8,128)(2,1)S(1)}, bf16[512,128]{1,0:T(8,128)(2,1)S(1)}, u32[]{:S(2)}, u32[]{:S(2)}) collective-permute-start(bf16[512,128]{1,0:T(8,128)(2,1)S(1)} %get-tuple-element.41), channel_id=1, source_target_pairs={{0,5},{4,9},{8,13},{5,0},{9,4},{13,8},{2,7},{6,11},{10,15},{7,2},{... | collective-permute-start | bytes 393224 | tf_op jit(solution)/shard_map/ppermute | solution.py:573
  21.5 1.7 %collective-permute-start.4 = (bf16[640,128]{1,0:T(8,128)(2,1)S(1)}, bf16[640,128]{1,0:T(8,128)(2,1)S(1)}, u32[]{:S(2)}, u32[]{:S(2)}) collective-permute-start(bf16[640,128]{1,0:T(8,128)(2,1)S(1)} %get-tuple-element.40.refs_0_), channel_id=1, source_target_pairs={{0,1},{1,0},{2,3},{3,2},{4,5},{5,4},{6,7},{7,6},{8,9},{9,8},{10,11... | collective-permute-start | bytes 491528 | tf_op jit(solution)/shard_map/ppermute | solution.py:498
  23.3 0.0 collective-permute-done.1.refs_1_
  23.3 0.1 collective-permute-start.5
  23.3 1.0 %collective-permute-start.7 = (bf16[512,128]{1,0:T(8,128)(2,1)S(1)}, bf16[512,128]{1,0:T(8,128)(2,1)S(1)}, u32[]{:S(2)}, u32[]{:S(2)}) collective-permute-start(bf16[512,128]{1,0:T(8,128)(2,1)S(1)} %collective-permute-done.3.refs_3_), channel_id=1, source_target_pairs={{0,1},{1,0},{2,3},{3,2},{4,5},{5,4},{6,7},{7,6},{8,9},{9,8},{10,11... | collective-permute-start | bytes 393224 | tf_op jit(solution)/shard_map/ppermute | solution.py:498
  24.3 1.6 %collective-permute-done.2.refs_2_ = bf16[512,128]{1,0:T(8,128)(2,1)S(1)} collective-permute-done((bf16[512,128]{1,0:T(8,128)(2,1)S(1)}, bf16[512,128]{1,0:T(8,128)(2,1)S(1)}, u32[]{:S(2)}, u32[]{:S(2)}) %collective-permute-start.2) | collective-permute-done | bytes 131104 | tf_op jit(solution)/shard_map/ppermute | solution.py:573
  25.9 1.3 %indices.1 = (s32[8,128]{1,0:T(8,128)S(1)}, f32[8,128]{1,0:T(8,128)S(1)}) custom-call(s32[1]{0:T(128)} %bitcast.here_ref, s32[1]{0:T(128)} %bitcast.1.aux_ref, s32[2,16]{1,0:T(2,128)S(1)} %bitcast.9, s32[4,64]{1,0:T(4,128)S(1)} %bitcast.6, f32[4,16]{1,0:T(4,128)S(1)} %bitcast.7), custom_call_target="tpu_custom_call" | custom-call | flops 1000000 | bytes 65536 | tf_op jit(solution)/shard_map/indices/pallas_call | solution.py:143
  27.2 0.0 collective-permute-done.4.refs_4_
  27.2 0.0 collective-permute-done.7.refs_7_
  27.3 0.0 collective-permute-done.5.refs_5_
  27.3 0.9 %exchange.1 = (f32[8,128,128]{2,1,0:T(8,128)S(1)}, bf16[8,128,128]{2,1,0:T(8,128)(2,1)S(1)}, bf16[4,128,128]{2,1,0:T(8,128)(2,1)S(1)}) custom-call(s32[1]{0:T(128)} %bitcast.1.aux_ref, s32[8,128]{1,0:T(8,128)S(1)} %get-tuple-element.31.index_ref, bf16[640,128]{1,0:T(8,128)(2,1)S(1)} %get-tuple-element.40.refs_0_, ...), custom_call_target="tpu_custom_call" | custom-call | flops 134217728 | bytes 2621440 | tf_op jit(solution)/shard_map/exchange/pallas_call | solution.py:242
  28.1 2.4 %collective-permute-start.11 = (bf16[4,128,128]{2,1,0:T(8,128)(2,1)S(1)}, bf16[4,128,128]{2,1,0:T(8,128)(2,1)S(1)}, u32[]{:S(2)}, u32[]{:S(2)}) collective-permute-start(bf16[4,128,128]{2,1,0:T(8,128)(2,1)S(1)} %get-tuple-element.46), channel_id=1, source_target_pairs={{4,12},{8,0},{0,4},{12,8},{5,13},{9,1},{1,5},{13,9},{6,14},{10,2},... | collective-permute-start | bytes 393224 | tf_op jit(solution)/shard_map/ppermute | solution.py:599
  30.5 1.3 %collective-permute-start.10 = (bf16[8,128,128]{2,1,0:T(8,128)(2,1)S(1)}, bf16[8,128,128]{2,1,0:T(8,128)(2,1)S(1)}, u32[]{:S(2)}, u32[]{:S(2)}) collective-permute-start(bf16[8,128,128]{2,1,0:T(8,128)(2,1)S(1)} %get-tuple-element.45.refs_0_), channel_id=1, source_target_pairs={{4,8},{8,4},{5,1},{9,13},{6,10},{10,6},{7,3},{11,15},{20,24},{24,2... | collective-permute-start | bytes 786440 | tf_op jit(solution)/shard_map/ppermute | solution.py:507
  31.8 3.0 %collective-permute-start.9 = (bf16[8,128,128]{2,1,0:T(8,128)(2,1)S(1)}, bf16[8,128,128]{2,1,0:T(8,128)(2,1)S(1)}, u32[]{:S(2)}, u32[]{:S(2)}) collective-permute-start(bf16[8,128,128]{2,1,0:T(8,128)(2,1)S(1)} %get-tuple-element.45.refs_0_), channel_id=1, source_target_pairs={{4,0},{8,12},{5,9},{9,5},{6,2},{10,14},{7,11},{11,7},{20,16},{24,2... | collective-permute-start | bytes 786440 | tf_op jit(solution)/shard_map/ppermute | solution.py:507
  34.8 0.1 collective-permute-start.8
  34.9 0.0 collective-permute-done.11.piece_ref.refs_4_
  34.9 0.5 collective-permute-start.12
  35.4 0.2 collective-permute-start.14
  35.6 1.0 %collective-permute-done.12.piece_ref.refs_5_ = bf16[4,128,128]{2,1,0:T(8,128)(2,1)S(1)} collective-permute-done((bf16[4,128,128]{2,1,0:T(8,128)(2,1)S(1)}, bf16[4,128,128]{2,1,0:T(8,128)(2,1)S(1)}, u32[]{:S(2)}, u32[]{:S(2)}) %collective-permute-start.12) | collective-permute-done | bytes 131104 | tf_op jit(solution)/shard_map/ppermute | solution.py:498
  36.6 0.0 collective-permute-done.10.right_ref
  36.6 5.3 %collective-permute-done.9.left_ref = bf16[8,128,128]{2,1,0:T(8,128)(2,1)S(1)} collective-permute-done((bf16[8,128,128]{2,1,0:T(8,128)(2,1)S(1)}, bf16[8,128,128]{2,1,0:T(8,128)(2,1)S(1)}, u32[]{:S(2)}, u32[]{:S(2)}) %collective-permute-start.9) | collective-permute-done | bytes 262176 | tf_op jit(solution)/shard_map/ppermute | solution.py:507
  41.9 0.1 joined.2.refs_2_
  41.9 0.5 collective-permute-start.13
  42.4 0.0 collective-permute-done.14.refs_6_
  42.4 0.1 collective-permute-start.15
  42.5 0.0 collective-permute-done.8.refs_1_
  42.5 1.2 %collective-permute-done.15.refs_7_ = bf16[4,128,128]{2,1,0:T(8,128)(2,1)S(1)} collective-permute-done((bf16[4,128,128]{2,1,0:T(8,128)(2,1)S(1)}, bf16[4,128,128]{2,1,0:T(8,128)(2,1)S(1)}, u32[]{:S(2)}, u32[]{:S(2)}) %collective-permute-start.15) | collective-permute-done | bytes 131104 | tf_op jit(solution)/shard_map/ppermute | solution.py:498
  43.7 0.8 %sweep_part.1 = (bf16[4,128,128]{2,1,0:T(8,128)(2,1)S(1)}, bf16[48,128,128]{2,1,0:T(8,128)(2,1)S(1)}) custom-call(s32[1]{0:T(128)} %bitcast.here_ref, s32[1]{0:T(128)} %bitcast.1.aux_ref, s32[8,128]{1,0:T(8,128)S(1)} %get-tuple-element.31.index_ref, f32[8,128]{1,0:T(8,128)S(1)} %get-tuple-element.32.weight_ref, ...), custom_call_target="tpu_custom_call" | custom-call | flops 268435456 | bytes 2883584 | tf_op jit(solution)/shard_map/sweep_part/pallas_call | solution.py:329
  44.5 0.7 %collective-permute-start.19 = (bf16[4,128,128]{2,1,0:T(8,128)(2,1)S(1)}, bf16[4,128,128]{2,1,0:T(8,128)(2,1)S(1)}, u32[]{:S(2)}, u32[]{:S(2)}) collective-permute-start(bf16[4,128,128]{2,1,0:T(8,128)(2,1)S(1)} %get-tuple-element.49.refs_1_), channel_id=1, source_target_pairs={{4,12},{8,0},{0,4},{12,8},{5,13},{9,1},{1,5},{13,9},{6,14},{10,2},... | collective-permute-start | bytes 393224 | tf_op jit(solution)/shard_map/ppermute | solution.py:599
  45.3 0.8 %sweep_rest.1.refs_0_ = bf16[8,128,128]{2,1,0:T(8,128)(2,1)S(1)} custom-call(s32[1]{0:T(128)} %bitcast.here_ref, s32[1]{0:T(128)} %bitcast.1.aux_ref, s32[8,128]{1,0:T(8,128)S(1)} %get-tuple-element.31.index_ref, f32[8,128]{1,0:T(8,128)S(1)} %get-tuple-element.32.weight_ref, bf16[48,128,128]{2,1,0:T(8,128)(2,1)S(1)} %get-tuple-element.48.refs_0_, ...), custom_call_target="tpu_custom_call" | custom-call | flops 268435456 | bytes 2883584 | tf_op jit(solution)/shard_map/sweep_rest/pallas_call | solution.py:329
  46.0 2.7 %collective-permute-start.18 = (bf16[8,128,128]{2,1,0:T(8,128)(2,1)S(1)}, bf16[8,128,128]{2,1,0:T(8,128)(2,1)S(1)}, u32[]{:S(2)}, u32[]{:S(2)}) collective-permute-start(bf16[8,128,128]{2,1,0:T(8,128)(2,1)S(1)} %sweep_rest.1.refs_0_), channel_id=1, source_target_pairs={{4,8},{8,4},{5,1},{9,13},{6,10},{10,6},{7,3},{11,15},{20,24},{24,2... | collective-permute-start | bytes 786440 | tf_op jit(solution)/shard_map/ppermute | solution.py:507
  48.7 1.9 %collective-permute-start.17 = (bf16[8,128,128]{2,1,0:T(8,128)(2,1)S(1)}, bf16[8,128,128]{2,1,0:T(8,128)(2,1)S(1)}, u32[]{:S(2)}, u32[]{:S(2)}) collective-permute-start(bf16[8,128,128]{2,1,0:T(8,128)(2,1)S(1)} %sweep_rest.1.refs_0_), channel_id=1, source_target_pairs={{4,0},{8,12},{5,9},{9,5},{6,2},{10,14},{7,11},{11,7},{20,16},{24,2... | collective-permute-start | bytes 786440 | tf_op jit(solution)/shard_map/ppermute | solution.py:507
  50.7 0.1 collective-permute-start.16
  50.7 0.0 collective-permute-done.19.piece_ref.refs_4_
  50.8 0.5 collective-permute-start.20
  51.2 0.2 collective-permute-start.22
  51.5 1.5 %collective-permute-done.18.right_ref = bf16[8,128,128]{2,1,0:T(8,128)(2,1)S(1)} collective-permute-done((bf16[8,128,128]{2,1,0:T(8,128)(2,1)S(1)}, bf16[8,128,128]{2,1,0:T(8,128)(2,1)S(1)}, u32[]{:S(2)}, u32[]{:S(2)}) %collective-permute-start.18) | collective-permute-done | bytes 262176 | tf_op jit(solution)/shard_map/ppermute | solution.py:507
  53.0 4.1 %collective-permute-done.17.left_ref = bf16[8,128,128]{2,1,0:T(8,128)(2,1)S(1)} collective-permute-done((bf16[8,128,128]{2,1,0:T(8,128)(2,1)S(1)}, bf16[8,128,128]{2,1,0:T(8,128)(2,1)S(1)}, u32[]{:S(2)}, u32[]{:S(2)}) %collective-permute-start.17) | collective-permute-done | bytes 262176 | tf_op jit(solution)/shard_map/ppermute | solution.py:507
  57.1 0.0 collective-permute-done.20.piece_ref.refs_5_
  57.1 0.1 joined.3.refs_2_
  57.1 0.1 collective-permute-start.21
  57.2 0.5 collective-permute-start.23
  57.7 1.2 %collective-permute-done.23.refs_7_ = bf16[4,128,128]{2,1,0:T(8,128)(2,1)S(1)} collective-permute-done((bf16[4,128,128]{2,1,0:T(8,128)(2,1)S(1)}, bf16[4,128,128]{2,1,0:T(8,128)(2,1)S(1)}, u32[]{:S(2)}, u32[]{:S(2)}) %collective-permute-start.23) | collective-permute-done | bytes 131104 | tf_op jit(solution)/shard_map/ppermute | solution.py:498
  58.9 2.5 %sweep_last.1 = (f32[8,128,128]{2,1,0:T(8,128)S(1)}, f32[2,128,128]{2,1,0:T(8,128)S(1)}, bf16[2,128,128]{2,1,0:T(8,128)(2,1)S(1)}, bf16[2,128,128]{2,1,0:T(8,128)(2,1)S(1)}) custom-call(s32[1]{0:T(128)} %bitcast.here_ref, s32[1]{0:T(128)} %bitcast.1.aux_ref, s32[8,128]{1,0:T(8,128)S(1)} %get-tuple-element.31.index_ref, ...), custom_call_target="tpu_custom_call" | custom-call | flops 268435456 | bytes 2883584 | tf_op jit(solution)/shard_map/sweep_last/pallas_call | solution.py:329
  61.5 0.2 collective-permute-start.24
  61.7 0.2 collective-permute-start.25
  61.9 2.6 %collective-permute-start.26 = (bf16[2,128,128]{2,1,0:T(8,128)(2,1)S(1)}, bf16[2,128,128]{2,1,0:T(8,128)(2,1)S(1)}, u32[]{:S(2)}, u32[]{:S(2)}) collective-permute-start(bf16[2,128,128]{2,1,0:T(8,128)(2,1)S(1)} %get-tuple-element.55), channel_id=1, source_target_pairs={{4,8},{8,4},{5,9},{9,5},{6,10},{10,6},{7,11},{11,7},{20,24},{24,20... | collective-permute-start | bytes 196616 | tf_op jit(solution)/shard_map/ppermute | solution.py:503
  64.5 2.3 %first_terms.1 = (f32[16,128,128]{2,1,0:T(8,128)}, f32[2,128,128]{2,1,0:T(8,128)S(1)}) custom-call(s32[1]{0:T(128)} %bitcast.1.aux_ref, s32[8,128]{1,0:T(8,128)S(1)} %get-tuple-element.31.index_ref, f32[8,128,128]{2,1,0:T(8,128)S(1)} %get-tuple-element.50.amps_ref, f32[8,128,128]{2,1,0:T(8,128)S(1)} %collective-permute-done.24.others_ref, ...), custom_call_target="tpu_custom_call" | custom-call | flops 201326592 | bytes 2097152 | tf_op jit(solution)/shard_map/first_terms/pallas_call | solution.py:429
  66.9 0.0 collective-permute-done.26
  66.9 1.6 %collective-permute-start.27 = (f32[2,128,128]{2,1,0:T(8,128)S(1)}, f32[2,128,128]{2,1,0:T(8,128)S(1)}, u32[]{:S(2)}, u32[]{:S(2)}) collective-permute-start(f32[2,128,128]{2,1,0:T(8,128)S(1)} %convert_add_fusion), channel_id=1, source_target_pairs={{0,1},{1,0},{2,3},{3,2},{4,5},{5,4},{6,7},{7,6},{8,9},{9,8},{10,11... | collective-permute-start | bytes 393224 | tf_op jit(solution)/shard_map/ppermute | solution.py:498
  68.6 1.0 %collective-permute-done.27 = f32[2,128,128]{2,1,0:T(8,128)S(1)} collective-permute-done((f32[2,128,128]{2,1,0:T(8,128)S(1)}, f32[2,128,128]{2,1,0:T(8,128)S(1)}, u32[]{:S(2)}, u32[]{:S(2)}) %collective-permute-start.27) | collective-permute-done | bytes 131104 | tf_op jit(solution)/shard_map/ppermute | solution.py:498
  69.6 0.7 add_multiply_fusion
  (26 shorter events, 0.1 us)
Async XLA Ops:
  0.6 25.2 %copy-start.5 = (s32[64,4]{0,1:T(4,128)S(1)}, s32[64,4]{0,1:T(4,128)}, u32[]{:S(2)}) copy-start(s32[64,4]{0,1:T(4,128)} %param.19) | copy-start | bytes 3076
  0.6 25.2 %copy-start.8 = (s32[16,2]{0,1:T(2,128)S(1)}, s32[16,2]{0,1:T(2,128)}, u32[]{:S(2)}) copy-start(s32[16,2]{0,1:T(2,128)} %param.18) | copy-start | bytes 388
  0.7 25.2 %copy-start.6 = (f32[16,4]{0,1:T(4,128)S(1)}, f32[16,4]{0,1:T(4,128)}, u32[]{:S(2)}) copy-start(f32[16,4]{0,1:T(4,128)} %param.14) | copy-start | bytes 772
  0.7 13.4 %collective-permute-start = (bf16[2,1536,128]{2,1,0:T(8,128)(2,1)}, bf16[2,1536,128]{2,1,0:T(8,128)(2,1)S(1)}, u32[]{:S(2)}, u32[]{:S(2)}) collective-permute-start(bf16[2,1536,128]{2,1,0:T(8,128)(2,1)} %ints_ref), channel_id=1, source_target_pairs={{4,0},{8,4},{12,8},{1,5},{5,9},{9,13},{6,2},{10,6},{14,10},{3,7},{... | collective-permute-start | bytes 2359304 | tf_op jit(solution)/shard_map/ppermute | solution.py:526
  4.0 1.1 %copy-start.1 = (bf16[2,1536,128]{2,1,0:T(8,128)(2,1)S(1)}, bf16[2,1536,128]{2,1,0:T(8,128)(2,1)}, u32[]{:S(2)}) copy-start(bf16[2,1536,128]{2,1,0:T(8,128)(2,1)} %ints_ref) | copy-start | bytes 2359300
  5.2 1.0 %copy-start.2 = (bf16[16,128,128]{2,1,0:T(8,128)(2,1)S(1)}, bf16[16,128,128]{2,1,0:T(8,128)(2,1)}, u32[]{:S(2)}) copy-start(bf16[16,128,128]{2,1,0:T(8,128)(2,1)} %first_ref.1) | copy-start | bytes 1572868
  6.2 1.0 %copy-start.3 = (bf16[16,128,128]{2,1,0:T(8,128)(2,1)S(1)}, bf16[16,128,128]{2,1,0:T(8,128)(2,1)}, u32[]{:S(2)}) copy-start(bf16[16,128,128]{2,1,0:T(8,128)(2,1)} %second_ref.1) | copy-start | bytes 1572868
  7.2 0.7 copy-start.4
  7.9 0.7 copy-start.7
  8.6 0.7 copy-start.9
  14.6 8.7 %collective-permute-start.1 = (bf16[640,128]{1,0:T(8,128)(2,1)S(1)}, bf16[640,128]{1,0:T(8,128)(2,1)S(1)}, u32[]{:S(2)}, u32[]{:S(2)}) collective-permute-start(bf16[640,128]{1,0:T(8,128)(2,1)S(1)} %get-tuple-element.40.refs_0_), channel_id=1, source_target_pairs={{0,2},{1,3},{2,0},{3,1},{4,6},{5,7},{6,4},{7,5},{8,10},{9,11},{10,... | collective-permute-start | bytes 491528 | tf_op jit(solution)/shard_map/ppermute | solution.py:498
  14.9 8.5 %collective-permute-start.3 = (bf16[512,128]{1,0:T(8,128)(2,1)S(1)}, bf16[512,128]{1,0:T(8,128)(2,1)S(1)}, u32[]{:S(2)}, u32[]{:S(2)}) collective-permute-start(bf16[512,128]{1,0:T(8,128)(2,1)S(1)} %get-tuple-element.41), channel_id=1, source_target_pairs={{0,7},{4,11},{8,15},{5,2},{9,6},{13,10},{2,5},{6,9},{10,13},{7,0},... | collective-permute-start | bytes 393224 | tf_op jit(solution)/shard_map/ppermute | solution.py:573
  19.6 6.3 %collective-permute-start.2 = (bf16[512,128]{1,0:T(8,128)(2,1)S(1)}, bf16[512,128]{1,0:T(8,128)(2,1)S(1)}, u32[]{:S(2)}, u32[]{:S(2)}) collective-permute-start(bf16[512,128]{1,0:T(8,128)(2,1)S(1)} %get-tuple-element.41), channel_id=1, source_target_pairs={{0,5},{4,9},{8,13},{5,0},{9,4},{13,8},{2,7},{6,11},{10,15},{7,2},{... | collective-permute-start | bytes 393224 | tf_op jit(solution)/shard_map/ppermute | solution.py:573
  21.5 5.7 %collective-permute-start.4 = (bf16[640,128]{1,0:T(8,128)(2,1)S(1)}, bf16[640,128]{1,0:T(8,128)(2,1)S(1)}, u32[]{:S(2)}, u32[]{:S(2)}) collective-permute-start(bf16[640,128]{1,0:T(8,128)(2,1)S(1)} %get-tuple-element.40.refs_0_), channel_id=1, source_target_pairs={{0,1},{1,0},{2,3},{3,2},{4,5},{5,4},{6,7},{7,6},{8,9},{9,8},{10,11... | collective-permute-start | bytes 491528 | tf_op jit(solution)/shard_map/ppermute | solution.py:498
  23.3 4.0 %collective-permute-start.5 = (bf16[640,128]{1,0:T(8,128)(2,1)S(1)}, bf16[640,128]{1,0:T(8,128)(2,1)S(1)}, u32[]{:S(2)}, u32[]{:S(2)}) collective-permute-start(bf16[640,128]{1,0:T(8,128)(2,1)S(1)} %collective-permute-done.1.refs_1_), channel_id=1, source_target_pairs={{0,1},{1,0},{2,3},{3,2},{4,5},{5,4},{6,7},{7,6},{8,9},{9,8},{10,11... | collective-permute-start | bytes 491528 | tf_op jit(solution)/shard_map/ppermute | solution.py:498
  23.3 3.9 %collective-permute-start.7 = (bf16[512,128]{1,0:T(8,128)(2,1)S(1)}, bf16[512,128]{1,0:T(8,128)(2,1)S(1)}, u32[]{:S(2)}, u32[]{:S(2)}) collective-permute-start(bf16[512,128]{1,0:T(8,128)(2,1)S(1)} %collective-permute-done.3.refs_3_), channel_id=1, source_target_pairs={{0,1},{1,0},{2,3},{3,2},{4,5},{5,4},{6,7},{7,6},{8,9},{9,8},{10,11... | collective-permute-start | bytes 393224 | tf_op jit(solution)/shard_map/ppermute | solution.py:498
  25.9 1.4 %collective-permute-start.6 = (bf16[512,128]{1,0:T(8,128)(2,1)S(1)}, bf16[512,128]{1,0:T(8,128)(2,1)S(1)}, u32[]{:S(2)}, u32[]{:S(2)}) collective-permute-start(bf16[512,128]{1,0:T(8,128)(2,1)S(1)} %collective-permute-done.2.refs_2_), channel_id=1, source_target_pairs={{0,1},{1,0},{2,3},{3,2},{4,5},{5,4},{6,7},{7,6},{8,9},{9,8},{10,11... | collective-permute-start | bytes 393224 | tf_op jit(solution)/shard_map/ppermute | solution.py:498
  28.1 6.7 %collective-permute-start.11 = (bf16[4,128,128]{2,1,0:T(8,128)(2,1)S(1)}, bf16[4,128,128]{2,1,0:T(8,128)(2,1)S(1)}, u32[]{:S(2)}, u32[]{:S(2)}) collective-permute-start(bf16[4,128,128]{2,1,0:T(8,128)(2,1)S(1)} %get-tuple-element.46), channel_id=1, source_target_pairs={{4,12},{8,0},{0,4},{12,8},{5,13},{9,1},{1,5},{13,9},{6,14},{10,2},... | collective-permute-start | bytes 393224 | tf_op jit(solution)/shard_map/ppermute | solution.py:599
  30.5 6.1 %collective-permute-start.10 = (bf16[8,128,128]{2,1,0:T(8,128)(2,1)S(1)}, bf16[8,128,128]{2,1,0:T(8,128)(2,1)S(1)}, u32[]{:S(2)}, u32[]{:S(2)}) collective-permute-start(bf16[8,128,128]{2,1,0:T(8,128)(2,1)S(1)} %get-tuple-element.45.refs_0_), channel_id=1, source_target_pairs={{4,8},{8,4},{5,1},{9,13},{6,10},{10,6},{7,3},{11,15},{20,24},{24,2... | collective-permute-start | bytes 786440 | tf_op jit(solution)/shard_map/ppermute | solution.py:507
  31.8 10.1 %collective-permute-start.9 = (bf16[8,128,128]{2,1,0:T(8,128)(2,1)S(1)}, bf16[8,128,128]{2,1,0:T(8,128)(2,1)S(1)}, u32[]{:S(2)}, u32[]{:S(2)}) collective-permute-start(bf16[8,128,128]{2,1,0:T(8,128)(2,1)S(1)} %get-tuple-element.45.refs_0_), channel_id=1, source_target_pairs={{4,0},{8,12},{5,9},{9,5},{6,2},{10,14},{7,11},{11,7},{20,16},{24,2... | collective-permute-start | bytes 786440 | tf_op jit(solution)/shard_map/ppermute | solution.py:507
  34.8 7.7 %collective-permute-start.8 = (bf16[8,128,128]{2,1,0:T(8,128)(2,1)S(1)}, bf16[8,128,128]{2,1,0:T(8,128)(2,1)S(1)}, u32[]{:S(2)}, u32[]{:S(2)}) collective-permute-start(bf16[8,128,128]{2,1,0:T(8,128)(2,1)S(1)} %get-tuple-element.45.refs_0_), channel_id=1, source_target_pairs={{0,1},{1,0},{2,3},{3,2},{4,5},{5,4},{6,7},{7,6},{8,9},{9,8},{10,11... | collective-permute-start | bytes 786440 | tf_op jit(solution)/shard_map/ppermute | solution.py:498
  34.9 1.7 %collective-permute-start.12 = (bf16[4,128,128]{2,1,0:T(8,128)(2,1)S(1)}, bf16[4,128,128]{2,1,0:T(8,128)(2,1)S(1)}, u32[]{:S(2)}, u32[]{:S(2)}) collective-permute-start(bf16[4,128,128]{2,1,0:T(8,128)(2,1)S(1)} %collective-permute-done.11.piece_ref.refs_4_), channel_id=1, source_target_pairs={{0,1},{1,0},{2,3},{3,2},{4,5},{5,4},{6,7},{7,6},{8,9},{9,8},{10,11... | collective-permute-start | bytes 393224 | tf_op jit(solution)/shard_map/ppermute | solution.py:498
  35.4 8.4 %copy-start = (bf16[16,4,128,128]{3,2,1,0:T(8,128)(2,1)S(1)}, bf16[16,4,128,128]{3,2,1,0:T(8,128)(2,1)}, u32[]{:S(2)}) copy-start(bf16[16,4,128,128]{3,2,1,0:T(8,128)(2,1)} %refs_8_.3) | copy-start | bytes 6291460
  35.4 7.0 %collective-permute-start.14 = (bf16[4,128,128]{2,1,0:T(8,128)(2,1)S(1)}, bf16[4,128,128]{2,1,0:T(8,128)(2,1)S(1)}, u32[]{:S(2)}, u32[]{:S(2)}) collective-permute-start(bf16[4,128,128]{2,1,0:T(8,128)(2,1)S(1)} %collective-permute-done.11.piece_ref.refs_4_), channel_id=1, source_target_pairs={{0,2},{1,3},{2,0},{3,1},{4,6},{5,7},{6,4},{7,5},{8,10},{9,11},{10,... | collective-permute-start | bytes 393224 | tf_op jit(solution)/shard_map/ppermute | solution.py:498
  41.9 1.8 %collective-permute-start.13 = (bf16[8,128,128]{2,1,0:T(8,128)(2,1)S(1)}, bf16[8,128,128]{2,1,0:T(8,128)(2,1)S(1)}, u32[]{:S(2)}, u32[]{:S(2)}) collective-permute-start(bf16[8,128,128]{2,1,0:T(8,128)(2,1)S(1)} %joined.2.refs_2_), channel_id=1, source_target_pairs={{0,1},{1,0},{2,3},{3,2},{4,5},{5,4},{6,7},{7,6},{8,9},{9,8},{10,11... | collective-permute-start | bytes 786440 | tf_op jit(solution)/shard_map/ppermute | solution.py:498
  42.4 1.3 %collective-permute-start.15 = (bf16[4,128,128]{2,1,0:T(8,128)(2,1)S(1)}, bf16[4,128,128]{2,1,0:T(8,128)(2,1)S(1)}, u32[]{:S(2)}, u32[]{:S(2)}) collective-permute-start(bf16[4,128,128]{2,1,0:T(8,128)(2,1)S(1)} %collective-permute-done.14.refs_6_), channel_id=1, source_target_pairs={{0,1},{1,0},{2,3},{3,2},{4,5},{5,4},{6,7},{7,6},{8,9},{9,8},{10,11... | collective-permute-start | bytes 393224 | tf_op jit(solution)/shard_map/ppermute | solution.py:498
  44.5 6.2 %collective-permute-start.19 = (bf16[4,128,128]{2,1,0:T(8,128)(2,1)S(1)}, bf16[4,128,128]{2,1,0:T(8,128)(2,1)S(1)}, u32[]{:S(2)}, u32[]{:S(2)}) collective-permute-start(bf16[4,128,128]{2,1,0:T(8,128)(2,1)S(1)} %get-tuple-element.49.refs_1_), channel_id=1, source_target_pairs={{4,12},{8,0},{0,4},{12,8},{5,13},{9,1},{1,5},{13,9},{6,14},{10,2},... | collective-permute-start | bytes 393224 | tf_op jit(solution)/shard_map/ppermute | solution.py:599
  46.0 6.9 %collective-permute-start.18 = (bf16[8,128,128]{2,1,0:T(8,128)(2,1)S(1)}, bf16[8,128,128]{2,1,0:T(8,128)(2,1)S(1)}, u32[]{:S(2)}, u32[]{:S(2)}) collective-permute-start(bf16[8,128,128]{2,1,0:T(8,128)(2,1)S(1)} %sweep_rest.1.refs_0_), channel_id=1, source_target_pairs={{4,8},{8,4},{5,1},{9,13},{6,10},{10,6},{7,3},{11,15},{20,24},{24,2... | collective-permute-start | bytes 786440 | tf_op jit(solution)/shard_map/ppermute | solution.py:507
  48.7 8.3 %collective-permute-start.17 = (bf16[8,128,128]{2,1,0:T(8,128)(2,1)S(1)}, bf16[8,128,128]{2,1,0:T(8,128)(2,1)S(1)}, u32[]{:S(2)}, u32[]{:S(2)}) collective-permute-start(bf16[8,128,128]{2,1,0:T(8,128)(2,1)S(1)} %sweep_rest.1.refs_0_), channel_id=1, source_target_pairs={{4,0},{8,12},{5,9},{9,5},{6,2},{10,14},{7,11},{11,7},{20,16},{24,2... | collective-permute-start | bytes 786440 | tf_op jit(solution)/shard_map/ppermute | solution.py:507
  50.7 7.0 %collective-permute-start.16 = (bf16[8,128,128]{2,1,0:T(8,128)(2,1)S(1)}, bf16[8,128,128]{2,1,0:T(8,128)(2,1)S(1)}, u32[]{:S(2)}, u32[]{:S(2)}) collective-permute-start(bf16[8,128,128]{2,1,0:T(8,128)(2,1)S(1)} %sweep_rest.1.refs_0_), channel_id=1, source_target_pairs={{0,1},{1,0},{2,3},{3,2},{4,5},{5,4},{6,7},{7,6},{8,9},{9,8},{10,11... | collective-permute-start | bytes 786440 | tf_op jit(solution)/shard_map/ppermute | solution.py:498
  50.8 6.3 %collective-permute-start.20 = (bf16[4,128,128]{2,1,0:T(8,128)(2,1)S(1)}, bf16[4,128,128]{2,1,0:T(8,128)(2,1)S(1)}, u32[]{:S(2)}, u32[]{:S(2)}) collective-permute-start(bf16[4,128,128]{2,1,0:T(8,128)(2,1)S(1)} %collective-permute-done.19.piece_ref.refs_4_), channel_id=1, source_target_pairs={{0,1},{1,0},{2,3},{3,2},{4,5},{5,4},{6,7},{7,6},{8,9},{9,8},{10,11... | collective-permute-start | bytes 393224 | tf_op jit(solution)/shard_map/ppermute | solution.py:498
  51.2 6.0 %collective-permute-start.22 = (bf16[4,128,128]{2,1,0:T(8,128)(2,1)S(1)}, bf16[4,128,128]{2,1,0:T(8,128)(2,1)S(1)}, u32[]{:S(2)}, u32[]{:S(2)}) collective-permute-start(bf16[4,128,128]{2,1,0:T(8,128)(2,1)S(1)} %collective-permute-done.19.piece_ref.refs_4_), channel_id=1, source_target_pairs={{0,2},{1,3},{2,0},{3,1},{4,6},{5,7},{6,4},{7,5},{8,10},{9,11},{10,... | collective-permute-start | bytes 393224 | tf_op jit(solution)/shard_map/ppermute | solution.py:498
  57.1 1.8 %collective-permute-start.21 = (bf16[8,128,128]{2,1,0:T(8,128)(2,1)S(1)}, bf16[8,128,128]{2,1,0:T(8,128)(2,1)S(1)}, u32[]{:S(2)}, u32[]{:S(2)}) collective-permute-start(bf16[8,128,128]{2,1,0:T(8,128)(2,1)S(1)} %joined.3.refs_2_), channel_id=1, source_target_pairs={{0,1},{1,0},{2,3},{3,2},{4,5},{5,4},{6,7},{7,6},{8,9},{9,8},{10,11... | collective-permute-start | bytes 786440 | tf_op jit(solution)/shard_map/ppermute | solution.py:498
  57.2 1.7 %collective-permute-start.23 = (bf16[4,128,128]{2,1,0:T(8,128)(2,1)S(1)}, bf16[4,128,128]{2,1,0:T(8,128)(2,1)S(1)}, u32[]{:S(2)}, u32[]{:S(2)}) collective-permute-start(bf16[4,128,128]{2,1,0:T(8,128)(2,1)S(1)} %collective-permute-done.22.refs_6_), channel_id=1, source_target_pairs={{0,1},{1,0},{2,3},{3,2},{4,5},{5,4},{6,7},{7,6},{8,9},{9,8},{10,11... | collective-permute-start | bytes 393224 | tf_op jit(solution)/shard_map/ppermute | solution.py:498
  61.5 3.0 %collective-permute-start.24 = (f32[8,128,128]{2,1,0:T(8,128)S(1)}, f32[8,128,128]{2,1,0:T(8,128)S(1)}, u32[]{:S(2)}, u32[]{:S(2)}) collective-permute-start(f32[8,128,128]{2,1,0:T(8,128)S(1)} %get-tuple-element.50.amps_ref), channel_id=1, source_target_pairs={{0,1},{1,0},{2,3},{3,2},{4,5},{5,4},{6,7},{7,6},{8,9},{9,8},{10,11... | collective-permute-start | bytes 1572872 | tf_op jit(solution)/shard_map/ppermute | solution.py:498
  61.7 5.2 %collective-permute-start.25 = (bf16[2,128,128]{2,1,0:T(8,128)(2,1)S(1)}, bf16[2,128,128]{2,1,0:T(8,128)(2,1)S(1)}, u32[]{:S(2)}, u32[]{:S(2)}) collective-permute-start(bf16[2,128,128]{2,1,0:T(8,128)(2,1)S(1)} %get-tuple-element.54), channel_id=1, source_target_pairs={{0,4},{4,0},{8,12},{12,8},{1,5},{5,1},{9,13},{13,9},{2,6},{6,2},{1... | collective-permute-start | bytes 196616 | tf_op jit(solution)/shard_map/ppermute | solution.py:503
  61.9 5.0 %collective-permute-start.26 = (bf16[2,128,128]{2,1,0:T(8,128)(2,1)S(1)}, bf16[2,128,128]{2,1,0:T(8,128)(2,1)S(1)}, u32[]{:S(2)}, u32[]{:S(2)}) collective-permute-start(bf16[2,128,128]{2,1,0:T(8,128)(2,1)S(1)} %get-tuple-element.55), channel_id=1, source_target_pairs={{4,8},{8,4},{5,9},{9,5},{6,10},{10,6},{7,11},{11,7},{20,24},{24,20... | collective-permute-start | bytes 196616 | tf_op jit(solution)/shard_map/ppermute | solution.py:503
  66.9 2.6 %collective-permute-start.27 = (f32[2,128,128]{2,1,0:T(8,128)S(1)}, f32[2,128,128]{2,1,0:T(8,128)S(1)}, u32[]{:S(2)}, u32[]{:S(2)}) collective-permute-start(f32[2,128,128]{2,1,0:T(8,128)S(1)} %convert_add_fusion), channel_id=1, source_target_pairs={{0,1},{1,0},{2,3},{3,2},{4,5},{5,4},{6,7},{7,6},{8,9},{9,8},{10,11... | collective-permute-start | bytes 393224 | tf_op jit(solution)/shard_map/ppermute | solution.py:498
